TPU v7x, 32 devices: a whole 2x2x4 slice. The times are simulated.
32 devices in a mesh: dp: 16 (over z, x, core), mp: 2 (over y).
Axes of the slice: x: 2, y: 2, z: 4, core: 2. Of those that a mesh axis runs over, the one named last changes fastest.
Arguments:
- tokens: bfloat16 [2, 16, 1280, 1024], P(None, 'dp', 'mp'), may hold values from -6 to 6
- cotangent: bfloat16 [2, 16, 1280, 1024], P(None, 'dp', 'mp'), may hold values from -6 to 6
- patch_count: int32 [2, 16], P(None, 'dp'), may hold values from 256 to 576, as said below
- first_gain: float32 [1024], replicated, may hold values from 0.25 to 1.75
- first_shift: float32 [1024], replicated, may hold values from -1.75 to 1.75
- heads_weight: bfloat16 [1024, 3, 1024], P(None, None, 'mp'), may hold values from -0.1875 to 0.1875
- heads_bias: float32 [3, 1024], P(None, 'mp'), may hold values from -1.75 to 1.75
- merge_weight: bfloat16 [1024, 1024], P('mp'), may hold values from -3 to 3
- merge_bias: float32 [1024], replicated, may hold values from -1.75 to 1.75
- second_gain: float32 [1024], replicated, may hold values from 0.25 to 1.75
- second_shift: float32 [1024], replicated, may hold values from -1.75 to 1.75
- expand_weight: bfloat16 [1024, 4096], P(None, 'mp'), may hold values from -0.1875 to 0.1875
- expand_bias: float32 [4096], P('mp'), may hold values from -3 to 3
- reduce_weight: bfloat16 [4096, 1024], P('mp'), may hold values from -0.09375 to 0.09375
- reduce_bias: float32 [1024], replicated, may hold values from -1.75 to 1.75
Outputs:
- layer_out: bfloat16 [2, 16, 1280, 1024], P(None, 'dp', 'mp')
- tokens_grad: float32 [2, 16, 1280, 1024], P(None, 'dp', 'mp')
- first_gain_grad: float32 [1024], replicated
- first_shift_grad: float32 [1024], replicated
- heads_weight_grad: float32 [1024, 3, 1024], P(None, None, 'mp')
- heads_bias_grad: float32 [3, 1024], P(None, 'mp')
- merge_weight_grad: float32 [1024, 1024], P('mp')
- merge_bias_grad: float32 [1024], replicated
- second_gain_grad: float32 [1024], replicated
- second_shift_grad: float32 [1024], replicated
- expand_weight_grad: float32 [1024, 4096], P(None, 'mp')
- expand_bias_grad: float32 [4096], P('mp')
- reduce_weight_grad: float32 [4096, 1024], P('mp')
- reduce_bias_grad: float32 [1024], replicated
Inputs may be any that keep to these rules, and one draw needn't show every extreme that they name: `patch_count`: each entry is 256 or 576, and exactly half of the entries are each.
All inputs are finite; a program needn't handle non-finite values.
Results may differ from a plain program's by a relative error of at most 0.017.
Values may be sent and summed in bfloat16 or wider, within the bound.
No kernel may reach another device: no remote copies, remote signals or barrier semaphores. Data moves between devices by JAX's collectives and lax.ppermute only.
A program may use at most 320 MiB of HBM per device.

v0:
```python
import math

import jax
import jax.numpy as jnp
from jax import lax
from jax.sharding import PartitionSpec as P

HEAD_DIM = 64
FRAMES = 2
SIDE_SMALL = 16
SIDE_LARGE = 24


EPSILON = 1e-06
MASKED = -1e30
ROOT_HALF = 0.7071067811865476
GAUSS_NORM = 0.3989422804014327


def slot_layout(count_one, length):
    large_count = SIDE_LARGE * SIDE_LARGE
    grid_side = jnp.where(count_one == large_count, SIDE_LARGE, SIDE_SMALL).astype(jnp.int32)
    frame_len = grid_side * grid_side + 2
    clip_len = FRAMES * frame_len
    clip_total = jnp.where(count_one == large_count, 1, 2).astype(jnp.int32)
    slot_id = jnp.arange(length, dtype=jnp.int32)
    clip_id = jnp.minimum(slot_id // clip_len, clip_total)
    offset_in = slot_id - clip_id * clip_len
    frame_id = offset_in // frame_len
    place_in = offset_in - frame_id * frame_len - 2
    patch_id = jnp.maximum(place_in, 0)
    is_live = clip_id < clip_total
    is_patch = is_live & (place_in >= 0)
    frame_id = jnp.where(is_live, frame_id, 0)
    patch_row = jnp.where(is_patch, patch_id // grid_side, 0)
    column = jnp.where(is_patch, patch_id - patch_id // grid_side * grid_side, 0)
    return (clip_id, frame_id, patch_row, column)


def rotary_tables(frame_id, patch_row, column, head_width):
    segment = 2 * (head_width // 3 // 2)
    half_width = segment // 2
    dim_index = jnp.arange(head_width, dtype=jnp.int32)
    segment_id = dim_index // segment
    exponent = (dim_index % segment % half_width).astype(jnp.float32)
    frequency = jnp.exp(exponent * (-math.log(10000.0) / half_width))
    position = (
        jnp.where(segment_id == 0, 1.0, 0.0).astype(jnp.float32)[None, :]
        * frame_id[:, None].astype(jnp.float32)
        + jnp.where(segment_id == 1, 1.0, 0.0).astype(jnp.float32)[None, :]
        * patch_row[:, None].astype(jnp.float32)
        + jnp.where(segment_id == 2, 1.0, 0.0).astype(jnp.float32)[None, :]
        * column[:, None].astype(jnp.float32)
    )
    angles = position * frequency[None, :]
    return (jnp.cos(angles)[:, None, :], jnp.sin(angles)[:, None, :])


def partner(values_in):
    head_width = values_in.shape[-1]
    segment = 2 * (head_width // 3 // 2)
    half_width = segment // 2
    pieces_out = []
    for number in range(3):
        offset = number * segment
        pieces_out.append(-values_in[..., offset + half_width : offset + segment])
        pieces_out.append(values_in[..., offset : offset + half_width])
    pieces_out.append(jnp.zeros_like(values_in[..., 3 * segment :]))
    return jnp.concatenate(pieces_out, -1)


def rotate(values_in, cos_table, sin_table):
    return values_in * cos_table + partner(values_in) * sin_table


def unrotate(grad_in, cos_table, sin_table):
    return grad_in * cos_table - partner(grad_in * sin_table)


def standardize(values_in):
    row_mean = jnp.mean(values_in, -1, keepdims=True)
    centred = values_in - row_mean
    norm_scale = lax.rsqrt(jnp.mean(centred * centred, -1, keepdims=True) + EPSILON)
    return (centred * norm_scale, norm_scale)


def norm_back(grad_in, normed, norm_scale):
    return norm_scale * (
        grad_in
        - jnp.mean(grad_in, -1, keepdims=True)
        - normed * jnp.mean(grad_in * normed, -1, keepdims=True)
    )


def column_sums(matrix):
    unit_column = jnp.ones((matrix.shape[0],), matrix.dtype)
    flattened = matrix.reshape(matrix.shape[0], -1)
    return jnp.dot(unit_column, flattened, preferred_element_type=jnp.float32).reshape(
        matrix.shape[1:]
    )


def gelu_slope(values_in):
    return (
        0.5 * (1.0 + lax.erf(values_in * ROOT_HALF))
        + values_in * jnp.exp(-0.5 * values_in * values_in) * GAUSS_NORM
    )


def masked_scores(query_rows, key_rows, allowed, scale):
    scores = (
        jnp.einsum("gqd,gkd->gqk", query_rows, key_rows, preferred_element_type=jnp.float32) * scale
    )
    return jnp.where(allowed[None], scores, MASKED)


def attend(query_rows, key_rows, value_rows, allowed, scale):
    scores = masked_scores(query_rows, key_rows, allowed, scale)
    row_max = jnp.max(scores, -1, keepdims=True)
    exp_scores = jnp.exp(scores - row_max)
    row_total = jnp.sum(exp_scores, -1, keepdims=True)
    softmax_out = (exp_scores / row_total).astype(jnp.bfloat16)
    mixed_rows = jnp.einsum(
        "gqk,gkd->gqd", softmax_out, value_rows, preferred_element_type=jnp.float32
    )
    return (mixed_rows, row_max + jnp.log(row_total))


def attend_back(query_rows, key_rows, value_rows, grad_rows, log_total, allowed, scale):
    scores = masked_scores(query_rows, key_rows, allowed, scale)
    softmax_out = jnp.exp(scores - log_total)
    grad_values = jnp.einsum(
        "gqk,gqd->gkd",
        softmax_out.astype(jnp.bfloat16),
        grad_rows,
        preferred_element_type=jnp.float32,
    )
    grad_probs = jnp.einsum(
        "gqd,gkd->gqk", grad_rows, value_rows, preferred_element_type=jnp.float32
    )
    grad_scores = (
        softmax_out * (grad_probs - jnp.sum(softmax_out * grad_probs, -1, keepdims=True))
    ).astype(jnp.bfloat16)
    grad_queries = (
        jnp.einsum("gqk,gkd->gqd", grad_scores, key_rows, preferred_element_type=jnp.float32)
        * scale
    )
    grad_keys = (
        jnp.einsum("gqk,gqd->gkd", grad_scores, query_rows, preferred_element_type=jnp.float32)
        * scale
    )
    return (grad_queries, grad_keys, grad_values)


def on_device(
    tokens,
    cotangent,
    patch_count,
    first_gain,
    first_shift,
    heads_weight,
    heads_bias,
    merge_weight,
    merge_bias,
    second_gain,
    second_shift,
    expand_weight,
    expand_bias,
    reduce_weight,
    reduce_bias,
):
    micro_count = tokens.shape[0]
    head_width = HEAD_DIM
    local_width = heads_weight.shape[2]
    local_heads = local_width // head_width
    head_group = math.gcd(local_heads, 4)
    scale = head_width ** (-0.5)

    def by_group(array):
        return array.transpose(1, 0, 2).reshape(
            local_heads // head_group, head_group, array.shape[0], head_width
        )

    def by_row(array):
        return array.reshape(local_heads, array.shape[2], head_width).transpose(1, 0, 2)

    mlp_sums = (
        jnp.zeros(expand_weight.shape, jnp.float32),
        jnp.zeros(expand_bias.shape, jnp.float32),
        jnp.zeros(reduce_weight.shape, jnp.float32),
        jnp.zeros(reduce_bias.shape, jnp.float32),
    )
    attn_sums = (
        jnp.zeros(heads_weight.shape, jnp.float32),
        jnp.zeros(heads_bias.shape, jnp.float32),
        jnp.zeros(merge_weight.shape, jnp.float32),
        jnp.zeros(merge_bias.shape, jnp.float32),
    )
    norm_sums = (
        jnp.zeros(first_gain.shape, jnp.float32),
        jnp.zeros(first_shift.shape, jnp.float32),
        jnp.zeros(second_gain.shape, jnp.float32),
        jnp.zeros(second_shift.shape, jnp.float32),
    )
    outputs = []
    stream_grads = []
    for batch_index in range(micro_count):
        stream = tokens[batch_index, 0].astype(jnp.float32)
        first_norm, first_scale = standardize(stream)
        first_local = (first_norm * first_gain + first_shift).astype(jnp.bfloat16)
        first_out = lax.all_gather(first_local, "mp", axis=0, tiled=True)
        length = first_out.shape[0]
        clip_id, frame_id, patch_row, column = slot_layout(patch_count[batch_index, 0], length)
        cos_table, sin_table = rotary_tables(frame_id, patch_row, column, head_width)
        allowed = (clip_id[:, None] == clip_id[None, :]) & (frame_id[None, :] <= frame_id[:, None])
        head_proj = (
            jnp.einsum("sd,dkf->skf", first_out, heads_weight, preferred_element_type=jnp.float32)
            + heads_bias
        )
        head_proj = head_proj.reshape(length, 3, local_heads, head_width)
        queries = by_group(rotate(head_proj[:, 0], cos_table, sin_table).astype(jnp.bfloat16))
        keys = by_group(rotate(head_proj[:, 1], cos_table, sin_table).astype(jnp.bfloat16))
        values = by_group(head_proj[:, 2].astype(jnp.bfloat16))
        mixed_heads, log_total = lax.map(
            lambda pieces: attend(pieces[0], pieces[1], pieces[2], allowed, scale),
            (queries, keys, values),
        )
        mixed_heads = by_row(mixed_heads).reshape(length, local_width).astype(jnp.bfloat16)
        branch_one = lax.psum_scatter(
            jnp.dot(mixed_heads, merge_weight, preferred_element_type=jnp.float32).astype(
                jnp.bfloat16
            ),
            "mp",
            scatter_dimension=0,
            tiled=True,
        ).astype(jnp.float32)
        residual = stream + (branch_one + merge_bias)
        second_norm, second_scale = standardize(residual)
        second_local = (second_norm * second_gain + second_shift).astype(jnp.bfloat16)
        second_out = lax.all_gather(second_local, "mp", axis=0, tiled=True)
        pre_gelu = (
            jnp.dot(second_out, expand_weight, preferred_element_type=jnp.float32) + expand_bias
        )
        active = jax.nn.gelu(pre_gelu, approximate=False).astype(jnp.bfloat16)
        branch_two = lax.psum_scatter(
            jnp.dot(active, reduce_weight, preferred_element_type=jnp.float32).astype(jnp.bfloat16),
            "mp",
            scatter_dimension=0,
            tiled=True,
        ).astype(jnp.float32)
        outputs.append((residual + (branch_two + reduce_bias)).astype(jnp.bfloat16))
        grad_out = cotangent[batch_index, 0].astype(jnp.float32)
        grad_two = lax.all_gather(grad_out.astype(jnp.bfloat16), "mp", axis=0, tiled=True)
        grad_reduce_bias = column_sums(grad_two)
        grad_reduce_weight = jnp.einsum(
            "sf,sd->fd", active, grad_two, preferred_element_type=jnp.float32
        )
        grad_active = jnp.einsum(
            "sd,fd->sf", grad_two, reduce_weight, preferred_element_type=jnp.float32
        )
        grad_pre = (grad_active * gelu_slope(pre_gelu)).astype(jnp.bfloat16)
        grad_expand_bias = column_sums(grad_pre)
        grad_expand_weight = jnp.einsum(
            "sd,sf->df", second_out, grad_pre, preferred_element_type=jnp.float32
        )
        mlp_sums = (
            mlp_sums[0] + grad_expand_weight,
            mlp_sums[1] + grad_expand_bias,
            mlp_sums[2] + grad_reduce_weight,
            mlp_sums[3] + grad_reduce_bias,
        )
        grad_second = lax.psum_scatter(
            jnp.einsum(
                "sf,df->sd", grad_pre, expand_weight, preferred_element_type=jnp.float32
            ).astype(jnp.bfloat16),
            "mp",
            scatter_dimension=0,
            tiled=True,
        ).astype(jnp.float32)
        second_gain_term = jnp.sum(grad_second * second_norm, 0)
        second_shift_term = jnp.sum(grad_second, 0)
        grad_residual = grad_out + norm_back(grad_second * second_gain, second_norm, second_scale)
        grad_one = lax.all_gather(grad_residual.astype(jnp.bfloat16), "mp", axis=0, tiled=True)
        grad_merge_bias = column_sums(grad_one)
        grad_merge_weight = jnp.einsum(
            "sf,sd->fd", mixed_heads, grad_one, preferred_element_type=jnp.float32
        )
        grad_mixed = jnp.einsum(
            "sd,fd->sf", grad_one, merge_weight, preferred_element_type=jnp.float32
        )
        grad_mixed = by_group(
            grad_mixed.astype(jnp.bfloat16).reshape(length, local_heads, head_width)
        )
        grad_queries, grad_keys, grad_values = lax.map(
            lambda pieces: attend_back(
                pieces[0], pieces[1], pieces[2], pieces[3], pieces[4], allowed, scale
            ),
            (queries, keys, values, grad_mixed, log_total),
        )
        grad_heads = jnp.stack(
            [
                unrotate(by_row(grad_queries), cos_table, sin_table),
                unrotate(by_row(grad_keys), cos_table, sin_table),
                by_row(grad_values),
            ],
            1,
        )
        grad_heads = grad_heads.reshape(length, 3, local_width).astype(jnp.bfloat16)
        grad_heads_bias = column_sums(grad_heads)
        grad_heads_weight = jnp.einsum(
            "sd,skf->dkf", first_out, grad_heads, preferred_element_type=jnp.float32
        )
        attn_sums = (
            attn_sums[0] + grad_heads_weight,
            attn_sums[1] + grad_heads_bias,
            attn_sums[2] + grad_merge_weight,
            attn_sums[3] + grad_merge_bias,
        )
        grad_first = lax.psum_scatter(
            jnp.einsum(
                "skf,dkf->sd", grad_heads, heads_weight, preferred_element_type=jnp.float32
            ).astype(jnp.bfloat16),
            "mp",
            scatter_dimension=0,
            tiled=True,
        ).astype(jnp.float32)
        norm_sums = (
            norm_sums[0] + jnp.sum(grad_first * first_norm, 0),
            norm_sums[1] + jnp.sum(grad_first, 0),
            norm_sums[2] + second_gain_term,
            norm_sums[3] + second_shift_term,
        )
        stream_grads.append(
            grad_residual + norm_back(grad_first * first_gain, first_norm, first_scale)
        )
    summed = lax.psum(
        (
            mlp_sums[0],
            mlp_sums[1],
            mlp_sums[2],
            mlp_sums[3],
            attn_sums[0],
            attn_sums[1],
            attn_sums[2],
            attn_sums[3],
        ),
        "dp",
    )
    mlp_sums = summed[:4]
    attn_sums = summed[4:]
    norm_totals = lax.psum((norm_sums[0], norm_sums[1], norm_sums[2], norm_sums[3]), ("dp", "mp"))
    return (
        jnp.stack(outputs)[:, None],
        jnp.stack(stream_grads)[:, None],
        norm_totals[0],
        norm_totals[1],
        attn_sums[0],
        attn_sums[1],
        attn_sums[2],
        attn_sums[3],
        norm_totals[2],
        norm_totals[3],
        mlp_sums[0],
        mlp_sums[1],
        mlp_sums[2],
        mlp_sums[3],
    )


def solution(mesh):
    return jax.shard_map(
        on_device,
        mesh=mesh,
        in_specs=(
            P(None, "dp", "mp", None),
            P(None, "dp", "mp", None),
            P(None, "dp"),
            P(),
            P(),
            P(None, None, "mp"),
            P(None, "mp"),
            P("mp", None),
            P(),
            P(),
            P(),
            P(None, "mp"),
            P("mp"),
            P("mp", None),
            P(),
        ),
        out_specs=(
            P(None, "dp", "mp", None),
            P(None, "dp", "mp", None),
            P(),
            P(),
            P(None, None, "mp"),
            P(None, "mp"),
            P("mp", None),
            P(),
            P(),
            P(),
            P(None, "mp"),
            P("mp"),
            P("mp", None),
            P(),
        ),
        check_vma=False,
    )
```

profile of v0, /device:TPU:0, one launch (start us, length us, event | category | flops | bytes accessed | tf_op | source)
XLA Modules:
  0.0 1885.8 jit_solution(1667103855893519252)
XLA Ops:
  28.6 26.4 %all-gather.11.cloned.1.call-done = bf16[1280,1024]{1,0:T(8,128)(2,1)} async-done(((bf16[640,1024]{1,0:T(8,128)(2,1)}), bf16[1280,1024]{1,0:T(8,128)(2,1)}) %all-gather.11.cloned.1.call-update) | async-done | bytes 2621456 | tf_op jit(solution)/shard_map/all_gather | solution.py:211
  68.1 28.1 %all-gather.15.cloned.1.call-done = bf16[1280,1024]{1,0:T(8,128)(2,1)} async-done(((bf16[640,1024]{1,0:T(8,128)(2,1)}), bf16[1280,1024]{1,0:T(8,128)(2,1)}) %all-gather.15.cloned.1.call-update) | async-done | bytes 2621456 | tf_op jit(solution)/shard_map/all_gather | solution.py:211
  113.4 28.7 %concatenate.27 = f32[1280,8,64]{0,2,1:T(8,128)} concatenate(f32[1280,8,10]{0,2,1:T(8,128)} %get-tuple-element.521, f32[1280,8,10]{0,2,1:T(8,128)} %get-tuple-element.520, f32[1280,8,10]{0,2,1:T(8,128)} %get-tuple-element.519, f32[1280,8,10]{0,2,1:T(8,128)} %get-tuple-element.518, f32[1280,8,10]{0,2,1:T(8,128)} %get-tuple-element.517, f32[1280,8,10]{0,2,1:T(8,128)} %get-tuple-element.516, ...), dimensions={2} | concatenate | bytes 5242880 | tf_op jit(solution)/shard_map/concatenate | solution.py:69
  142.1 28.9 %concatenate.26 = f32[1280,8,64]{0,2,1:T(8,128)} concatenate(f32[1280,8,10]{0,2,1:T(8,128)} %get-tuple-element.527, f32[1280,8,10]{0,2,1:T(8,128)} %get-tuple-element.526, f32[1280,8,10]{0,2,1:T(8,128)} %get-tuple-element.525, f32[1280,8,10]{0,2,1:T(8,128)} %get-tuple-element.524, f32[1280,8,10]{0,2,1:T(8,128)} %get-tuple-element.523, f32[1280,8,10]{0,2,1:T(8,128)} %get-tuple-element.522, ...), dimensions={2} | concatenate | bytes 5242880 | tf_op jit(solution)/shard_map/concatenate | solution.py:69
  177.7 74.2 %while.56 = (s32[]{:T(128)}, bf16[2,4,1280,64]{2,3,1,0:T(8,128)(2,1)}, f32[2,4,1280,1]{2,1,3,0:T(4,128)S(1)}, bf16[2,4,1280,64]{2,3,1,0:T(8,128)(2,1)}, bf16[2,4...) while((s32[]{:T(128)}, ...), condition=%wide.region_5.6_spmd.clone, body=%wide.region_2.5_spmd.clone.sunk | while | flops 1735060480 | bytes 101101760 | solution.py:224
  263.4 29.1 %concatenate.29 = f32[1280,8,64]{0,2,1:T(8,128)} concatenate(f32[1280,8,10]{0,2,1:T(8,128)} %get-tuple-element.509, f32[1280,8,10]{0,2,1:T(8,128)} %get-tuple-element.508, f32[1280,8,10]{0,2,1:T(8,128)} %get-tuple-element.507, f32[1280,8,10]{0,2,1:T(8,128)} %get-tuple-element.506, f32[1280,8,10]{0,2,1:T(8,128)} %get-tuple-element.505, f32[1280,8,10]{0,2,1:T(8,128)} %get-tuple-element.504, ...), dimensions={2} | concatenate | bytes 5242880 | tf_op jit(solution)/shard_map/concatenate | solution.py:69
  292.5 28.7 %concatenate.28 = f32[1280,8,64]{0,2,1:T(8,128)} concatenate(f32[1280,8,10]{0,2,1:T(8,128)} %get-tuple-element.515, f32[1280,8,10]{0,2,1:T(8,128)} %get-tuple-element.514, f32[1280,8,10]{0,2,1:T(8,128)} %get-tuple-element.513, f32[1280,8,10]{0,2,1:T(8,128)} %get-tuple-element.512, f32[1280,8,10]{0,2,1:T(8,128)} %get-tuple-element.511, f32[1280,8,10]{0,2,1:T(8,128)} %get-tuple-element.510, ...), dimensions={2} | concatenate | bytes 5242880 | tf_op jit(solution)/shard_map/concatenate | solution.py:69
  328.0 74.0 %while.57 = (s32[]{:T(128)}, bf16[2,4,1280,64]{2,3,1,0:T(8,128)(2,1)}, f32[2,4,1280,1]{2,1,3,0:T(4,128)S(1)}, bf16[2,4,1280,64]{2,3,1,0:T(8,128)(2,1)}, bf16[2,4...) while((s32[]{:T(128)}, ...), condition=%wide.region_15.16_spmd.clone, body=%wide.region_12.15_spmd.clone.sunk | while | flops 1735060480 | bytes 101101760 | solution.py:224
  406.9 37.4 %reduce-scatter.13.cloned.1.call-done = bf16[640,1024]{1,0:T(8,128)(2,1)} async-done(((bf16[1280,1024]{1,0:T(8,128)(2,1)}), bf16[640,1024]{1,0:T(8,128)(2,1)}) %reduce-scatter.13.cloned.1.call-update) | async-done | bytes 1310736 | tf_op jit(solution)/shard_map/reduce_scatter | solution.py:229
  457.6 34.1 %all-gather.17.cloned.1.call-done = bf16[1280,1024]{1,0:T(8,128)(2,1)} async-done(((bf16[640,1024]{1,0:T(8,128)(2,1)}), bf16[1280,1024]{1,0:T(8,128)(2,1)}) %all-gather.17.cloned.1.call-update) | async-done | bytes 2621456 | tf_op jit(solution)/shard_map/all_gather | solution.py:240
  502.3 30.4 %all-gather.25.cloned.1.call-done = bf16[1,1,1280,1024]{3,2,1,0:T(8,128)(2,1)} async-done(((bf16[1,1,640,1024]{3,2,1,0:T(8,128)(2,1)}), bf16[1,1,1280,1024]{3,2,1,0:T(8,128)(2,1)}) %all-gather.25.cloned.1.call-update) | async-done | bytes 2621456 | tf_op jit(solution)/shard_map/all_gather | solution.py:253
  573.9 53.4 %fusion.106 = (bf16[1280,2048]{1,0:T(8,128)(2,1)}, bf16[1280,2048]{1,0:T(8,128)(2,1)}, f32[1280,2048]{1,0:T(8,128)}) fusion(f32[2048]{0:T(1024)S(1)} %copy-done.95, f32[1280,2048]{1,0:T(8,128)} %fusion.271, bf16[1280,1024]{1,0:T(8,128)(2,1)} %all-gather.13.cloned.1.call-done, bf16[1024,2048]{1,0:T(8,128)(2,1)} %param.34), kind=kOutput, calls=%fused_computation.122 | convolution fusion | flops 5714739200 | bytes 38281216 | tf_op jit(solution)/shard_map/dot_general | solution.py:242
  672.3 23.6 %reduce-scatter.17.cloned.1.call-done = bf16[640,1024]{1,0:T(8,128)(2,1)} async-done(((bf16[1280,1024]{1,0:T(8,128)(2,1)}), bf16[640,1024]{1,0:T(8,128)(2,1)}) %reduce-scatter.17.cloned.1.call-update) | async-done | bytes 1310736 | tf_op jit(solution)/shard_map/reduce_scatter | solution.py:272
  695.9 40.5 %reduce-scatter.11.cloned.1.call-done = bf16[640,1024]{1,0:T(8,128)(2,1)} async-done(((bf16[1280,1024]{1,0:T(8,128)(2,1)}), bf16[640,1024]{1,0:T(8,128)(2,1)}) %reduce-scatter.11.cloned.1.call-update) | async-done | bytes 1310736 | tf_op jit(solution)/shard_map/reduce_scatter | solution.py:245
  736.4 39.8 %reduce-scatter.15.cloned.1.call-done = bf16[640,1024]{1,0:T(8,128)(2,1)} async-done(((bf16[1280,1024]{1,0:T(8,128)(2,1)}), bf16[640,1024]{1,0:T(8,128)(2,1)}) %reduce-scatter.15.cloned.1.call-update) | async-done | bytes 1310736 | tf_op jit(solution)/shard_map/reduce_scatter | solution.py:245
  836.9 174.4 %while.59 = (s32[]{:T(128)}, f32[2,4,1280,64]{2,3,1,0:T(8,128)}, f32[2,4,1280,64]{2,3,1,0:T(8,128)}, bf16[2,4,1280,64]{2,3,1,0:T(8,128)(2,1)}, bf16[2,4,1280,64]...) while((s32[]{:T(128)}, f32[2,4,1280,64]{2,3,1,0:T(8,128)}, ...), condition=%wide.region_34.35_spmd.clone, body=%wide.region_32.34_spmd.clone.sunk | while | flops 4258851840 | bytes 213765296 | solution.py:294
  1020.6 28.7 %concatenate.33 = f32[1280,8,64]{0,2,1:T(8,128)} concatenate(f32[1280,8,10]{0,2,1:T(8,128)} %get-tuple-element.501, f32[1280,8,10]{0,2,1:T(8,128)} %get-tuple-element.500, f32[1280,8,10]{0,2,1:T(8,128)} %get-tuple-element.499, f32[1280,8,10]{0,2,1:T(8,128)} %get-tuple-element.498, f32[1280,8,10]{0,2,1:T(8,128)} %get-tuple-element.497, f32[1280,8,10]{0,2,1:T(8,128)} %get-tuple-element.496, ...), dimensions={2} | concatenate | bytes 5242880 | tf_op jit(solution)/shard_map/concatenate | solution.py:69
  1049.3 28.7 %concatenate.32 = f32[1280,8,64]{0,2,1:T(8,128)} concatenate(f32[1280,8,10]{0,2,1:T(8,128)} %get-tuple-element.495, f32[1280,8,10]{0,2,1:T(8,128)} %get-tuple-element.494, f32[1280,8,10]{0,2,1:T(8,128)} %get-tuple-element.493, f32[1280,8,10]{0,2,1:T(8,128)} %get-tuple-element.492, f32[1280,8,10]{0,2,1:T(8,128)} %get-tuple-element.491, f32[1280,8,10]{0,2,1:T(8,128)} %get-tuple-element.490, ...), dimensions={2} | concatenate | bytes 5242880 | tf_op jit(solution)/shard_map/concatenate | solution.py:69
  1107.4 173.2 %while.58 = (s32[]{:T(128)}, f32[2,4,1280,64]{2,3,1,0:T(8,128)}, f32[2,4,1280,64]{2,3,1,0:T(8,128)}, bf16[2,4,1280,64]{2,3,1,0:T(8,128)(2,1)}, bf16[2,4,1280,64]...) while((s32[]{:T(128)}, f32[2,4,1280,64]{2,3,1,0:T(8,128)}, ...), condition=%wide.region_25.26_spmd.clone, body=%wide.region_23.25_spmd.clone.sunk | while | flops 4258851840 | bytes 213765296 | solution.py:294
  1289.6 28.7 %concatenate.31 = f32[1280,8,64]{0,2,1:T(8,128)} concatenate(f32[1280,8,10]{0,2,1:T(8,128)} %get-tuple-element.485, f32[1280,8,10]{0,2,1:T(8,128)} %get-tuple-element.484, f32[1280,8,10]{0,2,1:T(8,128)} %get-tuple-element.483, f32[1280,8,10]{0,2,1:T(8,128)} %get-tuple-element.482, f32[1280,8,10]{0,2,1:T(8,128)} %get-tuple-element.481, f32[1280,8,10]{0,2,1:T(8,128)} %get-tuple-element.480, ...), dimensions={2} | concatenate | bytes 5242880 | tf_op jit(solution)/shard_map/concatenate | solution.py:69
  1322.8 28.7 %concatenate.30 = f32[1280,8,64]{0,2,1:T(8,128)} concatenate(f32[1280,8,10]{0,2,1:T(8,128)} %get-tuple-element.479, f32[1280,8,10]{0,2,1:T(8,128)} %get-tuple-element.478, f32[1280,8,10]{0,2,1:T(8,128)} %get-tuple-element.477, f32[1280,8,10]{0,2,1:T(8,128)} %get-tuple-element.476, f32[1280,8,10]{0,2,1:T(8,128)} %get-tuple-element.475, f32[1280,8,10]{0,2,1:T(8,128)} %get-tuple-element.474, ...), dimensions={2} | concatenate | bytes 5242880 | tf_op jit(solution)/shard_map/concatenate | solution.py:69
  1442.0 64.8 %all-reduce.1 = (f32[3,512]{1,0:T(4,128)}, f32[1024]{0:T(1024)}, f32[2048]{0:T(1024)}, f32[1024]{0:T(1024)}) all-reduce(f32[3,512]{1,0:T(4,128)S(1)} %bitcast_add_fusion, f32[1024]{0:T(1024)S(1)} %add.532, f32[2048]{0:T(1024)S(1)} %add.536, f32[1024]{0:T(1024)S(1)} %add.538), channel_id=1, replica_groups=mesh['dp'=16,'mp'=2] {'dp'}, use_global_device_ids=true, to_apply=%region_45.46 | all-reduce | flops 5632 | bytes 45056 | tf_op jit(solution)/shard_map/psum | solution.py:336
  1511.7 38.8 %all-reduce = (f32[1024]{0:T(1024)}, f32[1024]{0:T(1024)}, f32[1024]{0:T(1024)}, f32[1024]{0:T(1024)}) all-reduce(f32[1024]{0:T(1024)S(1)} %add.527, f32[1024]{0:T(1024)S(1)} %add.528, f32[1024]{0:T(1024)S(1)} %add.533, f32[1024]{0:T(1024)S(1)} %add.534), channel_id=1, replica_groups=mesh['dp'=16,'mp'=2] {'dp','mp'}, use_global_device_ids=true, to_apply=%region_40.41 | all-reduce | flops 4096 | bytes 32768 | tf_op jit(solution)/shard_map/psum | solution.py:351
  1558.8 302.4 %all-reduce.5.cloned.1.call-done = (f32[1024,3,512]{2,0,1:T(8,128)}, f32[512,1024]{1,0:T(8,128)}, f32[1024,2048]{1,0:T(8,128)}, f32[2048,1024]{1,0:T(8,128)}) async-done(((f32[1024,3,512]{2,0,1:T(8,128)}, f32[512,1024]{1,0:T(8,128)}, f32[1024,2048]{1,0:T(8,128)}, f32[2048,1024]{1,0:T(8,128)}), (f32[1024,3,512]{2,0,1:T(8,128)}, f32[512,1024]{1,0:T(8,128)}, f32[1024,2048]{1,0:T(8,128)}, ...) | async-done | bytes 25165840 | tf_op jit(solution)/shard_map/psum | solution.py:336
  (427 shorter events, 918.1 us)
Async XLA Ops:
  7.2 47.8 %all-gather.11.cloned.1.call-start = ((), (), s32[]{:S(2)}) async-start(), calls=%async_computation.8 | async-start | bytes 3932160 | tf_op jit(solution)/shard_map/all_gather | solution.py:211
  13.1 83.1 %all-gather.15.cloned.1.call-start = ((), (), s32[]{:S(2)}) async-start(), calls=%async_computation.12 | async-start | bytes 3932160 | tf_op jit(solution)/shard_map/all_gather | solution.py:211
  13.9 393.0 %reduce-scatter.9.cloned.1.call-start = ((), (), s32[]{:S(2)}) async-start(), calls=%async_computation.9 | async-start | bytes 3932160 | tf_op jit(solution)/shard_map/reduce_scatter | solution.py:229
  256.7 187.6 %reduce-scatter.13.cloned.1.call-start = ((), (), s32[]{:S(2)}) async-start(), calls=%async_computation.13 | async-start | bytes 3932160 | tf_op jit(solution)/shard_map/reduce_scatter | solution.py:229
  406.6 85.1 %all-gather.17.cloned.1.call-start = ((), (), s32[]{:S(2)}) async-start(), calls=%async_computation.14 | async-start | bytes 3932160 | tf_op jit(solution)/shard_map/all_gather | solution.py:240
  452.5 80.2 %all-gather.25.cloned.1.call-start = ((), (), s32[]{:S(2)}) async-start(), calls=%async_computation.23 | async-start | bytes 3932160 | tf_op jit(solution)/shard_map/all_gather | solution.py:253
  456.0 117.9 %all-gather.13.cloned.1.call-start = ((), (), s32[]{:S(2)}) async-start(), calls=%async_computation.10 | async-start | bytes 3932160 | tf_op jit(solution)/shard_map/all_gather | solution.py:240
  456.8 170.6 %all-gather.23.cloned.1.call-start = ((), (), s32[]{:S(2)}) async-start(), calls=%async_computation.22 | async-start | bytes 3932160 | tf_op jit(solution)/shard_map/all_gather | solution.py:253
  457.5 214.8 %reduce-scatter.21.cloned.1.call-start = ((), (), s32[]{:S(2)}) async-start(), calls=%async_computation.19 | async-start | bytes 3932160 | tf_op jit(solution)/shard_map/reduce_scatter | solution.py:272
  555.1 140.8 %reduce-scatter.17.cloned.1.call-start = ((), (), s32[]{:S(2)}) async-start(), calls=%async_computation.16 | async-start | bytes 3932160 | tf_op jit(solution)/shard_map/reduce_scatter | solution.py:272
  649.9 86.4 %reduce-scatter.11.cloned.1.call-start = ((), (), s32[]{:S(2)}) async-start(), calls=%async_computation.11 | async-start | bytes 3932160 | tf_op jit(solution)/shard_map/reduce_scatter | solution.py:245
  659.8 116.4 %reduce-scatter.15.cloned.1.call-start = ((), (), s32[]{:S(2)}) async-start(), calls=%async_computation.15 | async-start | bytes 3932160 | tf_op jit(solution)/shard_map/reduce_scatter | solution.py:245
  669.7 106.5 %copy-start.65 = (f32[640]{0:T(1024)S(1)}, f32[640]{0:T(1024)}, u32[]{:S(2)}) copy-start(f32[640]{0:T(1024)} %copy-done.64) | copy-start | bytes 7684
  669.7 106.5 %copy-start.67 = (f32[640]{0:T(1024)S(1)}, f32[640]{0:T(1024)}, u32[]{:S(2)}) copy-start(f32[640]{0:T(1024)} %copy-done.66) | copy-start | bytes 7684
  669.7 106.5 %copy-start.69 = (f32[1024]{0:T(1024)S(1)}, f32[1024]{0:T(1024)}, u32[]{:S(2)}) copy-start(f32[1024]{0:T(1024)} %param.31) | copy-start | bytes 12292
  669.7 106.5 %copy-start.75 = (f32[640]{0:T(1024)S(1)}, f32[640]{0:T(1024)}, u32[]{:S(2)}) copy-start(f32[640]{0:T(1024)} %copy-done.74) | copy-start | bytes 7684
  669.7 106.5 %copy-start.77 = (f32[640]{0:T(1024)S(1)}, f32[640]{0:T(1024)}, u32[]{:S(2)}) copy-start(f32[640]{0:T(1024)} %copy-done.76) | copy-start | bytes 7684
  669.7 106.5 %copy-start.81 = (f32[1024]{0:T(1024)S(1)}, f32[1024]{0:T(1024)}, u32[]{:S(2)}) copy-start(f32[1024]{0:T(1024)} %param.32) | copy-start | bytes 12292
  669.8 159.0 %all-gather.21.cloned.1.call-start = ((), (), s32[]{:S(2)}) async-start(), calls=%async_computation.20 | async-start | bytes 3932160 | tf_op jit(solution)/shard_map/all_gather | solution.py:283
  789.6 309.7 %all-gather.19.cloned.1.call-start = ((), (), s32[]{:S(2)}) async-start(), calls=%async_computation.17 | async-start | bytes 3932160 | tf_op jit(solution)/shard_map/all_gather | solution.py:283
  809.6 697.2 %reduce-scatter.23.cloned.1.call-start = ((), (), s32[]{:S(2)}) async-start(), calls=%async_computation.21 | async-start | bytes 3932160 | tf_op jit(solution)/shard_map/reduce_scatter | solution.py:319
  836.9 174.4 %copy-start.44 = (f32[1280,64]{0,1:T(8,128)S(1)}, f32[1280,64]{0,1:T(8,128)}, u32[]{:S(2)}) copy-start(f32[1280,64]{0,1:T(8,128)} %get-tuple-element.537) | copy-start | bytes 983044
  1099.2 407.6 %reduce-scatter.19.cloned.1.call-start = ((), (), s32[]{:S(2)}) async-start(), calls=%async_computation.18 | async-start | bytes 3932160 | tf_op jit(solution)/shard_map/reduce_scatter | solution.py:319
  1372.9 488.3 %all-reduce.5.cloned.1.call-start = ((), (), s32[]{:S(2)}) async-start(), calls=%async_computation.24 | async-start | bytes 50331648 | tf_op jit(solution)/shard_map/psum | solution.py:336
  (99 other events, 1170.1 us)
Sparse Core Ops, SparseCore 0:
  13.2 41.7 all-gather.10
  57.2 39.0 all-gather.14
  256.8 37.5 reduce-scatter.8
  406.8 37.4 reduce-scatter.12
  452.6 39.0 all-gather.16
  493.7 39.0 all-gather.24
  534.9 39.0 all-gather.12
  576.0 39.0 all-gather.22
  617.9 37.5 reduce-scatter.20
  658.3 37.5 reduce-scatter.16
  698.7 37.6 reduce-scatter.10
  738.6 37.5 reduce-scatter.14
  789.7 39.0 all-gather.20
  830.2 39.0 all-gather.18
  1099.3 37.6 reduce-scatter.22
  1373.0 37.7 reduce-scatter.18
  1416.7 444.4 all-reduce.4
where the time goes:
time: 1900 us; the launch traced here: 1890 us
  waiting for transfers between devices  603 us (32%)
  matrix products  578 us (30%)
  local copies, waits for them, and re-layouts  325 us (17%)
  other arithmetic  258 us (14%)
  blocking collectives  104 us (5%)
    psum x1, waiting for transfers between devices, on_device(): lax.psum((mlp_sums[0], mlp_sums[1], mlp_sums[2], mlp_sums[3], attn_sums[0...  302 us
    concatenate x8, local copies, waits for them, and re-layouts, partner(): return jnp.concatenate(pieces_out, -1)  230 us
    dot_general x8, matrix products, masked_scores(): jnp.einsum('gqd,gkd->gqk', query_rows, key_rows, preferred_element_type=j...  122 us
    convert_element_type x4, other arithmetic, attend_back(): grad_scores = (softmax_out * (grad_probs - jnp.sum(softmax_out * grad_pro...  88.3 us
    reduce_scatter x2, waiting for transfers between devices, on_device(): lax.psum_scatter(jnp.dot(active, reduce_weight, preferred_element_type=jn...  80.3 us
    psum x1, blocking collectives, on_device(): lax.psum((mlp_sums[0], mlp_sums[1], mlp_sums[2], mlp_sums[3], attn_sums[0...  64.8 us
    dot_general x2, matrix products, on_device(): jnp.dot(second_out, expand_weight, preferred_element_type=jnp.float32)  64.1 us
    all_gather x2, waiting for transfers between devices, on_device(): first_out = lax.all_gather(first_local, 'mp', axis=0, tiled=True)  54.5 us
  transfers between devices with their start and end apart: 17, of which 11 were waited for; matrix products, arithmetic and copies ran while one was open for 50% of the time, Pallas kernels for 0%

commit v1 on v0

v1 whole, which is shorter than its diff:
```python
import functools
import math

import jax
import jax.numpy as jnp
from jax import lax
from jax.experimental import pallas as pl
from jax.experimental.pallas import tpu as pltpu
from jax.sharding import PartitionSpec as P

HEAD_DIM = 64
FRAMES = 2
SIDE_SMALL = 16
SIDE_LARGE = 24
EPSILON = 1e-06
ROOT_HALF = 0.7071067811865476
GAUSS_NORM = 0.3989422804014327
MIB = 2**20

PAIR = 128
NEG = -1e30
STRIPS = ((0, 512, 592), (512, 640, 1168), (640, 1024, 1168), (1024, 1280, 1280))

def strips(bq):
    out = []
    for a, b, stop in STRIPS:
        for s in range(a, b, bq):
            out.append((s, min(s + bq, b), stop))
    return out

def fwd_kernel(bq, q_ref, k_ref, v_ref, lo_ref, hi_ref, o_ref, rl_ref, ea_ref, eb_ref):
    lane = lax.broadcasted_iota(jnp.int32, (1, PAIR), 1)
    c = (64 ** -0.5) * math.log2(math.e)
    vt = v_ref[...].T
    for (a, b, stop) in strips(bq):
        n = b - a
        q = q_ref[a:b, :]
        lo = lo_ref[:, a:b]
        hi = hi_ref[:, a:b]
        key = lax.broadcasted_iota(jnp.int32, (stop, n), 0)
        ok = (key >= lo) & (key < hi)
        outs, rls = [], []
        for h in range(2):
            qm = jnp.where((lane >= 64) == (h == 1), q, jnp.zeros_like(q))
            s = lax.dot_general(k_ref[0:stop, :], qm, (((1,), (1,)), ((), ())), preferred_element_type=jnp.float32)
            s = jnp.where(ok, s, NEG)
            m = jnp.max(s, 0, keepdims=True)
            e = jnp.exp2((s - m) * c)
            l = jnp.sum(e, 0, keepdims=True)
            eb16 = e.astype(jnp.bfloat16)
            if b <= 512:
                ea_ref[h, :, a:b] = eb16
            else:
                eb_ref[h, 0:stop, a - 512:b - 512] = eb16
            ot = lax.dot_general(vt[h * 64:(h + 1) * 64, 0:stop], eb16, (((1,), (0,)), ((), ())), preferred_element_type=jnp.float32)
            rl = 1.0 / l
            outs.append(ot * rl)
            rls.append(jnp.broadcast_to(rl, (64, n)))
        o_ref[a:b, :] = jnp.concatenate(outs, 0).T.astype(jnp.bfloat16)
        rl_ref[a:b, :] = jnp.concatenate(rls, 0).T

def attn_fwd(q, k, v, lo, hi, bq=256):
    rows, width = q.shape
    pairs = width // PAIR
    full = lambda i: (0, i)
    return pl.pallas_call(
        functools.partial(fwd_kernel, bq),
        grid=(pairs,),
        in_specs=[pl.BlockSpec((rows, PAIR), full)] * 3 + [pl.BlockSpec((1, rows), lambda i: (0, 0))] * 2,
        out_specs=[pl.BlockSpec((rows, PAIR), full), pl.BlockSpec((rows, PAIR), full),
                   pl.BlockSpec((2, 592, 512), lambda i: (i, 0, 0)), pl.BlockSpec((2, 1280, 768), lambda i: (i, 0, 0))],
        out_shape=[jax.ShapeDtypeStruct((rows, width), jnp.bfloat16), jax.ShapeDtypeStruct((rows, width), jnp.float32),
                   jax.ShapeDtypeStruct((2 * pairs, 592, 512), jnp.bfloat16), jax.ShapeDtypeStruct((2 * pairs, 1280, 768), jnp.bfloat16)],
        compiler_params=pltpu.CompilerParams(vmem_limit_bytes=50 * 2**20),
        name="attend",
    )(q, k, v, lo, hi)

def spin(x, cos, sa, sb):
    return x * cos + pltpu.roll(x, PAIR - 10, 1) * sa + pltpu.roll(x, 10, 1) * sb

def bwd_kernel(bq, q_ref, k_ref, v_ref, g_ref, o_ref, rl_ref, ea_ref, eb_ref, cos_ref, sa_ref, sb_ref,
               gq_ref, gk_ref, gv_ref, cs_ref, dk_acc, dv_acc, dqt_acc):
    lane = lax.broadcasted_iota(jnp.int32, (1, PAIR), 1)
    scale = 64 ** -0.5
    kt = k_ref[...].T
    rows = q_ref.shape[0]
    done = 0
    for (a, b, stop) in strips(bq)[::-1]:
        n = b - a
        q = q_ref[a:b, :]
        gf = g_ref[a:b, :].astype(jnp.float32) * rl_ref[a:b, :]
        go = (gf * o_ref[a:b, :].astype(jnp.float32)).T
        g = gf.astype(jnp.bfloat16)
        dk = dv = None
        for h in range(2):
            mask = (lane >= 64) == (h == 1)
            qm = jnp.where(mask, q, jnp.zeros_like(q))
            gm = jnp.where(mask, g, jnp.zeros_like(g))
            delta = jnp.sum(go[h * 64:(h + 1) * 64, :], 0, keepdims=True)
            dpt = lax.dot_general(v_ref[0:stop, :], gm, (((1,), (1,)), ((), ())), preferred_element_type=jnp.float32)
            e = ea_ref[h, :, a:b] if b <= 512 else eb_ref[h, 0:stop, a - 512:b - 512]
            ds = (e.astype(jnp.float32) * (dpt - delta)).astype(jnp.bfloat16)
            dqt_acc[h * 64:(h + 1) * 64, a:b] = lax.dot_general(kt[h * 64:(h + 1) * 64, 0:stop], ds, (((1,), (0,)), ((), ())), preferred_element_type=jnp.float32)
            dk_h = jnp.dot(ds, qm, preferred_element_type=jnp.float32)
            dv_h = jnp.dot(e, gm, preferred_element_type=jnp.float32)
            dk = dk_h if dk is None else dk + dk_h
            dv = dv_h if dv is None else dv + dv_h
        if done == 0:
            assert stop == rows
            dk_acc[...] = dk
            dv_acc[...] = dv
            done = 1
        else:
            dk_acc[0:stop, :] += dk
            dv_acc[0:stop, :] += dv
    cos, sa, sb = cos_ref[...], -sa_ref[...], -sb_ref[...]
    gq = spin(dqt_acc[...].T * scale, cos, sa, sb).astype(jnp.bfloat16)
    gk = spin(dk_acc[...] * scale, cos, sa, sb).astype(jnp.bfloat16)
    gv = dv_acc[...].astype(jnp.bfloat16)
    gq_ref[...] = gq
    gk_ref[...] = gk
    gv_ref[...] = gv
    f = lambda x: jnp.broadcast_to(jnp.sum(x.astype(jnp.float32), 0, keepdims=True), (8, PAIR))
    cs_ref[0] = f(gq)
    cs_ref[1] = f(gk)
    cs_ref[2] = f(gv)

def attn_bwd(q, k, v, g, o, rl, ea, eb, cos, sa, sb, bq=256):
    rows, width = q.shape
    pairs = width // PAIR
    full = lambda i: (0, i)
    blk = pl.BlockSpec((rows, PAIR), full)
    tab = pl.BlockSpec((rows, PAIR), lambda i: (0, 0))
    return pl.pallas_call(
        functools.partial(bwd_kernel, bq),
        grid=(pairs,),
        in_specs=[blk] * 6 + [pl.BlockSpec((2, 592, 512), lambda i: (i, 0, 0)), pl.BlockSpec((2, 1280, 768), lambda i: (i, 0, 0))] + [tab] * 3,
        out_specs=[blk] * 3 + [pl.BlockSpec((3, 8, PAIR), lambda i: (0, 0, i))],
        out_shape=[jax.ShapeDtypeStruct((rows, width), jnp.bfloat16)] * 3 + [jax.ShapeDtypeStruct((3, 8, width), jnp.float32)],
        scratch_shapes=[pltpu.VMEM((rows, PAIR), jnp.float32), pltpu.VMEM((rows, PAIR), jnp.float32), pltpu.VMEM((PAIR, rows), jnp.float32)],
        compiler_params=pltpu.CompilerParams(vmem_limit_bytes=56 * 2**20),
        name="attend_back",
    )(q, k, v, g, o, rl, ea, eb, cos, sa, sb)


def slot_layout(count_one, length):
    large_count = SIDE_LARGE * SIDE_LARGE
    grid_side = jnp.where(count_one == large_count, SIDE_LARGE, SIDE_SMALL).astype(jnp.int32)
    frame_len = grid_side * grid_side + 2
    clip_len = FRAMES * frame_len
    clip_total = jnp.where(count_one == large_count, 1, 2).astype(jnp.int32)
    slot_id = jnp.arange(length, dtype=jnp.int32)
    clip_id = jnp.minimum(slot_id // clip_len, clip_total)
    offset_in = slot_id - clip_id * clip_len
    frame_id = offset_in // frame_len
    place_in = offset_in - frame_id * frame_len - 2
    patch_id = jnp.maximum(place_in, 0)
    is_live = clip_id < clip_total
    is_patch = is_live & (place_in >= 0)
    frame_id = jnp.where(is_live, frame_id, 0)
    patch_row = jnp.where(is_patch, patch_id // grid_side, 0)
    column = jnp.where(is_patch, patch_id - patch_id // grid_side * grid_side, 0)
    first_key = clip_id * clip_len
    past_key = jnp.where(is_live, first_key + (frame_id + 1) * frame_len, length)
    return (first_key, past_key, frame_id, patch_row, column)


def rotary_tables(frame_id, patch_row, column):
    segment = 2 * (HEAD_DIM // 3 // 2)
    half_width = segment // 2
    dim_index = jnp.arange(PAIR, dtype=jnp.int32) % HEAD_DIM
    segment_id = dim_index // segment
    exponent = (dim_index % segment % half_width).astype(jnp.float32)
    frequency = jnp.exp(exponent * (-math.log(10000.0) / half_width))
    pick = lambda number: jnp.where(segment_id == number, 1.0, 0.0).astype(jnp.float32)[None, :]
    position = (
        pick(0) * frame_id[:, None].astype(jnp.float32)
        + pick(1) * patch_row[:, None].astype(jnp.float32)
        + pick(2) * column[:, None].astype(jnp.float32)
    )
    angles = position * frequency[None, :]
    lower = (dim_index % segment < half_width)[None, :]
    turning = (segment_id < 3)[None, :]
    sine = jnp.where(turning, jnp.sin(angles), 0.0)
    return (jnp.cos(angles), jnp.where(lower, -sine, 0.0), jnp.where(lower, 0.0, sine))


def project_kernel(x_ref, w_ref, b_ref, cos_ref, up_ref, down_ref, out_ref):
    y = jnp.dot(x_ref[...], w_ref[0], preferred_element_type=jnp.float32) + b_ref[0]
    part = pl.program_id(0)

    @pl.when(part == 2)
    def _():
        out_ref[0] = y.astype(jnp.bfloat16)

    @pl.when(part < 2)
    def _():
        cos, up, down = cos_ref[...], up_ref[...], down_ref[...]
        for at in range(0, y.shape[1], PAIR):
            out_ref[0, :, at : at + PAIR] = spin(y[:, at : at + PAIR], cos, up, down).astype(
                jnp.bfloat16
            )


def project(x, weight, bias, tables):
    rows, depth = x.shape
    width = weight.shape[2]
    table = pl.BlockSpec((rows, PAIR), lambda i: (0, 0))
    return pl.pallas_call(
        project_kernel,
        grid=(3,),
        in_specs=[
            pl.BlockSpec((rows, depth), lambda i: (0, 0)),
            pl.BlockSpec((1, depth, width), lambda i: (i, 0, 0)),
            pl.BlockSpec((1, 1, width), lambda i: (i, 0, 0)),
            table,
            table,
            table,
        ],
        out_specs=pl.BlockSpec((1, rows, width), lambda i: (i, 0, 0)),
        out_shape=jax.ShapeDtypeStruct((3, rows, width), jnp.bfloat16),
        compiler_params=pltpu.CompilerParams(vmem_limit_bytes=50 * MIB),
        name="project",
    )(x, weight, bias[:, None, :], *tables)


def standardize(values_in):
    row_mean = jnp.mean(values_in, -1, keepdims=True)
    centred = values_in - row_mean
    norm_scale = lax.rsqrt(jnp.mean(centred * centred, -1, keepdims=True) + EPSILON)
    return (centred * norm_scale, norm_scale)


def norm_back(grad_in, normed, norm_scale):
    return norm_scale * (
        grad_in
        - jnp.mean(grad_in, -1, keepdims=True)
        - normed * jnp.mean(grad_in * normed, -1, keepdims=True)
    )


def column_sums(matrix):
    unit_column = jnp.ones((matrix.shape[0],), matrix.dtype)
    return jnp.dot(unit_column, matrix, preferred_element_type=jnp.float32)


def dot(left, right):
    return jnp.dot(left, right, preferred_element_type=jnp.float32)


def dot_nt(left, right):
    return lax.dot_general(
        left, right, (((1,), (1,)), ((), ())), preferred_element_type=jnp.float32
    )


def dot_tn(left, right):
    return lax.dot_general(
        left, right, (((0,), (0,)), ((), ())), preferred_element_type=jnp.float32
    )


def low(array):
    return array.astype(jnp.bfloat16)


def wide(array):
    return array.astype(jnp.float32)


def on_device(
    spread,
    tokens,
    cotangent,
    patch_count,
    first_gain,
    first_shift,
    heads_weight,
    heads_bias,
    merge_weight,
    merge_bias,
    second_gain,
    second_shift,
    expand_weight,
    expand_bias,
    reduce_weight,
    reduce_bias,
):
    levels = spread.bit_length() - 1
    place = lax.axis_index("dp")
    side = lax.axis_index("mp")

    def bit(level):
        return (place >> level) & 1

    def swap(array, level):
        return lax.ppermute(array, "dp", [(i, i ^ (1 << level)) for i in range(spread)])

    def cross(array):
        return lax.ppermute(array, "mp", [(0, 1), (1, 0)])

    def ordered(flag, mine, theirs):
        return jnp.where(
            flag == 0,
            jnp.concatenate([mine, theirs], 0),
            jnp.concatenate([theirs, mine], 0),
        )

    def half_of(array, flag):
        size = array.shape[0] // 2
        return lax.dynamic_slice_in_dim(array, flag * size, size, 0)

    def scatter(array, levels_in):
        for level in levels_in:
            arrived = swap(half_of(array, 1 - bit(level)), level)
            array = low(wide(half_of(array, bit(level))) + wide(arrived))
        return array

    def gather(array, levels_in):
        for level in levels_in[::-1]:
            array = ordered(bit(level), array, swap(array, level))
        return array

    def fetch(array):
        near = list(range(min(3, levels)))
        piece = array
        for level in near:
            piece = half_of(piece, bit(level))
        return gather(cross(piece), near)

    def whole_rows(array):
        mine = lax.dynamic_index_in_dim(array[:, 0], side, 0, False)
        other = lax.dynamic_index_in_dim(array[:, 0], 1 - side, 0, False)
        return ordered(side, mine, cross(other))

    def give_back(array):
        size = array.shape[0] // 2
        mine = half_of(array, side)
        arrived = cross(half_of(array, 1 - side))
        return ordered(side, mine[None], arrived[None])[:, None]

    stream = whole_rows(tokens)
    length = stream.shape[0]
    heads_own = heads_weight.transpose(1, 0, 2)
    heads_width = heads_own.shape[2]
    heads_far = fetch(heads_own.reshape(-1, heads_width)).reshape(heads_own.shape)
    biases = jnp.concatenate([heads_bias.reshape(-1), expand_bias])
    biases_far = cross(biases)
    heads_biases = (heads_bias, biases_far[: heads_bias.size].reshape(heads_bias.shape))
    expand_biases = (expand_bias, biases_far[heads_bias.size :])
    merge_far = fetch(merge_weight)
    expand_far = fetch(expand_weight)
    reduce_far = fetch(reduce_weight)
    heads_both = (heads_own, heads_far)
    merge_both = (merge_weight, merge_far)
    expand_both = (expand_weight, expand_far)
    reduce_both = (reduce_weight, reduce_far)
    grad_two = whole_rows(cotangent)

    count_one = lax.dynamic_index_in_dim(patch_count[:, 0], side, 0, False)
    first_key, past_key, frame_id, patch_row, column = slot_layout(count_one, length)
    tables = rotary_tables(frame_id, patch_row, column)
    first_key, past_key = first_key[None], past_key[None]

    stream = wide(stream)
    first_norm, first_scale = standardize(stream)
    first_out = low(first_norm * first_gain + first_shift)
    parts = (0, 1)
    heads = [project(first_out, heads_both[p], heads_biases[p], tables) for p in parts]
    seen = [attn_fwd(heads[p][0], heads[p][1], heads[p][2], first_key, past_key, 512) for p in parts]
    mixed = [seen[p][0] for p in parts]
    residual = stream + (dot(mixed[0], merge_both[0]) + dot(mixed[1], merge_both[1]) + merge_bias)
    second_norm, second_scale = standardize(residual)
    second_out = low(second_norm * second_gain + second_shift)
    active, slope = [], []
    for p in parts:
        pre_gelu = dot(second_out, expand_both[p]) + expand_biases[p]
        below = 0.5 * (1.0 + lax.erf(pre_gelu * ROOT_HALF))
        active.append(low(pre_gelu * below))
        slope.append(low(below + pre_gelu * jnp.exp(-0.5 * pre_gelu * pre_gelu) * GAUSS_NORM))
    branch_two = dot(active[0], reduce_both[0]) + dot(active[1], reduce_both[1])
    layer_out = low(residual + (branch_two + reduce_bias))

    grad_pre = [low(dot_nt(grad_two, reduce_both[p]) * wide(slope[p])) for p in parts]
    reduce_grads = [low(dot_tn(active[p], grad_two)) for p in parts]
    expand_grads = [low(dot_tn(second_out, grad_pre[p])) for p in parts]
    grad_second = dot_nt(grad_pre[0], expand_both[0]) + dot_nt(grad_pre[1], expand_both[1])
    grad_residual = wide(grad_two) + norm_back(grad_second * second_gain, second_norm, second_scale)
    grad_one = low(grad_residual)
    merge_grads = [low(dot_tn(mixed[p], grad_one)) for p in parts]
    grad_mixed = [low(dot_nt(grad_one, merge_both[p])) for p in parts]
    heads_grads, grad_first, heads_bias_grads = [], 0.0, []
    for p in parts:
        _, root, early, late = seen[p]
        g_q, g_k, g_v, sums = attn_bwd(
            heads[p][0], heads[p][1], heads[p][2], grad_mixed[p], mixed[p], root, early, late, *tables, 512
        )
        heads_bias_grads.append(sums[:, 0].reshape(-1))
        heads_grads.append(
            jnp.concatenate([low(dot_tn(first_out, g)) for g in (g_q, g_k, g_v)], 0)
        )
        for number, g in enumerate((g_q, g_k, g_v)):
            grad_first = grad_first + dot_nt(g, heads_both[p][number])
    tokens_grad = grad_residual + norm_back(grad_first * first_gain, first_norm, first_scale)

    def reduced(grads):
        own, far = (scatter(g, [0]) for g in grads)
        piece = low(wide(own) + wide(cross(far)))
        rest = list(range(1, levels))
        return wide(gather(scatter(piece, rest), [0] + rest))

    reduce_total = reduced(reduce_grads)
    expand_total = reduced(expand_grads)
    merge_total = reduced(merge_grads)
    heads_total = reduced(heads_grads)

    far_sums = jnp.concatenate([heads_bias_grads[1], column_sums(grad_pre[1])])
    own_sums = jnp.concatenate([heads_bias_grads[0], column_sums(grad_pre[0])])
    both_sums = jnp.concatenate(
        [
            column_sums(grad_one),
            column_sums(grad_two),
            jnp.sum(grad_first * first_norm, 0),
            jnp.sum(grad_first, 0),
            jnp.sum(grad_second * second_norm, 0),
            jnp.sum(grad_second, 0),
        ]
    )
    arrived = cross(jnp.concatenate([far_sums, both_sums]))
    sums = jnp.concatenate([own_sums, both_sums]) + arrived
    for level in range(levels):
        sums = sums + swap(sums, level)
    bounds = [heads_bias.size, expand_bias.size] + [merge_bias.size] * 6
    cuts = [sum(bounds[:i]) for i in range(1, len(bounds))]
    (heads_bias_total, expand_bias_total, merge_bias_total, reduce_bias_total, first_gain_total,
     first_shift_total, second_gain_total, second_shift_total) = jnp.split(sums, cuts)
    return (
        give_back(layer_out),
        wide(give_back(low(tokens_grad))),
        first_gain_total,
        first_shift_total,
        heads_total.reshape(heads_own.shape).transpose(1, 0, 2),
        heads_bias_total.reshape(heads_bias.shape),
        merge_total,
        merge_bias_total,
        second_gain_total,
        second_shift_total,
        expand_total,
        expand_bias_total,
        reduce_total,
        reduce_bias_total,
    )


def solution(mesh):
    return jax.shard_map(
        functools.partial(on_device, mesh.shape["dp"]),
        mesh=mesh,
        in_specs=(
            P(None, "dp", "mp", None),
            P(None, "dp", "mp", None),
            P(None, "dp"),
            P(),
            P(),
            P(None, None, "mp"),
            P(None, "mp"),
            P("mp", None),
            P(),
            P(),
            P(),
            P(None, "mp"),
            P("mp"),
            P("mp", None),
            P(),
        ),
        out_specs=(
            P(None, "dp", "mp", None),
            P(None, "dp", "mp", None),
            P(),
            P(),
            P(None, None, "mp"),
            P(None, "mp"),
            P("mp", None),
            P(),
            P(),
            P(),
            P(None, "mp"),
            P("mp"),
            P("mp", None),
            P(),
        ),
        check_vma=False,
    )
```

time: 1900 us -> 893 us (0.47)
  matrix products: 578 us -> 213 us
  waiting for transfers between devices: 603 us -> 295 us
  local copies, waits for them, and re-layouts: 325 us -> 47.4 us
  Pallas kernels: 0 us -> 159 us
  other arithmetic: 258 us -> 112 us
  blocking collectives: 104 us -> 0 us
  starting transfers between devices: 1.28 us -> 55.8 us
    dot_general x60 -> x34, matrix products: 578 us -> 213 us  [the longest x12 97.7 us: dot_nt(): lax.dot_general(left, right, (((1,), (1,)), ((), ())), preferred_element_...]
    psum x1 -> x0, waiting for transfers between devices: 302 us -> none  [on_device(): lax.psum((mlp_sums[0], mlp_sums[1], mlp_sums[2], mlp_sums[3], attn_sums[0...]
    ppermute x0 -> x66, waiting for transfers between devices: none -> 295 us  [the longest x52 157 us: swap(): lax.ppermute(array, 'dp', [(i, i ^ 1 << level) for i in range(spread)])]
    concatenate x8 -> x3, local copies, waits for them, and re-layouts: 230 us -> 3.03 us  [the longest x2 3.03 us: ordered(): jnp.concatenate([mine, theirs], 0)]
    pallas_call x0 -> x6, Pallas kernels: none -> 159 us  [the longest x2 68.7 us: attn_fwd(): pl.pallas_call(functools.partial(fwd_kernel, bq), grid=(pairs,), in_specs...]
    all_gather x8 -> x0, waiting for transfers between devices: 157 us -> none  [the longest x2 54.5 us: on_device(): first_out = lax.all_gather(first_local, 'mp', axis=0, tiled=True)]
    reduce_scatter x8 -> x0, waiting for transfers between devices: 141 us -> none  [the longest x2 80.3 us: on_device(): lax.psum_scatter(jnp.dot(active, reduce_weight, preferred_element_type=jn...]
    psum x2 -> x0, blocking collectives: 104 us -> none  [the longest x1 64.8 us: on_device(): lax.psum((mlp_sums[0], mlp_sums[1], mlp_sums[2], mlp_sums[3], attn_sums[0...]
  transfers between devices with their start and end apart: 17 -> 66, of which waited for: 11 -> 23; matrix products, arithmetic and copies ran while one was open for 50% -> 40% of each run, Pallas kernels for 0% -> 18%
where the time goes in v1:
time: 893 us; the launch traced here: 885 us
  waiting for transfers between devices  295 us (33%)
  matrix products  213 us (24%)
  Pallas kernels  159 us (18%)
  other arithmetic  112 us (13%)
  starting transfers between devices  55.8 us (6%)
  local copies, waits for them, and re-layouts  47.4 us (5%)
    ppermute x52, waiting for transfers between devices, swap(): lax.ppermute(array, 'dp', [(i, i ^ 1 << level) for i in range(spread)])  157 us
    ppermute x14, waiting for transfers between devices, cross(): return lax.ppermute(array, 'mp', [(0, 1), (1, 0)])  137 us
    dot_general x12, matrix products, dot_nt(): lax.dot_general(left, right, (((1,), (1,)), ((), ())), preferred_element_...  97.7 us
    pallas_call x2, Pallas kernels, attn_fwd(): pl.pallas_call(functools.partial(fwd_kernel, bq), grid=(pairs,), in_specs...  68.7 us
    pallas_call x2, Pallas kernels, attn_bwd(): pl.pallas_call(functools.partial(bwd_kernel, bq), grid=(pairs,), in_specs...  68.6 us
    dot_general x12, matrix products, dot_tn(): lax.dot_general(left, right, (((0,), (0,)), ((), ())), preferred_element_...  56 us
    dot_general x6, matrix products, dot(): return jnp.dot(left, right, preferred_element_type=jnp.float32)  50.7 us
    convert_element_type x24, other arithmetic, low(): return array.astype(jnp.bfloat16)  40.9 us
  transfers between devices with their start and end apart: 66, of which 23 were waited for; matrix products, arithmetic and copies ran while one was open for 40% of the time, Pallas kernels for 18%

profile of v1, /device:TPU:0, one launch (start us, length us, event | category | flops | bytes accessed | tf_op | source)
XLA Modules:
  0.0 885.4 jit_solution(1346957300124709272)
XLA Ops:
  28.0 40.5 %collective-permute-done.5 = f32[3584]{0:T(1024)S(1)} collective-permute-done((f32[3584]{0:T(1024)S(1)}, f32[3584]{0:T(1024)S(1)}, u32[]{:S(2)}, u32[]{:S(2)}) %collective-permute-start.5) | collective-permute-done | bytes 14368 | tf_op jit(solution)/shard_map/ppermute | solution.py:300
  117.1 10.8 %project.2 = bf16[3,1280,512]{2,1,0:T(8,128)(2,1)} custom-call(bf16[1280,1024]{1,0:T(8,128)(2,1)} %fusion.17.x_ref, bf16[3,1024,512]{2,1,0:T(8,128)(2,1)} %bitcast.105, f32[3,1,512]{2,1,0:T(1,128)S(1)} %broadcast_in_dim.49.b_ref, f32[1280,128]{1,0:T(8,128)S(1)} %get-tuple-element.78.cos_ref, f32[1280,128]{1,0:T(8,128)S(1)} %get-tuple-element.77.up_ref.sa_ref, ...), custom_call_target="tpu_custom_call" | custom-call | tf_op jit(solution)/shard_map/project/pallas_call | solution.py:209
  132.0 34.6 %attend.2 = (bf16[1280,512]{1,0:T(8,128)(2,1)S(1)}, f32[1280,512]{1,0:T(8,128)}, bf16[8,592,512]{2,1,0:T(8,128)(2,1)}, bf16[8,1280,768]{2,1,0:T(8,128)(2,1)}) custom-call(bf16[1280,512]{1,0:T(8,128)(2,1)S(1)} %get-tuple-element.61.q_ref, bf16[1280,512]{1,0:T(8,128)(2,1)S(1)} %get-tuple-element.60.k_ref, bf16[1280,512]{1,0:T(8,128)(2,1)} %get-tuple-element.59.v_ref, ...), custom_call_target="tpu_custom_call" | custom-call | tf_op jit(solution)/shard_map/attend/pallas_call | solution.py:66
  186.0 11.0 %project.3 = bf16[3,1280,512]{2,1,0:T(8,128)(2,1)} custom-call(bf16[1280,1024]{1,0:T(8,128)(2,1)} %fusion.17.x_ref, bf16[3,1024,512]{2,1,0:T(8,128)(2,1)} %bitcast.102, f32[3,1,512]{2,1,0:T(1,128)S(1)} %slice.79.b_ref, f32[1280,128]{1,0:T(8,128)S(1)} %get-tuple-element.78.cos_ref, f32[1280,128]{1,0:T(8,128)S(1)} %get-tuple-element.77.up_ref.sa_ref, ...), custom_call_target="tpu_custom_call" | custom-call | tf_op jit(solution)/shard_map/project/pallas_call | solution.py:209
  200.4 34.1 %attend.3 = (bf16[1280,512]{1,0:T(8,128)(2,1)S(1)}, f32[1280,512]{1,0:T(8,128)}, bf16[8,592,512]{2,1,0:T(8,128)(2,1)}, bf16[8,1280,768]{2,1,0:T(8,128)(2,1)}) custom-call(bf16[1280,512]{1,0:T(8,128)(2,1)S(1)} %get-tuple-element.58.q_ref, bf16[1280,512]{1,0:T(8,128)(2,1)S(1)} %get-tuple-element.57.k_ref, bf16[1280,512]{1,0:T(8,128)(2,1)} %get-tuple-element.56.v_ref, ...), custom_call_target="tpu_custom_call" | custom-call | tf_op jit(solution)/shard_map/attend/pallas_call | solution.py:66
  254.4 13.0 %multiply_convert_fusion.1 = bf16[1280,2048]{1,0:T(8,128)(2,1)S(1)} fusion(bf16[2048,1024]{1,0:T(8,128)(2,1)S(1)} %copy-done.47, f32[1280,2048]{1,0:T(8,128)} %get-tuple-element.94, f32[2048]{0:T(1024)S(1)} %copy-done.55, bf16[640,1024]{1,0:T(8,128)(2,1)} %collective-permute-done.19, bf16[640,1024]{1,0:T(8,128)(2,1)S(1)} %copy-done.21, pred[]{:T(512)S(6)} %eq.38), kind=kOutput, calls=%fused_computation.13 | convolution fusion | flops 5414584320 | bytes 22552576 | tf_op jit(solution)/shard_map/dot_general | solution.py:252
  304.2 12.6 %multiply_convert_fusion.2 = (bf16[1280,2048]{1,0:T(8,128)(2,1)}, f32[1280,2048]{1,0:T(8,128)}) fusion(f32[2048]{0:T(1024)S(1)} %slice.99, bf16[1280,1024]{1,0:T(8,128)(2,1)S(1)} %add_convert_fusion.1, bf16[512,2048]{1,0:T(8,128)(2,1)} %collective-permute-done.13, bf16[512,2048]{1,0:T(8,128)(2,1)} %maximum_select_fusion.10, pred[]{:T(512)S(6)} %eq.84), kind=kOutput, calls=%fused_computation.14 | convolution fusion | flops 5403312128 | bytes 22552576 | tf_op jit(solution)/shard_map/dot_general | solution.py:248
  316.8 20.2 %multiply_convert_fusion = bf16[1280,2048]{1,0:T(8,128)(2,1)} fusion(f32[1280,2048]{1,0:T(8,128)} %get-tuple-element.96, f32[2048]{0:T(1024)S(1)} %slice.99, bf16[1024,1024]{1,0:T(8,128)(2,1)} %collective-permute-done.17, bf16[1024,1024]{1,0:T(8,128)(2,1)} %maximum_select_fusion.11, pred[]{:T(512)S(6)} %eq.84, ...), kind=kOutput, calls=%fused_computation.12 | convolution fusion | flops 5433458688 | bytes 22552578 | tf_op jit(solution)/shard_map/dot_general | solution.py:252
  340.4 10.6 %convolution_convert_fusion.2 = bf16[1024,2048]{1,0:T(8,128)(2,1)} fusion(bf16[1280,1024]{1,0:T(8,128)(2,1)} %copy-done.35, bf16[1280,2048]{1,0:T(8,128)(2,1)} %multiply_convert_fusion), kind=kOutput, calls=%fused_computation.62 | convolution fusion | flops 5370806272 | bytes 12058624 | tf_op jit(solution)/shard_map/dot_general | solution.py:258
  351.1 15.9 %multiply_reduce_fusion = (f32[1024]{0:T(1024)S(1)}, f32[1280]{0:T(1024)S(1)}, f32[1280]{0:T(1024)S(1)}, f32[1024]{0:T(1024)S(1)}, f32[1280,1024]{1,0:T(8,128)}) fusion(f32[1280,1024]{1,0:T(8,128)S(1)} %bitcast.97, f32[1280]{0:T(1024)S(1)} %add_rsqrt_fusion, f32[1280]{0:T(1024)S(1)} %broadcast_multiply_fusion.4, f32[1024]{0:T(1024)S(1)} %copy-done.54, ...), kind=kOutput, calls=%fused_computation.37 | convolution fusion | flops 5400686592 | bytes 25198592 | tf_op jit(solution)/shard_map/dot_general | solution.py:252
  386.6 34.2 %attend_back.3 = (bf16[1280,512]{1,0:T(8,128)(2,1)}, bf16[1280,512]{1,0:T(8,128)(2,1)}, bf16[1280,512]{1,0:T(8,128)(2,1)}, f32[3,8,512]{2,1,0:T(8,128)}) custom-call(bf16[1280,512]{1,0:T(8,128)(2,1)} %copy-done.8, bf16[1280,512]{1,0:T(8,128)(2,1)} %copy-done.7, bf16[1280,512]{1,0:T(8,128)(2,1)} %get-tuple-element.56.v_ref, ...), custom_call_target="tpu_custom_call" | custom-call | tf_op jit(solution)/shard_map/attend_back/pallas_call | solution.py:134
  435.3 34.3 %attend_back.2 = (bf16[1280,512]{1,0:T(8,128)(2,1)}, bf16[1280,512]{1,0:T(8,128)(2,1)}, bf16[1280,512]{1,0:T(8,128)(2,1)}, f32[3,8,512]{2,1,0:T(8,128)}) custom-call(bf16[1280,512]{1,0:T(8,128)(2,1)} %copy-done.6, bf16[1280,512]{1,0:T(8,128)(2,1)} %copy-done.5, bf16[1280,512]{1,0:T(8,128)(2,1)} %get-tuple-element.59.v_ref, ...), custom_call_target="tpu_custom_call" | custom-call | tf_op jit(solution)/shard_map/attend_back/pallas_call | solution.py:134
  512.6 13.4 %fusion.23 = (f32[1024]{0:T(1024)S(1)}, f32[1280]{0:T(1024)S(1)}, f32[1280]{0:T(1024)S(1)}, f32[1024]{0:T(1024)S(1)}, f32[1280,1024]{1,0:T(8,128)S(1)}) fusion(f32[1280]{0:T(1024)S(1)} %copy-done.44, f32[1280]{0:T(1024)S(1)} %copy-done.42, bf16[640,1024]{1,0:T(8,128)(2,1)S(1)} %copy-done.15, bf16[640,1024]{1,0:T(8,128)(2,1)} %collective-permute-done, ...), kind=kOutput, calls=%fused_computation.35 | convolution fusion | flops 1373629952 | bytes 36470784 | tf_op jit(solution)/shard_map/dot_general | solution.py:252
  532.4 11.9 %collective-permute-done.38 = bf16[256,1024]{1,0:T(8,128)(2,1)S(1)} collective-permute-done((bf16[256,1024]{1,0:T(8,128)(2,1)S(1)}, bf16[256,1024]{1,0:T(8,128)(2,1)S(1)}, u32[]{:S(2)}, u32[]{:S(2)}) %collective-permute-start.38) | collective-permute-done | bytes 524320 | tf_op jit(solution)/shard_map/ppermute | solution.py:300
  564.1 11.1 %add_convert_fusion = bf16[1280,1024]{1,0:T(8,128)(2,1)S(1)} fusion(f32[1280,1024]{1,0:T(8,128)S(1)} %bitcast.99, f32[1280,1024]{1,0:T(8,128)} %fusion.72, bf16[1280,2048]{1,0:T(8,128)(2,1)} %get-tuple-element.95, f32[1024]{0:T(1024)S(1)} %copy-done.66, bf16[1024,1024]{1,0:T(8,128)(2,1)} %collective-permute-done.17, ...), kind=kOutput, calls=%fused_computation.41 | convolution fusion | flops 5392826368 | bytes 22548480 | tf_op jit(solution)/shard_map/dot_general | solution.py:248
  579.1 20.5 %collective-permute-done.28 = bf16[1536,512]{1,0:T(8,128)(2,1)} collective-permute-done((bf16[1536,512]{1,0:T(8,128)(2,1)}, bf16[1536,512]{1,0:T(8,128)(2,1)}, u32[]{:S(2)}, u32[]{:S(2)}) %collective-permute-start.28) | collective-permute-done | bytes 1572896 | tf_op jit(solution)/shard_map/ppermute | solution.py:300
  605.0 39.6 %collective-permute-done.48 = bf16[512,2048]{1,0:T(8,128)(2,1)} collective-permute-done((bf16[512,2048]{1,0:T(8,128)(2,1)}, bf16[512,2048]{1,0:T(8,128)(2,1)}, u32[]{:S(2)}, u32[]{:S(2)}) %collective-permute-start.48) | collective-permute-done | bytes 2097184 | tf_op jit(solution)/shard_map/ppermute | solution.py:300
  648.7 13.6 %collective-permute-done.29 = bf16[768,512]{1,0:T(8,128)(2,1)S(1)} collective-permute-done((bf16[768,512]{1,0:T(8,128)(2,1)S(1)}, bf16[768,512]{1,0:T(8,128)(2,1)S(1)}, u32[]{:S(2)}, u32[]{:S(2)}) %collective-permute-start.29) | collective-permute-done | bytes 786464 | tf_op jit(solution)/shard_map/ppermute | solution.py:297
  663.9 24.5 %collective-permute-done.58 = bf16[1024,1024]{1,0:T(8,128)(2,1)S(1)} collective-permute-done((bf16[1024,1024]{1,0:T(8,128)(2,1)S(1)}, bf16[1024,1024]{1,0:T(8,128)(2,1)S(1)}, u32[]{:S(2)}, u32[]{:S(2)}) %collective-permute-start.58) | collective-permute-done | bytes 2097184 | tf_op jit(solution)/shard_map/ppermute | solution.py:300
  702.3 11.9 %collective-permute-done.59 = bf16[512,1024]{1,0:T(8,128)(2,1)S(1)} collective-permute-done((bf16[512,1024]{1,0:T(8,128)(2,1)S(1)}, bf16[512,1024]{1,0:T(8,128)(2,1)S(1)}, u32[]{:S(2)}, u32[]{:S(2)}) %collective-permute-start.59) | collective-permute-done | bytes 1048608 | tf_op jit(solution)/shard_map/ppermute | solution.py:297
  718.1 14.3 %collective-permute-done.60 = bf16[256,1024]{1,0:T(8,128)(2,1)S(1)} collective-permute-done((bf16[256,1024]{1,0:T(8,128)(2,1)S(1)}, bf16[256,1024]{1,0:T(8,128)(2,1)S(1)}, u32[]{:S(2)}, u32[]{:S(2)}) %collective-permute-start.60) | collective-permute-done | bytes 524320 | tf_op jit(solution)/shard_map/ppermute | solution.py:297
  735.8 15.6 %collective-permute-done.61 = bf16[128,1024]{1,0:T(8,128)(2,1)S(1)} collective-permute-done((bf16[128,1024]{1,0:T(8,128)(2,1)S(1)}, bf16[128,1024]{1,0:T(8,128)(2,1)S(1)}, u32[]{:S(2)}, u32[]{:S(2)}) %collective-permute-start.61) | collective-permute-done | bytes 262176 | tf_op jit(solution)/shard_map/ppermute | solution.py:297
  778.6 16.6 %collective-permute-done.63 = bf16[256,1024]{1,0:T(8,128)(2,1)S(1)} collective-permute-done((bf16[256,1024]{1,0:T(8,128)(2,1)S(1)}, bf16[256,1024]{1,0:T(8,128)(2,1)S(1)}, u32[]{:S(2)}, u32[]{:S(2)}) %collective-permute-start.63) | collective-permute-done | bytes 524320 | tf_op jit(solution)/shard_map/ppermute | solution.py:297
  822.9 25.1 %collective-permute-done.44 = bf16[128,1024]{1,0:T(8,128)(2,1)S(1)} collective-permute-done((bf16[128,1024]{1,0:T(8,128)(2,1)S(1)}, bf16[128,1024]{1,0:T(8,128)(2,1)S(1)}, u32[]{:S(2)}, u32[]{:S(2)}) %collective-permute-start.44) | collective-permute-done | bytes 262176 | tf_op jit(solution)/shard_map/ppermute | solution.py:297
  (443 shorter events, 391.4 us)
Async XLA Ops:
  6.8 63.2 %collective-permute-start.1 = (bf16[384,512]{1,0:T(8,128)(2,1)}, bf16[384,512]{1,0:T(8,128)(2,1)}, u32[]{:S(2)}, u32[]{:S(2)}) collective-permute-start(bf16[384,512]{1,0:T(8,128)(2,1)} %constant_dynamic-slice_fusion.25), channel_id=1, source_target_pairs={{0,1},{1,0},{2,3},{3,2},{4,5},{5,4},{6,7},{7,6},{8,9},{9,8},{10,11... | collective-permute-start | bytes 1179656 | tf_op jit(solution)/shard_map/ppermute | solution.py:300
  8.8 64.1 %collective-permute-start.14 = (bf16[256,1024]{1,0:T(8,128)(2,1)}, bf16[256,1024]{1,0:T(8,128)(2,1)}, u32[]{:S(2)}, u32[]{:S(2)}) collective-permute-start(bf16[256,1024]{1,0:T(8,128)(2,1)} %constant_dynamic-slice_fusion.22), channel_id=1, source_target_pairs={{0,1},{1,0},{2,3},{3,2},{4,5},{5,4},{6,7},{7,6},{8,9},{9,8},{10,11... | collective-permute-start | bytes 1572872 | tf_op jit(solution)/shard_map/ppermute | solution.py:300
  12.8 58.8 %collective-permute-start.10 = (bf16[128,2048]{1,0:T(8,128)(2,1)}, bf16[128,2048]{1,0:T(8,128)(2,1)}, u32[]{:S(2)}, u32[]{:S(2)}) collective-permute-start(bf16[128,2048]{1,0:T(8,128)(2,1)} %constant_dynamic-slice_fusion.23), channel_id=1, source_target_pairs={{0,1},{1,0},{2,3},{3,2},{4,5},{5,4},{6,7},{7,6},{8,9},{9,8},{10,11... | collective-permute-start | bytes 1572872 | tf_op jit(solution)/shard_map/ppermute | solution.py:300
  16.4 88.4 %collective-permute-start = (bf16[640,1024]{1,0:T(8,128)(2,1)}, bf16[640,1024]{1,0:T(8,128)(2,1)}, u32[]{:S(2)}, u32[]{:S(2)}) collective-permute-start(bf16[640,1024]{1,0:T(8,128)(2,1)} %get-tuple-element.68), channel_id=1, source_target_pairs={{0,1},{1,0},{2,3},{3,2},{4,5},{5,4},{6,7},{7,6},{8,9},{9,8},{10,11... | collective-permute-start | bytes 3932168 | tf_op jit(solution)/shard_map/ppermute | solution.py:300
  78.1 88.5 %collective-permute-start.19 = (bf16[640,1024]{1,0:T(8,128)(2,1)}, bf16[640,1024]{1,0:T(8,128)(2,1)}, u32[]{:S(2)}, u32[]{:S(2)}) collective-permute-start(bf16[640,1024]{1,0:T(8,128)(2,1)} %get-tuple-element.65), channel_id=1, source_target_pairs={{0,1},{1,0},{2,3},{3,2},{4,5},{5,4},{6,7},{7,6},{8,9},{9,8},{10,11... | collective-permute-start | bytes 3932168 | tf_op jit(solution)/shard_map/ppermute | solution.py:300
  82.3 152.1 %collective-permute-start.9 = (bf16[256,1024]{1,0:T(8,128)(2,1)}, bf16[256,1024]{1,0:T(8,128)(2,1)}, u32[]{:S(2)}, u32[]{:S(2)}) collective-permute-start(bf16[256,1024]{1,0:T(8,128)(2,1)} %maximum_select_fusion.28), channel_id=1, source_target_pairs={{0,2},{2,0},{4,6},{6,4},{8,10},{10,8},{12,14},{14,12},{16,18},{18,... | collective-permute-start | bytes 1572872 | tf_op jit(solution)/shard_map/ppermute | solution.py:297
  102.3 76.3 %collective-permute-start.12 = (bf16[256,2048]{1,0:T(8,128)(2,1)S(1)}, bf16[256,2048]{1,0:T(8,128)(2,1)}, u32[]{:S(2)}, u32[]{:S(2)}) collective-permute-start(bf16[256,2048]{1,0:T(8,128)(2,1)S(1)} %maximum_select_fusion.17), channel_id=1, source_target_pairs={{0,4},{2,6},{4,0},{6,2},{8,12},{10,14},{12,8},{14,10},{16,20},{18,... | collective-permute-start | bytes 3145736 | tf_op jit(solution)/shard_map/ppermute | solution.py:297
  104.8 69.2 %collective-permute-start.16 = (bf16[512,1024]{1,0:T(8,128)(2,1)S(1)}, bf16[512,1024]{1,0:T(8,128)(2,1)}, u32[]{:S(2)}, u32[]{:S(2)}) collective-permute-start(bf16[512,1024]{1,0:T(8,128)(2,1)S(1)} %maximum_select_fusion.18), channel_id=1, source_target_pairs={{0,4},{2,6},{4,0},{6,2},{8,12},{10,14},{12,8},{14,10},{16,20},{18,... | collective-permute-start | bytes 3145736 | tf_op jit(solution)/shard_map/ppermute | solution.py:297
  128.5 54.0 %collective-permute-start.4 = (bf16[1536,512]{1,0:T(8,128)(2,1)S(1)}, bf16[1536,512]{1,0:T(8,128)(2,1)}, u32[]{:S(2)}, u32[]{:S(2)}) collective-permute-start(bf16[1536,512]{1,0:T(8,128)(2,1)S(1)} %maximum_select_fusion.14), channel_id=1, source_target_pairs={{0,2},{2,0},{4,6},{6,4},{8,10},{10,8},{12,14},{14,12},{16,18},{18,... | collective-permute-start | bytes 4718600 | tf_op jit(solution)/shard_map/ppermute | solution.py:297
  178.0 138.8 %collective-permute-start.17 = (bf16[1024,1024]{1,0:T(8,128)(2,1)}, bf16[1024,1024]{1,0:T(8,128)(2,1)}, u32[]{:S(2)}, u32[]{:S(2)}) collective-permute-start(bf16[1024,1024]{1,0:T(8,128)(2,1)} %maximum_select_fusion.11), channel_id=1, source_target_pairs={{0,2},{2,0},{4,6},{6,4},{8,10},{10,8},{12,14},{14,12},{16,18},{18,... | collective-permute-start | bytes 6291464 | tf_op jit(solution)/shard_map/ppermute | solution.py:297
  182.4 121.8 %collective-permute-start.13 = (bf16[512,2048]{1,0:T(8,128)(2,1)}, bf16[512,2048]{1,0:T(8,128)(2,1)}, u32[]{:S(2)}, u32[]{:S(2)}) collective-permute-start(bf16[512,2048]{1,0:T(8,128)(2,1)} %maximum_select_fusion.10), channel_id=1, source_target_pairs={{0,2},{2,0},{4,6},{6,4},{8,10},{10,8},{12,14},{14,12},{16,18},{18,... | collective-permute-start | bytes 6291464 | tf_op jit(solution)/shard_map/ppermute | solution.py:297
  282.7 319.6 %collective-permute-start.46 = (bf16[512,2048]{1,0:T(8,128)(2,1)}, bf16[512,2048]{1,0:T(8,128)(2,1)}, u32[]{:S(2)}, u32[]{:S(2)}) collective-permute-start(bf16[512,2048]{1,0:T(8,128)(2,1)} %constant_dynamic-slice_fusion.9), channel_id=1, source_target_pairs={{0,2},{2,0},{4,6},{6,4},{8,10},{10,8},{12,14},{14,12},{16,18},{18,... | collective-permute-start | bytes 6291464 | tf_op jit(solution)/shard_map/ppermute | solution.py:297
  485.4 71.5 %collective-permute-start.47 = (bf16[512,2048]{1,0:T(8,128)(2,1)}, bf16[512,2048]{1,0:T(8,128)(2,1)}, u32[]{:S(2)}, u32[]{:S(2)}) collective-permute-start(bf16[512,2048]{1,0:T(8,128)(2,1)} %constant_dynamic-slice_fusion.8), channel_id=1, source_target_pairs={{0,2},{2,0},{4,6},{6,4},{8,10},{10,8},{12,14},{14,12},{16,18},{18,... | collective-permute-start | bytes 6291464 | tf_op jit(solution)/shard_map/ppermute | solution.py:297
  506.2 46.0 %collective-permute-start.27 = (bf16[1536,512]{1,0:T(8,128)(2,1)}, bf16[1536,512]{1,0:T(8,128)(2,1)}, u32[]{:S(2)}, u32[]{:S(2)}) collective-permute-start(bf16[1536,512]{1,0:T(8,128)(2,1)} %constant_dynamic-slice_fusion.18), channel_id=1, source_target_pairs={{0,2},{2,0},{4,6},{6,4},{8,10},{10,8},{12,14},{14,12},{16,18},{18,... | collective-permute-start | bytes 4718600 | tf_op jit(solution)/shard_map/ppermute | solution.py:297
  562.5 82.1 %collective-permute-start.48 = (bf16[512,2048]{1,0:T(8,128)(2,1)}, bf16[512,2048]{1,0:T(8,128)(2,1)}, u32[]{:S(2)}, u32[]{:S(2)}) collective-permute-start(bf16[512,2048]{1,0:T(8,128)(2,1)} %add_convert_fusion.6), channel_id=1, source_target_pairs={{0,1},{1,0},{2,3},{3,2},{4,5},{5,4},{6,7},{7,6},{8,9},{9,8},{10,11... | collective-permute-start | bytes 6291464 | tf_op jit(solution)/shard_map/ppermute | solution.py:300
  575.3 87.8 %collective-permute-start.56 = (bf16[1024,1024]{1,0:T(8,128)(2,1)}, bf16[1024,1024]{1,0:T(8,128)(2,1)S(1)}, u32[]{:S(2)}, u32[]{:S(2)}) collective-permute-start(bf16[1024,1024]{1,0:T(8,128)(2,1)} %constant_dynamic-slice_fusion.4), channel_id=1, source_target_pairs={{0,2},{2,0},{4,6},{6,4},{8,10},{10,8},{12,14},{14,12},{16,18},{18,... | collective-permute-start | bytes 6291464 | tf_op jit(solution)/shard_map/ppermute | solution.py:297
  578.6 109.8 %collective-permute-start.58 = (bf16[1024,1024]{1,0:T(8,128)(2,1)S(1)}, bf16[1024,1024]{1,0:T(8,128)(2,1)S(1)}, u32[]{:S(2)}, u32[]{:S(2)}) collective-permute-start(bf16[1024,1024]{1,0:T(8,128)(2,1)S(1)} %add_convert_fusion.3), channel_id=1, source_target_pairs={{0,1},{1,0},{2,3},{3,2},{4,5},{5,4},{6,7},{7,6},{8,9},{9,8},{10,11... | collective-permute-start | bytes 6291464 | tf_op jit(solution)/shard_map/ppermute | solution.py:300
  599.7 174.2 %collective-permute-start.22 = (f32[9728]{0:T(1024)S(1)}, f32[9728]{0:T(1024)S(1)}, u32[]{:S(2)}, u32[]{:S(2)}) collective-permute-start(f32[9728]{0:T(1024)S(1)} %add.567), channel_id=1, source_target_pairs={{0,2},{2,0},{4,6},{6,4},{8,10},{10,8},{12,14},{14,12},{16,18},{18,... | collective-permute-start | bytes 116744 | tf_op jit(solution)/shard_map/ppermute | solution.py:297
  602.3 172.2 %collective-permute-start.41 = (bf16[32,1024]{1,0:T(8,128)(2,1)S(1)}, bf16[32,1024]{1,0:T(8,128)(2,1)S(1)}, u32[]{:S(2)}, u32[]{:S(2)}) collective-permute-start(bf16[32,1024]{1,0:T(8,128)(2,1)S(1)} %constant_dynamic-slice_fusion.10), channel_id=1, source_target_pairs={{0,16},{2,18},{4,20},{6,22},{8,24},{10,26},{12,28},{14,30},{16,0},... | collective-permute-start | bytes 196616 | tf_op jit(solution)/shard_map/ppermute | solution.py:297
  701.7 49.8 %collective-permute-start.32 = (bf16[192,512]{1,0:T(8,128)(2,1)S(1)}, bf16[192,512]{1,0:T(8,128)(2,1)S(1)}, u32[]{:S(2)}, u32[]{:S(2)}) collective-permute-start(bf16[192,512]{1,0:T(8,128)(2,1)S(1)} %add_convert_fusion.23), channel_id=1, source_target_pairs={{0,16},{2,18},{4,20},{6,22},{8,24},{10,26},{12,28},{14,30},{16,0},... | collective-permute-start | bytes 589832 | tf_op jit(solution)/shard_map/ppermute | solution.py:297
  796.9 52.1 %collective-permute-start.54 = (bf16[256,2048]{1,0:T(8,128)(2,1)S(1)}, bf16[256,2048]{1,0:T(8,128)(2,1)S(1)}, u32[]{:S(2)}, u32[]{:S(2)}) collective-permute-start(bf16[256,2048]{1,0:T(8,128)(2,1)S(1)} %maximum_select_fusion.20), channel_id=1, source_target_pairs={{0,4},{2,6},{4,0},{6,2},{8,12},{10,14},{12,8},{14,10},{16,20},{18,... | collective-permute-start | bytes 3145736 | tf_op jit(solution)/shard_map/ppermute | solution.py:297
  799.4 52.3 %collective-permute-start.20 = (bf16[640,1024]{1,0:T(8,128)(2,1)S(1)}, bf16[640,1024]{1,0:T(8,128)(2,1)}, u32[]{:S(2)}, u32[]{:S(2)}) collective-permute-start(bf16[640,1024]{1,0:T(8,128)(2,1)S(1)} %get-tuple-element.63), channel_id=1, source_target_pairs={{0,1},{1,0},{2,3},{3,2},{4,5},{5,4},{6,7},{7,6},{8,9},{9,8},{10,11... | collective-permute-start | bytes 3932168 | tf_op jit(solution)/shard_map/ppermute | solution.py:300
  814.5 44.6 %collective-permute-start.18 = (bf16[640,1024]{1,0:T(8,128)(2,1)}, bf16[640,1024]{1,0:T(8,128)(2,1)}, u32[]{:S(2)}, u32[]{:S(2)}) collective-permute-start(bf16[640,1024]{1,0:T(8,128)(2,1)} %get-tuple-element.67), channel_id=1, source_target_pairs={{0,1},{1,0},{2,3},{3,2},{4,5},{5,4},{6,7},{7,6},{8,9},{9,8},{10,11... | collective-permute-start | bytes 3932168 | tf_op jit(solution)/shard_map/ppermute | solution.py:300
  821.9 43.7 %collective-permute-start.35 = (bf16[1536,512]{1,0:T(8,128)(2,1)}, bf16[1536,512]{1,0:T(8,128)(2,1)}, u32[]{:S(2)}, u32[]{:S(2)}) collective-permute-start(bf16[1536,512]{1,0:T(8,128)(2,1)} %maximum_select_fusion.15), channel_id=1, source_target_pairs={{0,2},{2,0},{4,6},{6,4},{8,10},{10,8},{12,14},{14,12},{16,18},{18,... | collective-permute-start | bytes 4718600 | tf_op jit(solution)/shard_map/ppermute | solution.py:297
  (120 other events, 2524.1 us)

commit v2 on v1

v2 whole, which is shorter than its diff:
```python
import functools
import math

import jax
import jax.numpy as jnp
from jax import lax
from jax.experimental import pallas as pl
from jax.experimental.pallas import tpu as pltpu
from jax.sharding import PartitionSpec as P

HEAD_DIM = 64
FRAMES = 2
SIDE_SMALL = 16
SIDE_LARGE = 24
EPSILON = 1e-06
ROOT_HALF = 0.7071067811865476
GAUSS_NORM = 0.3989422804014327
LOG2E = math.log2(math.e)
PAIR = 128
NEG = -1e30
STRIPS = ((0, 512, 592), (512, 640, 1168), (640, 1024, 1168), (1024, 1280, 1280))
EARLY = 512


def params(mib=50):
    return pltpu.CompilerParams(vmem_limit_bytes=mib * 2**20)


def takes(microseconds):
    return pl.CostEstimate(
        flops=int(microseconds * 1.1e9), bytes_accessed=int(microseconds * 1e6), transcendentals=0
    )


def low(array):
    return array.astype(jnp.bfloat16)


def wide(array):
    return array.astype(jnp.float32)


def dot(left, right):
    return jnp.dot(left, right, preferred_element_type=jnp.float32)


def dot_nt(left, right):
    return lax.dot_general(
        left, right, (((1,), (1,)), ((), ())), preferred_element_type=jnp.float32
    )


def dot_tn(left, right):
    return lax.dot_general(
        left, right, (((0,), (0,)), ((), ())), preferred_element_type=jnp.float32
    )


def slot_layout(count_one, length):
    large_count = SIDE_LARGE * SIDE_LARGE
    grid_side = jnp.where(count_one == large_count, SIDE_LARGE, SIDE_SMALL).astype(jnp.int32)
    frame_len = grid_side * grid_side + 2
    clip_len = FRAMES * frame_len
    clip_total = jnp.where(count_one == large_count, 1, 2).astype(jnp.int32)
    slot_id = jnp.arange(length, dtype=jnp.int32)
    clip_id = jnp.minimum(slot_id // clip_len, clip_total)
    offset_in = slot_id - clip_id * clip_len
    frame_id = offset_in // frame_len
    place_in = offset_in - frame_id * frame_len - 2
    patch_id = jnp.maximum(place_in, 0)
    is_live = clip_id < clip_total
    is_patch = is_live & (place_in >= 0)
    frame_id = jnp.where(is_live, frame_id, 0)
    patch_row = jnp.where(is_patch, patch_id // grid_side, 0)
    column = jnp.where(is_patch, patch_id - patch_id // grid_side * grid_side, 0)
    first_key = clip_id * clip_len
    past_key = jnp.where(is_live, first_key + (frame_id + 1) * frame_len, length)
    return (first_key, past_key, frame_id, patch_row, column)


def rotary_tables(frame_id, patch_row, column):
    segment = 2 * (HEAD_DIM // 3 // 2)
    half_width = segment // 2
    dim_index = jnp.arange(PAIR, dtype=jnp.int32) % HEAD_DIM
    segment_id = dim_index // segment
    exponent = (dim_index % segment % half_width).astype(jnp.float32)
    frequency = jnp.exp(exponent * (-math.log(10000.0) / half_width))
    pick = lambda number: wide(jnp.where(segment_id == number, 1.0, 0.0))[None, :]
    position = (
        pick(0) * wide(frame_id[:, None])
        + pick(1) * wide(patch_row[:, None])
        + pick(2) * wide(column[:, None])
    )
    angles = position * frequency[None, :]
    lower = (dim_index % segment < half_width)[None, :]
    sine = jnp.where((segment_id < 3)[None, :], jnp.sin(angles), 0.0)
    return (jnp.cos(angles), jnp.where(lower, -sine, 0.0), jnp.where(lower, 0.0, sine))


def spin(x, cos, up, down):
    turn = HEAD_DIM // 3 // 2
    return x * cos + pltpu.roll(x, PAIR - turn, 1) * up + pltpu.roll(x, turn, 1) * down


def standardize(values_in):
    row_mean = jnp.mean(values_in, -1, keepdims=True)
    centred = values_in - row_mean
    norm_scale = lax.rsqrt(jnp.mean(centred * centred, -1, keepdims=True) + EPSILON)
    return (centred * norm_scale, norm_scale)


def fold(x):
    return jnp.sum(x.reshape(x.shape[0] // 8, 8, x.shape[1]), 0)


def whole(array):
    return pl.BlockSpec(array.shape, lambda *_: (0,) * array.ndim, pipeline_mode=pl.Buffered(1))


def enter_kernel(side_ref, mine_ref, arrived_ref, gain_ref, shift_ref, stream_ref, out_ref):
    def step(rows):
        stream_ref[...] = rows
        normed, _ = standardize(wide(rows))
        out_ref[...] = low(normed * gain_ref[...] + shift_ref[...])

    @pl.when(pl.program_id(0) == 0)
    def _():
        step(mine_ref[0])

    @pl.when(pl.program_id(0) == 1)
    def _():
        step(arrived_ref[...])


def enter(side, tokens, arrived, gain, shift):
    _, half, depth = tokens.shape
    vector = pl.BlockSpec((1, depth), lambda i, side: (0, 0))
    out = pl.BlockSpec((half, depth), lambda i, side: (jnp.where(i == 0, side[0], 1 - side[0]), 0))
    return pl.pallas_call(
        enter_kernel,
        grid_spec=pltpu.PrefetchScalarGridSpec(
            num_scalar_prefetch=1,
            grid=(2,),
            in_specs=[
                pl.BlockSpec((1, half, depth), lambda i, side: (side[0], 0, 0)),
                pl.BlockSpec((half, depth), lambda i, side: (0, 0)),
                vector,
                vector,
            ],
            out_specs=[out, out],
        ),
        out_shape=[jax.ShapeDtypeStruct((2 * half, depth), jnp.bfloat16)] * 2,
        compiler_params=params(),
        cost_estimate=takes(5),
        name="enter",
    )(side, tokens, arrived, gain[None], shift[None])


def project_kernel(chunk, x_ref, w_ref, b_ref, cos_ref, up_ref, down_ref, out_ref):
    part = pl.program_id(0)
    for at in range(0, x_ref.shape[0], chunk):
        rows = slice(at, at + chunk)
        y = dot(x_ref[rows, :], w_ref[...]) + b_ref[...]

        @pl.when(part == 2)
        def _():
            out_ref[rows, :] = low(y)

        @pl.when(part < 2)
        def _():
            cos, up, down = cos_ref[rows, :], up_ref[rows, :], down_ref[rows, :]
            for lane in range(0, y.shape[1], PAIR):
                lanes = slice(lane, lane + PAIR)
                out_ref[rows, lanes] = low(spin(y[:, lanes], cos, up, down))


def project(x, weight, bias, tables):
    rows, depth = x.shape
    width = weight.shape[1] // 3
    return pl.pallas_call(
        functools.partial(project_kernel, rows),
        grid=(3,),
        in_specs=[
            whole(x),
            pl.BlockSpec((depth, width), lambda i: (0, i)),
            pl.BlockSpec((1, width), lambda i: (0, i)),
        ]
        + [whole(table) for table in tables],
        out_specs=pl.BlockSpec((rows, width), lambda i: (0, i)),
        out_shape=jax.ShapeDtypeStruct((rows, 3 * width), jnp.bfloat16),
        compiler_params=params(),
        cost_estimate=takes(7),
        name="project",
    )(x, weight, bias[None], *tables)


def attend_kernel(q_ref, k_ref, v_ref, lo_ref, hi_ref, out_ref, root_ref, early_ref, late_ref):
    lane = lax.broadcasted_iota(jnp.int32, (1, PAIR), 1)
    factor = HEAD_DIM**-0.5 * LOG2E
    values = v_ref[...].T
    for first, past, stop in STRIPS:
        count = past - first
        q = q_ref[first:past, :]
        key = lax.broadcasted_iota(jnp.int32, (stop, count), 0)
        allowed = (key >= lo_ref[:, first:past]) & (key < hi_ref[:, first:past])
        outs, roots = [], []
        for head in range(2):
            own = (lane >= HEAD_DIM) == (head == 1)
            scores = dot_nt(k_ref[0:stop, :], jnp.where(own, q, jnp.zeros_like(q)))
            scores = jnp.where(allowed, scores, NEG)
            powers = jnp.exp2((scores - jnp.max(scores, 0, keepdims=True)) * factor)
            root = 1.0 / jnp.sum(powers, 0, keepdims=True)
            powers = low(powers)
            if past <= EARLY:
                early_ref[head, :, first:past] = powers
            else:
                late_ref[head, 0:stop, first - EARLY : past - EARLY] = powers
            rows = slice(head * HEAD_DIM, (head + 1) * HEAD_DIM)
            outs.append(dot(values[rows, 0:stop], powers) * root)
            roots.append(jnp.broadcast_to(root, (HEAD_DIM, count)))
        out_ref[first:past, :] = low(jnp.concatenate(outs, 0).T)
        root_ref[first:past, :] = jnp.concatenate(roots, 0).T


def kept_specs(rows):
    return [
        pl.BlockSpec((2, STRIPS[0][2], EARLY), lambda i: (i, 0, 0)),
        pl.BlockSpec((2, rows, rows - EARLY), lambda i: (i, 0, 0)),
    ]


def attend(heads, first_key, past_key):
    rows, width = heads.shape[0], heads.shape[1] // 3
    pairs = width // PAIR
    block = pl.BlockSpec((rows, PAIR), lambda i: (0, i))
    part = lambda number: pl.BlockSpec((rows, PAIR), lambda i: (0, number * pairs + i))
    return pl.pallas_call(
        attend_kernel,
        grid=(pairs,),
        in_specs=[part(0), part(1), part(2), whole(first_key), whole(past_key)],
        out_specs=[block, block] + kept_specs(rows),
        out_shape=[
            jax.ShapeDtypeStruct((rows, width), jnp.bfloat16),
            jax.ShapeDtypeStruct((rows, width), jnp.float32),
            jax.ShapeDtypeStruct((2 * pairs, STRIPS[0][2], EARLY), jnp.bfloat16),
            jax.ShapeDtypeStruct((2 * pairs, rows, rows - EARLY), jnp.bfloat16),
        ],
        compiler_params=params(),
        cost_estimate=takes(17),
        name="attend",
    )(heads, heads, heads, first_key, past_key)


def attend_back_kernel(
    q_ref, k_ref, v_ref, g_ref, o_ref, root_ref, early_ref, late_ref, cos_ref, up_ref, down_ref,
    out_ref, sums_ref, keys_acc, values_acc, queries_acc,
):
    pair = pl.program_id(0)
    pairs = out_ref.shape[1] // (3 * PAIR)
    lane = lax.broadcasted_iota(jnp.int32, (1, PAIR), 1)
    scale = HEAD_DIM**-0.5
    keys = k_ref[...].T
    for first, past, stop in STRIPS[::-1]:
        q = q_ref[first:past, :]
        g = wide(g_ref[first:past, :]) * root_ref[first:past, :]
        inner = (g * wide(o_ref[first:past, :])).T
        g = low(g)
        for head in range(2):
            own = (lane >= HEAD_DIM) == (head == 1)
            rows = slice(head * HEAD_DIM, (head + 1) * HEAD_DIM)
            g_own = jnp.where(own, g, jnp.zeros_like(g))
            shift = jnp.sum(inner[rows, :], 0, keepdims=True)
            if past <= EARLY:
                powers = early_ref[head, :, first:past]
            else:
                powers = late_ref[head, 0:stop, first - EARLY : past - EARLY]
            g_scores = low(wide(powers) * (dot_nt(v_ref[0:stop, :], g_own) - shift))
            queries_acc[rows, first:past] = dot(keys[rows, 0:stop], g_scores)
            g_keys = dot(g_scores, jnp.where(own, q, jnp.zeros_like(q)))
            g_values = dot(powers, g_own)
            if head == 0:
                total_keys, total_values = g_keys, g_values
            else:
                total_keys, total_values = total_keys + g_keys, total_values + g_values
        if past == STRIPS[-1][1]:
            keys_acc[...] = total_keys
            values_acc[...] = total_values
        else:
            keys_acc[0:stop, :] += total_keys
            values_acc[0:stop, :] += total_values
    cos, up, down = cos_ref[...], -up_ref[...], -down_ref[...]
    grads = (
        low(spin(queries_acc[...].T * scale, cos, up, down)),
        low(spin(keys_acc[...] * scale, cos, up, down)),
        low(values_acc[...]),
    )
    for number, grad in enumerate(grads):
        lanes = pl.ds(pl.multiple_of((number * pairs + pair) * PAIR, PAIR), PAIR)
        out_ref[:, lanes] = grad
        sums_ref[:, lanes] = fold(wide(grad))


def attend_back(heads, g, out, root, early, late, tables):
    rows, width = g.shape
    pairs = width // PAIR
    block = pl.BlockSpec((rows, PAIR), lambda i: (0, i))
    part = lambda number: pl.BlockSpec((rows, PAIR), lambda i: (0, number * pairs + i))
    return pl.pallas_call(
        attend_back_kernel,
        grid=(pairs,),
        in_specs=[part(0), part(1), part(2), block, block, block]
        + kept_specs(rows)
        + [whole(table) for table in tables],
        out_specs=[
            pl.BlockSpec((rows, 3 * width), lambda i: (0, 0)),
            pl.BlockSpec((8, 3 * width), lambda i: (0, 0)),
        ],
        out_shape=[
            jax.ShapeDtypeStruct((rows, 3 * width), jnp.bfloat16),
            jax.ShapeDtypeStruct((8, 3 * width), jnp.float32),
        ],
        scratch_shapes=[
            pltpu.VMEM((rows, PAIR), jnp.float32),
            pltpu.VMEM((rows, PAIR), jnp.float32),
            pltpu.VMEM((PAIR, rows), jnp.float32),
        ],
        compiler_params=params(56),
        cost_estimate=takes(20),
        name="attend_back",
    )(heads, heads, heads, g, out, root, early, late, *tables)


def merge_kernel(count, *refs):
    rights, lefts = refs[:count], refs[count : 2 * count]
    x_ref, bias_ref, gain_ref, shift_ref, residual_ref, out_ref = refs[2 * count :]
    total = wide(x_ref[...]) + bias_ref[...]
    for left, right in zip(lefts, rights):
        total = total + dot(left[...], right[...])
    residual_ref[...] = total
    normed, _ = standardize(total)
    out_ref[...] = low(normed * gain_ref[...] + shift_ref[...])


def merge(lefts, rights, x, bias, gain, shift, block=256):
    rows, depth = x.shape
    row = lambda array: pl.BlockSpec((block, array.shape[1]), lambda i: (i, 0))
    vectors = (bias[None], gain[None], shift[None])
    return pl.pallas_call(
        functools.partial(merge_kernel, len(lefts)),
        grid=(rows // block,),
        in_specs=[whole(w) for w in rights]
        + [row(a) for a in lefts]
        + [row(x)]
        + [whole(v) for v in vectors],
        out_specs=[row(x), row(x)],
        out_shape=[
            jax.ShapeDtypeStruct((rows, depth), jnp.float32),
            jax.ShapeDtypeStruct((rows, depth), jnp.bfloat16),
        ],
        compiler_params=params(),
        cost_estimate=takes(8),
        name="merge",
    )(*rights, *lefts, x, *vectors)


def expand_kernel(chunk, x_ref, w_ref, b_ref, active_ref, slope_ref):
    for at in range(0, x_ref.shape[0], chunk):
        rows = slice(at, at + chunk)
        v = dot(x_ref[rows, :], w_ref[...]) + b_ref[...]
        below = 0.5 + 0.5 * lax.erf(v * ROOT_HALF)
        active_ref[rows, :] = low(v * below)
        slope_ref[rows, :] = low(below + v * jnp.exp(-0.5 * v * v) * GAUSS_NORM)


def expand(x, weight, bias, block=512, chunk=256):
    rows, depth = x.shape
    width = weight.shape[1]
    out = pl.BlockSpec((rows, block), lambda i: (0, i))
    return pl.pallas_call(
        functools.partial(expand_kernel, chunk),
        grid=(width // block,),
        in_specs=[
            whole(x),
            pl.BlockSpec((depth, block), lambda i: (0, i)),
            pl.BlockSpec((1, block), lambda i: (0, i)),
        ],
        out_specs=[out, out],
        out_shape=[jax.ShapeDtypeStruct((rows, width), jnp.bfloat16)] * 2,
        compiler_params=params(),
        cost_estimate=takes(8.5),
        name="expand",
    )(x, weight, bias[None])


def reduce_kernel(count, half, side_ref, *refs):
    rights, lefts = refs[:count], refs[count : 2 * count]
    x_ref, bias_ref, send_ref, keep_ref = refs[2 * count :]
    total = x_ref[...] + bias_ref[...]
    for left, right in zip(lefts, rights):
        total = total + dot(left[...], right[...])

    @pl.when(pl.program_id(0) < half)
    def _():
        send_ref[...] = low(total)

    @pl.when(pl.program_id(0) >= half)
    def _():
        keep_ref[...] = low(total)


def reduce_rows(side, lefts, rights, x, bias, block=320):
    rows, depth = x.shape
    half = rows // 2 // block
    at = lambda i, side: jnp.where(i < half, (1 - side[0]) * half + i, side[0] * half + i - half)
    row = lambda array: pl.BlockSpec((block, array.shape[1]), lambda i, side: (at(i, side), 0))
    return pl.pallas_call(
        functools.partial(reduce_kernel, len(lefts), half),
        grid_spec=pltpu.PrefetchScalarGridSpec(
            num_scalar_prefetch=1,
            grid=(2 * half,),
            in_specs=[whole(w) for w in rights]
            + [row(a) for a in lefts]
            + [row(x), whole(bias[None])],
            out_specs=[
                pl.BlockSpec((block, depth), lambda i, side: (jnp.minimum(i, half - 1), 0)),
                pl.BlockSpec((block, depth), lambda i, side: (jnp.maximum(i - half, 0), 0)),
            ],
        ),
        out_shape=[jax.ShapeDtypeStruct((rows // 2, depth), jnp.bfloat16)] * 2,
        compiler_params=params(),
        cost_estimate=takes(18),
        name="reduce_rows",
    )(side, *rights, *lefts, x, bias[None])


def back_kernel(count, at_ref, *refs):
    rights, lefts = refs[:count], refs[count : 2 * count]
    base_ref, above_ref, gain_ref, out_ref, sums_ref = refs[2 * count :]

    @pl.when(pl.program_id(0) == 0)
    def _():
        sums_ref[...] = jnp.zeros_like(sums_ref)

    g = dot_nt(lefts[0][...], rights[0][...])
    for left, right in zip(lefts[1:], rights[1:]):
        g = g + dot_nt(left[...], right[...])
    normed, scale = standardize(wide(base_ref[...]))
    u = g * gain_ref[...]
    above = wide(above_ref[...])
    inner = jnp.mean(u, -1, keepdims=True) + normed * jnp.mean(u * normed, -1, keepdims=True)
    out = low(above + scale * (u - inner))
    out_ref[...] = out
    sums_ref[0] += fold(g * normed)
    sums_ref[1] += fold(g)
    sums_ref[2] += fold(wide(out))
    sums_ref[3] += fold(above)


def back_norm(at, rows, lefts, rights, base, above, gain, block=320):
    depth = base.shape[1]
    row = lambda array: pl.BlockSpec((block, array.shape[1]), lambda i, at: (at[0] + i, 0))
    return pl.pallas_call(
        functools.partial(back_kernel, len(lefts)),
        grid_spec=pltpu.PrefetchScalarGridSpec(
            num_scalar_prefetch=1,
            grid=(rows // block,),
            in_specs=[whole(w) for w in rights]
            + [row(a) for a in lefts]
            + [row(base), row(above), whole(gain[None])],
            out_specs=[
                pl.BlockSpec((block, depth), lambda i, at: (i, 0)),
                pl.BlockSpec((4, 8, depth), lambda i, at: (0, 0, 0)),
            ],
        ),
        out_shape=[
            jax.ShapeDtypeStruct((rows, depth), jnp.bfloat16),
            jax.ShapeDtypeStruct((4, 8, depth), jnp.float32),
        ],
        compiler_params=params(),
        cost_estimate=takes(20 * rows / 1280),
        name="back_norm",
    )(at, *rights, *lefts, base, above, gain[None])


def place_kernel(steps, flag_ref, mine_ref, theirs_ref, out_ref):
    @pl.when(pl.program_id(0) < steps)
    def _():
        out_ref[...] = mine_ref[...].astype(out_ref.dtype).reshape(out_ref.shape)

    @pl.when(pl.program_id(0) >= steps)
    def _():
        out_ref[...] = theirs_ref[...].astype(out_ref.dtype).reshape(out_ref.shape)


def place(flag, mine, theirs, steps, in_block, in_index, out_shape, out_block, out_index, dtype):
    def target(i, flag):
        return out_index(jnp.where(i < steps, flag[0], 1 - flag[0]), jnp.where(i < steps, i, i - steps))

    return pl.pallas_call(
        functools.partial(place_kernel, steps),
        grid_spec=pltpu.PrefetchScalarGridSpec(
            num_scalar_prefetch=1,
            grid=(2 * steps,),
            in_specs=[
                pl.BlockSpec(in_block, lambda i, flag: in_index(jnp.minimum(i, steps - 1))),
                pl.BlockSpec(in_block, lambda i, flag: in_index(jnp.maximum(i - steps, 0))),
            ],
            out_specs=pl.BlockSpec(out_block, target),
        ),
        out_shape=jax.ShapeDtypeStruct(out_shape, dtype),
        compiler_params=params(),
        cost_estimate=takes(4),
        name="place",
    )(flag, mine, theirs)


def place_rows(flag, mine, theirs, steps, dtype):
    rows, width = mine.shape
    block = (rows // steps, width)
    return place(
        flag, mine, theirs, steps, block, lambda j: (j, 0),
        (2 * rows, width), block, lambda half, j: (half * steps + j, 0), dtype,
    )


def place_columns(flag, mine, theirs, steps, dtype):
    rows, width = mine.shape
    block = (rows // steps, width)
    return place(
        flag, mine, theirs, steps, block, lambda j: (j, 0),
        (rows, 2 * width), block, lambda half, j: (j, half), dtype,
    )


def place_heads(flag, mine, theirs, dtype):
    rows, width = mine.shape[0], mine.shape[1] // 3
    return place(
        flag, mine, theirs, 3, (rows, width), lambda j: (0, j),
        (3, rows, 2 * width), (1, rows, width), lambda half, j: (j, 0, half), dtype,
    )


def column_sums(matrix):
    unit_column = jnp.ones((matrix.shape[0],), matrix.dtype)
    return jnp.dot(unit_column, matrix, preferred_element_type=jnp.float32)


KEEP, SEND = 0, 1
OWN, FAR = 0, 1
QUARTERS = ((FAR, SEND), (FAR, KEEP), (OWN, SEND), (OWN, KEEP))


def on_device(
    spread,
    tokens,
    cotangent,
    patch_count,
    first_gain,
    first_shift,
    heads_weight,
    heads_bias,
    merge_weight,
    merge_bias,
    second_gain,
    second_shift,
    expand_weight,
    expand_bias,
    reduce_weight,
    reduce_bias,
):
    levels = spread.bit_length() - 1
    rest = list(range(1, levels))
    chunks = spread // 2
    location = lax.axis_index("dp")
    side = lax.axis_index("mp")
    sides = side[None].astype(jnp.int32)
    previous = []

    def bit(level):
        return (location >> level) & 1

    core = bit(0)[None].astype(jnp.int32)

    def tie(array, *others):
        return lax.optimization_barrier((array,) + others)[0] if others else array

    def after(array):
        return tie(array, *previous)

    def did(*arrays):
        previous[:] = arrays
        return arrays[0] if len(arrays) == 1 else arrays

    def swap(array, level):
        return lax.ppermute(array, "dp", [(i, i ^ (1 << level)) for i in range(spread)])

    def cross(array):
        return lax.ppermute(array, "mp", [(0, 1), (1, 0)])

    def half_of(array, flag, axis=0):
        size = array.shape[axis] // 2
        return lax.dynamic_slice_in_dim(array, flag * size, size, axis)

    def chunk_of(array):
        size = array.shape[0] // chunks
        return lax.dynamic_slice_in_dim(array, (location >> 1) * size, size, 0)

    def split(array, level):
        left = spread >> (level + 1)
        four = array.reshape(left, 2, -1, array.shape[1])
        part = lambda flag: lax.dynamic_index_in_dim(four, flag, 1, False).reshape(-1, array.shape[1])
        return part(bit(level)), part(1 - bit(level))

    def join(mine, theirs, level):
        left = spread >> (level + 1)
        four = lambda array: array.reshape(left, 1, -1, array.shape[1])
        pair = jnp.where(
            bit(level) == 0,
            jnp.concatenate([four(mine), four(theirs)], 1),
            jnp.concatenate([four(theirs), four(mine)], 1),
        )
        return pair.reshape(-1, mine.shape[1])

    def quarters_of(own, axis):
        return [half_of(own, bit(0), axis), half_of(own, 1 - bit(0), axis)]

    tokens, cotangent = tokens[:, 0], cotangent[:, 0]
    tokens_far = cross(lax.dynamic_index_in_dim(tokens, 1 - side, 0, False))
    heads_three = heads_weight.transpose(1, 0, 2)
    heads_own = [
        jnp.concatenate([half_of(heads_three[n], flag, 1) for n in range(3)], 1)
        for flag in (bit(0), 1 - bit(0))
    ]
    merge_own = quarters_of(merge_weight, 0)
    expand_own = quarters_of(expand_weight, 1)
    reduce_own = quarters_of(reduce_weight, 0)
    pack = lambda hb, eb: jnp.concatenate([hb.reshape(-1), eb])
    bias_own = [
        pack(half_of(heads_bias, flag, 1), half_of(expand_bias, flag)) for flag in (bit(0), 1 - bit(0))
    ]
    three = heads_bias.size // 2
    near = rest[:2]
    heads_piece = heads_own[KEEP]
    for level in near:
        heads_piece = split(heads_piece, level)[0]
    up_piece = jnp.concatenate([chunk_of(expand_own[KEEP]), chunk_of(merge_own[KEEP])])
    down_piece = chunk_of(reduce_own[KEEP])

    count_one = lax.dynamic_index_in_dim(patch_count[:, 0], side, 0, False)
    length = 2 * tokens.shape[1]
    first_key, past_key, frame_id, patch_row, column = slot_layout(count_one, length)
    tables = rotary_tables(frame_id, patch_row, column)
    first_key, past_key = first_key[None], past_key[None]

    heads_piece = cross(tie(heads_piece, tokens_far))
    up_piece = cross(tie(up_piece, tokens_far))
    bias_both = cross(tie(jnp.concatenate(bias_own), tokens_far))
    bias_far = [bias_both[: bias_both.size // 2], bias_both[bias_both.size // 2 :]]
    stream, first_out = did(*enter(sides, tokens, tokens_far, first_gain, first_shift))
    heads, seen = {}, {}
    heads_all = [heads_own, None]
    bias_all = (bias_own, bias_far)

    def look(p, c):
        heads[p, c] = did(project(after(first_out), heads_all[p][c], bias_all[p][c][:three], tables))

    def attention(p, c):
        seen[p, c] = did(*attend(after(heads[p, c]), first_key, past_key))

    def gathered(array, *splits):
        array = lax.all_gather(array, "dp", axis=0, tiled=True)
        array = array.reshape(chunks, 2, -1, array.shape[1])
        quarters, at = [], 0
        for size in splits:
            part = array[:, :, at : at + size]
            quarters.append(
                [
                    lax.dynamic_index_in_dim(part, flag, 1, False).reshape(-1, array.shape[3])
                    for flag in (bit(0), 1 - bit(0))
                ]
            )
            at += size
        return quarters

    look(OWN, KEEP)
    heads_piece = did(after(heads_piece))
    if len(near) > 1:
        heads_next = swap(heads_piece, near[1])
    look(OWN, SEND)
    up_sizes = (expand_own[0].shape[0] // chunks, merge_own[0].shape[0] // chunks)
    up_gathered = gathered(after(up_piece), *up_sizes)
    down_piece = cross(after(down_piece))
    if len(near) > 1:
        heads_piece = did(join(after(heads_piece), heads_next, near[1]))
    heads_next = swap(heads_piece, near[0])
    attention(OWN, KEEP)
    attention(OWN, SEND)
    heads_piece = did(join(after(heads_piece), heads_next, near[0]))
    heads_all[FAR] = [heads_piece, swap(heads_piece, 0)]
    cotangent_far = cross(after(lax.dynamic_index_in_dim(cotangent, 1 - side, 0, False)))
    (reduce_far,) = gathered(after(down_piece), down_piece.shape[0])
    look(FAR, KEEP)
    attention(FAR, KEEP)
    look(FAR, SEND)
    attention(FAR, SEND)
    expand_far, merge_far = ([after(q) for q in quarters] for quarters in up_gathered)
    merge_all = (merge_own, merge_far)
    expand_all = (expand_own, expand_far)
    reduce_all = (reduce_own, reduce_far)
    mixed = {q: seen[q][0] for q in QUARTERS}
    residual, second_out = did(
        *merge(
            [mixed[q] for q in QUARTERS], [merge_all[p][c] for p, c in QUARTERS],
            after(stream), merge_bias, second_gain, second_shift,
        )
    )
    cotangent_far = after(cotangent_far)
    grad_two = jnp.where(
        side == 0,
        jnp.concatenate([cotangent[0], cotangent_far]),
        jnp.concatenate([cotangent_far, cotangent[1]]),
    )

    active, slope, grad_pre = {}, {}, {}

    def widen(p, c):
        active[p, c], slope[p, c] = did(
            *expand(after(second_out), expand_all[p][c], bias_all[p][c][three:])
        )

    def back_active(p, c):
        grad_pre[p, c] = did(low(dot_nt(after(grad_two), reduce_all[p][c]) * wide(slope[p, c])))

    def product(left, right, *arrived):
        total = dot_tn(after(left), right)
        for array in arrived:
            total = total + wide(array)
        return did(low(total))

    def scattered(array, level):
        keep, send = split(after(array), level)
        did(send)
        return keep, swap(send, level)

    def summed(keep, arrived):
        return did(low(wide(after(keep)) + wide(arrived)))

    widen(FAR, SEND)
    widen(FAR, KEEP)
    sent = swap(product(active[FAR, SEND], grad_two), 0)
    widen(OWN, SEND)
    reduce_far_sum = product(active[FAR, KEEP], grad_two, sent)
    reduce_cross = cross(reduce_far_sum)
    widen(OWN, KEEP)
    sent = swap(product(active[OWN, SEND], grad_two), 0)
    back_active(FAR, SEND)
    reduce_sum = product(active[OWN, KEEP], grad_two, sent)
    back_active(FAR, KEEP)
    sent = swap(product(second_out, grad_pre[FAR, SEND]), 0)
    back_active(OWN, SEND)
    expand_far_sum = product(second_out, grad_pre[FAR, KEEP], sent)
    back_active(OWN, KEEP)
    sent = swap(product(second_out, grad_pre[OWN, SEND]), 0)
    reduce_sum = summed(reduce_sum, reduce_cross)
    expand_cross = cross(tie(expand_far_sum, reduce_cross))
    reduce_keep, reduce_next = scattered(reduce_sum, rest[0])
    layer_send, layer_keep = did(
        *reduce_rows(
            sides, [active[q] for q in QUARTERS], [reduce_all[p][c] for p, c in QUARTERS],
            after(residual), reduce_bias,
        )
    )
    expand_sum = product(second_out, grad_pre[OWN, KEEP], sent)
    zero = jnp.zeros((1,), jnp.int32)
    reduce_sum = summed(reduce_keep, reduce_next)
    reduce_keep, reduce_next = scattered(reduce_sum, rest[1])
    grad_one, second_sums = did(
        *back_norm(
            zero, length, [grad_pre[q] for q in QUARTERS], [expand_all[p][c] for p, c in QUARTERS],
            after(residual), grad_two, second_gain,
        )
    )
    reduce_sum = summed(reduce_keep, reduce_next)
    for level in rest[2:]:
        reduce_keep, reduce_next = scattered(reduce_sum, level)
        reduce_sum = low(wide(reduce_keep) + wide(reduce_next))

    grad_mixed, grad_heads, head_sums = {}, {}, {}

    def back_mixed(p, c):
        grad_mixed[p, c] = did(low(dot_nt(after(grad_one), merge_all[p][c])))

    def back_attention(q):
        out, root, early, late = seen[q]
        grad_heads[q], sums = did(
            *attend_back(heads[q], after(grad_mixed[q]), out, root, early, late, tables)
        )
        head_sums[q] = jnp.sum(sums, 0)

    sent_far = swap(product(mixed[FAR, SEND], grad_one), 0)
    sent_own = swap(product(mixed[OWN, SEND], grad_one), 0)
    for p, c in QUARTERS:
        back_mixed(p, c)
    merge_far_sum = product(mixed[FAR, KEEP], grad_one, sent_far)
    merge_sum = product(mixed[OWN, KEEP], grad_one, sent_own)
    expand_sum = summed(expand_sum, expand_cross)
    merge_cross = cross(tie(merge_far_sum, expand_cross))
    layer_far = cross(tie(layer_send, expand_cross))
    expand_keep, expand_next = scattered(expand_sum, rest[0])
    back_attention((FAR, SEND))
    reduce_total = lax.all_gather(after(reduce_sum), "dp", axis=0, tiled=True)
    expand_sum = summed(expand_keep, expand_next)
    expand_keep, expand_next = scattered(expand_sum, rest[1])
    sent = swap(product(first_out, grad_heads[FAR, SEND]), 0)
    merge_sum = summed(merge_sum, merge_cross)
    merge_keep, merge_next = scattered(merge_sum, rest[0])
    back_attention((FAR, KEEP))
    heads_far_sum = product(first_out, grad_heads[FAR, KEEP], sent)
    heads_cross = cross(heads_far_sum)
    expand_sum = summed(expand_keep, expand_next)
    merge_sum = summed(merge_keep, merge_next)
    merge_keep, merge_next = scattered(merge_sum, rest[1])
    for level in rest[2:]:
        expand_keep, expand_next = scattered(expand_sum, level)
        expand_sum = low(wide(expand_keep) + wide(expand_next))
    back_attention((OWN, SEND))
    merge_sum = summed(merge_keep, merge_next)
    for level in rest[2:]:
        merge_keep, merge_next = scattered(merge_sum, level)
        merge_sum = low(wide(merge_keep) + wide(merge_next))
    sent = swap(product(first_out, grad_heads[OWN, SEND]), 0)
    back_attention((OWN, KEEP))
    expand_total = lax.all_gather(
        after(jnp.concatenate([expand_sum, merge_sum])), "dp", axis=0, tiled=True
    )
    heads_sum = product(first_out, grad_heads[OWN, KEEP], sent, heads_cross)
    heads_keep, heads_next = scattered(heads_sum, rest[0])

    lefts = [grad_heads[q] for q in QUARTERS]
    rights = [heads_all[p][c] for p, c in QUARTERS]
    per_half = length // 2 // 320
    tokens_send, sums_a = did(
        *back_norm(
            (1 - sides) * per_half, length // 2, lefts, rights, stream, grad_one, after(first_gain)
        )
    )
    tokens_cross = cross(tokens_send)
    heads_sum = summed(heads_keep, heads_next)
    heads_keep, heads_next = scattered(heads_sum, rest[1])
    tokens_keep, sums_b = did(
        *back_norm(sides * per_half, length // 2, lefts, rights, stream, grad_one, after(first_gain))
    )
    first_sums = sums_a + sums_b
    heads_sum = summed(heads_keep, heads_next)
    for level in rest[2:]:
        heads_keep, heads_next = scattered(heads_sum, level)
        heads_sum = summed(heads_keep, heads_next)

    small = {q: jnp.concatenate([head_sums[q], column_sums(grad_pre[q])]) for q in QUARTERS}
    both = jnp.concatenate(
        [
            jnp.sum(part, 0)
            for part in (
                first_sums[0], first_sums[1], second_sums[0], second_sums[1], second_sums[2], second_sums[3],
            )
        ]
    )
    arrived = swap(jnp.concatenate([small[FAR, SEND], small[OWN, SEND], both]), 0)
    size = small[OWN, KEEP].size
    far = small[FAR, KEEP] + arrived[:size]
    mine = jnp.concatenate([small[OWN, KEEP], both]) + arrived[size:]
    mine = mine + cross(jnp.concatenate([far, mine[size:]]))
    for level in rest:
        mine = mine + swap(mine, level)
    both = mine[size:]
    mine = mine[:size]
    theirs = swap(mine, 0)
    first = jnp.where(bit(0) == 0, mine, theirs)
    second = jnp.where(bit(0) == 0, theirs, mine)
    heads_bias_total = jnp.concatenate([first[:three].reshape(3, -1), second[:three].reshape(3, -1)], 1)
    expand_bias_total = jnp.concatenate([first[three:], second[three:]])
    (first_gain_total, first_shift_total, second_gain_total, second_shift_total, merge_bias_total,
     reduce_bias_total) = both.reshape(6, -1)

    def rows_out(keep, arrived, dtype):
        return place_rows(sides, keep, arrived, 1, dtype).reshape(2, 1, length // 2, -1)

    def in_rows(array):
        return wide(array.transpose(1, 0, 2, 3).reshape(-1, array.shape[3]))

    reduce_total = reduce_total.reshape(chunks, 2, -1, reduce_total.shape[1])
    expand_total = expand_total.reshape(chunks, 2, -1, expand_total.shape[1])
    rows = expand_sum.shape[0]
    merge_total = expand_total[:, :, rows:]
    expand_total = expand_total[:, :, :rows]
    expand_total = jnp.concatenate(
        [expand_total[:, n].reshape(-1, expand_total.shape[3]) for n in range(2)], 1
    )
    layer_out = rows_out(after(layer_keep), layer_far, jnp.bfloat16)
    reduce_out = in_rows(reduce_total)
    for level in rest[::-1]:
        heads_sum = join(heads_sum, swap(heads_sum, level), level)
    heads_out = place_heads(core, heads_sum, swap(heads_sum, 0), jnp.float32)
    return (
        layer_out,
        rows_out(tokens_keep, tokens_cross, jnp.float32),
        first_gain_total,
        first_shift_total,
        heads_out.transpose(1, 0, 2),
        heads_bias_total,
        in_rows(merge_total),
        merge_bias_total,
        second_gain_total,
        second_shift_total,
        wide(expand_total),
        expand_bias_total,
        reduce_out,
        reduce_bias_total,
    )


def solution(mesh):
    rows = P(None, "dp", "mp", None)
    columns = P(None, "mp")
    heads = P(None, None, "mp")
    return jax.shard_map(
        functools.partial(on_device, mesh.shape["dp"]),
        mesh=mesh,
        in_specs=(
            rows, rows, P(None, "dp"), P(), P(), heads, columns, P("mp", None), P(), P(), P(), columns,
            P("mp"), P("mp", None), P(),
        ),
        out_specs=(
            rows, rows, P(), P(), heads, columns, P("mp", None), P(), P(), P(), columns, P("mp"),
            P("mp", None), P(),
        ),
        check_vma=False,
    )
```

time: 893 us -> 710 us (0.80)
  Pallas kernels: 159 us -> 300 us
  waiting for transfers between devices: 295 us -> 162 us
  matrix products: 213 us -> 90.1 us
  other arithmetic: 112 us -> 31.4 us
  starting transfers between devices: 55.8 us -> 41.8 us
  between operations: 3.94 us -> 17 us
  local copies, waits for them, and re-layouts: 47.4 us -> 59.2 us
    pallas_call x6 -> x25, Pallas kernels: 159 us -> 300 us  [the longest x4 81.1 us: attend_back(): pl.pallas_call(attend_back_kernel, grid=(pairs,), in_specs=[part(0), part...]
    dot_general x12 -> x8, matrix products: 97.7 us -> 24.1 us  [dot_nt(): lax.dot_general(left, right, (((1,), (1,)), ((), ())), preferred_element_...]
    ppermute x52 -> x32, waiting for transfers between devices: 157 us -> 83.9 us  [swap(): lax.ppermute(array, 'dp', [(i, i ^ 1 << level) for i in range(spread)])]
    ppermute x14 -> x13, waiting for transfers between devices: 137 us -> 77.7 us  [cross(): return lax.ppermute(array, 'mp', [(0, 1), (1, 0)])]
    dot_general x6 -> x0, matrix products: 50.7 us -> none  [dot(): return jnp.dot(left, right, preferred_element_type=jnp.float32)]
    select_n x25 -> x10, other arithmetic: 34.8 us -> 3.79 us  [the longest x1 2.58 us: on_device(): jnp.where(side == 0, jnp.concatenate([cotangent[0], cotangent_far]), jnp....]
    convert_element_type x24 -> x17, other arithmetic: 40.9 us -> 10.3 us  [low(): return array.astype(jnp.bfloat16)]
    ppermute x52 -> x32, starting transfers between devices: 39.5 us -> 25.8 us  [swap(): lax.ppermute(array, 'dp', [(i, i ^ 1 << level) for i in range(spread)])]
  transfers between devices with their start and end apart: 66 -> 49, of which waited for: 23 -> 17; matrix products, arithmetic and copies ran while one was open for 40% -> 19% of each run, Pallas kernels for 18% -> 43%
where the time goes in v2:
time: 710 us; the launch traced here: 701 us
  Pallas kernels  300 us (42%)
  waiting for transfers between devices  162 us (23%)
  matrix products  90.1 us (13%)
  local copies, waits for them, and re-layouts  59.2 us (8%)
  starting transfers between devices  41.8 us (6%)
  other arithmetic  31.4 us (4%)
  between operations  17 us (2%)
    ppermute x32, waiting for transfers between devices, swap(): lax.ppermute(array, 'dp', [(i, i ^ 1 << level) for i in range(spread)])  83.9 us
    pallas_call x4, Pallas kernels, attend_back(): pl.pallas_call(attend_back_kernel, grid=(pairs,), in_specs=[part(0), part...  81.1 us
    ppermute x13, waiting for transfers between devices, cross(): return lax.ppermute(array, 'mp', [(0, 1), (1, 0)])  77.7 us
    pallas_call x4, Pallas kernels, attend(): pl.pallas_call(attend_kernel, grid=(pairs,), in_specs=[part(0), part(1),...  71.1 us
    dot_general x16, matrix products, dot_tn(): lax.dot_general(left, right, (((0,), (0,)), ((), ())), preferred_element_...  61.3 us
    pallas_call x3, Pallas kernels, back_norm(): pl.pallas_call(functools.partial(back_kernel, len(lefts)), grid_spec=pltp...  41.7 us
    pallas_call x4, Pallas kernels, expand(): pl.pallas_call(functools.partial(expand_kernel, chunk), grid=(width // bl...  36.1 us
    pallas_call x4, Pallas kernels, project(): pl.pallas_call(functools.partial(project_kernel, rows), grid=(3,), in_spe...  28.9 us
  transfers between devices with their start and end apart: 49, of which 17 were waited for; matrix products, arithmetic and copies ran while one was open for 19% of the time, Pallas kernels for 43%

profile of v2, /device:TPU:0, one launch (start us, length us, event | category | flops | bytes accessed | tf_op | source)
XLA Modules:
  0.0 701.1 jit_solution(1826279268014681383)
XLA Ops:
  26.9 14.8 %collective-permute-done.arrived_ref = bf16[640,1024]{1,0:T(8,128)(2,1)S(1)} collective-permute-done((bf16[640,1024]{1,0:T(8,128)(2,1)}, bf16[640,1024]{1,0:T(8,128)(2,1)S(1)}, u32[]{:S(2)}, u32[]{:S(2)}) %collective-permute-start) | collective-permute-done | bytes 1310752 | tf_op jit(solution)/shard_map/ppermute | solution.py:598
  80.3 15.4 %collective-permute-done.3 = bf16[256,768]{1,0:T(8,128)(2,1)S(1)} collective-permute-done((bf16[256,768]{1,0:T(8,128)(2,1)S(1)}, bf16[256,768]{1,0:T(8,128)(2,1)S(1)}, u32[]{:S(2)}, u32[]{:S(2)}) %collective-permute-start.3) | collective-permute-done | bytes 393248 | tf_op jit(solution)/shard_map/ppermute | solution.py:595
  98.9 17.6 %attend.4 = (bf16[1280,256]{1,0:T(8,128)(2,1)S(1)}, f32[1280,256]{1,0:T(8,128)S(1)}, bf16[4,592,512]{2,1,0:T(8,128)(2,1)}, bf16[4,1280,768]{2,1,0:T(8,128)(2,1)}) custom-call(bf16[1280,768]{1,0:T(8,128)(2,1)S(1)} %copy-done.48, bf16[1280,768]{1,0:T(8,128)(2,1)S(1)} %copy-done.48, bf16[1280,768]{1,0:T(8,128)(2,1)S(1)} %copy-done.48, ...), custom_call_target="tpu_custom_call" | custom-call | flops 18699999232 | bytes 17000000 | tf_op jit(solution)/shard_map/attend/pallas_call | solution.py:237
  118.5 17.8 %attend.5 = (bf16[1280,256]{1,0:T(8,128)(2,1)S(1)}, f32[1280,256]{1,0:T(8,128)S(1)}, bf16[4,592,512]{2,1,0:T(8,128)(2,1)}, bf16[4,1280,768]{2,1,0:T(8,128)(2,1)}) custom-call(bf16[1280,768]{1,0:T(8,128)(2,1)S(1)} %copy-done.49, bf16[1280,768]{1,0:T(8,128)(2,1)S(1)} %copy-done.49, bf16[1280,768]{1,0:T(8,128)(2,1)S(1)} %copy-done.49, ...), custom_call_target="tpu_custom_call" | custom-call | flops 18699999232 | bytes 17000000 | tf_op jit(solution)/shard_map/attend/pallas_call | solution.py:237
  146.8 18.0 %attend.6 = (bf16[1280,256]{1,0:T(8,128)(2,1)S(1)}, f32[1280,256]{1,0:T(8,128)S(1)}, bf16[4,592,512]{2,1,0:T(8,128)(2,1)}, bf16[4,1280,768]{2,1,0:T(8,128)(2,1)}) custom-call(bf16[1280,768]{1,0:T(8,128)(2,1)S(1)} %copy-done.50, bf16[1280,768]{1,0:T(8,128)(2,1)S(1)} %copy-done.50, bf16[1280,768]{1,0:T(8,128)(2,1)S(1)} %copy-done.50, ...), custom_call_target="tpu_custom_call" | custom-call | flops 18699999232 | bytes 17000000 | tf_op jit(solution)/shard_map/attend/pallas_call | solution.py:237
  176.5 17.6 %attend.7 = (bf16[1280,256]{1,0:T(8,128)(2,1)S(1)}, f32[1280,256]{1,0:T(8,128)S(1)}, bf16[4,592,512]{2,1,0:T(8,128)(2,1)}, bf16[4,1280,768]{2,1,0:T(8,128)(2,1)}) custom-call(bf16[1280,768]{1,0:T(8,128)(2,1)S(1)} %copy-done.51, bf16[1280,768]{1,0:T(8,128)(2,1)S(1)} %copy-done.51, bf16[1280,768]{1,0:T(8,128)(2,1)S(1)} %copy-done.51, ...), custom_call_target="tpu_custom_call" | custom-call | flops 18699999232 | bytes 17000000 | tf_op jit(solution)/shard_map/attend/pallas_call | solution.py:237
  237.6 10.0 %expand.6 = (bf16[1280,1024]{1,0:T(8,128)(2,1)}, bf16[1280,1024]{1,0:T(8,128)(2,1)}) custom-call(bf16[1280,1024]{1,0:T(8,128)(2,1)} %get-tuple-element.208.x_ref, bf16[1024,1024]{1,0:T(8,128)(2,1)S(1)} %get-tuple-element.311.w_ref.refs_2_, f32[1,1024]{1,0:T(1,128)S(1)} %bitcast.216), custom_call_target="tpu_custom_call" | custom-call | flops 9349999616 | bytes 8500000 | tf_op jit(solution)/shard_map/expand/pallas_call | solution.py:379
  251.8 9.0 %expand.7 = (bf16[1280,1024]{1,0:T(8,128)(2,1)}, bf16[1280,1024]{1,0:T(8,128)(2,1)}) custom-call(bf16[1280,1024]{1,0:T(8,128)(2,1)} %get-tuple-element.208.x_ref, bf16[1024,1024]{1,0:T(8,128)(2,1)S(1)} %get-tuple-element.310.w_ref.refs_3_, f32[1,1024]{1,0:T(1,128)S(1)} %bitcast.215), custom_call_target="tpu_custom_call" | custom-call | flops 9349999616 | bytes 8500000 | tf_op jit(solution)/shard_map/expand/pallas_call | solution.py:379
  313.2 20.6 %collective-permute-done.12 = bf16[1024,1024]{1,0:T(8,128)(2,1)S(1)} collective-permute-done((bf16[1024,1024]{1,0:T(8,128)(2,1)}, bf16[1024,1024]{1,0:T(8,128)(2,1)S(1)}, u32[]{:S(2)}, u32[]{:S(2)}) %collective-permute-start.12) | collective-permute-done | bytes 2097184 | tf_op jit(solution)/shard_map/ppermute | solution.py:598
  336.3 18.0 %reduce_rows.1 = (bf16[640,1024]{1,0:T(8,128)(2,1)}, bf16[640,1024]{1,0:T(8,128)(2,1)S(1)}) custom-call(s32[1]{0:T(128)} %bitcast.side_ref.flag_ref, bf16[1024,1024]{1,0:T(8,128)(2,1)} %bitcast.262, bf16[1024,1024]{1,0:T(8,128)(2,1)} %bitcast.260, bf16[1024,1024]{1,0:T(8,128)(2,1)} %get-tuple-element.393.refs_2_, ...), custom_call_target="tpu_custom_call" | custom-call | flops 19800000512 | bytes 18000000 | tf_op jit(solution)/shard_map/reduce_rows/pallas_call | solution.py:416
  361.7 20.4 %back_norm.3 = (bf16[1280,1024]{1,0:T(8,128)(2,1)}, f32[4,8,1024]{2,1,0:T(8,128)S(1)}) custom-call(s32[1]{0:T(128)} %constant.257.clone.1.at_ref, bf16[1024,1024]{1,0:T(8,128)(2,1)S(1)} %bitcast.204, bf16[1024,1024]{1,0:T(8,128)(2,1)} %bitcast.202, bf16[1024,1024]{1,0:T(8,128)(2,1)} %copy-done.4, bf16[1024,1024]{1,0:T(8,128)(2,1)} %copy-done.3, ...), custom_call_target="tpu_custom_call" | custom-call | flops 22000001024 | bytes 20000000 | tf_op jit(solution)/shard_map/back_norm/pallas_call | solution.py:462
  406.7 20.3 %attend_back.4 = (bf16[1280,768]{1,0:T(8,128)(2,1)}, f32[8,768]{1,0:T(8,128)}) custom-call(bf16[1280,768]{1,0:T(8,128)(2,1)} %project.7.q_ref.k_ref.v_ref, bf16[1280,768]{1,0:T(8,128)(2,1)} %project.7.q_ref.k_ref.v_ref, bf16[1280,768]{1,0:T(8,128)(2,1)} %project.7.q_ref.k_ref.v_ref, bf16[1280,256]{1,0:T(8,128)(2,1)} %convolution_convert_fusion.3.g_ref, ...), custom_call_target="tpu_custom_call" | custom-call | flops 22000001024 | bytes 20000000 | tf_op jit(solution)/shard_map/attend_back/pallas_call | solution.py:308
  441.9 20.1 %attend_back.5 = (bf16[1280,768]{1,0:T(8,128)(2,1)}, f32[8,768]{1,0:T(8,128)}) custom-call(bf16[1280,768]{1,0:T(8,128)(2,1)} %project.6.q_ref.k_ref.v_ref, bf16[1280,768]{1,0:T(8,128)(2,1)} %project.6.q_ref.k_ref.v_ref, bf16[1280,768]{1,0:T(8,128)(2,1)} %project.6.q_ref.k_ref.v_ref, bf16[1280,256]{1,0:T(8,128)(2,1)} %convolution_convert_fusion.2.g_ref, ...), custom_call_target="tpu_custom_call" | custom-call | flops 22000001024 | bytes 20000000 | tf_op jit(solution)/shard_map/attend_back/pallas_call | solution.py:308
  472.3 20.1 %attend_back.6 = (bf16[1280,768]{1,0:T(8,128)(2,1)}, f32[8,768]{1,0:T(8,128)}) custom-call(bf16[1280,768]{1,0:T(8,128)(2,1)} %project.5.q_ref.k_ref.v_ref, bf16[1280,768]{1,0:T(8,128)(2,1)} %project.5.q_ref.k_ref.v_ref, bf16[1280,768]{1,0:T(8,128)(2,1)} %project.5.q_ref.k_ref.v_ref, bf16[1280,256]{1,0:T(8,128)(2,1)} %convolution_convert_fusion.1.g_ref, ...), custom_call_target="tpu_custom_call" | custom-call | flops 22000001024 | bytes 20000000 | tf_op jit(solution)/shard_map/attend_back/pallas_call | solution.py:308
  498.6 20.5 %attend_back.7 = (bf16[1280,768]{1,0:T(8,128)(2,1)}, f32[8,768]{1,0:T(8,128)}) custom-call(bf16[1280,768]{1,0:T(8,128)(2,1)} %project.4.q_ref.k_ref.v_ref, bf16[1280,768]{1,0:T(8,128)(2,1)} %project.4.q_ref.k_ref.v_ref, bf16[1280,768]{1,0:T(8,128)(2,1)} %project.4.q_ref.k_ref.v_ref, bf16[1280,256]{1,0:T(8,128)(2,1)} %convolution_convert_fusion.g_ref, ...), custom_call_target="tpu_custom_call" | custom-call | flops 22000001024 | bytes 20000000 | tf_op jit(solution)/shard_map/attend_back/pallas_call | solution.py:308
  529.4 11.2 %back_norm.4 = (bf16[640,1024]{1,0:T(8,128)(2,1)}, f32[4,8,1024]{2,1,0:T(8,128)S(1)}) custom-call(s32[1]{0:T(128)S(6)} %mul.201.at_ref, bf16[1024,768]{1,0:T(8,128)(2,1)} %collective-permute-done.7.w_ref.refs_0_, bf16[1024,768]{1,0:T(8,128)(2,1)} %bitcast.207, bf16[1024,768]{1,0:T(8,128)(2,1)} %copy-done.5, bf16[1024,768]{1,0:T(8,128)(2,1)} %copy-done.6, ...), custom_call_target="tpu_custom_call" | custom-call | flops 11000000512 | bytes 10000000 | tf_op jit(solution)/shard_map/back_norm/pallas_call | solution.py:462
  540.6 10.3 %collective-permute-done.27 = bf16[512,768]{1,0:T(8,128)(2,1)S(1)} collective-permute-done((bf16[512,768]{1,0:T(8,128)(2,1)S(1)}, bf16[512,768]{1,0:T(8,128)(2,1)S(1)}, u32[]{:S(2)}, u32[]{:S(2)}) %collective-permute-start.27) | collective-permute-done | bytes 786464 | tf_op jit(solution)/shard_map/ppermute | solution.py:595
  552.7 10.1 %back_norm.5 = (bf16[640,1024]{1,0:T(8,128)(2,1)S(1)}, f32[4,8,1024]{2,1,0:T(8,128)S(1)}) custom-call(s32[1]{0:T(128)S(6)} %mul.202.at_ref, bf16[1024,768]{1,0:T(8,128)(2,1)} %collective-permute-done.7.w_ref.refs_0_, bf16[1024,768]{1,0:T(8,128)(2,1)} %bitcast.208, bf16[1024,768]{1,0:T(8,128)(2,1)} %copy-done.5, bf16[1024,768]{1,0:T(8,128)(2,1)} %copy-done.6, ...), custom_call_target="tpu_custom_call" | custom-call | flops 11000000512 | bytes 10000000 | tf_op jit(solution)/shard_map/back_norm/pallas_call | solution.py:462
  563.9 17.1 %collective-permute-done.28 = bf16[256,768]{1,0:T(8,128)(2,1)S(1)} collective-permute-done((bf16[256,768]{1,0:T(8,128)(2,1)S(1)}, bf16[256,768]{1,0:T(8,128)(2,1)S(1)}, u32[]{:S(2)}, u32[]{:S(2)}) %collective-permute-start.28) | collective-permute-done | bytes 393248 | tf_op jit(solution)/shard_map/ppermute | solution.py:595
  581.2 11.1 %collective-permute-done.29 = bf16[128,768]{1,0:T(8,128)(2,1)S(1)} collective-permute-done((bf16[128,768]{1,0:T(8,128)(2,1)S(1)}, bf16[128,768]{1,0:T(8,128)(2,1)S(1)}, u32[]{:S(2)}, u32[]{:S(2)}) %collective-permute-start.29) | collective-permute-done | bytes 196640 | tf_op jit(solution)/shard_map/ppermute | solution.py:595
  592.6 11.0 %collective-permute-done.37 = bf16[128,768]{1,0:T(8,128)(2,1)S(1)} collective-permute-done((bf16[128,768]{1,0:T(8,128)(2,1)S(1)}, bf16[128,768]{1,0:T(8,128)(2,1)S(1)}, u32[]{:S(2)}, u32[]{:S(2)}) %collective-permute-start.37) | collective-permute-done | bytes 196640 | tf_op jit(solution)/shard_map/ppermute | solution.py:595
  605.8 8.9 %collective-permute-done.38 = bf16[256,768]{1,0:T(8,128)(2,1)S(1)} collective-permute-done((bf16[256,768]{1,0:T(8,128)(2,1)S(1)}, bf16[256,768]{1,0:T(8,128)(2,1)S(1)}, u32[]{:S(2)}, u32[]{:S(2)}) %collective-permute-start.38) | collective-permute-done | bytes 393248 | tf_op jit(solution)/shard_map/ppermute | solution.py:595
  616.6 19.2 %collective-permute-done.33 = f32[7936]{0:T(1024)S(1)} collective-permute-done((f32[7936]{0:T(1024)S(1)}, f32[7936]{0:T(1024)S(1)}, u32[]{:S(2)}, u32[]{:S(2)}) %collective-permute-start.33) | collective-permute-done | bytes 31776 | tf_op jit(solution)/shard_map/ppermute | solution.py:598
  656.7 13.3 %collective-permute-done.30.theirs_ref = bf16[640,1024]{1,0:T(8,128)(2,1)} collective-permute-done((bf16[640,1024]{1,0:T(8,128)(2,1)}, bf16[640,1024]{1,0:T(8,128)(2,1)}, u32[]{:S(2)}, u32[]{:S(2)}) %collective-permute-start.30) | collective-permute-done | bytes 1310752 | tf_op jit(solution)/shard_map/ppermute | solution.py:598
  (473 shorter events, 311.6 us)
Async XLA Ops:
  7.2 187.9 %all-gather.7.cloned.1.call-start = ((), (), s32[]{:S(2)}) async-start(), calls=%async_computation.1 | async-start | bytes 5570560 | tf_op jit(solution)/shard_map/all_gather | solution.py:671
  9.7 32.0 %collective-permute-start = (bf16[640,1024]{1,0:T(8,128)(2,1)}, bf16[640,1024]{1,0:T(8,128)(2,1)S(1)}, u32[]{:S(2)}, u32[]{:S(2)}) collective-permute-start(bf16[640,1024]{1,0:T(8,128)(2,1)} %dynamic-slice_bitcast_fusion.1), channel_id=1, source_target_pairs={{0,1},{1,0},{2,3},{3,2},{4,5},{5,4},{6,7},{7,6},{8,9},{9,8},{10,11... | collective-permute-start | bytes 3932168 | tf_op jit(solution)/shard_map/ppermute | solution.py:598
  66.1 199.5 %all-gather.5.cloned.1.call-start = ((), (), s32[]{:S(2)}) async-start(), calls=%async_computation | async-start | bytes 4456448 | tf_op jit(solution)/shard_map/all_gather | solution.py:671
  79.7 57.9 %collective-permute-start.2 = (bf16[128,1024]{1,0:T(8,128)(2,1)}, bf16[128,1024]{1,0:T(8,128)(2,1)}, u32[]{:S(2)}, u32[]{:S(2)}) collective-permute-start(bf16[128,1024]{1,0:T(8,128)(2,1)} %constant_dynamic-slice_fusion.36), channel_id=1, source_target_pairs={{0,1},{1,0},{2,3},{3,2},{4,5},{5,4},{6,7},{7,6},{8,9},{9,8},{10,11... | collective-permute-start | bytes 786440 | tf_op jit(solution)/shard_map/ppermute | solution.py:598
  95.8 40.5 %collective-permute-start.4 = (bf16[512,768]{1,0:T(8,128)(2,1)S(1)}, bf16[512,768]{1,0:T(8,128)(2,1)S(1)}, u32[]{:S(2)}, u32[]{:S(2)}) collective-permute-start(bf16[512,768]{1,0:T(8,128)(2,1)S(1)} %bitcast.257), channel_id=1, source_target_pairs={{0,4},{2,6},{4,0},{6,2},{8,12},{10,14},{12,8},{14,10},{16,20},{18,... | collective-permute-start | bytes 2359304 | tf_op jit(solution)/shard_map/ppermute | solution.py:595
  137.6 29.4 %collective-permute-start.7 = (bf16[1024,768]{1,0:T(8,128)(2,1)S(1)}, bf16[1024,768]{1,0:T(8,128)(2,1)}, u32[]{:S(2)}, u32[]{:S(2)}) collective-permute-start(bf16[1024,768]{1,0:T(8,128)(2,1)S(1)} %bitcast.205), channel_id=1, source_target_pairs={{0,2},{2,0},{4,6},{6,4},{8,10},{10,8},{12,14},{14,12},{16,18},{18,... | collective-permute-start | bytes 4718600 | tf_op jit(solution)/shard_map/ppermute | solution.py:595
  137.6 80.6 %collective-permute-start.8 = (bf16[640,1024]{1,0:T(8,128)(2,1)}, bf16[640,1024]{1,0:T(8,128)(2,1)}, u32[]{:S(2)}, u32[]{:S(2)}) collective-permute-start(bf16[640,1024]{1,0:T(8,128)(2,1)} %get-tuple-element.186), channel_id=1, source_target_pairs={{0,1},{1,0},{2,3},{3,2},{4,5},{5,4},{6,7},{7,6},{8,9},{9,8},{10,11... | collective-permute-start | bytes 3932168 | tf_op jit(solution)/shard_map/ppermute | solution.py:598
  166.9 506.0 %all-gather.11.cloned.1.call-start = ((), (), s32[]{:S(2)}) async-start(), calls=%async_computation.3 | async-start | bytes 4456448 | tf_op jit(solution)/shard_map/all_gather | solution.py:811
  285.7 48.2 %collective-permute-start.12 = (bf16[1024,1024]{1,0:T(8,128)(2,1)}, bf16[1024,1024]{1,0:T(8,128)(2,1)S(1)}, u32[]{:S(2)}, u32[]{:S(2)}) collective-permute-start(bf16[1024,1024]{1,0:T(8,128)(2,1)} %add_convert_fusion.5), channel_id=1, source_target_pairs={{0,1},{1,0},{2,3},{3,2},{4,5},{5,4},{6,7},{7,6},{8,9},{9,8},{10,11... | collective-permute-start | bytes 6291464 | tf_op jit(solution)/shard_map/ppermute | solution.py:598
  313.2 42.2 %collective-permute-start.13 = (bf16[1024,1024]{1,0:T(8,128)(2,1)}, bf16[1024,1024]{1,0:T(8,128)(2,1)S(1)}, u32[]{:S(2)}, u32[]{:S(2)}) collective-permute-start(bf16[1024,1024]{1,0:T(8,128)(2,1)} %convolution_convert_fusion.4), channel_id=1, source_target_pairs={{0,2},{2,0},{4,6},{6,4},{8,10},{10,8},{12,14},{14,12},{16,18},{18,... | collective-permute-start | bytes 6291464 | tf_op jit(solution)/shard_map/ppermute | solution.py:595
  354.3 48.1 %collective-permute-start.18 = (bf16[1024,1024]{1,0:T(8,128)(2,1)}, bf16[1024,1024]{1,0:T(8,128)(2,1)}, u32[]{:S(2)}, u32[]{:S(2)}) collective-permute-start(bf16[1024,1024]{1,0:T(8,128)(2,1)} %add_convert_fusion.3), channel_id=1, source_target_pairs={{0,1},{1,0},{2,3},{3,2},{4,5},{5,4},{6,7},{7,6},{8,9},{9,8},{10,11... | collective-permute-start | bytes 6291464 | tf_op jit(solution)/shard_map/ppermute | solution.py:598
  405.2 25.2 %collective-permute-start.19 = (bf16[512,1024]{1,0:T(8,128)(2,1)S(1)}, bf16[512,1024]{1,0:T(8,128)(2,1)S(1)}, u32[]{:S(2)}, u32[]{:S(2)}) collective-permute-start(bf16[512,1024]{1,0:T(8,128)(2,1)S(1)} %bitcast.277), channel_id=1, source_target_pairs={{0,4},{2,6},{4,0},{6,2},{8,12},{10,14},{12,8},{14,10},{16,20},{18,... | collective-permute-start | bytes 3145736 | tf_op jit(solution)/shard_map/ppermute | solution.py:595
  427.0 257.0 %all-gather.9.cloned.1.call-start = ((), (), s32[]{:S(2)}) async-start(), calls=%async_computation.2 | async-start | bytes 5570560 | tf_op jit(solution)/shard_map/all_gather | solution.py:833
  430.9 37.5 %collective-permute-start.22 = (bf16[256,1024]{1,0:T(8,128)(2,1)S(1)}, bf16[256,1024]{1,0:T(8,128)(2,1)S(1)}, u32[]{:S(2)}, u32[]{:S(2)}) collective-permute-start(bf16[256,1024]{1,0:T(8,128)(2,1)S(1)} %bitcast.289), channel_id=1, source_target_pairs={{0,8},{2,10},{4,12},{6,14},{8,0},{10,2},{12,4},{14,6},{16,24},{18,... | collective-permute-start | bytes 1572872 | tf_op jit(solution)/shard_map/ppermute | solution.py:595
  441.3 27.3 %collective-permute-start.23 = (bf16[128,1024]{1,0:T(8,128)(2,1)S(1)}, bf16[128,1024]{1,0:T(8,128)(2,1)S(1)}, u32[]{:S(2)}, u32[]{:S(2)}) collective-permute-start(bf16[128,1024]{1,0:T(8,128)(2,1)S(1)} %bitcast.297), channel_id=1, source_target_pairs={{0,4},{2,6},{4,0},{6,2},{8,12},{10,14},{12,8},{14,10},{16,20},{18,... | collective-permute-start | bytes 786440 | tf_op jit(solution)/shard_map/ppermute | solution.py:595
  469.8 49.4 %collective-permute-start.42 = (bf16[128,1024]{1,0:T(8,128)(2,1)S(1)}, bf16[128,1024]{1,0:T(8,128)(2,1)S(1)}, u32[]{:S(2)}, u32[]{:S(2)}) collective-permute-start(bf16[128,1024]{1,0:T(8,128)(2,1)S(1)} %dynamic-slice_bitcast_fusion.5), channel_id=1, source_target_pairs={{0,16},{2,18},{4,20},{6,22},{8,24},{10,26},{12,28},{14,30},{16,0},... | collective-permute-start | bytes 786440 | tf_op jit(solution)/shard_map/ppermute | solution.py:595
  472.0 53.4 %collective-permute-start.26 = (bf16[1024,768]{1,0:T(8,128)(2,1)}, bf16[1024,768]{1,0:T(8,128)(2,1)}, u32[]{:S(2)}, u32[]{:S(2)}) collective-permute-start(bf16[1024,768]{1,0:T(8,128)(2,1)} %add_convert_fusion.7), channel_id=1, source_target_pairs={{0,1},{1,0},{2,3},{3,2},{4,5},{5,4},{6,7},{7,6},{8,9},{9,8},{10,11... | collective-permute-start | bytes 4718600 | tf_op jit(solution)/shard_map/ppermute | solution.py:598
  492.5 26.7 %collective-permute-start.43 = (bf16[32,1024]{1,0:T(8,128)(2,1)S(1)}, bf16[32,1024]{1,0:T(8,128)(2,1)S(1)}, u32[]{:S(2)}, u32[]{:S(2)}) collective-permute-start(bf16[32,1024]{1,0:T(8,128)(2,1)S(1)} %dynamic-slice_bitcast_fusion.9), channel_id=1, source_target_pairs={{0,16},{2,18},{4,20},{6,22},{8,24},{10,26},{12,28},{14,30},{16,0},... | collective-permute-start | bytes 196616 | tf_op jit(solution)/shard_map/ppermute | solution.py:595
  498.6 26.9 %collective-permute-start.25 = (bf16[1024,768]{1,0:T(8,128)(2,1)}, bf16[1024,768]{1,0:T(8,128)(2,1)}, u32[]{:S(2)}, u32[]{:S(2)}) collective-permute-start(bf16[1024,768]{1,0:T(8,128)(2,1)} %convolution_convert_fusion.8), channel_id=1, source_target_pairs={{0,2},{2,0},{4,6},{6,4},{8,10},{10,8},{12,14},{14,12},{16,18},{18,... | collective-permute-start | bytes 4718600 | tf_op jit(solution)/shard_map/ppermute | solution.py:595
  551.1 29.8 %collective-permute-start.28 = (bf16[256,768]{1,0:T(8,128)(2,1)S(1)}, bf16[256,768]{1,0:T(8,128)(2,1)S(1)}, u32[]{:S(2)}, u32[]{:S(2)}) collective-permute-start(bf16[256,768]{1,0:T(8,128)(2,1)S(1)} %bitcast.293), channel_id=1, source_target_pairs={{0,8},{2,10},{4,12},{6,14},{8,0},{10,2},{12,4},{14,6},{16,24},{18,... | collective-permute-start | bytes 1179656 | tf_op jit(solution)/shard_map/ppermute | solution.py:595
  604.2 47.3 %collective-permute-start.31 = (bf16[640,1024]{1,0:T(8,128)(2,1)}, bf16[640,1024]{1,0:T(8,128)(2,1)}, u32[]{:S(2)}, u32[]{:S(2)}) collective-permute-start(bf16[640,1024]{1,0:T(8,128)(2,1)} %get-tuple-element.248), channel_id=1, source_target_pairs={{0,1},{1,0},{2,3},{3,2},{4,5},{5,4},{6,7},{7,6},{8,9},{9,8},{10,11... | collective-permute-start | bytes 3932168 | tf_op jit(solution)/shard_map/ppermute | solution.py:598
  614.8 35.0 %collective-permute-start.39 = (bf16[512,768]{1,0:T(8,128)(2,1)S(1)}, bf16[512,768]{1,0:T(8,128)(2,1)S(1)}, u32[]{:S(2)}, u32[]{:S(2)}) collective-permute-start(bf16[512,768]{1,0:T(8,128)(2,1)S(1)} %bitcast.255), channel_id=1, source_target_pairs={{0,4},{2,6},{4,0},{6,2},{8,12},{10,14},{12,8},{14,10},{16,20},{18,... | collective-permute-start | bytes 2359304 | tf_op jit(solution)/shard_map/ppermute | solution.py:595
  641.5 28.5 %collective-permute-start.30 = (bf16[640,1024]{1,0:T(8,128)(2,1)}, bf16[640,1024]{1,0:T(8,128)(2,1)}, u32[]{:S(2)}, u32[]{:S(2)}) collective-permute-start(bf16[640,1024]{1,0:T(8,128)(2,1)} %get-tuple-element.257), channel_id=1, source_target_pairs={{0,1},{1,0},{2,3},{3,2},{4,5},{5,4},{6,7},{7,6},{8,9},{9,8},{10,11... | collective-permute-start | bytes 3932168 | tf_op jit(solution)/shard_map/ppermute | solution.py:598
  650.0 30.4 %collective-permute-start.40 = (bf16[1024,768]{1,0:T(8,128)(2,1)S(1)}, bf16[1024,768]{1,0:T(8,128)(2,1)S(1)}, u32[]{:S(2)}, u32[]{:S(2)}) collective-permute-start(bf16[1024,768]{1,0:T(8,128)(2,1)S(1)} %bitcast.209), channel_id=1, source_target_pairs={{0,2},{2,0},{4,6},{6,4},{8,10},{10,8},{12,14},{14,12},{16,18},{18,... | collective-permute-start | bytes 4718600 | tf_op jit(solution)/shard_map/ppermute | solution.py:595
  (135 other events, 1764.6 us)
Sparse Core Ops, SparseCore 0:
  66.2 74.9 all-gather.6
  167.0 51.3 all-gather.4
  427.1 62.0 all-gather.10
  520.2 63.6 all-gather.8

commit v3 on v2

--- a/solution.py
+++ b/solution.py
@@ -28,7 +28,7 @@
 
 def takes(microseconds):
     return pl.CostEstimate(
-        flops=int(microseconds * 1.1e9), bytes_accessed=int(microseconds * 1e6), transcendentals=0
+        flops=int(microseconds * 4e9), bytes_accessed=int(microseconds * 4e6), transcendentals=0
     )
 
 
@@ -428,7 +428,7 @@
         ),
         out_shape=[jax.ShapeDtypeStruct((rows // 2, depth), jnp.bfloat16)] * 2,
         compiler_params=params(),
-        cost_estimate=takes(18),
+        cost_estimate=takes(0.1),
         name="reduce_rows",
     )(side, *rights, *lefts, x, bias[None])
 
@@ -477,7 +477,7 @@
             jax.ShapeDtypeStruct((4, 8, depth), jnp.float32),
         ],
         compiler_params=params(),
-        cost_estimate=takes(20 * rows / 1280),
+        cost_estimate=takes(0.1 if rows == base.shape[0] else 10),
         name="back_norm",
     )(at, *rights, *lefts, base, above, gain[None])
 
@@ -605,14 +605,14 @@
         size = array.shape[0] // chunks
         return lax.dynamic_slice_in_dim(array, (location >> 1) * size, size, 0)
 
-    def split(array, level):
-        left = spread >> (level + 1)
+    def split(array, level, open_levels=None):
+        left = 1 << sum(other > level for other in (open_levels or rest))
         four = array.reshape(left, 2, -1, array.shape[1])
         part = lambda flag: lax.dynamic_index_in_dim(four, flag, 1, False).reshape(-1, array.shape[1])
         return part(bit(level)), part(1 - bit(level))
 
-    def join(mine, theirs, level):
-        left = spread >> (level + 1)
+    def join(mine, theirs, level, open_levels=None):
+        left = 1 << sum(other > level for other in (open_levels or rest))
         four = lambda array: array.reshape(left, 1, -1, array.shape[1])
         pair = jnp.where(
             bit(level) == 0,
@@ -641,8 +641,8 @@
     three = heads_bias.size // 2
     near = rest[:2]
     heads_piece = heads_own[KEEP]
-    for level in near:
-        heads_piece = split(heads_piece, level)[0]
+    for n, level in enumerate(near):
+        heads_piece = split(heads_piece, level, near[n:])[0]
     up_piece = jnp.concatenate([chunk_of(expand_own[KEEP]), chunk_of(merge_own[KEEP])])
     down_piece = chunk_of(reduce_own[KEEP])
 
@@ -652,11 +652,12 @@
     tables = rotary_tables(frame_id, patch_row, column)
     first_key, past_key = first_key[None], past_key[None]
 
+    did(heads_piece, up_piece, down_piece, *heads_own, *merge_own, *expand_own, *reduce_own, *tables)
     heads_piece = cross(tie(heads_piece, tokens_far))
     up_piece = cross(tie(up_piece, tokens_far))
     bias_both = cross(tie(jnp.concatenate(bias_own), tokens_far))
     bias_far = [bias_both[: bias_both.size // 2], bias_both[bias_both.size // 2 :]]
-    stream, first_out = did(*enter(sides, tokens, tokens_far, first_gain, first_shift))
+    stream, first_out = did(*enter(sides, after(tokens), tokens_far, first_gain, first_shift))
     heads, seen = {}, {}
     heads_all = [heads_own, None]
     bias_all = (bias_own, bias_far)
@@ -683,19 +684,19 @@
         return quarters
 
     look(OWN, KEEP)
+    look(OWN, SEND)
     heads_piece = did(after(heads_piece))
     if len(near) > 1:
         heads_next = swap(heads_piece, near[1])
-    look(OWN, SEND)
+    attention(OWN, KEEP)
     up_sizes = (expand_own[0].shape[0] // chunks, merge_own[0].shape[0] // chunks)
     up_gathered = gathered(after(up_piece), *up_sizes)
     down_piece = cross(after(down_piece))
     if len(near) > 1:
-        heads_piece = did(join(after(heads_piece), heads_next, near[1]))
+        heads_piece = did(join(after(heads_piece), heads_next, near[1], near[1:]))
     heads_next = swap(heads_piece, near[0])
-    attention(OWN, KEEP)
     attention(OWN, SEND)
-    heads_piece = did(join(after(heads_piece), heads_next, near[0]))
+    heads_piece = did(join(after(heads_piece), heads_next, near[0], near))
     heads_all[FAR] = [heads_piece, swap(heads_piece, 0)]
     cotangent_far = cross(after(lax.dynamic_index_in_dim(cotangent, 1 - side, 0, False)))
     (reduce_far,) = gathered(after(down_piece), down_piece.shape[0])
@@ -737,13 +738,16 @@
             total = total + wide(array)
         return did(low(total))
 
-    def scattered(array, level):
-        keep, send = split(after(array), level)
+    def scattered(array, level, open_levels=None):
+        keep, send = split(after(array), level, open_levels or rest[rest.index(level) :])
         did(send)
         return keep, swap(send, level)
 
     def summed(keep, arrived):
         return did(low(wide(after(keep)) + wide(arrived)))
+
+    def rows_out(keep, arrived, dtype):
+        return place_rows(sides, keep, arrived, 1, dtype).reshape(2, 1, length // 2, -1)
 
     widen(FAR, SEND)
     widen(FAR, KEEP)
@@ -757,6 +761,12 @@
     reduce_sum = product(active[OWN, KEEP], grad_two, sent)
     back_active(FAR, KEEP)
     sent = swap(product(second_out, grad_pre[FAR, SEND]), 0)
+    layer_send, layer_keep = did(
+        *reduce_rows(
+            sides, [active[q] for q in QUARTERS], [reduce_all[p][c] for p, c in QUARTERS],
+            after(residual), reduce_bias,
+        )
+    )
     back_active(OWN, SEND)
     expand_far_sum = product(second_out, grad_pre[FAR, KEEP], sent)
     back_active(OWN, KEEP)
@@ -764,16 +774,8 @@
     reduce_sum = summed(reduce_sum, reduce_cross)
     expand_cross = cross(tie(expand_far_sum, reduce_cross))
     reduce_keep, reduce_next = scattered(reduce_sum, rest[0])
-    layer_send, layer_keep = did(
-        *reduce_rows(
-            sides, [active[q] for q in QUARTERS], [reduce_all[p][c] for p, c in QUARTERS],
-            after(residual), reduce_bias,
-        )
-    )
     expand_sum = product(second_out, grad_pre[OWN, KEEP], sent)
     zero = jnp.zeros((1,), jnp.int32)
-    reduce_sum = summed(reduce_keep, reduce_next)
-    reduce_keep, reduce_next = scattered(reduce_sum, rest[1])
     grad_one, second_sums = did(
         *back_norm(
             zero, length, [grad_pre[q] for q in QUARTERS], [expand_all[p][c] for p, c in QUARTERS],
@@ -781,9 +783,7 @@
         )
     )
     reduce_sum = summed(reduce_keep, reduce_next)
-    for level in rest[2:]:
-        reduce_keep, reduce_next = scattered(reduce_sum, level)
-        reduce_sum = low(wide(reduce_keep) + wide(reduce_next))
+    reduce_keep, reduce_next = scattered(reduce_sum, rest[1])
 
     grad_mixed, grad_heads, head_sums = {}, {}, {}
 
@@ -807,6 +807,10 @@
     merge_cross = cross(tie(merge_far_sum, expand_cross))
     layer_far = cross(tie(layer_send, expand_cross))
     expand_keep, expand_next = scattered(expand_sum, rest[0])
+    reduce_sum = summed(reduce_keep, reduce_next)
+    for level in rest[2:]:
+        reduce_keep, reduce_next = scattered(reduce_sum, level)
+        reduce_sum = low(wide(reduce_keep) + wide(reduce_next))
     back_attention((FAR, SEND))
     reduce_total = lax.all_gather(after(reduce_sum), "dp", axis=0, tiled=True)
     expand_sum = summed(expand_keep, expand_next)
@@ -825,6 +829,8 @@
         expand_sum = low(wide(expand_keep) + wide(expand_next))
     back_attention((OWN, SEND))
     merge_sum = summed(merge_keep, merge_next)
+    layer_out = rows_out(after(layer_keep), layer_far, jnp.bfloat16)
+    merge_sum, layer_out = lax.optimization_barrier((merge_sum, layer_out))
     for level in rest[2:]:
         merge_keep, merge_next = scattered(merge_sum, level)
         merge_sum = low(wide(merge_keep) + wide(merge_next))
@@ -834,8 +840,24 @@
         after(jnp.concatenate([expand_sum, merge_sum])), "dp", axis=0, tiled=True
     )
     heads_sum = product(first_out, grad_heads[OWN, KEEP], sent, heads_cross)
-    heads_keep, heads_next = scattered(heads_sum, rest[0])
-
+    orders = [rest, rest[1:2] + rest[:1] + rest[2:]]
+    middle = heads_sum.shape[1] // 2
+    heads_sums = [heads_sum[:, :middle], heads_sum[:, middle:]]
+
+    def both_scattered(n):
+        return [scattered(total, order[n], order[n:]) for total, order in zip(heads_sums, orders)]
+
+    def both_summed(pairs):
+        return [summed(*pair) for pair in pairs]
+
+    def in_rows(array):
+        return wide(array.transpose(1, 0, 2, 3).reshape(-1, array.shape[3]))
+
+    reduce_total = reduce_total.reshape(chunks, 2, -1, reduce_total.shape[1])
+    expand_total = expand_total.reshape(chunks, 2, -1, expand_total.shape[1])
+    rows = expand_sum.shape[0]
+
+    pairs = both_scattered(0)
     lefts = [grad_heads[q] for q in QUARTERS]
     rights = [heads_all[p][c] for p, c in QUARTERS]
     per_half = length // 2 // 320
@@ -845,16 +867,12 @@
         )
     )
     tokens_cross = cross(tokens_send)
-    heads_sum = summed(heads_keep, heads_next)
-    heads_keep, heads_next = scattered(heads_sum, rest[1])
+    heads_sums = both_summed(pairs)
+    pairs = both_scattered(1)
     tokens_keep, sums_b = did(
         *back_norm(sides * per_half, length // 2, lefts, rights, stream, grad_one, after(first_gain))
     )
     first_sums = sums_a + sums_b
-    heads_sum = summed(heads_keep, heads_next)
-    for level in rest[2:]:
-        heads_keep, heads_next = scattered(heads_sum, level)
-        heads_sum = summed(heads_keep, heads_next)
 
     small = {q: jnp.concatenate([head_sums[q], column_sums(grad_pre[q])]) for q in QUARTERS}
     both = jnp.concatenate(
@@ -865,15 +883,53 @@
             )
         ]
     )
-    arrived = swap(jnp.concatenate([small[FAR, SEND], small[OWN, SEND], both]), 0)
-    size = small[OWN, KEEP].size
-    far = small[FAR, KEEP] + arrived[:size]
-    mine = jnp.concatenate([small[OWN, KEEP], both]) + arrived[size:]
-    mine = mine + cross(jnp.concatenate([far, mine[size:]]))
-    for level in rest:
-        mine = mine + swap(mine, level)
-    both = mine[size:]
-    mine = mine[:size]
+    far_send, own_send, both = did(*(after(v) for v in (small[FAR, SEND], small[OWN, SEND], both)))
+    arrived = swap(jnp.concatenate([far_send, own_send, both]), 0)
+    size = own_send.size
+    heads_sums = both_summed(pairs)
+    mine = jnp.concatenate([small[FAR, KEEP] + arrived[:size], small[OWN, KEEP], both])
+    mine = did(
+        jnp.concatenate([mine[:size], mine[size:] + after(arrived)[size:]])
+    )
+    for n in range(2, len(rest)):
+        pairs = both_scattered(n)
+        small_next = swap(mine, rest[n])
+        if n == 2:
+            reduce_out = in_rows(after(reduce_total))
+            mine, reduce_out = lax.optimization_barrier((mine, reduce_out))
+            did(mine)
+        heads_sums = both_summed(pairs)
+        mine = did(mine + after(small_next))
+    for n in range(len(rest))[::-1]:
+        arrived = [swap(total, order[n]) for total, order in zip(heads_sums, orders)]
+        small_next = swap(mine, rest[n]) if n < 2 else None
+        if n == len(rest) - 1:
+            expand_out = wide(
+                jnp.concatenate(
+                    [
+                        after(expand_total)[:, n, :rows].reshape(-1, expand_total.shape[3])
+                        for n in range(2)
+                    ],
+                    1,
+                )
+            )
+            mine, expand_out = lax.optimization_barrier((mine, expand_out))
+            did(mine)
+        if n == 0:
+            tokens_out = rows_out(after(tokens_keep), tokens_cross, jnp.float32)
+            mine, tokens_out = lax.optimization_barrier((mine, tokens_out))
+            did(mine)
+        heads_sums = [
+            did(join(after(total), other, order[n], order[n:]))
+            for total, other, order in zip(heads_sums, arrived, orders)
+        ]
+        if n < 2:
+            mine = did(mine + after(small_next))
+    heads_sum = jnp.concatenate(heads_sums, 1)
+    heads_next = swap(heads_sum, 0)
+    arrived = cross(jnp.concatenate([mine[:size], mine[2 * size :]]))
+    both = mine[2 * size :] + arrived[size:]
+    mine = mine[size : 2 * size] + arrived[:size]
     theirs = swap(mine, 0)
     first = jnp.where(bit(0) == 0, mine, theirs)
     second = jnp.where(bit(0) == 0, theirs, mine)
@@ -881,38 +937,19 @@
     expand_bias_total = jnp.concatenate([first[three:], second[three:]])
     (first_gain_total, first_shift_total, second_gain_total, second_shift_total, merge_bias_total,
      reduce_bias_total) = both.reshape(6, -1)
-
-    def rows_out(keep, arrived, dtype):
-        return place_rows(sides, keep, arrived, 1, dtype).reshape(2, 1, length // 2, -1)
-
-    def in_rows(array):
-        return wide(array.transpose(1, 0, 2, 3).reshape(-1, array.shape[3]))
-
-    reduce_total = reduce_total.reshape(chunks, 2, -1, reduce_total.shape[1])
-    expand_total = expand_total.reshape(chunks, 2, -1, expand_total.shape[1])
-    rows = expand_sum.shape[0]
-    merge_total = expand_total[:, :, rows:]
-    expand_total = expand_total[:, :, :rows]
-    expand_total = jnp.concatenate(
-        [expand_total[:, n].reshape(-1, expand_total.shape[3]) for n in range(2)], 1
-    )
-    layer_out = rows_out(after(layer_keep), layer_far, jnp.bfloat16)
-    reduce_out = in_rows(reduce_total)
-    for level in rest[::-1]:
-        heads_sum = join(heads_sum, swap(heads_sum, level), level)
-    heads_out = place_heads(core, heads_sum, swap(heads_sum, 0), jnp.float32)
+    heads_out = place_heads(core, heads_sum, heads_next, jnp.float32)
     return (
         layer_out,
-        rows_out(tokens_keep, tokens_cross, jnp.float32),
+        tokens_out,
         first_gain_total,
         first_shift_total,
         heads_out.transpose(1, 0, 2),
         heads_bias_total,
-        in_rows(merge_total),
+        in_rows(expand_total[:, :, rows:]),
         merge_bias_total,
         second_gain_total,
         second_shift_total,
-        wide(expand_total),
+        expand_out,
         expand_bias_total,
         reduce_out,
         reduce_bias_total,

time: 710 us -> 623 us (0.88)
  waiting for transfers between devices: 162 us -> 63.8 us
  other arithmetic: 31.4 us -> 45 us
    ppermute x13, waiting for transfers between devices: 77.7 us -> 22 us  [cross(): return lax.ppermute(array, 'mp', [(0, 1), (1, 0)])]
    ppermute x32 -> x38, waiting for transfers between devices: 83.9 us -> 41.5 us  [swap(): lax.ppermute(array, 'dp', [(i, i ^ 1 << level) for i in range(spread)])]
    convert_element_type x17 -> x20, other arithmetic: 10.3 us -> 14.6 us  [low(): return array.astype(jnp.bfloat16)]
    ppermute x32 -> x38, starting transfers between devices: 25.8 us -> 29.1 us  [swap(): lax.ppermute(array, 'dp', [(i, i ^ 1 << level) for i in range(spread)])]
    unnamed x233 -> x213, local copies, waits for them, and re-layouts: 20.5 us -> 23.6 us
  transfers between devices with their start and end apart: 49 -> 55, of which waited for: 17 -> 14; matrix products, arithmetic and copies ran while one was open for 19% -> 25% of each run, Pallas kernels for 43% -> 46%
where the time goes in v3:
time: 623 us; the launch traced here: 614 us
  Pallas kernels  297 us (48%)
  matrix products  84.8 us (14%)
  local copies, waits for them, and re-layouts  65.5 us (11%)
  waiting for transfers between devices  63.8 us (10%)
  other arithmetic  45 us (7%)
  starting transfers between devices  41.4 us (7%)
  between operations  16.9 us (3%)
    pallas_call x4, Pallas kernels, attend_back(): pl.pallas_call(attend_back_kernel, grid=(pairs,), in_specs=[part(0), part...  81 us
    pallas_call x4, Pallas kernels, attend(): pl.pallas_call(attend_kernel, grid=(pairs,), in_specs=[part(0), part(1),...  71.2 us
    dot_general x16, matrix products, dot_tn(): lax.dot_general(left, right, (((0,), (0,)), ((), ())), preferred_element_...  57.3 us
    ppermute x38, waiting for transfers between devices, swap(): lax.ppermute(array, 'dp', [(i, i ^ 1 << level) for i in range(spread)])  41.5 us
    pallas_call x3, Pallas kernels, back_norm(): pl.pallas_call(functools.partial(back_kernel, len(lefts)), grid_spec=pltp...  41.3 us
    pallas_call x4, Pallas kernels, expand(): pl.pallas_call(functools.partial(expand_kernel, chunk), grid=(width // bl...  35.4 us
    ppermute x38, starting transfers between devices, swap(): lax.ppermute(array, 'dp', [(i, i ^ 1 << level) for i in range(spread)])  29.1 us
    pallas_call x4, Pallas kernels, project(): pl.pallas_call(functools.partial(project_kernel, rows), grid=(3,), in_spe...  28.1 us
  transfers between devices with their start and end apart: 55, of which 14 were waited for; matrix products, arithmetic and copies ran while one was open for 25% of the time, Pallas kernels for 46%

profile of v3, /device:TPU:0, one launch (start us, length us, event | category | flops | bytes accessed | tf_op | source)
XLA Modules:
  0.0 614.2 jit_solution(117193649697734853)
XLA Ops:
  50.2 7.0 %project.4.q_ref.k_ref.v_ref = bf16[1280,768]{1,0:T(8,128)(2,1)} custom-call(bf16[1280,1024]{1,0:T(8,128)(2,1)} %get-tuple-element.287.x_ref, bf16[1024,768]{1,0:T(8,128)(2,1)S(1)} %copy-done.5, f32[1,768]{1,0:T(1,128)S(1)} %bitcast.235, f32[1280,128]{1,0:T(8,128)S(1)} %copy-done.9, f32[1280,128]{1,0:T(8,128)S(1)} %get-tuple-element.431.up_ref, ...), custom_call_target="tpu_custom_call" | custom-call | flops 28000000000 | bytes 28000000 | tf_op jit(solution)/shard_map/project/pallas_call | solution.py:180
  59.3 7.0 %project.5.q_ref.k_ref.v_ref = bf16[1280,768]{1,0:T(8,128)(2,1)} custom-call(bf16[1280,1024]{1,0:T(8,128)(2,1)} %get-tuple-element.287.x_ref, bf16[1024,768]{1,0:T(8,128)(2,1)S(1)} %copy-done.6, f32[1,768]{1,0:T(1,128)S(1)} %bitcast.234, f32[1280,128]{1,0:T(8,128)S(1)} %copy-done.9, f32[1280,128]{1,0:T(8,128)S(1)} %get-tuple-element.431.up_ref, ...), custom_call_target="tpu_custom_call" | custom-call | flops 28000000000 | bytes 28000000 | tf_op jit(solution)/shard_map/project/pallas_call | solution.py:180
  71.3 17.8 %attend.4 = (bf16[1280,256]{1,0:T(8,128)(2,1)S(1)}, f32[1280,256]{1,0:T(8,128)S(1)}, bf16[4,592,512]{2,1,0:T(8,128)(2,1)}, bf16[4,1280,768]{2,1,0:T(8,128)(2,1)}) custom-call(bf16[1280,768]{1,0:T(8,128)(2,1)S(1)} %copy-done.43, bf16[1280,768]{1,0:T(8,128)(2,1)S(1)} %copy-done.43, bf16[1280,768]{1,0:T(8,128)(2,1)S(1)} %copy-done.43, ...), custom_call_target="tpu_custom_call" | custom-call | flops 67999997952 | bytes 68000000 | tf_op jit(solution)/shard_map/attend/pallas_call | solution.py:237
  96.3 17.8 %attend.5 = (bf16[1280,256]{1,0:T(8,128)(2,1)S(1)}, f32[1280,256]{1,0:T(8,128)S(1)}, bf16[4,592,512]{2,1,0:T(8,128)(2,1)}, bf16[4,1280,768]{2,1,0:T(8,128)(2,1)}) custom-call(bf16[1280,768]{1,0:T(8,128)(2,1)S(1)} %copy-done.44, bf16[1280,768]{1,0:T(8,128)(2,1)S(1)} %copy-done.44, bf16[1280,768]{1,0:T(8,128)(2,1)S(1)} %copy-done.44, ...), custom_call_target="tpu_custom_call" | custom-call | flops 67999997952 | bytes 68000000 | tf_op jit(solution)/shard_map/attend/pallas_call | solution.py:237
  117.4 6.9 %project.6.q_ref.k_ref.v_ref = bf16[1280,768]{1,0:T(8,128)(2,1)} custom-call(bf16[1280,1024]{1,0:T(8,128)(2,1)} %get-tuple-element.287.x_ref, bf16[1024,768]{1,0:T(8,128)(2,1)} %bitcast.23.w_ref.refs_1_, f32[1,768]{1,0:T(1,128)S(1)} %broadcast_in_dim.116.b_ref, f32[1280,128]{1,0:T(8,128)S(1)} %copy-done.10, f32[1280,128]{1,0:T(8,128)S(1)} %get-tuple-element.431.up_ref, ...), custom_call_target="tpu_custom_call" | custom-call | flops 28000000000 | bytes 28000000 | tf_op jit(solution)/shard_map/project/pallas_call | solution.py:180
  125.9 18.0 %attend.6 = (bf16[1280,256]{1,0:T(8,128)(2,1)S(1)}, f32[1280,256]{1,0:T(8,128)S(1)}, bf16[4,592,512]{2,1,0:T(8,128)(2,1)}, bf16[4,1280,768]{2,1,0:T(8,128)(2,1)}) custom-call(bf16[1280,768]{1,0:T(8,128)(2,1)S(1)} %copy-done.45, bf16[1280,768]{1,0:T(8,128)(2,1)S(1)} %copy-done.45, bf16[1280,768]{1,0:T(8,128)(2,1)S(1)} %copy-done.45, ...), custom_call_target="tpu_custom_call" | custom-call | flops 67999997952 | bytes 68000000 | tf_op jit(solution)/shard_map/attend/pallas_call | solution.py:237
  148.6 7.2 %project.7.q_ref.k_ref.v_ref = bf16[1280,768]{1,0:T(8,128)(2,1)} custom-call(bf16[1280,1024]{1,0:T(8,128)(2,1)} %get-tuple-element.287.x_ref, bf16[1024,768]{1,0:T(8,128)(2,1)} %collective-permute-done.6.w_ref.refs_0_, f32[1,768]{1,0:T(1,128)S(1)} %broadcast_in_dim.117.b_ref, f32[1280,128]{1,0:T(8,128)S(1)} %copy-done.11, ...), custom_call_target="tpu_custom_call" | custom-call | flops 28000000000 | bytes 28000000 | tf_op jit(solution)/shard_map/project/pallas_call | solution.py:180
  157.4 17.6 %attend.7 = (bf16[1280,256]{1,0:T(8,128)(2,1)S(1)}, f32[1280,256]{1,0:T(8,128)S(1)}, bf16[4,592,512]{2,1,0:T(8,128)(2,1)}, bf16[4,1280,768]{2,1,0:T(8,128)(2,1)}) custom-call(bf16[1280,768]{1,0:T(8,128)(2,1)S(1)} %copy-done.46, bf16[1280,768]{1,0:T(8,128)(2,1)S(1)} %copy-done.46, bf16[1280,768]{1,0:T(8,128)(2,1)S(1)} %copy-done.46, ...), custom_call_target="tpu_custom_call" | custom-call | flops 67999997952 | bytes 68000000 | tf_op jit(solution)/shard_map/attend/pallas_call | solution.py:237
  179.6 7.7 %merge.1 = (f32[1280,1024]{1,0:T(8,128)}, bf16[1280,1024]{1,0:T(8,128)(2,1)}) custom-call(bf16[256,1024]{1,0:T(8,128)(2,1)S(1)} %bitcast.225, bf16[256,1024]{1,0:T(8,128)(2,1)S(1)} %bitcast.223, bf16[256,1024]{1,0:T(8,128)(2,1)S(1)} %copy-done.13, bf16[256,1024]{1,0:T(8,128)(2,1)S(1)} %copy-done.12, bf16[1280,256]{1,0:T(8,128)(2,1)S(1)} %copy-done.38, ...), custom_call_target="tpu_custom_call" | custom-call | flops 32000000000 | bytes 32000000 | tf_op jit(solution)/shard_map/merge/pallas_call | solution.py:348
  190.7 9.8 %expand.4 = (bf16[1280,1024]{1,0:T(8,128)(2,1)}, bf16[1280,1024]{1,0:T(8,128)(2,1)}) custom-call(bf16[1280,1024]{1,0:T(8,128)(2,1)} %get-tuple-element.244.x_ref, bf16[1024,1024]{1,0:T(8,128)(2,1)S(1)} %bitcast.221, f32[1,1024]{1,0:T(1,128)S(1)} %bitcast.233), custom_call_target="tpu_custom_call" | custom-call | flops 33999998976 | bytes 34000000 | tf_op jit(solution)/shard_map/expand/pallas_call | solution.py:379
  200.6 8.5 %expand.5 = (bf16[1280,1024]{1,0:T(8,128)(2,1)}, bf16[1280,1024]{1,0:T(8,128)(2,1)}) custom-call(bf16[1280,1024]{1,0:T(8,128)(2,1)} %get-tuple-element.244.x_ref, bf16[1024,1024]{1,0:T(8,128)(2,1)S(1)} %bitcast.219, f32[1,1024]{1,0:T(1,128)S(1)} %bitcast.232), custom_call_target="tpu_custom_call" | custom-call | flops 33999998976 | bytes 34000000 | tf_op jit(solution)/shard_map/expand/pallas_call | solution.py:379
  216.1 8.5 %expand.6 = (bf16[1280,1024]{1,0:T(8,128)(2,1)}, bf16[1280,1024]{1,0:T(8,128)(2,1)}) custom-call(bf16[1280,1024]{1,0:T(8,128)(2,1)} %get-tuple-element.244.x_ref, bf16[1024,1024]{1,0:T(8,128)(2,1)S(1)} %copy-done.1, f32[1,1024]{1,0:T(1,128)S(1)} %bitcast.228), custom_call_target="tpu_custom_call" | custom-call | flops 33999998976 | bytes 34000000 | tf_op jit(solution)/shard_map/expand/pallas_call | solution.py:379
  228.8 8.6 %expand.7 = (bf16[1280,1024]{1,0:T(8,128)(2,1)}, bf16[1280,1024]{1,0:T(8,128)(2,1)}) custom-call(bf16[1280,1024]{1,0:T(8,128)(2,1)} %get-tuple-element.244.x_ref, bf16[1024,1024]{1,0:T(8,128)(2,1)S(1)} %get-tuple-element.459.w_ref.refs_3_, f32[1,1024]{1,0:T(1,128)S(1)} %bitcast.227), custom_call_target="tpu_custom_call" | custom-call | flops 33999998976 | bytes 34000000 | tf_op jit(solution)/shard_map/expand/pallas_call | solution.py:379
  263.5 17.9 %reduce_rows.1 = (bf16[640,1024]{1,0:T(8,128)(2,1)}, bf16[640,1024]{1,0:T(8,128)(2,1)S(1)}) custom-call(s32[1]{0:T(128)} %bitcast.side_ref.flag_ref, bf16[1024,1024]{1,0:T(8,128)(2,1)} %bitcast.245, bf16[1024,1024]{1,0:T(8,128)(2,1)} %bitcast.243, bf16[1024,1024]{1,0:T(8,128)(2,1)} %get-tuple-element.384.refs_2_, ...), custom_call_target="tpu_custom_call" | custom-call | flops 400000000 | bytes 400000 | tf_op jit(solution)/shard_map/reduce_rows/pallas_call | solution.py:416
  321.9 20.6 %back_norm.3 = (bf16[1280,1024]{1,0:T(8,128)(2,1)}, f32[4,8,1024]{2,1,0:T(8,128)S(1)}) custom-call(s32[1]{0:T(128)} %constant.295.clone.1.at_ref, bf16[1024,1024]{1,0:T(8,128)(2,1)S(1)} %bitcast.222, bf16[1024,1024]{1,0:T(8,128)(2,1)} %bitcast.220, bf16[1024,1024]{1,0:T(8,128)(2,1)} %get-tuple-element.460.w_ref.refs_2_, bf16[1024,1024]{1,0:T(8,128)(2,1)} %copy-done, ...), custom_call_target="tpu_custom_call" | custom-call | flops 400000000 | bytes 400000 | tf_op jit(solution)/shard_map/back_norm/pallas_call | solution.py:462
  354.2 10.1 %collective-permute-done.17 = bf16[1024,1024]{1,0:T(8,128)(2,1)S(1)} collective-permute-done((bf16[1024,1024]{1,0:T(8,128)(2,1)}, bf16[1024,1024]{1,0:T(8,128)(2,1)S(1)}, u32[]{:S(2)}, u32[]{:S(2)}) %collective-permute-start.17) | collective-permute-done | bytes 2097184 | tf_op jit(solution)/shard_map/ppermute | solution.py:598
  374.2 20.4 %attend_back.4 = (bf16[1280,768]{1,0:T(8,128)(2,1)}, f32[8,768]{1,0:T(8,128)}) custom-call(bf16[1280,768]{1,0:T(8,128)(2,1)} %project.7.q_ref.k_ref.v_ref, bf16[1280,768]{1,0:T(8,128)(2,1)} %project.7.q_ref.k_ref.v_ref, bf16[1280,768]{1,0:T(8,128)(2,1)} %project.7.q_ref.k_ref.v_ref, bf16[1280,256]{1,0:T(8,128)(2,1)} %convolution_convert_fusion.3.g_ref, ...), custom_call_target="tpu_custom_call" | custom-call | flops 80000000000 | bytes 80000000 | tf_op jit(solution)/shard_map/attend_back/pallas_call | solution.py:308
  409.6 20.1 %attend_back.5 = (bf16[1280,768]{1,0:T(8,128)(2,1)}, f32[8,768]{1,0:T(8,128)}) custom-call(bf16[1280,768]{1,0:T(8,128)(2,1)} %project.6.q_ref.k_ref.v_ref, bf16[1280,768]{1,0:T(8,128)(2,1)} %project.6.q_ref.k_ref.v_ref, bf16[1280,768]{1,0:T(8,128)(2,1)} %project.6.q_ref.k_ref.v_ref, bf16[1280,256]{1,0:T(8,128)(2,1)} %convolution_convert_fusion.2.g_ref, ...), custom_call_target="tpu_custom_call" | custom-call | flops 80000000000 | bytes 80000000 | tf_op jit(solution)/shard_map/attend_back/pallas_call | solution.py:308
  439.5 20.2 %attend_back.6 = (bf16[1280,768]{1,0:T(8,128)(2,1)}, f32[8,768]{1,0:T(8,128)}) custom-call(bf16[1280,768]{1,0:T(8,128)(2,1)} %project.5.q_ref.k_ref.v_ref, bf16[1280,768]{1,0:T(8,128)(2,1)} %project.5.q_ref.k_ref.v_ref, bf16[1280,768]{1,0:T(8,128)(2,1)} %project.5.q_ref.k_ref.v_ref, bf16[1280,256]{1,0:T(8,128)(2,1)} %convolution_convert_fusion.1.g_ref, ...), custom_call_target="tpu_custom_call" | custom-call | flops 80000000000 | bytes 80000000 | tf_op jit(solution)/shard_map/attend_back/pallas_call | solution.py:308
  470.5 20.3 %attend_back.7 = (bf16[1280,768]{1,0:T(8,128)(2,1)}, f32[8,768]{1,0:T(8,128)}) custom-call(bf16[1280,768]{1,0:T(8,128)(2,1)} %project.4.q_ref.k_ref.v_ref, bf16[1280,768]{1,0:T(8,128)(2,1)} %project.4.q_ref.k_ref.v_ref, bf16[1280,768]{1,0:T(8,128)(2,1)} %project.4.q_ref.k_ref.v_ref, bf16[1280,256]{1,0:T(8,128)(2,1)} %convolution_convert_fusion.g_ref, ...), custom_call_target="tpu_custom_call" | custom-call | flops 80000000000 | bytes 80000000 | tf_op jit(solution)/shard_map/attend_back/pallas_call | solution.py:308
  501.7 10.5 %back_norm.4 = (bf16[640,1024]{1,0:T(8,128)(2,1)S(1)}, f32[4,8,1024]{2,1,0:T(8,128)S(1)}) custom-call(s32[1]{0:T(128)S(6)} %mul.202.at_ref, bf16[1024,768]{1,0:T(8,128)(2,1)} %collective-permute-done.6.w_ref.refs_0_, bf16[1024,768]{1,0:T(8,128)(2,1)} %bitcast.23.w_ref.refs_1_, bf16[1024,768]{1,0:T(8,128)(2,1)} %pad_maximum_fusion.1.w_ref.refs_2_, ...), custom_call_target="tpu_custom_call" | custom-call | flops 40000000000 | bytes 40000000 | tf_op jit(solution)/shard_map/back_norm/pallas_call | solution.py:462
  514.4 6.8 %collective-permute-done.29 = bf16[512,384]{1,0:T(8,128)(2,1)S(1)} collective-permute-done((bf16[512,384]{1,0:T(8,128)(2,1)S(1)}, bf16[512,384]{1,0:T(8,128)(2,1)S(1)}, u32[]{:S(2)}, u32[]{:S(2)}) %collective-permute-start.29) | collective-permute-done | bytes 393248 | tf_op jit(solution)/shard_map/ppermute | solution.py:595
  521.5 10.2 %back_norm.5 = (bf16[640,1024]{1,0:T(8,128)(2,1)S(1)}, f32[4,8,1024]{2,1,0:T(8,128)S(1)}) custom-call(s32[1]{0:T(128)S(6)} %mul.201.at_ref, bf16[1024,768]{1,0:T(8,128)(2,1)} %collective-permute-done.6.w_ref.refs_0_, bf16[1024,768]{1,0:T(8,128)(2,1)} %bitcast.23.w_ref.refs_1_, bf16[1024,768]{1,0:T(8,128)(2,1)} %pad_maximum_fusion.1.w_ref.refs_2_, ...), custom_call_target="tpu_custom_call" | custom-call | flops 40000000000 | bytes 40000000 | tf_op jit(solution)/shard_map/back_norm/pallas_call | solution.py:462
  535.7 10.7 %collective-permute-done.31 = bf16[256,384]{1,0:T(8,128)(2,1)S(1)} collective-permute-done((bf16[256,384]{1,0:T(8,128)(2,1)S(1)}, bf16[256,384]{1,0:T(8,128)(2,1)S(1)}, u32[]{:S(2)}, u32[]{:S(2)}) %collective-permute-start.31) | collective-permute-done | bytes 196640 | tf_op jit(solution)/shard_map/ppermute | solution.py:595
  (477 shorter events, 287.0 us)
Async XLA Ops:
  7.2 169.7 %all-gather.5.cloned.1.call-start = ((), (), s32[]{:S(2)}) async-start(), calls=%async_computation | async-start | bytes 5570560 | tf_op jit(solution)/shard_map/all_gather | solution.py:672
  9.7 33.9 %collective-permute-start = (bf16[640,1024]{1,0:T(8,128)(2,1)}, bf16[640,1024]{1,0:T(8,128)(2,1)}, u32[]{:S(2)}, u32[]{:S(2)}) collective-permute-start(bf16[640,1024]{1,0:T(8,128)(2,1)} %dynamic-slice_bitcast_fusion.1), channel_id=1, source_target_pairs={{0,1},{1,0},{2,3},{3,2},{4,5},{5,4},{6,7},{7,6},{8,9},{9,8},{10,11... | collective-permute-start | bytes 3932168 | tf_op jit(solution)/shard_map/ppermute | solution.py:598
  59.3 32.4 %collective-permute-start.5 = (bf16[160,1024]{1,0:T(8,128)(2,1)S(1)}, bf16[160,1024]{1,0:T(8,128)(2,1)}, u32[]{:S(2)}, u32[]{:S(2)}) collective-permute-start(bf16[160,1024]{1,0:T(8,128)(2,1)S(1)} %copy-done.78), channel_id=1, source_target_pairs={{0,1},{1,0},{2,3},{3,2},{4,5},{5,4},{6,7},{7,6},{8,9},{9,8},{10,11... | collective-permute-start | bytes 983048 | tf_op jit(solution)/shard_map/ppermute | solution.py:598
  91.1 54.8 %collective-permute-start.9 = (bf16[128,1024]{1,0:T(8,128)(2,1)}, bf16[128,1024]{1,0:T(8,128)(2,1)}, u32[]{:S(2)}, u32[]{:S(2)}) collective-permute-start(bf16[128,1024]{1,0:T(8,128)(2,1)} %constant_dynamic-slice_fusion.35), channel_id=1, source_target_pairs={{0,1},{1,0},{2,3},{3,2},{4,5},{5,4},{6,7},{7,6},{8,9},{9,8},{10,11... | collective-permute-start | bytes 786440 | tf_op jit(solution)/shard_map/ppermute | solution.py:598
  91.7 150.6 %all-gather.7.cloned.1.call-start = ((), (), s32[]{:S(2)}) async-start(), calls=%async_computation.1 | async-start | bytes 4456448 | tf_op jit(solution)/shard_map/all_gather | solution.py:672
  117.4 30.1 %collective-permute-start.6 = (bf16[1024,768]{1,0:T(8,128)(2,1)}, bf16[1024,768]{1,0:T(8,128)(2,1)}, u32[]{:S(2)}, u32[]{:S(2)}) collective-permute-start(bf16[1024,768]{1,0:T(8,128)(2,1)} %bitcast.23.w_ref.refs_1_), channel_id=1, source_target_pairs={{0,2},{2,0},{4,6},{6,4},{8,10},{10,8},{12,14},{14,12},{16,18},{18,... | collective-permute-start | bytes 4718600 | tf_op jit(solution)/shard_map/ppermute | solution.py:595
  145.9 44.2 %collective-permute-start.7 = (bf16[640,1024]{1,0:T(8,128)(2,1)}, bf16[640,1024]{1,0:T(8,128)(2,1)}, u32[]{:S(2)}, u32[]{:S(2)}) collective-permute-start(bf16[640,1024]{1,0:T(8,128)(2,1)} %get-tuple-element.208), channel_id=1, source_target_pairs={{0,1},{1,0},{2,3},{3,2},{4,5},{5,4},{6,7},{7,6},{8,9},{9,8},{10,11... | collective-permute-start | bytes 3932168 | tf_op jit(solution)/shard_map/ppermute | solution.py:598
  147.4 402.8 %all-gather.9.cloned.1.call-start = ((), (), s32[]{:S(2)}) async-start(), calls=%async_computation.2 | async-start | bytes 4456448 | tf_op jit(solution)/shard_map/all_gather | solution.py:815
  263.4 48.2 %collective-permute-start.12 = (bf16[1024,1024]{1,0:T(8,128)(2,1)}, bf16[1024,1024]{1,0:T(8,128)(2,1)}, u32[]{:S(2)}, u32[]{:S(2)}) collective-permute-start(bf16[1024,1024]{1,0:T(8,128)(2,1)} %add_convert_fusion.5), channel_id=1, source_target_pairs={{0,1},{1,0},{2,3},{3,2},{4,5},{5,4},{6,7},{7,6},{8,9},{9,8},{10,11... | collective-permute-start | bytes 6291464 | tf_op jit(solution)/shard_map/ppermute | solution.py:598
  314.5 28.0 %collective-permute-start.14 = (bf16[512,1024]{1,0:T(8,128)(2,1)S(1)}, bf16[512,1024]{1,0:T(8,128)(2,1)S(1)}, u32[]{:S(2)}, u32[]{:S(2)}) collective-permute-start(bf16[512,1024]{1,0:T(8,128)(2,1)S(1)} %bitcast.290), channel_id=1, source_target_pairs={{0,4},{2,6},{4,0},{6,2},{8,12},{10,14},{12,8},{14,10},{16,20},{18,... | collective-permute-start | bytes 3145736 | tf_op jit(solution)/shard_map/ppermute | solution.py:595
  317.1 47.3 %collective-permute-start.17 = (bf16[1024,1024]{1,0:T(8,128)(2,1)}, bf16[1024,1024]{1,0:T(8,128)(2,1)S(1)}, u32[]{:S(2)}, u32[]{:S(2)}) collective-permute-start(bf16[1024,1024]{1,0:T(8,128)(2,1)} %add_convert_fusion.3), channel_id=1, source_target_pairs={{0,1},{1,0},{2,3},{3,2},{4,5},{5,4},{6,7},{7,6},{8,9},{9,8},{10,11... | collective-permute-start | bytes 6291464 | tf_op jit(solution)/shard_map/ppermute | solution.py:598
  346.9 23.7 %collective-permute-start.18 = (bf16[256,1024]{1,0:T(8,128)(2,1)S(1)}, bf16[256,1024]{1,0:T(8,128)(2,1)S(1)}, u32[]{:S(2)}, u32[]{:S(2)}) collective-permute-start(bf16[256,1024]{1,0:T(8,128)(2,1)S(1)} %bitcast.306), channel_id=1, source_target_pairs={{0,8},{2,10},{4,12},{6,14},{8,0},{10,2},{12,4},{14,6},{16,24},{18,... | collective-permute-start | bytes 1572872 | tf_op jit(solution)/shard_map/ppermute | solution.py:595
  364.3 96.8 %collective-permute-start.25 = (bf16[640,1024]{1,0:T(8,128)(2,1)}, bf16[640,1024]{1,0:T(8,128)(2,1)}, u32[]{:S(2)}, u32[]{:S(2)}) collective-permute-start(bf16[640,1024]{1,0:T(8,128)(2,1)} %get-tuple-element.279), channel_id=1, source_target_pairs={{0,1},{1,0},{2,3},{3,2},{4,5},{5,4},{6,7},{7,6},{8,9},{9,8},{10,11... | collective-permute-start | bytes 3932168 | tf_op jit(solution)/shard_map/ppermute | solution.py:598
  370.1 28.9 %collective-permute-start.19 = (bf16[512,1024]{1,0:T(8,128)(2,1)}, bf16[512,1024]{1,0:T(8,128)(2,1)}, u32[]{:S(2)}, u32[]{:S(2)}) collective-permute-start(bf16[512,1024]{1,0:T(8,128)(2,1)} %bitcast.51), channel_id=1, source_target_pairs={{0,4},{2,6},{4,0},{6,2},{8,12},{10,14},{12,8},{14,10},{16,20},{18,... | collective-permute-start | bytes 3145736 | tf_op jit(solution)/shard_map/ppermute | solution.py:595
  371.5 25.7 %collective-permute-start.33 = (bf16[128,1024]{1,0:T(8,128)(2,1)}, bf16[128,1024]{1,0:T(8,128)(2,1)}, u32[]{:S(2)}, u32[]{:S(2)}) collective-permute-start(bf16[128,1024]{1,0:T(8,128)(2,1)} %dynamic-slice_bitcast_fusion.6), channel_id=1, source_target_pairs={{0,16},{2,18},{4,20},{6,22},{8,24},{10,26},{12,28},{14,30},{16,0},... | collective-permute-start | bytes 786440 | tf_op jit(solution)/shard_map/ppermute | solution.py:595
  399.0 171.1 %all-gather.11.cloned.1.call-start = ((), (), s32[]{:S(2)}) async-start(), calls=%async_computation.3 | async-start | bytes 5570560 | tf_op jit(solution)/shard_map/all_gather | solution.py:839
  404.1 30.4 %collective-permute-start.21 = (bf16[1024,768]{1,0:T(8,128)(2,1)S(1)}, bf16[1024,768]{1,0:T(8,128)(2,1)S(1)}, u32[]{:S(2)}, u32[]{:S(2)}) collective-permute-start(bf16[1024,768]{1,0:T(8,128)(2,1)S(1)} %convolution_convert_fusion.9), channel_id=1, source_target_pairs={{0,2},{2,0},{4,6},{6,4},{8,10},{10,8},{12,14},{14,12},{16,18},{18,... | collective-permute-start | bytes 4718600 | tf_op jit(solution)/shard_map/ppermute | solution.py:595
  404.2 31.9 %collective-permute-start.22 = (bf16[256,1024]{1,0:T(8,128)(2,1)S(1)}, bf16[256,1024]{1,0:T(8,128)(2,1)S(1)}, u32[]{:S(2)}, u32[]{:S(2)}) collective-permute-start(bf16[256,1024]{1,0:T(8,128)(2,1)S(1)} %bitcast.307), channel_id=1, source_target_pairs={{0,8},{2,10},{4,12},{6,14},{8,0},{10,2},{12,4},{14,6},{16,24},{18,... | collective-permute-start | bytes 1572872 | tf_op jit(solution)/shard_map/ppermute | solution.py:595
  408.0 28.2 %collective-permute-start.23 = (bf16[128,1024]{1,0:T(8,128)(2,1)S(1)}, bf16[128,1024]{1,0:T(8,128)(2,1)S(1)}, u32[]{:S(2)}, u32[]{:S(2)}) collective-permute-start(bf16[128,1024]{1,0:T(8,128)(2,1)S(1)} %bitcast.314), channel_id=1, source_target_pairs={{0,4},{2,6},{4,0},{6,2},{8,12},{10,14},{12,8},{14,10},{16,20},{18,... | collective-permute-start | bytes 786440 | tf_op jit(solution)/shard_map/ppermute | solution.py:595
  437.8 57.0 %collective-permute-start.37 = (bf16[128,1024]{1,0:T(8,128)(2,1)}, bf16[128,1024]{1,0:T(8,128)(2,1)}, u32[]{:S(2)}, u32[]{:S(2)}) collective-permute-start(bf16[128,1024]{1,0:T(8,128)(2,1)} %dynamic-slice_bitcast_fusion.5), channel_id=1, source_target_pairs={{0,16},{2,18},{4,20},{6,22},{8,24},{10,26},{12,28},{14,30},{16,0},... | collective-permute-start | bytes 786440 | tf_op jit(solution)/shard_map/ppermute | solution.py:595
  438.3 58.3 %collective-permute-start.27 = (bf16[1024,768]{1,0:T(8,128)(2,1)}, bf16[1024,768]{1,0:T(8,128)(2,1)}, u32[]{:S(2)}, u32[]{:S(2)}) collective-permute-start(bf16[1024,768]{1,0:T(8,128)(2,1)} %add_convert_fusion.7), channel_id=1, source_target_pairs={{0,1},{1,0},{2,3},{3,2},{4,5},{5,4},{6,7},{7,6},{8,9},{9,8},{10,11... | collective-permute-start | bytes 4718600 | tf_op jit(solution)/shard_map/ppermute | solution.py:598
  464.2 30.6 %collective-permute-start.38 = (bf16[32,1024]{1,0:T(8,128)(2,1)S(1)}, bf16[32,1024]{1,0:T(8,128)(2,1)S(1)}, u32[]{:S(2)}, u32[]{:S(2)}) collective-permute-start(bf16[32,1024]{1,0:T(8,128)(2,1)S(1)} %dynamic-slice_bitcast_fusion.11), channel_id=1, source_target_pairs={{0,16},{2,18},{4,20},{6,22},{8,24},{10,26},{12,28},{14,30},{16,0},... | collective-permute-start | bytes 196616 | tf_op jit(solution)/shard_map/ppermute | solution.py:595
  470.5 26.1 %collective-permute-start.26 = (bf16[1024,768]{1,0:T(8,128)(2,1)}, bf16[1024,768]{1,0:T(8,128)(2,1)}, u32[]{:S(2)}, u32[]{:S(2)}) collective-permute-start(bf16[1024,768]{1,0:T(8,128)(2,1)} %convolution_convert_fusion.8), channel_id=1, source_target_pairs={{0,2},{2,0},{4,6},{6,4},{8,10},{10,8},{12,14},{14,12},{16,18},{18,... | collective-permute-start | bytes 4718600 | tf_op jit(solution)/shard_map/ppermute | solution.py:595
  533.6 54.8 %collective-permute-start.44 = (bf16[640,1024]{1,0:T(8,128)(2,1)S(1)}, bf16[640,1024]{1,0:T(8,128)(2,1)S(1)}, u32[]{:S(2)}, u32[]{:S(2)}) collective-permute-start(bf16[640,1024]{1,0:T(8,128)(2,1)S(1)} %get-tuple-element.291), channel_id=1, source_target_pairs={{0,1},{1,0},{2,3},{3,2},{4,5},{5,4},{6,7},{7,6},{8,9},{9,8},{10,11... | collective-permute-start | bytes 3932168 | tf_op jit(solution)/shard_map/ppermute | solution.py:598
  (134 other events, 1398.2 us)
Sparse Core Ops, SparseCore 0:
  91.8 58.4 all-gather.4
  152.5 49.1 all-gather.6
  399.1 62.5 all-gather.8
  496.7 73.3 all-gather.10

commit v4 on v3

--- a/solution.py
+++ b/solution.py
@@ -18,7 +18,7 @@
 LOG2E = math.log2(math.e)
 PAIR = 128
 NEG = -1e30
-STRIPS = ((0, 512, 592), (512, 640, 1168), (640, 1024, 1168), (1024, 1280, 1280))
+STRIPS = ((0, 512, 592), (512, 1024, 1168), (1024, 1280, 1280))
 EARLY = 512
 
 
@@ -75,7 +75,9 @@
     column = jnp.where(is_patch, patch_id - patch_id // grid_side * grid_side, 0)
     first_key = clip_id * clip_len
     past_key = jnp.where(is_live, first_key + (frame_id + 1) * frame_len, length)
-    return (first_key, past_key, frame_id, patch_row, column)
+    segment = FRAMES * clip_id + frame_id
+    starts = [n * frame_len for n in range(FRAMES * 2 + 1)]
+    return (first_key, past_key, frame_id, patch_row, column, segment, starts)
 
 
 def rotary_tables(frame_id, patch_row, column):
@@ -156,60 +158,67 @@
     )(side, tokens, arrived, gain[None], shift[None])
 
 
-def project_kernel(chunk, x_ref, w_ref, b_ref, cos_ref, up_ref, down_ref, out_ref):
-    part = pl.program_id(0)
+def project_kernel(chunk, count, x_ref, *refs):
+    weights, biases, outs = refs[:count], refs[count : 2 * count], refs[2 * count + 3]
+    tables = refs[2 * count : 2 * count + 3]
     for at in range(0, x_ref.shape[0], chunk):
         rows = slice(at, at + chunk)
-        y = dot(x_ref[rows, :], w_ref[...]) + b_ref[...]
-
-        @pl.when(part == 2)
-        def _():
-            out_ref[rows, :] = low(y)
-
-        @pl.when(part < 2)
-        def _():
-            cos, up, down = cos_ref[rows, :], up_ref[rows, :], down_ref[rows, :]
-            for lane in range(0, y.shape[1], PAIR):
-                lanes = slice(lane, lane + PAIR)
-                out_ref[rows, lanes] = low(spin(y[:, lanes], cos, up, down))
-
-
-def project(x, weight, bias, tables):
+        cos, up, down = (table[rows, :] for table in tables)
+        for number, (w_ref, b_ref) in enumerate(zip(weights, biases)):
+            base, width = number * w_ref.shape[1], w_ref.shape[1] // 3
+            y = dot(x_ref[rows, :], w_ref[...]) + b_ref[...]
+            for lane in range(0, 2 * width, PAIR):
+                turned = spin(y[:, lane : lane + PAIR], cos, up, down)
+                outs[rows, base + lane : base + lane + PAIR] = low(turned)
+            outs[rows, base + 2 * width : base + 3 * width] = low(y[:, 2 * width :])
+
+
+def project(x, weights, biases, tables, block=640, chunk=320):
     rows, depth = x.shape
-    width = weight.shape[1] // 3
+    width = weights[0].shape[1] * len(weights)
+    biases = [bias[None] for bias in biases]
+    row = lambda array: pl.BlockSpec((block, array.shape[1]), lambda i: (i, 0))
     return pl.pallas_call(
-        functools.partial(project_kernel, rows),
-        grid=(3,),
-        in_specs=[
-            whole(x),
-            pl.BlockSpec((depth, width), lambda i: (0, i)),
-            pl.BlockSpec((1, width), lambda i: (0, i)),
-        ]
-        + [whole(table) for table in tables],
-        out_specs=pl.BlockSpec((rows, width), lambda i: (0, i)),
-        out_shape=jax.ShapeDtypeStruct((rows, 3 * width), jnp.bfloat16),
+        functools.partial(project_kernel, chunk, len(weights)),
+        grid=(rows // block,),
+        in_specs=[row(x)] + [whole(a) for a in (*weights, *biases)] + [row(t) for t in tables],
+        out_specs=pl.BlockSpec((block, width), lambda i: (i, 0)),
+        out_shape=jax.ShapeDtypeStruct((rows, width), jnp.bfloat16),
         compiler_params=params(),
-        cost_estimate=takes(7),
+        cost_estimate=takes(9),
         name="project",
-    )(x, weight, bias[None], *tables)
-
-
-def attend_kernel(q_ref, k_ref, v_ref, lo_ref, hi_ref, out_ref, root_ref, early_ref, late_ref):
+    )(x, *weights, *biases, *tables)
+
+
+SEGMENTS = 5
+BOUND_LANE = SEGMENTS
+
+
+def segment_lanes(first_key, past_key, segment, starts):
+    lane = jnp.arange(PAIR, dtype=jnp.int32)[None, :] % HEAD_DIM
+    start = sum(jnp.where(lane == n, starts[n], 0) for n in range(SEGMENTS))
+    inside = (start >= first_key[:, None]) & (start < past_key[:, None])
+    for_query = jnp.where((lane < SEGMENTS) & ~inside, NEG, 0.0)
+    for_key = jnp.where((lane == segment[:, None]) | (lane == BOUND_LANE), 1.0, 0.0)
+    return low(for_query), low(for_key)
+
+
+def own_lanes(head):
     lane = lax.broadcasted_iota(jnp.int32, (1, PAIR), 1)
-    factor = HEAD_DIM**-0.5 * LOG2E
+    return (lane >= HEAD_DIM) == (head == 1), lane % HEAD_DIM
+
+
+def attend_strips(shifted, v_ref, out_ref, root_ref, early_ref, late_ref):
     values = v_ref[...].T
-    for first, past, stop in STRIPS:
-        count = past - first
-        q = q_ref[first:past, :]
-        key = lax.broadcasted_iota(jnp.int32, (stop, count), 0)
-        allowed = (key >= lo_ref[:, first:past]) & (key < hi_ref[:, first:past])
+    least = None
+    for strip in STRIPS:
+        first, past, stop = strip
         outs, roots = [], []
         for head in range(2):
-            own = (lane >= HEAD_DIM) == (head == 1)
-            scores = dot_nt(k_ref[0:stop, :], jnp.where(own, q, jnp.zeros_like(q)))
-            scores = jnp.where(allowed, scores, NEG)
-            powers = jnp.exp2((scores - jnp.max(scores, 0, keepdims=True)) * factor)
-            root = 1.0 / jnp.sum(powers, 0, keepdims=True)
+            powers = jnp.exp2(shifted(head, strip))
+            total = jnp.sum(powers, 0, keepdims=True)
+            least = jnp.min(total) if least is None else jnp.minimum(least, jnp.min(total))
+            root = 1.0 / total
             powers = low(powers)
             if past <= EARLY:
                 early_ref[head, :, first:past] = powers
@@ -217,28 +226,77 @@
                 late_ref[head, 0:stop, first - EARLY : past - EARLY] = powers
             rows = slice(head * HEAD_DIM, (head + 1) * HEAD_DIM)
             outs.append(dot(values[rows, 0:stop], powers) * root)
-            roots.append(jnp.broadcast_to(root, (HEAD_DIM, count)))
+            roots.append(jnp.broadcast_to(root, (HEAD_DIM, past - first)))
         out_ref[first:past, :] = low(jnp.concatenate(outs, 0).T)
         root_ref[first:past, :] = jnp.concatenate(roots, 0).T
-
-
-def kept_specs(rows):
+    return least
+
+
+def attend_kernel(
+    q_ref, k_ref, v_ref, query_ref, key_ref, lo_ref, hi_ref, out_ref, root_ref, early_ref, late_ref
+):
+    factor = HEAD_DIM**-0.5 * LOG2E
+    squares = wide(k_ref[...]) * wide(k_ref[...])
+    keys, longest = [], []
+    for head in range(2):
+        own, _ = own_lanes(head)
+        keys.append(jnp.where(own, k_ref[...], key_ref[...]))
+        length = jnp.sum(jnp.where(own, squares, 0.0), 1, keepdims=True)
+        longest.append(jnp.max(length, 0, keepdims=True))
+
+    def below_bound(head, strip):
+        first, past, stop = strip
+        own, lane = own_lanes(head)
+        q = q_ref[first:past, :]
+        length = jnp.sum(jnp.where(own, wide(q) * wide(q), 0.0), 1, keepdims=True)
+        bound = jnp.sqrt(length * longest[head]) * 1.01
+        beside = jnp.where(lane == BOUND_LANE, low(-bound), query_ref[first:past, :])
+        return dot_nt(keys[head][0:stop], jnp.where(own, q, beside)) * factor
+
+    outs = (v_ref, out_ref, root_ref, early_ref, late_ref)
+    least = attend_strips(below_bound, *outs)
+
+    @pl.when(jnp.logical_not(least > 1e-20))
+    def _():
+        def below_maximum(head, strip):
+            first, past, stop = strip
+            own, _ = own_lanes(head)
+            q = q_ref[first:past, :]
+            scores = dot_nt(k_ref[0:stop, :], jnp.where(own, q, jnp.zeros_like(q)))
+            key = lax.broadcasted_iota(jnp.int32, scores.shape, 0)
+            allowed = (key >= lo_ref[:, first:past]) & (key < hi_ref[:, first:past])
+            scores = jnp.where(allowed, scores, NEG)
+            return (scores - jnp.max(scores, 0, keepdims=True)) * factor
+
+        attend_strips(below_maximum, *outs)
+
+
+def kept_specs(rows, base):
     return [
-        pl.BlockSpec((2, STRIPS[0][2], EARLY), lambda i: (i, 0, 0)),
-        pl.BlockSpec((2, rows, rows - EARLY), lambda i: (i, 0, 0)),
+        pl.BlockSpec((2, STRIPS[0][2], EARLY), lambda i: (base + i, 0, 0)),
+        pl.BlockSpec((2, rows, rows - EARLY), lambda i: (base + i, 0, 0)),
     ]
 
 
-def attend(heads, first_key, past_key):
+QUARTER_PAIRS = 2
+
+
+def head_specs(rows, base):
+    pair = lambda i: (base + i) // QUARTER_PAIRS * 3 * QUARTER_PAIRS + (base + i) % QUARTER_PAIRS
+    part = lambda number: pl.BlockSpec((rows, PAIR), lambda i: (0, pair(i) + number * QUARTER_PAIRS))
+    return [part(0), part(1), part(2)], pl.BlockSpec((rows, PAIR), lambda i: (0, base + i))
+
+
+def attend(heads, lanes, first_key, past_key):
     rows, width = heads.shape[0], heads.shape[1] // 3
     pairs = width // PAIR
-    block = pl.BlockSpec((rows, PAIR), lambda i: (0, i))
-    part = lambda number: pl.BlockSpec((rows, PAIR), lambda i: (0, number * pairs + i))
+    parts, block = head_specs(rows, 0)
+    beside = (*lanes, first_key, past_key)
     return pl.pallas_call(
         attend_kernel,
         grid=(pairs,),
-        in_specs=[part(0), part(1), part(2), whole(first_key), whole(past_key)],
-        out_specs=[block, block] + kept_specs(rows),
+        in_specs=parts + [whole(array) for array in beside],
+        out_specs=[block, block] + kept_specs(rows, 0),
         out_shape=[
             jax.ShapeDtypeStruct((rows, width), jnp.bfloat16),
             jax.ShapeDtypeStruct((rows, width), jnp.float32),
@@ -246,9 +304,9 @@
             jax.ShapeDtypeStruct((2 * pairs, rows, rows - EARLY), jnp.bfloat16),
         ],
         compiler_params=params(),
-        cost_estimate=takes(17),
+        cost_estimate=takes(20),
         name="attend",
-    )(heads, heads, heads, first_key, past_key)
+    )(heads, heads, heads, *beside)
 
 
 def attend_back_kernel(
@@ -257,27 +315,35 @@
 ):
     pair = pl.program_id(0)
     pairs = out_ref.shape[1] // (3 * PAIR)
-    lane = lax.broadcasted_iota(jnp.int32, (1, PAIR), 1)
     scale = HEAD_DIM**-0.5
     keys = k_ref[...].T
+    values = []
+    for head in range(2):
+        own, lane = own_lanes(head)
+        values.append(jnp.where(own, v_ref[...], low(jnp.where(lane < 3, 1.0, 0.0))))
     for first, past, stop in STRIPS[::-1]:
         q = q_ref[first:past, :]
         g = wide(g_ref[first:past, :]) * root_ref[first:past, :]
-        inner = (g * wide(o_ref[first:past, :])).T
+        inner = g * wide(o_ref[first:past, :])
         g = low(g)
+        zero = jnp.zeros_like(g)
         for head in range(2):
-            own = (lane >= HEAD_DIM) == (head == 1)
+            own, lane = own_lanes(head)
             rows = slice(head * HEAD_DIM, (head + 1) * HEAD_DIM)
-            g_own = jnp.where(own, g, jnp.zeros_like(g))
-            shift = jnp.sum(inner[rows, :], 0, keepdims=True)
+            shift = -jnp.sum(jnp.where(own, inner, 0.0), 1, keepdims=True)
+            beside = zero
+            for number in range(3):
+                part = low(shift)
+                shift = shift - wide(part)
+                beside = jnp.where(lane == number, part, beside)
             if past <= EARLY:
                 powers = early_ref[head, :, first:past]
             else:
                 powers = late_ref[head, 0:stop, first - EARLY : past - EARLY]
-            g_scores = low(wide(powers) * (dot_nt(v_ref[0:stop, :], g_own) - shift))
+            g_scores = low(wide(powers) * dot_nt(values[head][0:stop], jnp.where(own, g, beside)))
             queries_acc[rows, first:past] = dot(keys[rows, 0:stop], g_scores)
-            g_keys = dot(g_scores, jnp.where(own, q, jnp.zeros_like(q)))
-            g_values = dot(powers, g_own)
+            g_keys = dot(g_scores, jnp.where(own, q, zero))
+            g_values = dot(powers, jnp.where(own, g, zero))
             if head == 0:
                 total_keys, total_values = g_keys, g_values
             else:
@@ -300,16 +366,16 @@
         sums_ref[:, lanes] = fold(wide(grad))
 
 
-def attend_back(heads, g, out, root, early, late, tables):
+def attend_back(quarter, heads, g, out, root, early, late, tables):
     rows, width = g.shape
     pairs = width // PAIR
-    block = pl.BlockSpec((rows, PAIR), lambda i: (0, i))
-    part = lambda number: pl.BlockSpec((rows, PAIR), lambda i: (0, number * pairs + i))
+    parts, block = head_specs(rows, quarter * pairs)
     return pl.pallas_call(
         attend_back_kernel,
         grid=(pairs,),
-        in_specs=[part(0), part(1), part(2), block, block, block]
-        + kept_specs(rows)
+        in_specs=parts
+        + [pl.BlockSpec((rows, PAIR), lambda i: (0, i)), block, block]
+        + kept_specs(rows, quarter * pairs)
         + [whole(table) for table in tables],
         out_specs=[
             pl.BlockSpec((rows, 3 * width), lambda i: (0, 0)),
@@ -325,23 +391,24 @@
             pltpu.VMEM((PAIR, rows), jnp.float32),
         ],
         compiler_params=params(56),
-        cost_estimate=takes(20),
+        cost_estimate=takes(16),
         name="attend_back",
     )(heads, heads, heads, g, out, root, early, late, *tables)
 
 
 def merge_kernel(count, *refs):
-    rights, lefts = refs[:count], refs[count : 2 * count]
-    x_ref, bias_ref, gain_ref, shift_ref, residual_ref, out_ref = refs[2 * count :]
+    rights, lefts = refs[: 2 * count], refs[2 * count : 3 * count]
+    x_ref, bias_ref, gain_ref, shift_ref, residual_ref, out_ref = refs[3 * count :]
     total = wide(x_ref[...]) + bias_ref[...]
-    for left, right in zip(lefts, rights):
-        total = total + dot(left[...], right[...])
+    for number, right in enumerate(rights):
+        left, width = lefts[number // 2], right.shape[0]
+        total = total + dot(left[:, number % 2 * width : (number % 2 + 1) * width], right[...])
     residual_ref[...] = total
     normed, _ = standardize(total)
     out_ref[...] = low(normed * gain_ref[...] + shift_ref[...])
 
 
-def merge(lefts, rights, x, bias, gain, shift, block=256):
+def merge(lefts, rights, x, bias, gain, shift, block=320):
     rows, depth = x.shape
     row = lambda array: pl.BlockSpec((block, array.shape[1]), lambda i: (i, 0))
     vectors = (bias[None], gain[None], shift[None])
@@ -648,11 +715,12 @@
 
     count_one = lax.dynamic_index_in_dim(patch_count[:, 0], side, 0, False)
     length = 2 * tokens.shape[1]
-    first_key, past_key, frame_id, patch_row, column = slot_layout(count_one, length)
+    first_key, past_key, frame_id, patch_row, column, segment, starts = slot_layout(count_one, length)
     tables = rotary_tables(frame_id, patch_row, column)
+    lanes = segment_lanes(first_key, past_key, segment, starts)
     first_key, past_key = first_key[None], past_key[None]
 
-    did(heads_piece, up_piece, down_piece, *heads_own, *merge_own, *expand_own, *reduce_own, *tables)
+    did(heads_piece, up_piece, down_piece, *heads_own, *merge_own, *expand_own, *reduce_own, *tables, *lanes)
     heads_piece = cross(tie(heads_piece, tokens_far))
     up_piece = cross(tie(up_piece, tokens_far))
     bias_both = cross(tie(jnp.concatenate(bias_own), tokens_far))
@@ -662,11 +730,12 @@
     heads_all = [heads_own, None]
     bias_all = (bias_own, bias_far)
 
-    def look(p, c):
-        heads[p, c] = did(project(after(first_out), heads_all[p][c], bias_all[p][c][:three], tables))
-
-    def attention(p, c):
-        seen[p, c] = did(*attend(after(heads[p, c]), first_key, past_key))
+    def look(p):
+        biases = [bias[:three] for bias in bias_all[p]]
+        heads[p] = did(project(after(first_out), heads_all[p], biases, tables))
+
+    def attention(p):
+        seen[p] = did(*attend(after(heads[p]), lanes, first_key, past_key))
 
     def gathered(array, *splits):
         array = lax.all_gather(array, "dp", axis=0, tiled=True)
@@ -683,35 +752,32 @@
             at += size
         return quarters
 
-    look(OWN, KEEP)
-    look(OWN, SEND)
+    look(OWN)
     heads_piece = did(after(heads_piece))
     if len(near) > 1:
         heads_next = swap(heads_piece, near[1])
-    attention(OWN, KEEP)
     up_sizes = (expand_own[0].shape[0] // chunks, merge_own[0].shape[0] // chunks)
     up_gathered = gathered(after(up_piece), *up_sizes)
     down_piece = cross(after(down_piece))
     if len(near) > 1:
         heads_piece = did(join(after(heads_piece), heads_next, near[1], near[1:]))
     heads_next = swap(heads_piece, near[0])
-    attention(OWN, SEND)
+    attention(OWN)
     heads_piece = did(join(after(heads_piece), heads_next, near[0], near))
     heads_all[FAR] = [heads_piece, swap(heads_piece, 0)]
     cotangent_far = cross(after(lax.dynamic_index_in_dim(cotangent, 1 - side, 0, False)))
     (reduce_far,) = gathered(after(down_piece), down_piece.shape[0])
-    look(FAR, KEEP)
-    attention(FAR, KEEP)
-    look(FAR, SEND)
-    attention(FAR, SEND)
+    look(FAR)
+    attention(FAR)
     expand_far, merge_far = ([after(q) for q in quarters] for quarters in up_gathered)
     merge_all = (merge_own, merge_far)
     expand_all = (expand_own, expand_far)
     reduce_all = (reduce_own, reduce_far)
-    mixed = {q: seen[q][0] for q in QUARTERS}
+    width = seen[OWN][0].shape[1] // 2
+    mixed = {(p, c): seen[p][0][:, c * width : (c + 1) * width] for p, c in QUARTERS}
     residual, second_out = did(
         *merge(
-            [mixed[q] for q in QUARTERS], [merge_all[p][c] for p, c in QUARTERS],
+            [seen[OWN][0], seen[FAR][0]], [merge_all[p][c] for p in (OWN, FAR) for c in (KEEP, SEND)],
             after(stream), merge_bias, second_gain, second_shift,
         )
     )
@@ -791,9 +857,9 @@
         grad_mixed[p, c] = did(low(dot_nt(after(grad_one), merge_all[p][c])))
 
     def back_attention(q):
-        out, root, early, late = seen[q]
+        p, c = q
         grad_heads[q], sums = did(
-            *attend_back(heads[q], after(grad_mixed[q]), out, root, early, late, tables)
+            *attend_back(c, heads[p], after(grad_mixed[q]), *seen[p], tables)
         )
         head_sums[q] = jnp.sum(sums, 0)
 

time: 623 us -> 577 us (0.926)
  Pallas kernels: 297 us -> 240 us
  waiting for transfers between devices: 63.8 us -> 86.8 us
  local copies, waits for them, and re-layouts: 65.5 us -> 57.1 us
  starting transfers between devices: 41.4 us -> 49.8 us
  matrix products: 84.8 us -> 77.2 us
    pallas_call x12 -> x8, Pallas kernels: 180 us -> 123 us  [the longest x4 69.7 us: attend_back(): pl.pallas_call(attend_back_kernel, grid=(pairs,), in_specs=parts + [pl.Bl...]
    ppermute x13, waiting for transfers between devices: 22 us -> 39 us  [cross(): return lax.ppermute(array, 'mp', [(0, 1), (1, 0)])]
    unnamed x213 -> x203, local copies, waits for them, and re-layouts: 23.6 us -> 15.2 us
    convert_element_type x20 -> x21, other arithmetic: 14.6 us -> 13.8 us  [low(): return array.astype(jnp.bfloat16)]
  transfers between devices with their start and end apart: 55 -> 55, of which waited for: 14 -> 18; matrix products, arithmetic and copies ran while one was open for 25% -> 25% of each run, Pallas kernels for 46% -> 41%
where the time goes in v4:
time: 577 us; the launch traced here: 568 us
  Pallas kernels  240 us (42%)
  waiting for transfers between devices  86.8 us (15%)
  matrix products  77.2 us (13%)
  local copies, waits for them, and re-layouts  57.1 us (10%)
  starting transfers between devices  49.8 us (9%)
  other arithmetic  40 us (7%)
  between operations  17.3 us (3%)
    pallas_call x4, Pallas kernels, attend_back(): pl.pallas_call(attend_back_kernel, grid=(pairs,), in_specs=parts + [pl.Bl...  69.7 us
    dot_general x16, matrix products, dot_tn(): lax.dot_general(left, right, (((0,), (0,)), ((), ())), preferred_element_...  52.9 us
    ppermute x38, waiting for transfers between devices, swap(): lax.ppermute(array, 'dp', [(i, i ^ 1 << level) for i in range(spread)])  47.5 us
    pallas_call x3, Pallas kernels, back_norm(): pl.pallas_call(functools.partial(back_kernel, len(lefts)), grid_spec=pltp...  41.4 us
    ppermute x13, waiting for transfers between devices, cross(): return lax.ppermute(array, 'mp', [(0, 1), (1, 0)])  39 us
    pallas_call x2, Pallas kernels, attend(): pl.pallas_call(attend_kernel, grid=(pairs,), in_specs=parts + [whole(arra...  36.8 us
    pallas_call x4, Pallas kernels, expand(): pl.pallas_call(functools.partial(expand_kernel, chunk), grid=(width // bl...  35.7 us
    ppermute x38, starting transfers between devices, swap(): lax.ppermute(array, 'dp', [(i, i ^ 1 << level) for i in range(spread)])  32.8 us
  transfers between devices with their start and end apart: 55, of which 18 were waited for; matrix products, arithmetic and copies ran while one was open for 25% of the time, Pallas kernels for 41%

profile of v4, /device:TPU:0, one launch (start us, length us, event | category | flops | bytes accessed | tf_op | source)
XLA Modules:
  0.0 567.8 jit_solution(10567783042300195283)
XLA Ops:
  23.5 6.6 %constant_dynamic-slice_fusion.29 = (bf16[1024,1024]{1,0:T(8,128)(2,1)}, bf16[1024,1024]{1,0:T(8,128)(2,1)}, bf16[1024,1024]{1,0:T(8,128)(2,1)S(1)}, bf16[1024,1024]{1,0:T(8,128)(2,1)}) fusion(bf16[2048,1024]{1,0:T(8,128)(2,1)} %param.28, s32[]{:T(128)S(6)} %select_n.583, s32[]{:T(128)S(6)} %select_n.577, bf16[1024,2048]{1,0:T(8,128)(2,1)} %param.26), kind=kLoop, calls=%fused_computation.132 | loop fusion | bytes 16777224 | tf_op jit(solution)/shard_map/dynamic_slice | solution.py:669
  48.1 8.0 %project.2.q_ref.k_ref.v_ref = bf16[1280,1536]{1,0:T(8,128)(2,1)} custom-call(bf16[1280,1024]{1,0:T(8,128)(2,1)} %get-tuple-element.263.x_ref, bf16[1024,768]{1,0:T(8,128)(2,1)S(1)} %pad_maximum_fusion.refs_0_.refs_3_, bf16[1024,768]{1,0:T(8,128)(2,1)} %pad_maximum_fusion.1.refs_1_.refs_2_, f32[1,768]{1,0:T(1,128)S(1)} %bitcast.234, f32[1,768]{1,0:T(1,128)S(1)} %bitcast.235, ...), custom_call_target="tpu_custom_call" | custom-call | flops 35999997952 | bytes 36000000 | tf_op jit(solution)/shard_map/project/pallas_call | solution.py:181
  66.8 7.0 %collective-permute-done.2 = bf16[256,768]{1,0:T(8,128)(2,1)S(1)} collective-permute-done((bf16[256,768]{1,0:T(8,128)(2,1)S(1)}, bf16[256,768]{1,0:T(8,128)(2,1)S(1)}, u32[]{:S(2)}, u32[]{:S(2)}) %collective-permute-start.2) | collective-permute-done | bytes 393248 | tf_op jit(solution)/shard_map/ppermute | solution.py:662
  77.1 18.4 %attend.2 = (bf16[1280,512]{1,0:T(8,128)(2,1)S(1)}, f32[1280,512]{1,0:T(8,128)}, bf16[8,592,512]{2,1,0:T(8,128)(2,1)}, bf16[8,1280,768]{2,1,0:T(8,128)(2,1)}) custom-call(bf16[1280,1536]{1,0:T(8,128)(2,1)} %project.2.q_ref.k_ref.v_ref, bf16[1280,1536]{1,0:T(8,128)(2,1)} %project.2.q_ref.k_ref.v_ref, bf16[1280,1536]{1,0:T(8,128)(2,1)} %project.2.q_ref.k_ref.v_ref, ...), custom_call_target="tpu_custom_call" | custom-call | flops 80000000000 | bytes 80000000 | tf_op jit(solution)/shard_map/attend/pallas_call | solution.py:295
  106.1 7.3 %collective-permute-done.9 = bf16[128,1024]{1,0:T(8,128)(2,1)} collective-permute-done((bf16[128,1024]{1,0:T(8,128)(2,1)}, bf16[128,1024]{1,0:T(8,128)(2,1)}, u32[]{:S(2)}, u32[]{:S(2)}) %collective-permute-start.9) | collective-permute-done | bytes 262176 | tf_op jit(solution)/shard_map/ppermute | solution.py:665
  117.2 8.4 %project.3.q_ref.k_ref.v_ref = bf16[1280,1536]{1,0:T(8,128)(2,1)} custom-call(bf16[1280,1024]{1,0:T(8,128)(2,1)} %get-tuple-element.263.x_ref, bf16[1024,768]{1,0:T(8,128)(2,1)} %bitcast.23.refs_0_.refs_1_, bf16[1024,768]{1,0:T(8,128)(2,1)} %collective-permute-done.4.refs_1_.refs_0_, f32[1,768]{1,0:T(1,128)S(1)} %broadcast_in_dim.159.refs_2_, ...), custom_call_target="tpu_custom_call" | custom-call | flops 35999997952 | bytes 36000000 | tf_op jit(solution)/shard_map/project/pallas_call | solution.py:181
  125.6 18.4 %attend.3 = (bf16[1280,512]{1,0:T(8,128)(2,1)S(1)}, f32[1280,512]{1,0:T(8,128)}, bf16[8,592,512]{2,1,0:T(8,128)(2,1)}, bf16[8,1280,768]{2,1,0:T(8,128)(2,1)}) custom-call(bf16[1280,1536]{1,0:T(8,128)(2,1)} %project.3.q_ref.k_ref.v_ref, bf16[1280,1536]{1,0:T(8,128)(2,1)} %project.3.q_ref.k_ref.v_ref, bf16[1280,1536]{1,0:T(8,128)(2,1)} %project.3.q_ref.k_ref.v_ref, ...), custom_call_target="tpu_custom_call" | custom-call | flops 80000000000 | bytes 80000000 | tf_op jit(solution)/shard_map/attend/pallas_call | solution.py:295
  146.7 7.8 %merge.1 = (f32[1280,1024]{1,0:T(8,128)}, bf16[1280,1024]{1,0:T(8,128)(2,1)}) custom-call(bf16[256,1024]{1,0:T(8,128)(2,1)S(1)} %copy-done.15, bf16[256,1024]{1,0:T(8,128)(2,1)S(1)} %copy-done.17, bf16[256,1024]{1,0:T(8,128)(2,1)S(1)} %bitcast.223, bf16[256,1024]{1,0:T(8,128)(2,1)S(1)} %bitcast.225, bf16[1280,512]{1,0:T(8,128)(2,1)S(1)} %get-tuple-element.168.refs_4_.o_ref, ...), custom_call_target="tpu_custom_call" | custom-call | flops 32000000000 | bytes 32000000 | tf_op jit(solution)/shard_map/merge/pallas_call | solution.py:415
  158.0 9.8 %expand.4 = (bf16[1280,1024]{1,0:T(8,128)(2,1)}, bf16[1280,1024]{1,0:T(8,128)(2,1)}) custom-call(bf16[1280,1024]{1,0:T(8,128)(2,1)} %get-tuple-element.220.x_ref, bf16[1024,1024]{1,0:T(8,128)(2,1)S(1)} %bitcast.221, f32[1,1024]{1,0:T(1,128)S(1)} %bitcast.233), custom_call_target="tpu_custom_call" | custom-call | flops 33999998976 | bytes 34000000 | tf_op jit(solution)/shard_map/expand/pallas_call | solution.py:446
  167.8 8.5 %expand.5 = (bf16[1280,1024]{1,0:T(8,128)(2,1)}, bf16[1280,1024]{1,0:T(8,128)(2,1)}) custom-call(bf16[1280,1024]{1,0:T(8,128)(2,1)} %get-tuple-element.220.x_ref, bf16[1024,1024]{1,0:T(8,128)(2,1)S(1)} %bitcast.219, f32[1,1024]{1,0:T(1,128)S(1)} %bitcast.232), custom_call_target="tpu_custom_call" | custom-call | flops 33999998976 | bytes 34000000 | tf_op jit(solution)/shard_map/expand/pallas_call | solution.py:446
  183.1 8.6 %expand.6 = (bf16[1280,1024]{1,0:T(8,128)(2,1)}, bf16[1280,1024]{1,0:T(8,128)(2,1)}) custom-call(bf16[1280,1024]{1,0:T(8,128)(2,1)} %get-tuple-element.220.x_ref, bf16[1024,1024]{1,0:T(8,128)(2,1)S(1)} %copy-done.1, f32[1,1024]{1,0:T(1,128)S(1)} %bitcast.228), custom_call_target="tpu_custom_call" | custom-call | flops 33999998976 | bytes 34000000 | tf_op jit(solution)/shard_map/expand/pallas_call | solution.py:446
  196.0 8.8 %expand.7 = (bf16[1280,1024]{1,0:T(8,128)(2,1)}, bf16[1280,1024]{1,0:T(8,128)(2,1)}) custom-call(bf16[1280,1024]{1,0:T(8,128)(2,1)} %get-tuple-element.220.x_ref, bf16[1024,1024]{1,0:T(8,128)(2,1)S(1)} %get-tuple-element.445.w_ref.refs_3_, f32[1,1024]{1,0:T(1,128)S(1)} %bitcast.227), custom_call_target="tpu_custom_call" | custom-call | flops 33999998976 | bytes 34000000 | tf_op jit(solution)/shard_map/expand/pallas_call | solution.py:446
  229.6 18.0 %reduce_rows.1 = (bf16[640,1024]{1,0:T(8,128)(2,1)}, bf16[640,1024]{1,0:T(8,128)(2,1)S(1)}) custom-call(s32[1]{0:T(128)} %bitcast.side_ref.flag_ref, bf16[1024,1024]{1,0:T(8,128)(2,1)} %bitcast.245, bf16[1024,1024]{1,0:T(8,128)(2,1)} %bitcast.243, bf16[1024,1024]{1,0:T(8,128)(2,1)} %get-tuple-element.360.refs_2_, ...), custom_call_target="tpu_custom_call" | custom-call | flops 400000000 | bytes 400000 | tf_op jit(solution)/shard_map/reduce_rows/pallas_call | solution.py:483
  267.7 9.9 %collective-permute-done.12 = bf16[1024,1024]{1,0:T(8,128)(2,1)S(1)} collective-permute-done((bf16[1024,1024]{1,0:T(8,128)(2,1)}, bf16[1024,1024]{1,0:T(8,128)(2,1)S(1)}, u32[]{:S(2)}, u32[]{:S(2)}) %collective-permute-start.12) | collective-permute-done | bytes 2097184 | tf_op jit(solution)/shard_map/ppermute | solution.py:665
  284.3 20.6 %back_norm.3 = (bf16[1280,1024]{1,0:T(8,128)(2,1)}, f32[4,8,1024]{2,1,0:T(8,128)S(1)}) custom-call(s32[1]{0:T(128)} %constant.312.clone.1.at_ref, bf16[1024,1024]{1,0:T(8,128)(2,1)S(1)} %bitcast.222, bf16[1024,1024]{1,0:T(8,128)(2,1)} %bitcast.220, bf16[1024,1024]{1,0:T(8,128)(2,1)} %get-tuple-element.446.w_ref.refs_2_, bf16[1024,1024]{1,0:T(8,128)(2,1)} %copy-done, ...), custom_call_target="tpu_custom_call" | custom-call | flops 400000000 | bytes 400000 | tf_op jit(solution)/shard_map/back_norm/pallas_call | solution.py:529
  317.4 10.0 %collective-permute-done.17 = bf16[1024,1024]{1,0:T(8,128)(2,1)S(1)} collective-permute-done((bf16[1024,1024]{1,0:T(8,128)(2,1)}, bf16[1024,1024]{1,0:T(8,128)(2,1)S(1)}, u32[]{:S(2)}, u32[]{:S(2)}) %collective-permute-start.17) | collective-permute-done | bytes 2097184 | tf_op jit(solution)/shard_map/ppermute | solution.py:665
  336.9 17.3 %attend_back.4 = (bf16[1280,768]{1,0:T(8,128)(2,1)}, f32[8,768]{1,0:T(8,128)}) custom-call(bf16[1280,1536]{1,0:T(8,128)(2,1)} %project.3.q_ref.k_ref.v_ref, bf16[1280,1536]{1,0:T(8,128)(2,1)} %project.3.q_ref.k_ref.v_ref, bf16[1280,1536]{1,0:T(8,128)(2,1)} %project.3.q_ref.k_ref.v_ref, bf16[1280,256]{1,0:T(8,128)(2,1)} %convolution_convert_fusion.3.g_ref, ...), custom_call_target="tpu_custom_call" | custom-call | flops 64000000000 | bytes 64000000 | tf_op jit(solution)/shard_map/attend_back/pallas_call | solution.py:373
  371.3 17.7 %attend_back.5 = (bf16[1280,768]{1,0:T(8,128)(2,1)}, f32[8,768]{1,0:T(8,128)}) custom-call(bf16[1280,1536]{1,0:T(8,128)(2,1)} %project.3.q_ref.k_ref.v_ref, bf16[1280,1536]{1,0:T(8,128)(2,1)} %project.3.q_ref.k_ref.v_ref, bf16[1280,1536]{1,0:T(8,128)(2,1)} %project.3.q_ref.k_ref.v_ref, bf16[1280,256]{1,0:T(8,128)(2,1)} %convolution_convert_fusion.2.g_ref, ...), custom_call_target="tpu_custom_call" | custom-call | flops 64000000000 | bytes 64000000 | tf_op jit(solution)/shard_map/attend_back/pallas_call | solution.py:373
  400.2 17.4 %attend_back.6 = (bf16[1280,768]{1,0:T(8,128)(2,1)}, f32[8,768]{1,0:T(8,128)}) custom-call(bf16[1280,1536]{1,0:T(8,128)(2,1)} %project.2.q_ref.k_ref.v_ref, bf16[1280,1536]{1,0:T(8,128)(2,1)} %project.2.q_ref.k_ref.v_ref, bf16[1280,1536]{1,0:T(8,128)(2,1)} %project.2.q_ref.k_ref.v_ref, bf16[1280,256]{1,0:T(8,128)(2,1)} %convolution_convert_fusion.1.g_ref, ...), custom_call_target="tpu_custom_call" | custom-call | flops 64000000000 | bytes 64000000 | tf_op jit(solution)/shard_map/attend_back/pallas_call | solution.py:373
  426.1 17.3 %attend_back.7 = (bf16[1280,768]{1,0:T(8,128)(2,1)}, f32[8,768]{1,0:T(8,128)}) custom-call(bf16[1280,1536]{1,0:T(8,128)(2,1)} %project.2.q_ref.k_ref.v_ref, bf16[1280,1536]{1,0:T(8,128)(2,1)} %project.2.q_ref.k_ref.v_ref, bf16[1280,1536]{1,0:T(8,128)(2,1)} %project.2.q_ref.k_ref.v_ref, bf16[1280,256]{1,0:T(8,128)(2,1)} %convolution_convert_fusion.g_ref, ...), custom_call_target="tpu_custom_call" | custom-call | flops 64000000000 | bytes 64000000 | tf_op jit(solution)/shard_map/attend_back/pallas_call | solution.py:373
  453.2 10.3 %back_norm.4 = (bf16[640,1024]{1,0:T(8,128)(2,1)S(1)}, f32[4,8,1024]{2,1,0:T(8,128)S(1)}) custom-call(s32[1]{0:T(128)S(6)} %mul.235.at_ref, bf16[1024,768]{1,0:T(8,128)(2,1)} %collective-permute-done.4.refs_1_.refs_0_, bf16[1024,768]{1,0:T(8,128)(2,1)} %bitcast.23.refs_0_.refs_1_, bf16[1024,768]{1,0:T(8,128)(2,1)} %pad_maximum_fusion.1.refs_1_.refs_2_, ...), custom_call_target="tpu_custom_call" | custom-call | flops 40000000000 | bytes 40000000 | tf_op jit(solution)/shard_map/back_norm/pallas_call | solution.py:529
  469.9 10.5 %back_norm.5 = (bf16[640,1024]{1,0:T(8,128)(2,1)S(1)}, f32[4,8,1024]{2,1,0:T(8,128)S(1)}) custom-call(s32[1]{0:T(128)S(6)} %mul.234.at_ref, bf16[1024,768]{1,0:T(8,128)(2,1)} %collective-permute-done.4.refs_1_.refs_0_, bf16[1024,768]{1,0:T(8,128)(2,1)} %bitcast.23.refs_0_.refs_1_, bf16[1024,768]{1,0:T(8,128)(2,1)} %pad_maximum_fusion.1.refs_1_.refs_2_, ...), custom_call_target="tpu_custom_call" | custom-call | flops 40000000000 | bytes 40000000 | tf_op jit(solution)/shard_map/back_norm/pallas_call | solution.py:529
  486.5 13.2 %collective-permute-done.31 = bf16[256,384]{1,0:T(8,128)(2,1)S(1)} collective-permute-done((bf16[256,384]{1,0:T(8,128)(2,1)S(1)}, bf16[256,384]{1,0:T(8,128)(2,1)S(1)}, u32[]{:S(2)}, u32[]{:S(2)}) %collective-permute-start.31) | collective-permute-done | bytes 196640 | tf_op jit(solution)/shard_map/ppermute | solution.py:662
  516.7 6.5 %collective-permute-done.36 = bf16[128,384]{1,0:T(8,128)(2,1)S(1)} collective-permute-done((bf16[128,384]{1,0:T(8,128)(2,1)S(1)}, bf16[128,384]{1,0:T(8,128)(2,1)S(1)}, u32[]{:S(2)}, u32[]{:S(2)}) %collective-permute-start.36) | collective-permute-done | bytes 98336 | tf_op jit(solution)/shard_map/ppermute | solution.py:662
  (470 shorter events, 264.0 us)
Async XLA Ops:
  7.2 137.9 %all-gather.5.cloned.1.call-start = ((), (), s32[]{:S(2)}) async-start(), calls=%async_computation | async-start | bytes 5570560 | tf_op jit(solution)/shard_map/all_gather | solution.py:741
  9.7 32.0 %collective-permute-start = (bf16[640,1024]{1,0:T(8,128)(2,1)}, bf16[640,1024]{1,0:T(8,128)(2,1)S(1)}, u32[]{:S(2)}, u32[]{:S(2)}) collective-permute-start(bf16[640,1024]{1,0:T(8,128)(2,1)} %dynamic-slice_bitcast_fusion.1), channel_id=1, source_target_pairs={{0,1},{1,0},{2,3},{3,2},{4,5},{5,4},{6,7},{7,6},{8,9},{9,8},{10,11... | collective-permute-start | bytes 3932168 | tf_op jit(solution)/shard_map/ppermute | solution.py:665
  64.1 145.4 %all-gather.7.cloned.1.call-start = ((), (), s32[]{:S(2)}) async-start(), calls=%async_computation.1 | async-start | bytes 4456448 | tf_op jit(solution)/shard_map/all_gather | solution.py:741
  104.5 52.9 %collective-permute-start.7 = (bf16[640,1024]{1,0:T(8,128)(2,1)}, bf16[640,1024]{1,0:T(8,128)(2,1)}, u32[]{:S(2)}, u32[]{:S(2)}) collective-permute-start(bf16[640,1024]{1,0:T(8,128)(2,1)} %get-tuple-element.184), channel_id=1, source_target_pairs={{0,1},{1,0},{2,3},{3,2},{4,5},{5,4},{6,7},{7,6},{8,9},{9,8},{10,11... | collective-permute-start | bytes 3932168 | tf_op jit(solution)/shard_map/ppermute | solution.py:665
  113.4 390.7 %all-gather.9.cloned.1.call-start = ((), (), s32[]{:S(2)}) async-start(), calls=%async_computation.2 | async-start | bytes 4456448 | tf_op jit(solution)/shard_map/all_gather | solution.py:881
  229.3 22.0 %collective-permute-start.11 = (bf16[1024,1024]{1,0:T(8,128)(2,1)}, bf16[1024,1024]{1,0:T(8,128)(2,1)}, u32[]{:S(2)}, u32[]{:S(2)}) collective-permute-start(bf16[1024,1024]{1,0:T(8,128)(2,1)} %convolution_convert_fusion.5), channel_id=1, source_target_pairs={{0,2},{2,0},{4,6},{6,4},{8,10},{10,8},{12,14},{14,12},{16,18},{18,... | collective-permute-start | bytes 6291464 | tf_op jit(solution)/shard_map/ppermute | solution.py:662
  229.4 48.2 %collective-permute-start.12 = (bf16[1024,1024]{1,0:T(8,128)(2,1)}, bf16[1024,1024]{1,0:T(8,128)(2,1)S(1)}, u32[]{:S(2)}, u32[]{:S(2)}) collective-permute-start(bf16[1024,1024]{1,0:T(8,128)(2,1)} %add_convert_fusion.5), channel_id=1, source_target_pairs={{0,1},{1,0},{2,3},{3,2},{4,5},{5,4},{6,7},{7,6},{8,9},{9,8},{10,11... | collective-permute-start | bytes 6291464 | tf_op jit(solution)/shard_map/ppermute | solution.py:665
  278.8 26.1 %collective-permute-start.14 = (bf16[512,1024]{1,0:T(8,128)(2,1)S(1)}, bf16[512,1024]{1,0:T(8,128)(2,1)S(1)}, u32[]{:S(2)}, u32[]{:S(2)}) collective-permute-start(bf16[512,1024]{1,0:T(8,128)(2,1)S(1)} %bitcast.291), channel_id=1, source_target_pairs={{0,4},{2,6},{4,0},{6,2},{8,12},{10,14},{12,8},{14,10},{16,20},{18,... | collective-permute-start | bytes 3145736 | tf_op jit(solution)/shard_map/ppermute | solution.py:662
  280.2 47.2 %collective-permute-start.17 = (bf16[1024,1024]{1,0:T(8,128)(2,1)}, bf16[1024,1024]{1,0:T(8,128)(2,1)S(1)}, u32[]{:S(2)}, u32[]{:S(2)}) collective-permute-start(bf16[1024,1024]{1,0:T(8,128)(2,1)} %add_convert_fusion.3), channel_id=1, source_target_pairs={{0,1},{1,0},{2,3},{3,2},{4,5},{5,4},{6,7},{7,6},{8,9},{9,8},{10,11... | collective-permute-start | bytes 6291464 | tf_op jit(solution)/shard_map/ppermute | solution.py:665
  308.5 22.1 %collective-permute-start.16 = (bf16[256,1024]{1,0:T(8,128)(2,1)S(1)}, bf16[256,1024]{1,0:T(8,128)(2,1)S(1)}, u32[]{:S(2)}, u32[]{:S(2)}) collective-permute-start(bf16[256,1024]{1,0:T(8,128)(2,1)S(1)} %convolution_convert_fusion.10), channel_id=1, source_target_pairs={{0,2},{2,0},{4,6},{6,4},{8,10},{10,8},{12,14},{14,12},{16,18},{18,... | collective-permute-start | bytes 1572872 | tf_op jit(solution)/shard_map/ppermute | solution.py:662
  309.1 24.8 %collective-permute-start.18 = (bf16[256,1024]{1,0:T(8,128)(2,1)S(1)}, bf16[256,1024]{1,0:T(8,128)(2,1)S(1)}, u32[]{:S(2)}, u32[]{:S(2)}) collective-permute-start(bf16[256,1024]{1,0:T(8,128)(2,1)S(1)} %bitcast.307), channel_id=1, source_target_pairs={{0,8},{2,10},{4,12},{6,14},{8,0},{10,2},{12,4},{14,6},{16,24},{18,... | collective-permute-start | bytes 1572872 | tf_op jit(solution)/shard_map/ppermute | solution.py:662
  327.4 91.6 %collective-permute-start.25 = (bf16[640,1024]{1,0:T(8,128)(2,1)}, bf16[640,1024]{1,0:T(8,128)(2,1)}, u32[]{:S(2)}, u32[]{:S(2)}) collective-permute-start(bf16[640,1024]{1,0:T(8,128)(2,1)} %get-tuple-element.255), channel_id=1, source_target_pairs={{0,1},{1,0},{2,3},{3,2},{4,5},{5,4},{6,7},{7,6},{8,9},{9,8},{10,11... | collective-permute-start | bytes 3932168 | tf_op jit(solution)/shard_map/ppermute | solution.py:665
  332.7 26.5 %collective-permute-start.19 = (bf16[512,1024]{1,0:T(8,128)(2,1)S(1)}, bf16[512,1024]{1,0:T(8,128)(2,1)}, u32[]{:S(2)}, u32[]{:S(2)}) collective-permute-start(bf16[512,1024]{1,0:T(8,128)(2,1)S(1)} %bitcast.290), channel_id=1, source_target_pairs={{0,4},{2,6},{4,0},{6,2},{8,12},{10,14},{12,8},{14,10},{16,20},{18,... | collective-permute-start | bytes 3145736 | tf_op jit(solution)/shard_map/ppermute | solution.py:662
  334.2 23.3 %collective-permute-start.33 = (bf16[128,1024]{1,0:T(8,128)(2,1)S(1)}, bf16[128,1024]{1,0:T(8,128)(2,1)}, u32[]{:S(2)}, u32[]{:S(2)}) collective-permute-start(bf16[128,1024]{1,0:T(8,128)(2,1)S(1)} %dynamic-slice_bitcast_fusion.6), channel_id=1, source_target_pairs={{0,16},{2,18},{4,20},{6,22},{8,24},{10,26},{12,28},{14,30},{16,0},... | collective-permute-start | bytes 786440 | tf_op jit(solution)/shard_map/ppermute | solution.py:662
  359.1 164.4 %all-gather.11.cloned.1.call-start = ((), (), s32[]{:S(2)}) async-start(), calls=%async_computation.3 | async-start | bytes 5570560 | tf_op jit(solution)/shard_map/all_gather | solution.py:905
  364.2 24.7 %collective-permute-start.21 = (bf16[1024,768]{1,0:T(8,128)(2,1)S(1)}, bf16[1024,768]{1,0:T(8,128)(2,1)S(1)}, u32[]{:S(2)}, u32[]{:S(2)}) collective-permute-start(bf16[1024,768]{1,0:T(8,128)(2,1)S(1)} %convolution_convert_fusion.9), channel_id=1, source_target_pairs={{0,2},{2,0},{4,6},{6,4},{8,10},{10,8},{12,14},{14,12},{16,18},{18,... | collective-permute-start | bytes 4718600 | tf_op jit(solution)/shard_map/ppermute | solution.py:662
  364.3 29.9 %collective-permute-start.22 = (bf16[256,1024]{1,0:T(8,128)(2,1)S(1)}, bf16[256,1024]{1,0:T(8,128)(2,1)S(1)}, u32[]{:S(2)}, u32[]{:S(2)}) collective-permute-start(bf16[256,1024]{1,0:T(8,128)(2,1)S(1)} %bitcast.308), channel_id=1, source_target_pairs={{0,8},{2,10},{4,12},{6,14},{8,0},{10,2},{12,4},{14,6},{16,24},{18,... | collective-permute-start | bytes 1572872 | tf_op jit(solution)/shard_map/ppermute | solution.py:662
  369.5 24.9 %collective-permute-start.23 = (bf16[128,1024]{1,0:T(8,128)(2,1)S(1)}, bf16[128,1024]{1,0:T(8,128)(2,1)S(1)}, u32[]{:S(2)}, u32[]{:S(2)}) collective-permute-start(bf16[128,1024]{1,0:T(8,128)(2,1)S(1)} %bitcast.317), channel_id=1, source_target_pairs={{0,4},{2,6},{4,0},{6,2},{8,12},{10,14},{12,8},{14,10},{16,20},{18,... | collective-permute-start | bytes 786440 | tf_op jit(solution)/shard_map/ppermute | solution.py:662
  395.8 51.5 %collective-permute-start.37 = (bf16[128,1024]{1,0:T(8,128)(2,1)}, bf16[128,1024]{1,0:T(8,128)(2,1)}, u32[]{:S(2)}, u32[]{:S(2)}) collective-permute-start(bf16[128,1024]{1,0:T(8,128)(2,1)} %dynamic-slice_bitcast_fusion.5), channel_id=1, source_target_pairs={{0,16},{2,18},{4,20},{6,22},{8,24},{10,26},{12,28},{14,30},{16,0},... | collective-permute-start | bytes 786440 | tf_op jit(solution)/shard_map/ppermute | solution.py:662
  400.1 49.1 %collective-permute-start.27 = (bf16[1024,768]{1,0:T(8,128)(2,1)}, bf16[1024,768]{1,0:T(8,128)(2,1)}, u32[]{:S(2)}, u32[]{:S(2)}) collective-permute-start(bf16[1024,768]{1,0:T(8,128)(2,1)} %add_convert_fusion.7), channel_id=1, source_target_pairs={{0,1},{1,0},{2,3},{3,2},{4,5},{5,4},{6,7},{7,6},{8,9},{9,8},{10,11... | collective-permute-start | bytes 4718600 | tf_op jit(solution)/shard_map/ppermute | solution.py:665
  422.1 25.2 %collective-permute-start.38 = (bf16[32,1024]{1,0:T(8,128)(2,1)S(1)}, bf16[32,1024]{1,0:T(8,128)(2,1)S(1)}, u32[]{:S(2)}, u32[]{:S(2)}) collective-permute-start(bf16[32,1024]{1,0:T(8,128)(2,1)S(1)} %dynamic-slice_bitcast_fusion.11), channel_id=1, source_target_pairs={{0,16},{2,18},{4,20},{6,22},{8,24},{10,26},{12,28},{14,30},{16,0},... | collective-permute-start | bytes 196616 | tf_op jit(solution)/shard_map/ppermute | solution.py:662
  426.1 23.1 %collective-permute-start.26 = (bf16[1024,768]{1,0:T(8,128)(2,1)}, bf16[1024,768]{1,0:T(8,128)(2,1)}, u32[]{:S(2)}, u32[]{:S(2)}) collective-permute-start(bf16[1024,768]{1,0:T(8,128)(2,1)} %convolution_convert_fusion.8), channel_id=1, source_target_pairs={{0,2},{2,0},{4,6},{6,4},{8,10},{10,8},{12,14},{14,12},{16,18},{18,... | collective-permute-start | bytes 4718600 | tf_op jit(solution)/shard_map/ppermute | solution.py:662
  482.3 59.4 %collective-permute-start.44 = (bf16[640,1024]{1,0:T(8,128)(2,1)S(1)}, bf16[640,1024]{1,0:T(8,128)(2,1)S(1)}, u32[]{:S(2)}, u32[]{:S(2)}) collective-permute-start(bf16[640,1024]{1,0:T(8,128)(2,1)S(1)} %get-tuple-element.267), channel_id=1, source_target_pairs={{0,1},{1,0},{2,3},{3,2},{4,5},{5,4},{6,7},{7,6},{8,9},{9,8},{10,11... | collective-permute-start | bytes 3932168 | tf_op jit(solution)/shard_map/ppermute | solution.py:665
  501.2 22.1 %collective-permute-start.34 = (f32[9728]{0:T(1024)S(1)}, f32[9728]{0:T(1024)S(1)}, u32[]{:S(2)}, u32[]{:S(2)}) collective-permute-start(f32[9728]{0:T(1024)S(1)} %pad_maximum_fusion.6), channel_id=1, source_target_pairs={{0,16},{2,18},{4,20},{6,22},{8,24},{10,26},{12,28},{14,30},{16,0},... | collective-permute-start | bytes 116744 | tf_op jit(solution)/shard_map/ppermute | solution.py:662
  (129 other events, 1333.3 us)
Sparse Core Ops, SparseCore 0:
  64.2 59.6 all-gather.4
  126.1 49.0 all-gather.6
  359.3 62.8 all-gather.8
  449.3 74.1 all-gather.10

commit v5 on v4

--- a/solution.py
+++ b/solution.py
@@ -156,6 +156,38 @@
         cost_estimate=takes(5),
         name="enter",
     )(side, tokens, arrived, gain[None], shift[None])
+
+
+def collect_kernel(side_ref, mine_ref, arrived_ref, out_ref):
+    @pl.when(pl.program_id(0) == 0)
+    def _():
+        out_ref[...] = mine_ref[0]
+
+    @pl.when(pl.program_id(0) == 1)
+    def _():
+        out_ref[...] = arrived_ref[...]
+
+
+def collect(side, array, arrived):
+    _, half, depth = array.shape
+    return pl.pallas_call(
+        collect_kernel,
+        grid_spec=pltpu.PrefetchScalarGridSpec(
+            num_scalar_prefetch=1,
+            grid=(2,),
+            in_specs=[
+                pl.BlockSpec((1, half, depth), lambda i, side: (side[0], 0, 0)),
+                pl.BlockSpec((half, depth), lambda i, side: (0, 0)),
+            ],
+            out_specs=pl.BlockSpec(
+                (half, depth), lambda i, side: (jnp.where(i == 0, side[0], 1 - side[0]), 0)
+            ),
+        ),
+        out_shape=jax.ShapeDtypeStruct((2 * half, depth), array.dtype),
+        compiler_params=params(),
+        cost_estimate=takes(2),
+        name="collect",
+    )(side, array, arrived)
 
 
 def project_kernel(chunk, count, x_ref, *refs):
@@ -523,14 +555,14 @@
     sums_ref[3] += fold(above)
 
 
-def back_norm(at, rows, lefts, rights, base, above, gain, block=320):
-    depth = base.shape[1]
-    row = lambda array: pl.BlockSpec((block, array.shape[1]), lambda i, at: (at[0] + i, 0))
+def back_norm(at, lefts, rights, base, above, gain, block=320):
+    rows, depth = base.shape
+    row = lambda array: pl.BlockSpec((block, array.shape[1]), lambda i, at: (at[i], 0))
     return pl.pallas_call(
         functools.partial(back_kernel, len(lefts)),
         grid_spec=pltpu.PrefetchScalarGridSpec(
             num_scalar_prefetch=1,
-            grid=(rows // block,),
+            grid=(at.size,),
             in_specs=[whole(w) for w in rights]
             + [row(a) for a in lefts]
             + [row(base), row(above), whole(gain[None])],
@@ -544,7 +576,7 @@
             jax.ShapeDtypeStruct((4, 8, depth), jnp.float32),
         ],
         compiler_params=params(),
-        cost_estimate=takes(0.1 if rows == base.shape[0] else 10),
+        cost_estimate=takes(0.1 if base.dtype == jnp.float32 else 20),
         name="back_norm",
     )(at, *rights, *lefts, base, above, gain[None])
 
@@ -692,8 +724,22 @@
         return [half_of(own, bit(0), axis), half_of(own, 1 - bit(0), axis)]
 
     tokens, cotangent = tokens[:, 0], cotangent[:, 0]
-    tokens_far = cross(lax.dynamic_index_in_dim(tokens, 1 - side, 0, False))
     heads_three = heads_weight.transpose(1, 0, 2)
+    near = rest[:2]
+    piece_rows = heads_three.shape[1] >> len(near)
+    piece_width = heads_three.shape[2] // 2
+    piece_at = ((location >> 1) & ((1 << len(near)) - 1)) * piece_rows
+    heads_piece = jnp.concatenate(
+        [
+            lax.dynamic_slice(
+                heads_three, (n, piece_at, bit(0) * piece_width), (1, piece_rows, piece_width)
+            )[0]
+            for n in range(3)
+        ],
+        1,
+    )
+    heads_cross = cross(heads_piece)
+    tokens_far = cross(lax.dynamic_index_in_dim(tie(tokens, heads_piece), 1 - side, 0, False))
     heads_own = [
         jnp.concatenate([half_of(heads_three[n], flag, 1) for n in range(3)], 1)
         for flag in (bit(0), 1 - bit(0))
@@ -706,10 +752,6 @@
         pack(half_of(heads_bias, flag, 1), half_of(expand_bias, flag)) for flag in (bit(0), 1 - bit(0))
     ]
     three = heads_bias.size // 2
-    near = rest[:2]
-    heads_piece = heads_own[KEEP]
-    for n, level in enumerate(near):
-        heads_piece = split(heads_piece, level, near[n:])[0]
     up_piece = jnp.concatenate([chunk_of(expand_own[KEEP]), chunk_of(merge_own[KEEP])])
     down_piece = chunk_of(reduce_own[KEEP])
 
@@ -720,10 +762,19 @@
     lanes = segment_lanes(first_key, past_key, segment, starts)
     first_key, past_key = first_key[None], past_key[None]
 
-    did(heads_piece, up_piece, down_piece, *heads_own, *merge_own, *expand_own, *reduce_own, *tables, *lanes)
-    heads_piece = cross(tie(heads_piece, tokens_far))
-    up_piece = cross(tie(up_piece, tokens_far))
-    bias_both = cross(tie(jnp.concatenate(bias_own), tokens_far))
+    bias_pieces = jnp.concatenate(bias_own)
+    did(*heads_own, *merge_own)
+    heads_piece = did(after(heads_cross))
+    if len(near) > 1:
+        heads_next = swap(heads_piece, near[1])
+        expand_own = quarters_of(after(expand_weight), 1)
+        up_piece = jnp.concatenate([chunk_of(expand_own[KEEP]), chunk_of(merge_own[KEEP])])
+        did(*expand_own, up_piece)
+        heads_piece = did(join(after(heads_piece), heads_next, near[1], near[1:]))
+    heads_next = swap(heads_piece, near[0])
+    up_piece = cross(tie(up_piece, heads_piece))
+    bias_both = cross(tie(bias_pieces, heads_piece))
+    did(heads_piece, down_piece, *heads_own, *merge_own, *expand_own, *reduce_own, *tables, *lanes)
     bias_far = [bias_both[: bias_both.size // 2], bias_both[bias_both.size // 2 :]]
     stream, first_out = did(*enter(sides, after(tokens), tokens_far, first_gain, first_shift))
     heads, seen = {}, {}
@@ -753,40 +804,28 @@
         return quarters
 
     look(OWN)
-    heads_piece = did(after(heads_piece))
-    if len(near) > 1:
-        heads_next = swap(heads_piece, near[1])
     up_sizes = (expand_own[0].shape[0] // chunks, merge_own[0].shape[0] // chunks)
     up_gathered = gathered(after(up_piece), *up_sizes)
     down_piece = cross(after(down_piece))
-    if len(near) > 1:
-        heads_piece = did(join(after(heads_piece), heads_next, near[1], near[1:]))
-    heads_next = swap(heads_piece, near[0])
-    attention(OWN)
     heads_piece = did(join(after(heads_piece), heads_next, near[0], near))
     heads_all[FAR] = [heads_piece, swap(heads_piece, 0)]
+    attention(OWN)
     cotangent_far = cross(after(lax.dynamic_index_in_dim(cotangent, 1 - side, 0, False)))
+    look(FAR)
     (reduce_far,) = gathered(after(down_piece), down_piece.shape[0])
-    look(FAR)
     attention(FAR)
     expand_far, merge_far = ([after(q) for q in quarters] for quarters in up_gathered)
     merge_all = (merge_own, merge_far)
     expand_all = (expand_own, expand_far)
     reduce_all = (reduce_own, reduce_far)
     width = seen[OWN][0].shape[1] // 2
-    mixed = {(p, c): seen[p][0][:, c * width : (c + 1) * width] for p, c in QUARTERS}
     residual, second_out = did(
         *merge(
             [seen[OWN][0], seen[FAR][0]], [merge_all[p][c] for p in (OWN, FAR) for c in (KEEP, SEND)],
             after(stream), merge_bias, second_gain, second_shift,
         )
     )
-    cotangent_far = after(cotangent_far)
-    grad_two = jnp.where(
-        side == 0,
-        jnp.concatenate([cotangent[0], cotangent_far]),
-        jnp.concatenate([cotangent_far, cotangent[1]]),
-    )
+    grad_two = did(collect(sides, after(cotangent), cotangent_far))
 
     active, slope, grad_pre = {}, {}, {}
 
@@ -827,30 +866,19 @@
     reduce_sum = product(active[OWN, KEEP], grad_two, sent)
     back_active(FAR, KEEP)
     sent = swap(product(second_out, grad_pre[FAR, SEND]), 0)
-    layer_send, layer_keep = did(
-        *reduce_rows(
-            sides, [active[q] for q in QUARTERS], [reduce_all[p][c] for p, c in QUARTERS],
-            after(residual), reduce_bias,
-        )
-    )
     back_active(OWN, SEND)
     expand_far_sum = product(second_out, grad_pre[FAR, KEEP], sent)
     back_active(OWN, KEEP)
     sent = swap(product(second_out, grad_pre[OWN, SEND]), 0)
-    reduce_sum = summed(reduce_sum, reduce_cross)
-    expand_cross = cross(tie(expand_far_sum, reduce_cross))
-    reduce_keep, reduce_next = scattered(reduce_sum, rest[0])
     expand_sum = product(second_out, grad_pre[OWN, KEEP], sent)
-    zero = jnp.zeros((1,), jnp.int32)
+    expand_cross = cross(expand_far_sum)
+    blocks = jnp.arange(length // 320, dtype=jnp.int32)
     grad_one, second_sums = did(
         *back_norm(
-            zero, length, [grad_pre[q] for q in QUARTERS], [expand_all[p][c] for p, c in QUARTERS],
+            blocks, [grad_pre[q] for q in QUARTERS], [expand_all[p][c] for p, c in QUARTERS],
             after(residual), grad_two, second_gain,
         )
     )
-    reduce_sum = summed(reduce_keep, reduce_next)
-    reduce_keep, reduce_next = scattered(reduce_sum, rest[1])
-
     grad_mixed, grad_heads, head_sums = {}, {}, {}
 
     def back_mixed(p, c):
@@ -863,42 +891,44 @@
         )
         head_sums[q] = jnp.sum(sums, 0)
 
-    sent_far = swap(product(mixed[FAR, SEND], grad_one), 0)
-    sent_own = swap(product(mixed[OWN, SEND], grad_one), 0)
+    merge_far_sum = product(seen[FAR][0], grad_one)
+    sent_far = swap(merge_far_sum[width:], 0)
+    merge_sum = product(seen[OWN][0], grad_one)
+    sent_own = swap(merge_sum[width:], 0)
     for p, c in QUARTERS:
         back_mixed(p, c)
-    merge_far_sum = product(mixed[FAR, KEEP], grad_one, sent_far)
-    merge_sum = product(mixed[OWN, KEEP], grad_one, sent_own)
+    merge_far_sum = summed(merge_far_sum[:width], sent_far)
+    merge_sum = summed(merge_sum[:width], sent_own)
+    merge_cross = cross(tie(merge_far_sum, reduce_cross))
+    reduce_sum = summed(reduce_sum, reduce_cross)
+    reduce_keep, reduce_next = scattered(reduce_sum, rest[0])
+    back_attention((FAR, SEND))
+    reduce_sum = summed(reduce_keep, reduce_next)
+    reduce_keep, reduce_next = scattered(reduce_sum, rest[1])
+    sent = swap(product(first_out, grad_heads[FAR, SEND]), 0)
     expand_sum = summed(expand_sum, expand_cross)
-    merge_cross = cross(tie(merge_far_sum, expand_cross))
-    layer_far = cross(tie(layer_send, expand_cross))
     expand_keep, expand_next = scattered(expand_sum, rest[0])
+    merge_sum = summed(merge_sum, merge_cross)
+    merge_keep, merge_next = scattered(merge_sum, rest[0])
     reduce_sum = summed(reduce_keep, reduce_next)
     for level in rest[2:]:
         reduce_keep, reduce_next = scattered(reduce_sum, level)
         reduce_sum = low(wide(reduce_keep) + wide(reduce_next))
-    back_attention((FAR, SEND))
+    back_attention((FAR, KEEP))
     reduce_total = lax.all_gather(after(reduce_sum), "dp", axis=0, tiled=True)
-    expand_sum = summed(expand_keep, expand_next)
-    expand_keep, expand_next = scattered(expand_sum, rest[1])
-    sent = swap(product(first_out, grad_heads[FAR, SEND]), 0)
-    merge_sum = summed(merge_sum, merge_cross)
-    merge_keep, merge_next = scattered(merge_sum, rest[0])
-    back_attention((FAR, KEEP))
     heads_far_sum = product(first_out, grad_heads[FAR, KEEP], sent)
     heads_cross = cross(heads_far_sum)
     expand_sum = summed(expand_keep, expand_next)
     merge_sum = summed(merge_keep, merge_next)
+    expand_keep, expand_next = scattered(expand_sum, rest[1])
     merge_keep, merge_next = scattered(merge_sum, rest[1])
+    back_attention((OWN, SEND))
+    expand_sum = summed(expand_keep, expand_next)
+    merge_sum = summed(merge_keep, merge_next)
     for level in rest[2:]:
         expand_keep, expand_next = scattered(expand_sum, level)
+        merge_keep, merge_next = scattered(merge_sum, level)
         expand_sum = low(wide(expand_keep) + wide(expand_next))
-    back_attention((OWN, SEND))
-    merge_sum = summed(merge_keep, merge_next)
-    layer_out = rows_out(after(layer_keep), layer_far, jnp.bfloat16)
-    merge_sum, layer_out = lax.optimization_barrier((merge_sum, layer_out))
-    for level in rest[2:]:
-        merge_keep, merge_next = scattered(merge_sum, level)
         merge_sum = low(wide(merge_keep) + wide(merge_next))
     sent = swap(product(first_out, grad_heads[OWN, SEND]), 0)
     back_attention((OWN, KEEP))
@@ -926,19 +956,14 @@
     pairs = both_scattered(0)
     lefts = [grad_heads[q] for q in QUARTERS]
     rights = [heads_all[p][c] for p, c in QUARTERS]
-    per_half = length // 2 // 320
-    tokens_send, sums_a = did(
-        *back_norm(
-            (1 - sides) * per_half, length // 2, lefts, rights, stream, grad_one, after(first_gain)
-        )
-    )
-    tokens_cross = cross(tokens_send)
+    half = length // 2
+    blocks = (blocks + (1 - sides) * (half // 320)) % (length // 320)
+    tokens_rows, first_sums = did(
+        *back_norm(blocks, lefts, rights, stream, grad_one, after(first_gain))
+    )
+    tokens_cross, tokens_keep = cross(tokens_rows[:half]), tokens_rows[half:]
     heads_sums = both_summed(pairs)
     pairs = both_scattered(1)
-    tokens_keep, sums_b = did(
-        *back_norm(sides * per_half, length // 2, lefts, rights, stream, grad_one, after(first_gain))
-    )
-    first_sums = sums_a + sums_b
 
     small = {q: jnp.concatenate([head_sums[q], column_sums(grad_pre[q])]) for q in QUARTERS}
     both = jnp.concatenate(
@@ -952,38 +977,48 @@
     far_send, own_send, both = did(*(after(v) for v in (small[FAR, SEND], small[OWN, SEND], both)))
     arrived = swap(jnp.concatenate([far_send, own_send, both]), 0)
     size = own_send.size
+    reduce_out = in_rows(after(reduce_total))
+    arrived, reduce_out = lax.optimization_barrier((arrived, reduce_out))
+    did(arrived)
     heads_sums = both_summed(pairs)
     mine = jnp.concatenate([small[FAR, KEEP] + arrived[:size], small[OWN, KEEP], both])
     mine = did(
         jnp.concatenate([mine[:size], mine[size:] + after(arrived)[size:]])
     )
-    for n in range(2, len(rest)):
+    for n in range(2, len(rest) - 1):
         pairs = both_scattered(n)
         small_next = swap(mine, rest[n])
-        if n == 2:
-            reduce_out = in_rows(after(reduce_total))
-            mine, reduce_out = lax.optimization_barrier((mine, reduce_out))
-            did(mine)
         heads_sums = both_summed(pairs)
         mine = did(mine + after(small_next))
-    for n in range(len(rest))[::-1]:
+    arrived = [swap(total, rest[-1]) for total in heads_sums]
+    small_next = swap(mine, rest[-1])
+    layer_send, layer_keep = did(
+        *reduce_rows(
+            sides, [active[q] for q in QUARTERS], [reduce_all[p][c] for p, c in QUARTERS],
+            after(residual), reduce_bias,
+        )
+    )
+    heads_sums = both_summed(zip(heads_sums, arrived))
+    mine = did(mine + after(small_next))
+    layer_far = cross(tie(layer_send, tokens_cross))
+    for n in range(len(rest) - 1)[::-1]:
         arrived = [swap(total, order[n]) for total, order in zip(heads_sums, orders)]
         small_next = swap(mine, rest[n]) if n < 2 else None
-        if n == len(rest) - 1:
+        if n == len(rest) - 2:
+            tokens_out = rows_out(after(tokens_keep), tokens_cross, jnp.float32)
+            mine, tokens_out = lax.optimization_barrier((mine, tokens_out))
+            did(mine)
+        if n == 0:
             expand_out = wide(
                 jnp.concatenate(
                     [
-                        after(expand_total)[:, n, :rows].reshape(-1, expand_total.shape[3])
-                        for n in range(2)
+                        after(expand_total)[:, half, :rows].reshape(-1, expand_total.shape[3])
+                        for half in range(2)
                     ],
                     1,
                 )
             )
             mine, expand_out = lax.optimization_barrier((mine, expand_out))
-            did(mine)
-        if n == 0:
-            tokens_out = rows_out(after(tokens_keep), tokens_cross, jnp.float32)
-            mine, tokens_out = lax.optimization_barrier((mine, tokens_out))
             did(mine)
         heads_sums = [
             did(join(after(total), other, order[n], order[n:]))
@@ -991,6 +1026,7 @@
         ]
         if n < 2:
             mine = did(mine + after(small_next))
+    layer_out = rows_out(layer_keep, layer_far, jnp.bfloat16)
     heads_sum = jnp.concatenate(heads_sums, 1)
     heads_next = swap(heads_sum, 0)
     arrived = cross(jnp.concatenate([mine[:size], mine[2 * size :]]))

time: 577 us -> 544 us (0.943)
  waiting for transfers between devices: 86.8 us -> 46.8 us
  other arithmetic: 40 us -> 53.5 us
  local copies, waits for them, and re-layouts: 57.1 us -> 49.5 us
    ppermute x38 -> x36, waiting for transfers between devices: 47.5 us -> 24.1 us  [swap(): lax.ppermute(array, 'dp', [(i, i ^ 1 << level) for i in range(spread)])]
    ppermute x13, waiting for transfers between devices: 39 us -> 21.4 us  [cross(): return lax.ppermute(array, 'mp', [(0, 1), (1, 0)])]
    unnamed x203 -> x191, local copies, waits for them, and re-layouts: 15.2 us -> 5.76 us
    convert_element_type x21 -> x23, other arithmetic: 13.8 us -> 19.7 us  [low(): return array.astype(jnp.bfloat16)]
    dot_general x16 -> x14, matrix products: 52.9 us -> 57.6 us  [dot_tn(): lax.dot_general(left, right, (((0,), (0,)), ((), ())), preferred_element_...]
    ppermute x38 -> x36, starting transfers between devices: 32.8 us -> 28.6 us  [swap(): lax.ppermute(array, 'dp', [(i, i ^ 1 << level) for i in range(spread)])]
    pallas_call x3 -> x2, Pallas kernels: 41.4 us -> 38 us  [back_norm(): pl.pallas_call(functools.partial(back_kernel, len(lefts)), grid_spec=pltp...]
  transfers between devices with their start and end apart: 55 -> 53, of which waited for: 18 -> 18; matrix products, arithmetic and copies ran while one was open for 25% -> 29% of each run, Pallas kernels for 41% -> 44%
where the time goes in v5:
time: 544 us; the launch traced here: 534 us
  Pallas kernels  241 us (44%)
  matrix products  82.4 us (15%)
  other arithmetic  53.5 us (10%)
  local copies, waits for them, and re-layouts  49.5 us (9%)
  waiting for transfers between devices  46.8 us (9%)
  starting transfers between devices  44.5 us (8%)
  between operations  16.9 us (3%)
    pallas_call x4, Pallas kernels, attend_back(): pl.pallas_call(attend_back_kernel, grid=(pairs,), in_specs=parts + [pl.Bl...  69.6 us
    dot_general x14, matrix products, dot_tn(): lax.dot_general(left, right, (((0,), (0,)), ((), ())), preferred_element_...  57.6 us
    pallas_call x2, Pallas kernels, back_norm(): pl.pallas_call(functools.partial(back_kernel, len(lefts)), grid_spec=pltp...  38 us
    pallas_call x2, Pallas kernels, attend(): pl.pallas_call(attend_kernel, grid=(pairs,), in_specs=parts + [whole(arra...  37.7 us
    pallas_call x4, Pallas kernels, expand(): pl.pallas_call(functools.partial(expand_kernel, chunk), grid=(width // bl...  35 us
    ppermute x36, starting transfers between devices, swap(): lax.ppermute(array, 'dp', [(i, i ^ 1 << level) for i in range(spread)])  28.6 us
    ppermute x36, waiting for transfers between devices, swap(): lax.ppermute(array, 'dp', [(i, i ^ 1 << level) for i in range(spread)])  24.1 us
    ppermute x13, waiting for transfers between devices, cross(): return lax.ppermute(array, 'mp', [(0, 1), (1, 0)])  21.4 us
  transfers between devices with their start and end apart: 53, of which 18 were waited for; matrix products, arithmetic and copies ran while one was open for 29% of the time, Pallas kernels for 44%

profile of v5, /device:TPU:0, one launch (start us, length us, event | category | flops | bytes accessed | tf_op | source)
XLA Modules:
  0.0 534.4 jit_solution(12220742268200557957)
XLA Ops:
  41.5 5.2 constant_dynamic-slice_fusion.29
  61.1 8.9 %project.2.q_ref.k_ref.v_ref = bf16[1280,1536]{1,0:T(8,128)(2,1)} custom-call(bf16[1280,1024]{1,0:T(8,128)(2,1)} %get-tuple-element.250.x_ref, bf16[1024,768]{1,0:T(8,128)(2,1)S(1)} %copy-done.7, bf16[1024,768]{1,0:T(8,128)(2,1)} %pad_maximum_fusion.1.refs_1_.refs_2_, f32[1,768]{1,0:T(1,128)S(1)} %bitcast.219, f32[1,768]{1,0:T(1,128)S(1)} %bitcast.220, ...), custom_call_target="tpu_custom_call" | custom-call | flops 35999997952 | bytes 36000000 | tf_op jit(solution)/shard_map/project/pallas_call | solution.py:213
  76.4 18.9 %attend.2 = (bf16[1280,512]{1,0:T(8,128)(2,1)S(1)}, f32[1280,512]{1,0:T(8,128)}, bf16[8,592,512]{2,1,0:T(8,128)(2,1)}, bf16[8,1280,768]{2,1,0:T(8,128)(2,1)}) custom-call(bf16[1280,1536]{1,0:T(8,128)(2,1)} %project.2.q_ref.k_ref.v_ref, bf16[1280,1536]{1,0:T(8,128)(2,1)} %project.2.q_ref.k_ref.v_ref, bf16[1280,1536]{1,0:T(8,128)(2,1)} %project.2.q_ref.k_ref.v_ref, ...), custom_call_target="tpu_custom_call" | custom-call | flops 80000000000 | bytes 80000000 | tf_op jit(solution)/shard_map/attend/pallas_call | solution.py:327
  97.0 8.4 %project.3.q_ref.k_ref.v_ref = bf16[1280,1536]{1,0:T(8,128)(2,1)} custom-call(bf16[1280,1024]{1,0:T(8,128)(2,1)} %get-tuple-element.250.x_ref, bf16[1024,768]{1,0:T(8,128)(2,1)S(1)} %bitcast.206, bf16[1024,768]{1,0:T(8,128)(2,1)} %copy-done.36, f32[1,768]{1,0:T(1,128)S(1)} %broadcast_in_dim.156.refs_2_, f32[1,768]{1,0:T(1,128)S(1)} %broadcast_in_dim.157.refs_3_, ...), custom_call_target="tpu_custom_call" | custom-call | flops 35999997952 | bytes 36000000 | tf_op jit(solution)/shard_map/project/pallas_call | solution.py:213
  105.4 18.8 %attend.3 = (bf16[1280,512]{1,0:T(8,128)(2,1)S(1)}, f32[1280,512]{1,0:T(8,128)}, bf16[8,592,512]{2,1,0:T(8,128)(2,1)}, bf16[8,1280,768]{2,1,0:T(8,128)(2,1)}) custom-call(bf16[1280,1536]{1,0:T(8,128)(2,1)} %project.3.q_ref.k_ref.v_ref, bf16[1280,1536]{1,0:T(8,128)(2,1)} %project.3.q_ref.k_ref.v_ref, bf16[1280,1536]{1,0:T(8,128)(2,1)} %project.3.q_ref.k_ref.v_ref, ...), custom_call_target="tpu_custom_call" | custom-call | flops 80000000000 | bytes 80000000 | tf_op jit(solution)/shard_map/attend/pallas_call | solution.py:327
  128.1 7.8 %merge.1 = (f32[1280,1024]{1,0:T(8,128)}, bf16[1280,1024]{1,0:T(8,128)(2,1)}) custom-call(bf16[256,1024]{1,0:T(8,128)(2,1)S(1)} %copy-done.20, bf16[256,1024]{1,0:T(8,128)(2,1)S(1)} %copy-done.22, bf16[256,1024]{1,0:T(8,128)(2,1)S(1)} %bitcast.208, bf16[256,1024]{1,0:T(8,128)(2,1)S(1)} %bitcast.210, bf16[1280,512]{1,0:T(8,128)(2,1)S(1)} %get-tuple-element.214.refs_4_.o_ref, ...), custom_call_target="tpu_custom_call" | custom-call | flops 32000000000 | bytes 32000000 | tf_op jit(solution)/shard_map/merge/pallas_call | solution.py:447
  142.8 9.2 %expand.4 = (bf16[1280,1024]{1,0:T(8,128)(2,1)}, bf16[1280,1024]{1,0:T(8,128)(2,1)}) custom-call(bf16[1280,1024]{1,0:T(8,128)(2,1)} %get-tuple-element.209.x_ref, bf16[1024,1024]{1,0:T(8,128)(2,1)S(1)} %bitcast.203, f32[1,1024]{1,0:T(1,128)S(1)} %bitcast.218), custom_call_target="tpu_custom_call" | custom-call | flops 33999998976 | bytes 34000000 | tf_op jit(solution)/shard_map/expand/pallas_call | solution.py:478
  152.0 8.5 %expand.5 = (bf16[1280,1024]{1,0:T(8,128)(2,1)}, bf16[1280,1024]{1,0:T(8,128)(2,1)}) custom-call(bf16[1280,1024]{1,0:T(8,128)(2,1)} %get-tuple-element.209.x_ref, bf16[1024,1024]{1,0:T(8,128)(2,1)S(1)} %bitcast.201, f32[1,1024]{1,0:T(1,128)S(1)} %bitcast.217), custom_call_target="tpu_custom_call" | custom-call | flops 33999998976 | bytes 34000000 | tf_op jit(solution)/shard_map/expand/pallas_call | solution.py:478
  164.9 8.7 %expand.6 = (bf16[1280,1024]{1,0:T(8,128)(2,1)}, bf16[1280,1024]{1,0:T(8,128)(2,1)}) custom-call(bf16[1280,1024]{1,0:T(8,128)(2,1)} %get-tuple-element.209.x_ref, bf16[1024,1024]{1,0:T(8,128)(2,1)S(1)} %copy-done.1, f32[1,1024]{1,0:T(1,128)S(1)} %bitcast.213), custom_call_target="tpu_custom_call" | custom-call | flops 33999998976 | bytes 34000000 | tf_op jit(solution)/shard_map/expand/pallas_call | solution.py:478
  177.8 8.7 %expand.7 = (bf16[1280,1024]{1,0:T(8,128)(2,1)}, bf16[1280,1024]{1,0:T(8,128)(2,1)}) custom-call(bf16[1280,1024]{1,0:T(8,128)(2,1)} %get-tuple-element.209.x_ref, bf16[1024,1024]{1,0:T(8,128)(2,1)S(1)} %get-tuple-element.425.w_ref.refs_3_, f32[1,1024]{1,0:T(1,128)S(1)} %bitcast.212), custom_call_target="tpu_custom_call" | custom-call | flops 33999998976 | bytes 34000000 | tf_op jit(solution)/shard_map/expand/pallas_call | solution.py:478
  232.4 5.7 %add_convert_fusion.2 = bf16[1024,1024]{1,0:T(8,128)(2,1)} fusion(bf16[1024,1024]{1,0:T(8,128)(2,1)} %collective-permute-done.12, bf16[1280,1024]{1,0:T(8,128)(2,1)S(1)} %copy-done.87, bf16[1280,1024]{1,0:T(8,128)(2,1)S(1)} %copy-done.51), kind=kOutput, calls=%fused_computation.8 | convolution fusion | flops 2687500288 | bytes 9437184 | tf_op jit(solution)/shard_map/dot_general | solution.py:54
  238.1 21.3 %back_norm.2 = (bf16[1280,1024]{1,0:T(8,128)(2,1)}, f32[4,8,1024]{2,1,0:T(8,128)S(1)}) custom-call(s32[4]{0:T(128)S(1)} %iota.92.at_ref, bf16[1024,1024]{1,0:T(8,128)(2,1)S(1)} %bitcast.204, bf16[1024,1024]{1,0:T(8,128)(2,1)} %bitcast.202, bf16[1024,1024]{1,0:T(8,128)(2,1)} %get-tuple-element.426.w_ref.refs_2_, bf16[1024,1024]{1,0:T(8,128)(2,1)} %copy-done, ...), custom_call_target="tpu_custom_call" | custom-call | flops 400000000 | bytes 400000 | tf_op jit(solution)/shard_map/back_norm/pallas_call | solution.py:561
  277.7 17.3 %attend_back.4 = (bf16[1280,768]{1,0:T(8,128)(2,1)}, f32[8,768]{1,0:T(8,128)}) custom-call(bf16[1280,1536]{1,0:T(8,128)(2,1)} %project.3.q_ref.k_ref.v_ref, bf16[1280,1536]{1,0:T(8,128)(2,1)} %project.3.q_ref.k_ref.v_ref, bf16[1280,1536]{1,0:T(8,128)(2,1)} %project.3.q_ref.k_ref.v_ref, bf16[1280,256]{1,0:T(8,128)(2,1)} %convolution_convert_fusion.3.g_ref, ...), custom_call_target="tpu_custom_call" | custom-call | flops 64000000000 | bytes 64000000 | tf_op jit(solution)/shard_map/attend_back/pallas_call | solution.py:405
  309.2 10.5 %collective-permute-done.17 = bf16[1024,1024]{1,0:T(8,128)(2,1)S(1)} collective-permute-done((bf16[1024,1024]{1,0:T(8,128)(2,1)}, bf16[1024,1024]{1,0:T(8,128)(2,1)S(1)}, u32[]{:S(2)}, u32[]{:S(2)}) %collective-permute-start.17) | collective-permute-done | bytes 2097184 | tf_op jit(solution)/shard_map/ppermute | solution.py:697
  321.6 8.7 %collective-permute-done.18 = bf16[256,1024]{1,0:T(8,128)(2,1)} collective-permute-done((bf16[256,1024]{1,0:T(8,128)(2,1)}, bf16[256,1024]{1,0:T(8,128)(2,1)}, u32[]{:S(2)}, u32[]{:S(2)}) %collective-permute-start.18) | collective-permute-done | bytes 524320 | tf_op jit(solution)/shard_map/ppermute | solution.py:697
  335.3 17.3 %attend_back.5 = (bf16[1280,768]{1,0:T(8,128)(2,1)}, f32[8,768]{1,0:T(8,128)}) custom-call(bf16[1280,1536]{1,0:T(8,128)(2,1)} %project.3.q_ref.k_ref.v_ref, bf16[1280,1536]{1,0:T(8,128)(2,1)} %project.3.q_ref.k_ref.v_ref, bf16[1280,1536]{1,0:T(8,128)(2,1)} %project.3.q_ref.k_ref.v_ref, bf16[1280,256]{1,0:T(8,128)(2,1)} %convolution_convert_fusion.2.g_ref, ...), custom_call_target="tpu_custom_call" | custom-call | flops 64000000000 | bytes 64000000 | tf_op jit(solution)/shard_map/attend_back/pallas_call | solution.py:405
  355.8 6.2 %add_convert_fusion.7 = bf16[1024,768]{1,0:T(8,128)(2,1)} fusion(bf16[1024,768]{1,0:T(8,128)(2,1)} %collective-permute-done.20, bf16[1280,1024]{1,0:T(8,128)(2,1)} %get-tuple-element.250.x_ref, bf16[1280,768]{1,0:T(8,128)(2,1)} %get-tuple-element.233.refs_5_), kind=kOutput, calls=%fused_computation.13 | convolution fusion | flops 2015625216 | bytes 7733248 | tf_op jit(solution)/shard_map/dot_general | solution.py:54
  367.5 17.6 %attend_back.6 = (bf16[1280,768]{1,0:T(8,128)(2,1)}, f32[8,768]{1,0:T(8,128)}) custom-call(bf16[1280,1536]{1,0:T(8,128)(2,1)} %project.2.q_ref.k_ref.v_ref, bf16[1280,1536]{1,0:T(8,128)(2,1)} %project.2.q_ref.k_ref.v_ref, bf16[1280,1536]{1,0:T(8,128)(2,1)} %project.2.q_ref.k_ref.v_ref, bf16[1280,256]{1,0:T(8,128)(2,1)} %convolution_convert_fusion.1.g_ref, ...), custom_call_target="tpu_custom_call" | custom-call | flops 64000000000 | bytes 64000000 | tf_op jit(solution)/shard_map/attend_back/pallas_call | solution.py:405
  391.4 5.0 convolution_convert_fusion.8
  396.4 17.4 %attend_back.7 = (bf16[1280,768]{1,0:T(8,128)(2,1)}, f32[8,768]{1,0:T(8,128)}) custom-call(bf16[1280,1536]{1,0:T(8,128)(2,1)} %project.2.q_ref.k_ref.v_ref, bf16[1280,1536]{1,0:T(8,128)(2,1)} %project.2.q_ref.k_ref.v_ref, bf16[1280,1536]{1,0:T(8,128)(2,1)} %project.2.q_ref.k_ref.v_ref, bf16[1280,256]{1,0:T(8,128)(2,1)} %convolution_convert_fusion.g_ref, ...), custom_call_target="tpu_custom_call" | custom-call | flops 64000000000 | bytes 64000000 | tf_op jit(solution)/shard_map/attend_back/pallas_call | solution.py:405
  427.2 16.7 %back_norm.3 = (bf16[1280,1024]{1,0:T(8,128)(2,1)}, f32[4,8,1024]{2,1,0:T(8,128)S(1)}) custom-call(s32[4]{0:T(128)S(1)} %and_select_fusion.2.at_ref, bf16[1024,768]{1,0:T(8,128)(2,1)S(1)} %copy-done.37, bf16[1024,768]{1,0:T(8,128)(2,1)S(1)} %bitcast.207, bf16[1024,768]{1,0:T(8,128)(2,1)} %pad_maximum_fusion.1.refs_1_.refs_2_, ...), custom_call_target="tpu_custom_call" | custom-call | flops 80000000000 | bytes 80000000 | tf_op jit(solution)/shard_map/back_norm/pallas_call | solution.py:561
  465.9 17.9 %reduce_rows.1 = (bf16[640,1024]{1,0:T(8,128)(2,1)}, bf16[640,1024]{1,0:T(8,128)(2,1)S(1)}) custom-call(s32[1]{0:T(128)} %bitcast.side_ref.flag_ref, bf16[1024,1024]{1,0:T(8,128)(2,1)} %bitcast.229, bf16[1024,1024]{1,0:T(8,128)(2,1)} %bitcast.227, bf16[1024,1024]{1,0:T(8,128)(2,1)} %get-tuple-element.344.refs_2_, ...), custom_call_target="tpu_custom_call" | custom-call | flops 400000000 | bytes 400000 | tf_op jit(solution)/shard_map/reduce_rows/pallas_call | solution.py:515
  483.9 5.5 %collective-permute-done.36 = bf16[256,384]{1,0:T(8,128)(2,1)S(1)} collective-permute-done((bf16[256,384]{1,0:T(8,128)(2,1)S(1)}, bf16[256,384]{1,0:T(8,128)(2,1)S(1)}, u32[]{:S(2)}, u32[]{:S(2)}) %collective-permute-start.36) | collective-permute-done | bytes 196640 | tf_op jit(solution)/shard_map/ppermute | solution.py:694
  489.4 5.8 %collective-permute-done.37 = bf16[256,384]{1,0:T(8,128)(2,1)S(1)} collective-permute-done((bf16[256,384]{1,0:T(8,128)(2,1)S(1)}, bf16[256,384]{1,0:T(8,128)(2,1)S(1)}, u32[]{:S(2)}, u32[]{:S(2)}) %collective-permute-start.37) | collective-permute-done | bytes 196640 | tf_op jit(solution)/shard_map/ppermute | solution.py:694
  (454 shorter events, 241.5 us)
Async XLA Ops:
  7.2 119.3 %all-gather.7.cloned.1.call-start = ((), (), s32[]{:S(2)}) async-start(), calls=%async_computation.1 | async-start | bytes 5570560 | tf_op jit(solution)/shard_map/all_gather | solution.py:792
  9.1 28.5 %collective-permute-start = (bf16[256,768]{1,0:T(8,128)(2,1)}, bf16[256,768]{1,0:T(8,128)(2,1)}, u32[]{:S(2)}, u32[]{:S(2)}) collective-permute-start(bf16[256,768]{1,0:T(8,128)(2,1)} %pad_maximum_fusion.3), channel_id=1, source_target_pairs={{0,1},{1,0},{2,3},{3,2},{4,5},{5,4},{6,7},{7,6},{8,9},{9,8},{10,11... | collective-permute-start | bytes 1179656 | tf_op jit(solution)/shard_map/ppermute | solution.py:697
  14.5 41.5 %collective-permute-start.2 = (bf16[640,1024]{1,0:T(8,128)(2,1)}, bf16[640,1024]{1,0:T(8,128)(2,1)}, u32[]{:S(2)}, u32[]{:S(2)}) collective-permute-start(bf16[640,1024]{1,0:T(8,128)(2,1)} %dynamic-slice_bitcast_fusion.1), channel_id=1, source_target_pairs={{0,1},{1,0},{2,3},{3,2},{4,5},{5,4},{6,7},{7,6},{8,9},{9,8},{10,11... | collective-permute-start | bytes 3932168 | tf_op jit(solution)/shard_map/ppermute | solution.py:697
  70.1 120.8 %all-gather.5.cloned.1.call-start = ((), (), s32[]{:S(2)}) async-start(), calls=%async_computation | async-start | bytes 4456448 | tf_op jit(solution)/shard_map/all_gather | solution.py:792
  70.1 55.1 %collective-permute-start.3 = (bf16[128,1024]{1,0:T(8,128)(2,1)}, bf16[128,1024]{1,0:T(8,128)(2,1)}, u32[]{:S(2)}, u32[]{:S(2)}) collective-permute-start(bf16[128,1024]{1,0:T(8,128)(2,1)} %constant_dynamic-slice_fusion.36), channel_id=1, source_target_pairs={{0,1},{1,0},{2,3},{3,2},{4,5},{5,4},{6,7},{7,6},{8,9},{9,8},{10,11... | collective-permute-start | bytes 786440 | tf_op jit(solution)/shard_map/ppermute | solution.py:697
  95.3 44.1 %collective-permute-start.8 = (bf16[640,1024]{1,0:T(8,128)(2,1)}, bf16[640,1024]{1,0:T(8,128)(2,1)}, u32[]{:S(2)}, u32[]{:S(2)}) collective-permute-start(bf16[640,1024]{1,0:T(8,128)(2,1)} %dynamic-slice_bitcast_fusion), channel_id=1, source_target_pairs={{0,1},{1,0},{2,3},{3,2},{4,5},{5,4},{6,7},{7,6},{8,9},{9,8},{10,11... | collective-permute-start | bytes 3932168 | tf_op jit(solution)/shard_map/ppermute | solution.py:697
  125.2 327.4 %all-gather.9.cloned.1.call-start = ((), (), s32[]{:S(2)}) async-start(), calls=%async_computation.2 | async-start | bytes 4456448 | tf_op jit(solution)/shard_map/all_gather | solution.py:918
  226.1 48.8 %collective-permute-start.15 = (bf16[1024,1024]{1,0:T(8,128)(2,1)}, bf16[1024,1024]{1,0:T(8,128)(2,1)S(1)}, u32[]{:S(2)}, u32[]{:S(2)}) collective-permute-start(bf16[1024,1024]{1,0:T(8,128)(2,1)} %add_convert_fusion.5), channel_id=1, source_target_pairs={{0,1},{1,0},{2,3},{3,2},{4,5},{5,4},{6,7},{7,6},{8,9},{9,8},{10,11... | collective-permute-start | bytes 6291464 | tf_op jit(solution)/shard_map/ppermute | solution.py:697
  230.2 89.6 %collective-permute-start.17 = (bf16[1024,1024]{1,0:T(8,128)(2,1)}, bf16[1024,1024]{1,0:T(8,128)(2,1)S(1)}, u32[]{:S(2)}, u32[]{:S(2)}) collective-permute-start(bf16[1024,1024]{1,0:T(8,128)(2,1)} %add_convert_fusion.3), channel_id=1, source_target_pairs={{0,1},{1,0},{2,3},{3,2},{4,5},{5,4},{6,7},{7,6},{8,9},{9,8},{10,11... | collective-permute-start | bytes 6291464 | tf_op jit(solution)/shard_map/ppermute | solution.py:697
  295.0 35.4 %collective-permute-start.18 = (bf16[256,1024]{1,0:T(8,128)(2,1)}, bf16[256,1024]{1,0:T(8,128)(2,1)}, u32[]{:S(2)}, u32[]{:S(2)}) collective-permute-start(bf16[256,1024]{1,0:T(8,128)(2,1)} %add_convert_fusion.14), channel_id=1, source_target_pairs={{0,1},{1,0},{2,3},{3,2},{4,5},{5,4},{6,7},{7,6},{8,9},{9,8},{10,11... | collective-permute-start | bytes 1572872 | tf_op jit(solution)/shard_map/ppermute | solution.py:697
  304.1 28.3 %collective-permute-start.19 = (bf16[256,1024]{1,0:T(8,128)(2,1)S(1)}, bf16[256,1024]{1,0:T(8,128)(2,1)S(1)}, u32[]{:S(2)}, u32[]{:S(2)}) collective-permute-start(bf16[256,1024]{1,0:T(8,128)(2,1)S(1)} %bitcast.281), channel_id=1, source_target_pairs={{0,8},{2,10},{4,12},{6,14},{8,0},{10,2},{12,4},{14,6},{16,24},{18,... | collective-permute-start | bytes 1572872 | tf_op jit(solution)/shard_map/ppermute | solution.py:694
  309.2 46.5 %collective-permute-start.20 = (bf16[1024,768]{1,0:T(8,128)(2,1)}, bf16[1024,768]{1,0:T(8,128)(2,1)}, u32[]{:S(2)}, u32[]{:S(2)}) collective-permute-start(bf16[1024,768]{1,0:T(8,128)(2,1)} %convolution_convert_fusion.9), channel_id=1, source_target_pairs={{0,2},{2,0},{4,6},{6,4},{8,10},{10,8},{12,14},{14,12},{16,18},{18,... | collective-permute-start | bytes 4718600 | tf_op jit(solution)/shard_map/ppermute | solution.py:694
  321.0 41.0 %collective-permute-start.21 = (bf16[512,1024]{1,0:T(8,128)(2,1)S(1)}, bf16[512,1024]{1,0:T(8,128)(2,1)}, u32[]{:S(2)}, u32[]{:S(2)}) collective-permute-start(bf16[512,1024]{1,0:T(8,128)(2,1)S(1)} %bitcast.268), channel_id=1, source_target_pairs={{0,4},{2,6},{4,0},{6,2},{8,12},{10,14},{12,8},{14,10},{16,20},{18,... | collective-permute-start | bytes 3145736 | tf_op jit(solution)/shard_map/ppermute | solution.py:694
  331.6 31.9 %collective-permute-start.22 = (bf16[128,1024]{1,0:T(8,128)(2,1)S(1)}, bf16[128,1024]{1,0:T(8,128)(2,1)S(1)}, u32[]{:S(2)}, u32[]{:S(2)}) collective-permute-start(bf16[128,1024]{1,0:T(8,128)(2,1)S(1)} %bitcast.288), channel_id=1, source_target_pairs={{0,4},{2,6},{4,0},{6,2},{8,12},{10,14},{12,8},{14,10},{16,20},{18,... | collective-permute-start | bytes 786440 | tf_op jit(solution)/shard_map/ppermute | solution.py:694
  355.7 148.2 %all-gather.11.cloned.1.call-start = ((), (), s32[]{:S(2)}) async-start(), calls=%async_computation.3 | async-start | bytes 5570560 | tf_op jit(solution)/shard_map/all_gather | solution.py:935
  365.9 56.8 %collective-permute-start.26 = (bf16[1024,768]{1,0:T(8,128)(2,1)}, bf16[1024,768]{1,0:T(8,128)(2,1)}, u32[]{:S(2)}, u32[]{:S(2)}) collective-permute-start(bf16[1024,768]{1,0:T(8,128)(2,1)} %add_convert_fusion.7), channel_id=1, source_target_pairs={{0,1},{1,0},{2,3},{3,2},{4,5},{5,4},{6,7},{7,6},{8,9},{9,8},{10,11... | collective-permute-start | bytes 4718600 | tf_op jit(solution)/shard_map/ppermute | solution.py:697
  387.7 33.1 %collective-permute-start.41 = (bf16[128,1024]{1,0:T(8,128)(2,1)S(1)}, bf16[128,1024]{1,0:T(8,128)(2,1)}, u32[]{:S(2)}, u32[]{:S(2)}) collective-permute-start(bf16[128,1024]{1,0:T(8,128)(2,1)S(1)} %dynamic-slice_bitcast_fusion.8), channel_id=1, source_target_pairs={{0,16},{2,18},{4,20},{6,22},{8,24},{10,26},{12,28},{14,30},{16,0},... | collective-permute-start | bytes 786440 | tf_op jit(solution)/shard_map/ppermute | solution.py:694
  389.5 30.5 %collective-permute-start.42 = (bf16[32,1024]{1,0:T(8,128)(2,1)}, bf16[32,1024]{1,0:T(8,128)(2,1)}, u32[]{:S(2)}, u32[]{:S(2)}) collective-permute-start(bf16[32,1024]{1,0:T(8,128)(2,1)} %dynamic-slice_bitcast_fusion.13), channel_id=1, source_target_pairs={{0,16},{2,18},{4,20},{6,22},{8,24},{10,26},{12,28},{14,30},{16,0},... | collective-permute-start | bytes 196616 | tf_op jit(solution)/shard_map/ppermute | solution.py:694
  396.4 26.4 %collective-permute-start.25 = (bf16[1024,768]{1,0:T(8,128)(2,1)}, bf16[1024,768]{1,0:T(8,128)(2,1)}, u32[]{:S(2)}, u32[]{:S(2)}) collective-permute-start(bf16[1024,768]{1,0:T(8,128)(2,1)} %convolution_convert_fusion.8), channel_id=1, source_target_pairs={{0,2},{2,0},{4,6},{6,4},{8,10},{10,8},{12,14},{14,12},{16,18},{18,... | collective-permute-start | bytes 4718600 | tf_op jit(solution)/shard_map/ppermute | solution.py:694
  447.1 36.7 %collective-permute-start.33 = (bf16[640,1024]{1,0:T(8,128)(2,1)}, bf16[640,1024]{1,0:T(8,128)(2,1)S(1)}, u32[]{:S(2)}, u32[]{:S(2)}) collective-permute-start(bf16[640,1024]{1,0:T(8,128)(2,1)} %get-tuple-element.355), channel_id=1, source_target_pairs={{0,1},{1,0},{2,3},{3,2},{4,5},{5,4},{6,7},{7,6},{8,9},{9,8},{10,11... | collective-permute-start | bytes 3932168 | tf_op jit(solution)/shard_map/ppermute | solution.py:697
  461.6 27.7 %collective-permute-start.36 = (bf16[256,384]{1,0:T(8,128)(2,1)S(1)}, bf16[256,384]{1,0:T(8,128)(2,1)S(1)}, u32[]{:S(2)}, u32[]{:S(2)}) collective-permute-start(bf16[256,384]{1,0:T(8,128)(2,1)S(1)} %add_convert_fusion.21), channel_id=1, source_target_pairs={{0,16},{2,18},{4,20},{6,22},{8,24},{10,26},{12,28},{14,30},{16,0},... | collective-permute-start | bytes 589832 | tf_op jit(solution)/shard_map/ppermute | solution.py:694
  462.7 32.5 %collective-permute-start.37 = (bf16[256,384]{1,0:T(8,128)(2,1)S(1)}, bf16[256,384]{1,0:T(8,128)(2,1)S(1)}, u32[]{:S(2)}, u32[]{:S(2)}) collective-permute-start(bf16[256,384]{1,0:T(8,128)(2,1)S(1)} %add_convert_fusion.20), channel_id=1, source_target_pairs={{0,16},{2,18},{4,20},{6,22},{8,24},{10,26},{12,28},{14,30},{16,0},... | collective-permute-start | bytes 589832 | tf_op jit(solution)/shard_map/ppermute | solution.py:694
  465.8 31.0 %collective-permute-start.35 = (f32[9728]{0:T(1024)S(1)}, f32[9728]{0:T(1024)S(1)}, u32[]{:S(2)}, u32[]{:S(2)}) collective-permute-start(f32[9728]{0:T(1024)S(1)} %pad_maximum_fusion.7), channel_id=1, source_target_pairs={{0,16},{2,18},{4,20},{6,22},{8,24},{10,26},{12,28},{14,30},{16,0},... | collective-permute-start | bytes 116744 | tf_op jit(solution)/shard_map/ppermute | solution.py:694
  483.8 30.8 %collective-permute-start.34 = (bf16[640,1024]{1,0:T(8,128)(2,1)}, bf16[640,1024]{1,0:T(8,128)(2,1)}, u32[]{:S(2)}, u32[]{:S(2)}) collective-permute-start(bf16[640,1024]{1,0:T(8,128)(2,1)} %get-tuple-element.272), channel_id=1, source_target_pairs={{0,1},{1,0},{2,3},{3,2},{4,5},{5,4},{6,7},{7,6},{8,9},{9,8},{10,11... | collective-permute-start | bytes 3932168 | tf_op jit(solution)/shard_map/ppermute | solution.py:697
  (121 other events, 1183.1 us)
Sparse Core Ops, SparseCore 0:
  70.2 56.2 all-gather.6
  128.7 49.1 all-gather.4
  355.8 67.1 all-gather.8
  425.7 68.8 all-gather.10

commit v6 on v5

--- a/solution.py
+++ b/solution.py
@@ -462,33 +462,32 @@
     )(*rights, *lefts, x, *vectors)
 
 
-def expand_kernel(chunk, x_ref, w_ref, b_ref, active_ref, slope_ref):
-    for at in range(0, x_ref.shape[0], chunk):
-        rows = slice(at, at + chunk)
-        v = dot(x_ref[rows, :], w_ref[...]) + b_ref[...]
-        below = 0.5 + 0.5 * lax.erf(v * ROOT_HALF)
-        active_ref[rows, :] = low(v * below)
-        slope_ref[rows, :] = low(below + v * jnp.exp(-0.5 * v * v) * GAUSS_NORM)
-
-
-def expand(x, weight, bias, block=512, chunk=256):
+def expand_kernel(chunk, count, x_ref, *refs):
+    weights, biases = refs[:count], refs[count : 2 * count]
+    actives, slopes = refs[2 * count : 3 * count], refs[3 * count :]
+    for w_ref, b_ref, active_ref, slope_ref in zip(weights, biases, actives, slopes):
+        for at in range(0, x_ref.shape[0], chunk):
+            rows = slice(at, at + chunk)
+            v = dot(x_ref[rows, :], w_ref[...]) + b_ref[...]
+            below = 0.5 + 0.5 * lax.erf(v * ROOT_HALF)
+            active_ref[rows, :] = low(v * below)
+            slope_ref[rows, :] = low(below + v * jnp.exp(-0.5 * v * v) * GAUSS_NORM)
+
+
+def expand(x, weights, biases, block=512, chunk=256):
     rows, depth = x.shape
-    width = weight.shape[1]
-    out = pl.BlockSpec((rows, block), lambda i: (0, i))
+    count, width = len(weights), weights[0].shape[1]
+    column = lambda size: pl.BlockSpec((size, block), lambda i: (0, i))
     return pl.pallas_call(
-        functools.partial(expand_kernel, chunk),
+        functools.partial(expand_kernel, chunk, count),
         grid=(width // block,),
-        in_specs=[
-            whole(x),
-            pl.BlockSpec((depth, block), lambda i: (0, i)),
-            pl.BlockSpec((1, block), lambda i: (0, i)),
-        ],
-        out_specs=[out, out],
-        out_shape=[jax.ShapeDtypeStruct((rows, width), jnp.bfloat16)] * 2,
+        in_specs=[whole(x)] + [column(depth)] * count + [column(1)] * count,
+        out_specs=[column(rows)] * (2 * count),
+        out_shape=[jax.ShapeDtypeStruct((rows, width), jnp.bfloat16)] * (2 * count),
         compiler_params=params(),
-        cost_estimate=takes(8.5),
+        cost_estimate=takes(14),
         name="expand",
-    )(x, weight, bias[None])
+    )(x, *weights, *[bias[None] for bias in biases])
 
 
 def reduce_kernel(count, half, side_ref, *refs):
@@ -829,9 +828,9 @@
 
     active, slope, grad_pre = {}, {}, {}
 
-    def widen(p, c):
-        active[p, c], slope[p, c] = did(
-            *expand(after(second_out), expand_all[p][c], bias_all[p][c][three:])
+    def widen(p):
+        active[p, KEEP], active[p, SEND], slope[p, KEEP], slope[p, SEND] = did(
+            *expand(after(second_out), expand_all[p], [bias[three:] for bias in bias_all[p]])
         )
 
     def back_active(p, c):
@@ -854,13 +853,11 @@
     def rows_out(keep, arrived, dtype):
         return place_rows(sides, keep, arrived, 1, dtype).reshape(2, 1, length // 2, -1)
 
-    widen(FAR, SEND)
-    widen(FAR, KEEP)
+    widen(FAR)
     sent = swap(product(active[FAR, SEND], grad_two), 0)
-    widen(OWN, SEND)
+    widen(OWN)
     reduce_far_sum = product(active[FAR, KEEP], grad_two, sent)
     reduce_cross = cross(reduce_far_sum)
-    widen(OWN, KEEP)
     sent = swap(product(active[OWN, SEND], grad_two), 0)
     back_active(FAR, SEND)
     reduce_sum = product(active[OWN, KEEP], grad_two, sent)

time: 544 us -> 540 us (level)
  Pallas kernels: 241 us -> 234 us
    pallas_call x4 -> x2, Pallas kernels: 35 us -> 28.6 us  [expand(): pl.pallas_call(functools.partial(expand_kernel, chunk, count), grid=(widt...]
  transfers between devices with their start and end apart: 53 -> 53, of which waited for: 18 -> 18; matrix products, arithmetic and copies ran while one was open for 29% -> 30% of each run, Pallas kernels for 44% -> 43%
where the time goes in v6:
time: 540 us; the launch traced here: 530 us
  Pallas kernels  234 us (43%)
  matrix products  84.2 us (16%)
  other arithmetic  53.3 us (10%)
  local copies, waits for them, and re-layouts  50.7 us (9%)
  waiting for transfers between devices  46.6 us (9%)
  starting transfers between devices  44.7 us (8%)
  between operations  16.9 us (3%)
    pallas_call x4, Pallas kernels, attend_back(): pl.pallas_call(attend_back_kernel, grid=(pairs,), in_specs=parts + [pl.Bl...  69.6 us
    dot_general x14, matrix products, dot_tn(): lax.dot_general(left, right, (((0,), (0,)), ((), ())), preferred_element_...  59.6 us
    pallas_call x2, Pallas kernels, back_norm(): pl.pallas_call(functools.partial(back_kernel, len(lefts)), grid_spec=pltp...  38 us
    pallas_call x2, Pallas kernels, attend(): pl.pallas_call(attend_kernel, grid=(pairs,), in_specs=parts + [whole(arra...  37.6 us
    ppermute x36, starting transfers between devices, swap(): lax.ppermute(array, 'dp', [(i, i ^ 1 << level) for i in range(spread)])  28.9 us
    pallas_call x2, Pallas kernels, expand(): pl.pallas_call(functools.partial(expand_kernel, chunk, count), grid=(widt...  28.6 us
    ppermute x36, waiting for transfers between devices, swap(): lax.ppermute(array, 'dp', [(i, i ^ 1 << level) for i in range(spread)])  23.8 us
    ppermute x13, waiting for transfers between devices, cross(): return lax.ppermute(array, 'mp', [(0, 1), (1, 0)])  21.4 us
  transfers between devices with their start and end apart: 53, of which 18 were waited for; matrix products, arithmetic and copies ran while one was open for 30% of the time, Pallas kernels for 43%

profile of v6, /device:TPU:0, one launch (start us, length us, event | category | flops | bytes accessed | tf_op | source)
XLA Modules:
  0.0 530.2 jit_solution(6109170738714839215)
XLA Ops:
  41.5 5.2 constant_dynamic-slice_fusion.29
  56.1 5.0 enter.1
  61.1 8.9 %project.2.q_ref.k_ref.v_ref = bf16[1280,1536]{1,0:T(8,128)(2,1)} custom-call(bf16[1280,1024]{1,0:T(8,128)(2,1)} %get-tuple-element.246.x_ref, bf16[1024,768]{1,0:T(8,128)(2,1)S(1)} %copy-done.5, bf16[1024,768]{1,0:T(8,128)(2,1)} %pad_maximum_fusion.1.refs_1_.refs_2_, f32[1,768]{1,0:T(1,128)S(1)} %bitcast.219, f32[1,768]{1,0:T(1,128)S(1)} %bitcast.220, ...), custom_call_target="tpu_custom_call" | custom-call | flops 35999997952 | bytes 36000000 | tf_op jit(solution)/shard_map/project/pallas_call | solution.py:213
  76.4 18.9 %attend.2 = (bf16[1280,512]{1,0:T(8,128)(2,1)S(1)}, f32[1280,512]{1,0:T(8,128)}, bf16[8,592,512]{2,1,0:T(8,128)(2,1)}, bf16[8,1280,768]{2,1,0:T(8,128)(2,1)}) custom-call(bf16[1280,1536]{1,0:T(8,128)(2,1)} %project.2.q_ref.k_ref.v_ref, bf16[1280,1536]{1,0:T(8,128)(2,1)} %project.2.q_ref.k_ref.v_ref, bf16[1280,1536]{1,0:T(8,128)(2,1)} %project.2.q_ref.k_ref.v_ref, ...), custom_call_target="tpu_custom_call" | custom-call | flops 80000000000 | bytes 80000000 | tf_op jit(solution)/shard_map/attend/pallas_call | solution.py:327
  97.0 8.3 %project.3.q_ref.k_ref.v_ref = bf16[1280,1536]{1,0:T(8,128)(2,1)} custom-call(bf16[1280,1024]{1,0:T(8,128)(2,1)} %get-tuple-element.246.x_ref, bf16[1024,768]{1,0:T(8,128)(2,1)S(1)} %bitcast.206, bf16[1024,768]{1,0:T(8,128)(2,1)} %copy-done.34, f32[1,768]{1,0:T(1,128)S(1)} %broadcast_in_dim.156.refs_2_, f32[1,768]{1,0:T(1,128)S(1)} %broadcast_in_dim.157.refs_3_, ...), custom_call_target="tpu_custom_call" | custom-call | flops 35999997952 | bytes 36000000 | tf_op jit(solution)/shard_map/project/pallas_call | solution.py:213
  105.3 18.8 %attend.3 = (bf16[1280,512]{1,0:T(8,128)(2,1)S(1)}, f32[1280,512]{1,0:T(8,128)}, bf16[8,592,512]{2,1,0:T(8,128)(2,1)}, bf16[8,1280,768]{2,1,0:T(8,128)(2,1)}) custom-call(bf16[1280,1536]{1,0:T(8,128)(2,1)} %project.3.q_ref.k_ref.v_ref, bf16[1280,1536]{1,0:T(8,128)(2,1)} %project.3.q_ref.k_ref.v_ref, bf16[1280,1536]{1,0:T(8,128)(2,1)} %project.3.q_ref.k_ref.v_ref, ...), custom_call_target="tpu_custom_call" | custom-call | flops 80000000000 | bytes 80000000 | tf_op jit(solution)/shard_map/attend/pallas_call | solution.py:327
  128.1 7.8 %merge.1 = (f32[1280,1024]{1,0:T(8,128)}, bf16[1280,1024]{1,0:T(8,128)(2,1)}) custom-call(bf16[256,1024]{1,0:T(8,128)(2,1)S(1)} %copy-done.18, bf16[256,1024]{1,0:T(8,128)(2,1)S(1)} %copy-done.20, bf16[256,1024]{1,0:T(8,128)(2,1)S(1)} %bitcast.208, bf16[256,1024]{1,0:T(8,128)(2,1)S(1)} %bitcast.210, bf16[1280,512]{1,0:T(8,128)(2,1)S(1)} %get-tuple-element.210.refs_4_.o_ref, ...), custom_call_target="tpu_custom_call" | custom-call | flops 32000000000 | bytes 32000000 | tf_op jit(solution)/shard_map/merge/pallas_call | solution.py:447
  143.3 14.6 %expand.2 = (bf16[1280,1024]{1,0:T(8,128)(2,1)}, bf16[1280,1024]{1,0:T(8,128)(2,1)}, bf16[1280,1024]{1,0:T(8,128)(2,1)}, bf16[1280,1024]{1,0:T(8,128)(2,1)}) custom-call(bf16[1280,1024]{1,0:T(8,128)(2,1)} %get-tuple-element.205.x_ref, bf16[1024,1024]{1,0:T(8,128)(2,1)S(1)} %bitcast.203, bf16[1024,1024]{1,0:T(8,128)(2,1)} %bitcast.201, ...), custom_call_target="tpu_custom_call" | custom-call | flops 56000000000 | bytes 56000000 | tf_op jit(solution)/shard_map/expand/pallas_call | solution.py:481
  157.9 5.9 %convolution_convert_fusion.7 = bf16[1024,1024]{1,0:T(8,128)(2,1)} fusion(bf16[1280,1024]{1,0:T(8,128)(2,1)} %get-tuple-element.189.refs_4_, bf16[1280,1024]{1,0:T(8,128)(2,1)S(1)} %collect.1.refs_9_), kind=kOutput, calls=%fused_computation.24 | convolution fusion | flops 2685403136 | bytes 7340032 | tf_op jit(solution)/shard_map/dot_general | solution.py:54
  164.1 14.0 %expand.3 = (bf16[1280,1024]{1,0:T(8,128)(2,1)}, bf16[1280,1024]{1,0:T(8,128)(2,1)}, bf16[1280,1024]{1,0:T(8,128)(2,1)}, bf16[1280,1024]{1,0:T(8,128)(2,1)}) custom-call(bf16[1280,1024]{1,0:T(8,128)(2,1)} %get-tuple-element.205.x_ref, bf16[1024,1024]{1,0:T(8,128)(2,1)S(1)} %get-tuple-element.421.refs_0_.refs_3_, ...), custom_call_target="tpu_custom_call" | custom-call | flops 56000000000 | bytes 56000000 | tf_op jit(solution)/shard_map/expand/pallas_call | solution.py:481
  228.4 5.7 %add_convert_fusion.2 = bf16[1024,1024]{1,0:T(8,128)(2,1)} fusion(bf16[1024,1024]{1,0:T(8,128)(2,1)} %collective-permute-done.12, bf16[1280,1024]{1,0:T(8,128)(2,1)S(1)} %copy-done.84, bf16[1280,1024]{1,0:T(8,128)(2,1)S(1)} %copy-done.49), kind=kOutput, calls=%fused_computation.8 | convolution fusion | flops 2687500288 | bytes 9437184 | tf_op jit(solution)/shard_map/dot_general | solution.py:54
  234.1 21.3 %back_norm.2 = (bf16[1280,1024]{1,0:T(8,128)(2,1)}, f32[4,8,1024]{2,1,0:T(8,128)S(1)}) custom-call(s32[4]{0:T(128)S(1)} %iota.92.at_ref, bf16[1024,1024]{1,0:T(8,128)(2,1)S(1)} %bitcast.202, bf16[1024,1024]{1,0:T(8,128)(2,1)} %bitcast.204, bf16[1024,1024]{1,0:T(8,128)(2,1)} %get-tuple-element.422.refs_1_.refs_2_, bf16[1024,1024]{1,0:T(8,128)(2,1)} %copy-done, ...), custom_call_target="tpu_custom_call" | custom-call | flops 400000000 | bytes 400000 | tf_op jit(solution)/shard_map/back_norm/pallas_call | solution.py:560
  273.7 17.3 %attend_back.4 = (bf16[1280,768]{1,0:T(8,128)(2,1)}, f32[8,768]{1,0:T(8,128)}) custom-call(bf16[1280,1536]{1,0:T(8,128)(2,1)} %project.3.q_ref.k_ref.v_ref, bf16[1280,1536]{1,0:T(8,128)(2,1)} %project.3.q_ref.k_ref.v_ref, bf16[1280,1536]{1,0:T(8,128)(2,1)} %project.3.q_ref.k_ref.v_ref, bf16[1280,256]{1,0:T(8,128)(2,1)} %convolution_convert_fusion.3.g_ref, ...), custom_call_target="tpu_custom_call" | custom-call | flops 64000000000 | bytes 64000000 | tf_op jit(solution)/shard_map/attend_back/pallas_call | solution.py:405
  305.2 10.5 %collective-permute-done.17 = bf16[1024,1024]{1,0:T(8,128)(2,1)S(1)} collective-permute-done((bf16[1024,1024]{1,0:T(8,128)(2,1)}, bf16[1024,1024]{1,0:T(8,128)(2,1)S(1)}, u32[]{:S(2)}, u32[]{:S(2)}) %collective-permute-start.17) | collective-permute-done | bytes 2097184 | tf_op jit(solution)/shard_map/ppermute | solution.py:696
  317.7 8.7 %collective-permute-done.18 = bf16[256,1024]{1,0:T(8,128)(2,1)} collective-permute-done((bf16[256,1024]{1,0:T(8,128)(2,1)}, bf16[256,1024]{1,0:T(8,128)(2,1)}, u32[]{:S(2)}, u32[]{:S(2)}) %collective-permute-start.18) | collective-permute-done | bytes 524320 | tf_op jit(solution)/shard_map/ppermute | solution.py:696
  331.3 17.4 %attend_back.5 = (bf16[1280,768]{1,0:T(8,128)(2,1)}, f32[8,768]{1,0:T(8,128)}) custom-call(bf16[1280,1536]{1,0:T(8,128)(2,1)} %project.3.q_ref.k_ref.v_ref, bf16[1280,1536]{1,0:T(8,128)(2,1)} %project.3.q_ref.k_ref.v_ref, bf16[1280,1536]{1,0:T(8,128)(2,1)} %project.3.q_ref.k_ref.v_ref, bf16[1280,256]{1,0:T(8,128)(2,1)} %convolution_convert_fusion.2.g_ref, ...), custom_call_target="tpu_custom_call" | custom-call | flops 64000000000 | bytes 64000000 | tf_op jit(solution)/shard_map/attend_back/pallas_call | solution.py:405
  351.8 6.2 %add_convert_fusion.7 = bf16[1024,768]{1,0:T(8,128)(2,1)} fusion(bf16[1024,768]{1,0:T(8,128)(2,1)} %collective-permute-done.20, bf16[1280,1024]{1,0:T(8,128)(2,1)} %get-tuple-element.246.x_ref, bf16[1280,768]{1,0:T(8,128)(2,1)} %get-tuple-element.229.refs_5_), kind=kOutput, calls=%fused_computation.13 | convolution fusion | flops 2015625216 | bytes 7733248 | tf_op jit(solution)/shard_map/dot_general | solution.py:54
  363.6 17.5 %attend_back.6 = (bf16[1280,768]{1,0:T(8,128)(2,1)}, f32[8,768]{1,0:T(8,128)}) custom-call(bf16[1280,1536]{1,0:T(8,128)(2,1)} %project.2.q_ref.k_ref.v_ref, bf16[1280,1536]{1,0:T(8,128)(2,1)} %project.2.q_ref.k_ref.v_ref, bf16[1280,1536]{1,0:T(8,128)(2,1)} %project.2.q_ref.k_ref.v_ref, bf16[1280,256]{1,0:T(8,128)(2,1)} %convolution_convert_fusion.1.g_ref, ...), custom_call_target="tpu_custom_call" | custom-call | flops 64000000000 | bytes 64000000 | tf_op jit(solution)/shard_map/attend_back/pallas_call | solution.py:405
  387.4 5.0 convolution_convert_fusion.8
  392.5 17.3 %attend_back.7 = (bf16[1280,768]{1,0:T(8,128)(2,1)}, f32[8,768]{1,0:T(8,128)}) custom-call(bf16[1280,1536]{1,0:T(8,128)(2,1)} %project.2.q_ref.k_ref.v_ref, bf16[1280,1536]{1,0:T(8,128)(2,1)} %project.2.q_ref.k_ref.v_ref, bf16[1280,1536]{1,0:T(8,128)(2,1)} %project.2.q_ref.k_ref.v_ref, bf16[1280,256]{1,0:T(8,128)(2,1)} %convolution_convert_fusion.g_ref, ...), custom_call_target="tpu_custom_call" | custom-call | flops 64000000000 | bytes 64000000 | tf_op jit(solution)/shard_map/attend_back/pallas_call | solution.py:405
  423.5 16.8 %back_norm.3 = (bf16[1280,1024]{1,0:T(8,128)(2,1)}, f32[4,8,1024]{2,1,0:T(8,128)S(1)}) custom-call(s32[4]{0:T(128)S(1)} %and_select_fusion.2.at_ref, bf16[1024,768]{1,0:T(8,128)(2,1)S(1)} %copy-done.35, bf16[1024,768]{1,0:T(8,128)(2,1)S(1)} %bitcast.207, bf16[1024,768]{1,0:T(8,128)(2,1)} %pad_maximum_fusion.1.refs_1_.refs_2_, ...), custom_call_target="tpu_custom_call" | custom-call | flops 80000000000 | bytes 80000000 | tf_op jit(solution)/shard_map/back_norm/pallas_call | solution.py:560
  461.6 17.9 %reduce_rows.1 = (bf16[640,1024]{1,0:T(8,128)(2,1)}, bf16[640,1024]{1,0:T(8,128)(2,1)S(1)}) custom-call(s32[1]{0:T(128)} %bitcast.side_ref.flag_ref, bf16[1024,1024]{1,0:T(8,128)(2,1)} %bitcast.229, bf16[1024,1024]{1,0:T(8,128)(2,1)} %bitcast.227, bf16[1024,1024]{1,0:T(8,128)(2,1)} %get-tuple-element.340.refs_2_, ...), custom_call_target="tpu_custom_call" | custom-call | flops 400000000 | bytes 400000 | tf_op jit(solution)/shard_map/reduce_rows/pallas_call | solution.py:514
  479.9 5.4 %collective-permute-done.36 = bf16[256,384]{1,0:T(8,128)(2,1)S(1)} collective-permute-done((bf16[256,384]{1,0:T(8,128)(2,1)S(1)}, bf16[256,384]{1,0:T(8,128)(2,1)S(1)}, u32[]{:S(2)}, u32[]{:S(2)}) %collective-permute-start.36) | collective-permute-done | bytes 196640 | tf_op jit(solution)/shard_map/ppermute | solution.py:693
  485.5 5.6 %collective-permute-done.37 = bf16[256,384]{1,0:T(8,128)(2,1)S(1)} collective-permute-done((bf16[256,384]{1,0:T(8,128)(2,1)S(1)}, bf16[256,384]{1,0:T(8,128)(2,1)S(1)}, u32[]{:S(2)}, u32[]{:S(2)}) %collective-permute-start.37) | collective-permute-done | bytes 196640 | tf_op jit(solution)/shard_map/ppermute | solution.py:693
  (446 shorter events, 233.2 us)
Async XLA Ops:
  7.2 119.3 %all-gather.7.cloned.1.call-start = ((), (), s32[]{:S(2)}) async-start(), calls=%async_computation.1 | async-start | bytes 5570560 | tf_op jit(solution)/shard_map/all_gather | solution.py:791
  9.1 28.5 %collective-permute-start = (bf16[256,768]{1,0:T(8,128)(2,1)}, bf16[256,768]{1,0:T(8,128)(2,1)}, u32[]{:S(2)}, u32[]{:S(2)}) collective-permute-start(bf16[256,768]{1,0:T(8,128)(2,1)} %pad_maximum_fusion.3), channel_id=1, source_target_pairs={{0,1},{1,0},{2,3},{3,2},{4,5},{5,4},{6,7},{7,6},{8,9},{9,8},{10,11... | collective-permute-start | bytes 1179656 | tf_op jit(solution)/shard_map/ppermute | solution.py:696
  14.5 41.5 %collective-permute-start.2 = (bf16[640,1024]{1,0:T(8,128)(2,1)}, bf16[640,1024]{1,0:T(8,128)(2,1)}, u32[]{:S(2)}, u32[]{:S(2)}) collective-permute-start(bf16[640,1024]{1,0:T(8,128)(2,1)} %dynamic-slice_bitcast_fusion.1), channel_id=1, source_target_pairs={{0,1},{1,0},{2,3},{3,2},{4,5},{5,4},{6,7},{7,6},{8,9},{9,8},{10,11... | collective-permute-start | bytes 3932168 | tf_op jit(solution)/shard_map/ppermute | solution.py:696
  70.1 116.9 %all-gather.5.cloned.1.call-start = ((), (), s32[]{:S(2)}) async-start(), calls=%async_computation | async-start | bytes 4456448 | tf_op jit(solution)/shard_map/all_gather | solution.py:791
  70.1 55.0 %collective-permute-start.3 = (bf16[128,1024]{1,0:T(8,128)(2,1)}, bf16[128,1024]{1,0:T(8,128)(2,1)}, u32[]{:S(2)}, u32[]{:S(2)}) collective-permute-start(bf16[128,1024]{1,0:T(8,128)(2,1)} %constant_dynamic-slice_fusion.36), channel_id=1, source_target_pairs={{0,1},{1,0},{2,3},{3,2},{4,5},{5,4},{6,7},{7,6},{8,9},{9,8},{10,11... | collective-permute-start | bytes 786440 | tf_op jit(solution)/shard_map/ppermute | solution.py:696
  95.2 45.4 %collective-permute-start.8 = (bf16[640,1024]{1,0:T(8,128)(2,1)}, bf16[640,1024]{1,0:T(8,128)(2,1)}, u32[]{:S(2)}, u32[]{:S(2)}) collective-permute-start(bf16[640,1024]{1,0:T(8,128)(2,1)} %dynamic-slice_bitcast_fusion), channel_id=1, source_target_pairs={{0,1},{1,0},{2,3},{3,2},{4,5},{5,4},{6,7},{7,6},{8,9},{9,8},{10,11... | collective-permute-start | bytes 3932168 | tf_op jit(solution)/shard_map/ppermute | solution.py:696
  125.2 323.3 %all-gather.9.cloned.1.call-start = ((), (), s32[]{:S(2)}) async-start(), calls=%async_computation.2 | async-start | bytes 4456448 | tf_op jit(solution)/shard_map/all_gather | solution.py:915
  222.1 48.8 %collective-permute-start.15 = (bf16[1024,1024]{1,0:T(8,128)(2,1)}, bf16[1024,1024]{1,0:T(8,128)(2,1)S(1)}, u32[]{:S(2)}, u32[]{:S(2)}) collective-permute-start(bf16[1024,1024]{1,0:T(8,128)(2,1)} %add_convert_fusion.5), channel_id=1, source_target_pairs={{0,1},{1,0},{2,3},{3,2},{4,5},{5,4},{6,7},{7,6},{8,9},{9,8},{10,11... | collective-permute-start | bytes 6291464 | tf_op jit(solution)/shard_map/ppermute | solution.py:696
  226.2 89.6 %collective-permute-start.17 = (bf16[1024,1024]{1,0:T(8,128)(2,1)}, bf16[1024,1024]{1,0:T(8,128)(2,1)S(1)}, u32[]{:S(2)}, u32[]{:S(2)}) collective-permute-start(bf16[1024,1024]{1,0:T(8,128)(2,1)} %add_convert_fusion.3), channel_id=1, source_target_pairs={{0,1},{1,0},{2,3},{3,2},{4,5},{5,4},{6,7},{7,6},{8,9},{9,8},{10,11... | collective-permute-start | bytes 6291464 | tf_op jit(solution)/shard_map/ppermute | solution.py:696
  291.1 35.4 %collective-permute-start.18 = (bf16[256,1024]{1,0:T(8,128)(2,1)}, bf16[256,1024]{1,0:T(8,128)(2,1)}, u32[]{:S(2)}, u32[]{:S(2)}) collective-permute-start(bf16[256,1024]{1,0:T(8,128)(2,1)} %add_convert_fusion.14), channel_id=1, source_target_pairs={{0,1},{1,0},{2,3},{3,2},{4,5},{5,4},{6,7},{7,6},{8,9},{9,8},{10,11... | collective-permute-start | bytes 1572872 | tf_op jit(solution)/shard_map/ppermute | solution.py:696
  300.1 28.3 %collective-permute-start.19 = (bf16[256,1024]{1,0:T(8,128)(2,1)S(1)}, bf16[256,1024]{1,0:T(8,128)(2,1)S(1)}, u32[]{:S(2)}, u32[]{:S(2)}) collective-permute-start(bf16[256,1024]{1,0:T(8,128)(2,1)S(1)} %bitcast.281), channel_id=1, source_target_pairs={{0,8},{2,10},{4,12},{6,14},{8,0},{10,2},{12,4},{14,6},{16,24},{18,... | collective-permute-start | bytes 1572872 | tf_op jit(solution)/shard_map/ppermute | solution.py:693
  305.2 46.6 %collective-permute-start.20 = (bf16[1024,768]{1,0:T(8,128)(2,1)}, bf16[1024,768]{1,0:T(8,128)(2,1)}, u32[]{:S(2)}, u32[]{:S(2)}) collective-permute-start(bf16[1024,768]{1,0:T(8,128)(2,1)} %convolution_convert_fusion.9), channel_id=1, source_target_pairs={{0,2},{2,0},{4,6},{6,4},{8,10},{10,8},{12,14},{14,12},{16,18},{18,... | collective-permute-start | bytes 4718600 | tf_op jit(solution)/shard_map/ppermute | solution.py:693
  316.9 41.1 %collective-permute-start.21 = (bf16[512,1024]{1,0:T(8,128)(2,1)S(1)}, bf16[512,1024]{1,0:T(8,128)(2,1)}, u32[]{:S(2)}, u32[]{:S(2)}) collective-permute-start(bf16[512,1024]{1,0:T(8,128)(2,1)S(1)} %bitcast.268), channel_id=1, source_target_pairs={{0,4},{2,6},{4,0},{6,2},{8,12},{10,14},{12,8},{14,10},{16,20},{18,... | collective-permute-start | bytes 3145736 | tf_op jit(solution)/shard_map/ppermute | solution.py:693
  327.7 32.0 %collective-permute-start.22 = (bf16[128,1024]{1,0:T(8,128)(2,1)S(1)}, bf16[128,1024]{1,0:T(8,128)(2,1)S(1)}, u32[]{:S(2)}, u32[]{:S(2)}) collective-permute-start(bf16[128,1024]{1,0:T(8,128)(2,1)S(1)} %bitcast.288), channel_id=1, source_target_pairs={{0,4},{2,6},{4,0},{6,2},{8,12},{10,14},{12,8},{14,10},{16,20},{18,... | collective-permute-start | bytes 786440 | tf_op jit(solution)/shard_map/ppermute | solution.py:693
  351.8 147.8 %all-gather.11.cloned.1.call-start = ((), (), s32[]{:S(2)}) async-start(), calls=%async_computation.3 | async-start | bytes 5570560 | tf_op jit(solution)/shard_map/all_gather | solution.py:932
  362.0 56.8 %collective-permute-start.26 = (bf16[1024,768]{1,0:T(8,128)(2,1)}, bf16[1024,768]{1,0:T(8,128)(2,1)}, u32[]{:S(2)}, u32[]{:S(2)}) collective-permute-start(bf16[1024,768]{1,0:T(8,128)(2,1)} %add_convert_fusion.7), channel_id=1, source_target_pairs={{0,1},{1,0},{2,3},{3,2},{4,5},{5,4},{6,7},{7,6},{8,9},{9,8},{10,11... | collective-permute-start | bytes 4718600 | tf_op jit(solution)/shard_map/ppermute | solution.py:696
  383.8 33.1 %collective-permute-start.41 = (bf16[128,1024]{1,0:T(8,128)(2,1)S(1)}, bf16[128,1024]{1,0:T(8,128)(2,1)}, u32[]{:S(2)}, u32[]{:S(2)}) collective-permute-start(bf16[128,1024]{1,0:T(8,128)(2,1)S(1)} %dynamic-slice_bitcast_fusion.8), channel_id=1, source_target_pairs={{0,16},{2,18},{4,20},{6,22},{8,24},{10,26},{12,28},{14,30},{16,0},... | collective-permute-start | bytes 786440 | tf_op jit(solution)/shard_map/ppermute | solution.py:693
  385.5 30.5 %collective-permute-start.42 = (bf16[32,1024]{1,0:T(8,128)(2,1)}, bf16[32,1024]{1,0:T(8,128)(2,1)}, u32[]{:S(2)}, u32[]{:S(2)}) collective-permute-start(bf16[32,1024]{1,0:T(8,128)(2,1)} %dynamic-slice_bitcast_fusion.13), channel_id=1, source_target_pairs={{0,16},{2,18},{4,20},{6,22},{8,24},{10,26},{12,28},{14,30},{16,0},... | collective-permute-start | bytes 196616 | tf_op jit(solution)/shard_map/ppermute | solution.py:693
  392.5 26.3 %collective-permute-start.25 = (bf16[1024,768]{1,0:T(8,128)(2,1)}, bf16[1024,768]{1,0:T(8,128)(2,1)}, u32[]{:S(2)}, u32[]{:S(2)}) collective-permute-start(bf16[1024,768]{1,0:T(8,128)(2,1)} %convolution_convert_fusion.8), channel_id=1, source_target_pairs={{0,2},{2,0},{4,6},{6,4},{8,10},{10,8},{12,14},{14,12},{16,18},{18,... | collective-permute-start | bytes 4718600 | tf_op jit(solution)/shard_map/ppermute | solution.py:693
  443.4 36.2 %collective-permute-start.33 = (bf16[640,1024]{1,0:T(8,128)(2,1)}, bf16[640,1024]{1,0:T(8,128)(2,1)S(1)}, u32[]{:S(2)}, u32[]{:S(2)}) collective-permute-start(bf16[640,1024]{1,0:T(8,128)(2,1)} %get-tuple-element.351), channel_id=1, source_target_pairs={{0,1},{1,0},{2,3},{3,2},{4,5},{5,4},{6,7},{7,6},{8,9},{9,8},{10,11... | collective-permute-start | bytes 3932168 | tf_op jit(solution)/shard_map/ppermute | solution.py:696
  457.4 27.9 %collective-permute-start.36 = (bf16[256,384]{1,0:T(8,128)(2,1)S(1)}, bf16[256,384]{1,0:T(8,128)(2,1)S(1)}, u32[]{:S(2)}, u32[]{:S(2)}) collective-permute-start(bf16[256,384]{1,0:T(8,128)(2,1)S(1)} %add_convert_fusion.21), channel_id=1, source_target_pairs={{0,16},{2,18},{4,20},{6,22},{8,24},{10,26},{12,28},{14,30},{16,0},... | collective-permute-start | bytes 589832 | tf_op jit(solution)/shard_map/ppermute | solution.py:693
  458.5 32.6 %collective-permute-start.37 = (bf16[256,384]{1,0:T(8,128)(2,1)S(1)}, bf16[256,384]{1,0:T(8,128)(2,1)S(1)}, u32[]{:S(2)}, u32[]{:S(2)}) collective-permute-start(bf16[256,384]{1,0:T(8,128)(2,1)S(1)} %add_convert_fusion.20), channel_id=1, source_target_pairs={{0,16},{2,18},{4,20},{6,22},{8,24},{10,26},{12,28},{14,30},{16,0},... | collective-permute-start | bytes 589832 | tf_op jit(solution)/shard_map/ppermute | solution.py:693
  461.5 31.1 %collective-permute-start.35 = (f32[9728]{0:T(1024)S(1)}, f32[9728]{0:T(1024)S(1)}, u32[]{:S(2)}, u32[]{:S(2)}) collective-permute-start(f32[9728]{0:T(1024)S(1)} %pad_maximum_fusion.7), channel_id=1, source_target_pairs={{0,16},{2,18},{4,20},{6,22},{8,24},{10,26},{12,28},{14,30},{16,0},... | collective-permute-start | bytes 116744 | tf_op jit(solution)/shard_map/ppermute | solution.py:693
  479.5 30.8 %collective-permute-start.34 = (bf16[640,1024]{1,0:T(8,128)(2,1)}, bf16[640,1024]{1,0:T(8,128)(2,1)}, u32[]{:S(2)}, u32[]{:S(2)}) collective-permute-start(bf16[640,1024]{1,0:T(8,128)(2,1)} %get-tuple-element.268), channel_id=1, source_target_pairs={{0,1},{1,0},{2,3},{3,2},{4,5},{5,4},{6,7},{7,6},{8,9},{9,8},{10,11... | collective-permute-start | bytes 3932168 | tf_op jit(solution)/shard_map/ppermute | solution.py:696
  (118 other events, 1145.3 us)
Sparse Core Ops, SparseCore 0:
  70.2 56.2 all-gather.6
  128.7 49.1 all-gather.4
  351.9 67.1 all-gather.8
  421.8 68.3 all-gather.10

commit v7 on v6

--- a/solution.py
+++ b/solution.py
@@ -933,7 +933,7 @@
         after(jnp.concatenate([expand_sum, merge_sum])), "dp", axis=0, tiled=True
     )
     heads_sum = product(first_out, grad_heads[OWN, KEEP], sent, heads_cross)
-    orders = [rest, rest[1:2] + rest[:1] + rest[2:]]
+    orders = [rest[:1] + rest[2:] + rest[1:2], rest[1:2] + rest[:1] + rest[2:]]
     middle = heads_sum.shape[1] // 2
     heads_sums = [heads_sum[:, :middle], heads_sum[:, middle:]]
 
@@ -974,9 +974,12 @@
     far_send, own_send, both = did(*(after(v) for v in (small[FAR, SEND], small[OWN, SEND], both)))
     arrived = swap(jnp.concatenate([far_send, own_send, both]), 0)
     size = own_send.size
-    reduce_out = in_rows(after(reduce_total))
-    arrived, reduce_out = lax.optimization_barrier((arrived, reduce_out))
-    did(arrived)
+    layer_send, layer_keep = did(
+        *reduce_rows(
+            sides, [active[q] for q in QUARTERS], [reduce_all[p][c] for p, c in QUARTERS],
+            after(residual), reduce_bias,
+        )
+    )
     heads_sums = both_summed(pairs)
     mine = jnp.concatenate([small[FAR, KEEP] + arrived[:size], small[OWN, KEEP], both])
     mine = did(
@@ -987,14 +990,11 @@
         small_next = swap(mine, rest[n])
         heads_sums = both_summed(pairs)
         mine = did(mine + after(small_next))
-    arrived = [swap(total, rest[-1]) for total in heads_sums]
+    arrived = [swap(total, order[-1]) for total, order in zip(heads_sums, orders)]
     small_next = swap(mine, rest[-1])
-    layer_send, layer_keep = did(
-        *reduce_rows(
-            sides, [active[q] for q in QUARTERS], [reduce_all[p][c] for p, c in QUARTERS],
-            after(residual), reduce_bias,
-        )
-    )
+    reduce_out = in_rows(after(reduce_total))
+    mine, reduce_out = lax.optimization_barrier((mine, reduce_out))
+    did(mine)
     heads_sums = both_summed(zip(heads_sums, arrived))
     mine = did(mine + after(small_next))
     layer_far = cross(tie(layer_send, tokens_cross))

time: 540 us -> 538 us (level)
  other arithmetic: 53.3 us -> 47.5 us
  transfers between devices with their start and end apart: 53 -> 53, of which waited for: 18 -> 17; matrix products, arithmetic and copies ran while one was open for 30% -> 29% of each run, Pallas kernels for 43% -> 44%
where the time goes in v7:
time: 538 us; the launch traced here: 528 us
  Pallas kernels  234 us (43%)
  matrix products  84.3 us (16%)
  local copies, waits for them, and re-layouts  51 us (9%)
  waiting for transfers between devices  50.7 us (9%)
  other arithmetic  47.5 us (9%)
  starting transfers between devices  43.4 us (8%)
  between operations  16.9 us (3%)
    pallas_call x4, Pallas kernels, attend_back(): pl.pallas_call(attend_back_kernel, grid=(pairs,), in_specs=parts + [pl.Bl...  69.6 us
    dot_general x14, matrix products, dot_tn(): lax.dot_general(left, right, (((0,), (0,)), ((), ())), preferred_element_...  60.3 us
    pallas_call x2, Pallas kernels, back_norm(): pl.pallas_call(functools.partial(back_kernel, len(lefts)), grid_spec=pltp...  38 us
    pallas_call x2, Pallas kernels, attend(): pl.pallas_call(attend_kernel, grid=(pairs,), in_specs=parts + [whole(arra...  37.6 us
    pallas_call x2, Pallas kernels, expand(): pl.pallas_call(functools.partial(expand_kernel, chunk, count), grid=(widt...  28.6 us
    ppermute x36, waiting for transfers between devices, swap(): lax.ppermute(array, 'dp', [(i, i ^ 1 << level) for i in range(spread)])  28.6 us
    ppermute x36, starting transfers between devices, swap(): lax.ppermute(array, 'dp', [(i, i ^ 1 << level) for i in range(spread)])  26.7 us
    dot_general x8, matrix products, dot_nt(): lax.dot_general(left, right, (((1,), (1,)), ((), ())), preferred_element_...  21.1 us
  transfers between devices with their start and end apart: 53, of which 17 were waited for; matrix products, arithmetic and copies ran while one was open for 29% of the time, Pallas kernels for 44%

profile of v7, /device:TPU:0, one launch (start us, length us, event | category | flops | bytes accessed | tf_op | source)
XLA Modules:
  0.0 528.1 jit_solution(8617242836888034777)
XLA Ops:
  41.0 5.2 constant_dynamic-slice_fusion.27
  55.6 5.0 enter.1
  60.6 8.9 %project.2.q_ref.k_ref.v_ref = bf16[1280,1536]{1,0:T(8,128)(2,1)} custom-call(bf16[1280,1024]{1,0:T(8,128)(2,1)} %get-tuple-element.246.x_ref, bf16[1024,768]{1,0:T(8,128)(2,1)S(1)} %copy-done.5, bf16[1024,768]{1,0:T(8,128)(2,1)} %pad_maximum_fusion.1.refs_1_.refs_2_, f32[1,768]{1,0:T(1,128)S(1)} %bitcast.221, f32[1,768]{1,0:T(1,128)S(1)} %bitcast.222, ...), custom_call_target="tpu_custom_call" | custom-call | flops 35999997952 | bytes 36000000 | tf_op jit(solution)/shard_map/project/pallas_call | solution.py:213
  75.9 18.9 %attend.2 = (bf16[1280,512]{1,0:T(8,128)(2,1)S(1)}, f32[1280,512]{1,0:T(8,128)}, bf16[8,592,512]{2,1,0:T(8,128)(2,1)}, bf16[8,1280,768]{2,1,0:T(8,128)(2,1)}) custom-call(bf16[1280,1536]{1,0:T(8,128)(2,1)} %project.2.q_ref.k_ref.v_ref, bf16[1280,1536]{1,0:T(8,128)(2,1)} %project.2.q_ref.k_ref.v_ref, bf16[1280,1536]{1,0:T(8,128)(2,1)} %project.2.q_ref.k_ref.v_ref, ...), custom_call_target="tpu_custom_call" | custom-call | flops 80000000000 | bytes 80000000 | tf_op jit(solution)/shard_map/attend/pallas_call | solution.py:327
  96.5 8.4 %project.3.q_ref.k_ref.v_ref = bf16[1280,1536]{1,0:T(8,128)(2,1)} custom-call(bf16[1280,1024]{1,0:T(8,128)(2,1)} %get-tuple-element.246.x_ref, bf16[1024,768]{1,0:T(8,128)(2,1)S(1)} %bitcast.208, bf16[1024,768]{1,0:T(8,128)(2,1)} %copy-done.34, f32[1,768]{1,0:T(1,128)S(1)} %broadcast_in_dim.156.refs_2_, f32[1,768]{1,0:T(1,128)S(1)} %broadcast_in_dim.157.refs_3_, ...), custom_call_target="tpu_custom_call" | custom-call | flops 35999997952 | bytes 36000000 | tf_op jit(solution)/shard_map/project/pallas_call | solution.py:213
  104.9 18.8 %attend.3 = (bf16[1280,512]{1,0:T(8,128)(2,1)S(1)}, f32[1280,512]{1,0:T(8,128)}, bf16[8,592,512]{2,1,0:T(8,128)(2,1)}, bf16[8,1280,768]{2,1,0:T(8,128)(2,1)}) custom-call(bf16[1280,1536]{1,0:T(8,128)(2,1)} %project.3.q_ref.k_ref.v_ref, bf16[1280,1536]{1,0:T(8,128)(2,1)} %project.3.q_ref.k_ref.v_ref, bf16[1280,1536]{1,0:T(8,128)(2,1)} %project.3.q_ref.k_ref.v_ref, ...), custom_call_target="tpu_custom_call" | custom-call | flops 80000000000 | bytes 80000000 | tf_op jit(solution)/shard_map/attend/pallas_call | solution.py:327
  127.6 7.8 %merge.1 = (f32[1280,1024]{1,0:T(8,128)}, bf16[1280,1024]{1,0:T(8,128)(2,1)}) custom-call(bf16[256,1024]{1,0:T(8,128)(2,1)S(1)} %copy-done.18, bf16[256,1024]{1,0:T(8,128)(2,1)S(1)} %copy-done.20, bf16[256,1024]{1,0:T(8,128)(2,1)S(1)} %bitcast.210, bf16[256,1024]{1,0:T(8,128)(2,1)S(1)} %bitcast.212, bf16[1280,512]{1,0:T(8,128)(2,1)S(1)} %get-tuple-element.210.refs_4_.o_ref, ...), custom_call_target="tpu_custom_call" | custom-call | flops 32000000000 | bytes 32000000 | tf_op jit(solution)/shard_map/merge/pallas_call | solution.py:447
  142.8 14.6 %expand.2 = (bf16[1280,1024]{1,0:T(8,128)(2,1)}, bf16[1280,1024]{1,0:T(8,128)(2,1)}, bf16[1280,1024]{1,0:T(8,128)(2,1)}, bf16[1280,1024]{1,0:T(8,128)(2,1)}) custom-call(bf16[1280,1024]{1,0:T(8,128)(2,1)} %get-tuple-element.205.x_ref, bf16[1024,1024]{1,0:T(8,128)(2,1)S(1)} %bitcast.205, bf16[1024,1024]{1,0:T(8,128)(2,1)} %bitcast.203, ...), custom_call_target="tpu_custom_call" | custom-call | flops 56000000000 | bytes 56000000 | tf_op jit(solution)/shard_map/expand/pallas_call | solution.py:481
  157.4 5.9 %convolution_convert_fusion.7 = bf16[1024,1024]{1,0:T(8,128)(2,1)} fusion(bf16[1280,1024]{1,0:T(8,128)(2,1)} %get-tuple-element.189.refs_4_, bf16[1280,1024]{1,0:T(8,128)(2,1)S(1)} %collect.1.refs_9_), kind=kOutput, calls=%fused_computation.24 | convolution fusion | flops 2685403136 | bytes 7340032 | tf_op jit(solution)/shard_map/dot_general | solution.py:54
  163.6 14.0 %expand.3 = (bf16[1280,1024]{1,0:T(8,128)(2,1)}, bf16[1280,1024]{1,0:T(8,128)(2,1)}, bf16[1280,1024]{1,0:T(8,128)(2,1)}, bf16[1280,1024]{1,0:T(8,128)(2,1)}) custom-call(bf16[1280,1024]{1,0:T(8,128)(2,1)} %get-tuple-element.205.x_ref, bf16[1024,1024]{1,0:T(8,128)(2,1)S(1)} %get-tuple-element.421.refs_0_.refs_3_, ...), custom_call_target="tpu_custom_call" | custom-call | flops 56000000000 | bytes 56000000 | tf_op jit(solution)/shard_map/expand/pallas_call | solution.py:481
  226.9 6.3 %add_convert_fusion.2 = bf16[1024,1024]{1,0:T(8,128)(2,1)} fusion(bf16[1024,1024]{1,0:T(8,128)(2,1)} %collective-permute-done.12, bf16[1280,1024]{1,0:T(8,128)(2,1)} %get-tuple-element.205.x_ref, bf16[1280,1024]{1,0:T(8,128)(2,1)S(1)} %copy-done.43), kind=kOutput, calls=%fused_computation.8 | convolution fusion | flops 2687500288 | bytes 9437184 | tf_op jit(solution)/shard_map/dot_general | solution.py:54
  233.2 21.3 %back_norm.2 = (bf16[1280,1024]{1,0:T(8,128)(2,1)}, f32[4,8,1024]{2,1,0:T(8,128)S(1)}) custom-call(s32[4]{0:T(128)S(1)} %iota.92.at_ref, bf16[1024,1024]{1,0:T(8,128)(2,1)S(1)} %bitcast.204, bf16[1024,1024]{1,0:T(8,128)(2,1)} %bitcast.206, bf16[1024,1024]{1,0:T(8,128)(2,1)} %get-tuple-element.422.refs_1_.refs_2_, bf16[1024,1024]{1,0:T(8,128)(2,1)} %copy-done, ...), custom_call_target="tpu_custom_call" | custom-call | flops 400000000 | bytes 400000 | tf_op jit(solution)/shard_map/back_norm/pallas_call | solution.py:560
  273.2 17.3 %attend_back.4 = (bf16[1280,768]{1,0:T(8,128)(2,1)}, f32[8,768]{1,0:T(8,128)}) custom-call(bf16[1280,1536]{1,0:T(8,128)(2,1)} %project.3.q_ref.k_ref.v_ref, bf16[1280,1536]{1,0:T(8,128)(2,1)} %project.3.q_ref.k_ref.v_ref, bf16[1280,1536]{1,0:T(8,128)(2,1)} %project.3.q_ref.k_ref.v_ref, bf16[1280,256]{1,0:T(8,128)(2,1)} %convolution_convert_fusion.3.g_ref, ...), custom_call_target="tpu_custom_call" | custom-call | flops 64000000000 | bytes 64000000 | tf_op jit(solution)/shard_map/attend_back/pallas_call | solution.py:405
  304.4 10.9 %collective-permute-done.17 = bf16[1024,1024]{1,0:T(8,128)(2,1)S(1)} collective-permute-done((bf16[1024,1024]{1,0:T(8,128)(2,1)}, bf16[1024,1024]{1,0:T(8,128)(2,1)S(1)}, u32[]{:S(2)}, u32[]{:S(2)}) %collective-permute-start.17) | collective-permute-done | bytes 2097184 | tf_op jit(solution)/shard_map/ppermute | solution.py:696
  317.2 8.7 %collective-permute-done.18 = bf16[256,1024]{1,0:T(8,128)(2,1)} collective-permute-done((bf16[256,1024]{1,0:T(8,128)(2,1)}, bf16[256,1024]{1,0:T(8,128)(2,1)}, u32[]{:S(2)}, u32[]{:S(2)}) %collective-permute-start.18) | collective-permute-done | bytes 524320 | tf_op jit(solution)/shard_map/ppermute | solution.py:696
  330.8 17.4 %attend_back.5 = (bf16[1280,768]{1,0:T(8,128)(2,1)}, f32[8,768]{1,0:T(8,128)}) custom-call(bf16[1280,1536]{1,0:T(8,128)(2,1)} %project.3.q_ref.k_ref.v_ref, bf16[1280,1536]{1,0:T(8,128)(2,1)} %project.3.q_ref.k_ref.v_ref, bf16[1280,1536]{1,0:T(8,128)(2,1)} %project.3.q_ref.k_ref.v_ref, bf16[1280,256]{1,0:T(8,128)(2,1)} %convolution_convert_fusion.2.g_ref, ...), custom_call_target="tpu_custom_call" | custom-call | flops 64000000000 | bytes 64000000 | tf_op jit(solution)/shard_map/attend_back/pallas_call | solution.py:405
  349.0 6.2 %add_convert_fusion.7 = bf16[1024,768]{1,0:T(8,128)(2,1)} fusion(bf16[1024,768]{1,0:T(8,128)(2,1)} %collective-permute-done.20, bf16[1280,1024]{1,0:T(8,128)(2,1)} %get-tuple-element.246.x_ref, bf16[1280,768]{1,0:T(8,128)(2,1)} %get-tuple-element.228.refs_5_), kind=kOutput, calls=%fused_computation.13 | convolution fusion | flops 2015625216 | bytes 7733248 | tf_op jit(solution)/shard_map/dot_general | solution.py:54
  360.6 17.6 %attend_back.6 = (bf16[1280,768]{1,0:T(8,128)(2,1)}, f32[8,768]{1,0:T(8,128)}) custom-call(bf16[1280,1536]{1,0:T(8,128)(2,1)} %project.2.q_ref.k_ref.v_ref, bf16[1280,1536]{1,0:T(8,128)(2,1)} %project.2.q_ref.k_ref.v_ref, bf16[1280,1536]{1,0:T(8,128)(2,1)} %project.2.q_ref.k_ref.v_ref, bf16[1280,256]{1,0:T(8,128)(2,1)} %convolution_convert_fusion.1.g_ref, ...), custom_call_target="tpu_custom_call" | custom-call | flops 64000000000 | bytes 64000000 | tf_op jit(solution)/shard_map/attend_back/pallas_call | solution.py:405
  383.8 5.0 convolution_convert_fusion.8
  388.8 17.3 %attend_back.7 = (bf16[1280,768]{1,0:T(8,128)(2,1)}, f32[8,768]{1,0:T(8,128)}) custom-call(bf16[1280,1536]{1,0:T(8,128)(2,1)} %project.2.q_ref.k_ref.v_ref, bf16[1280,1536]{1,0:T(8,128)(2,1)} %project.2.q_ref.k_ref.v_ref, bf16[1280,1536]{1,0:T(8,128)(2,1)} %project.2.q_ref.k_ref.v_ref, bf16[1280,256]{1,0:T(8,128)(2,1)} %convolution_convert_fusion.g_ref, ...), custom_call_target="tpu_custom_call" | custom-call | flops 64000000000 | bytes 64000000 | tf_op jit(solution)/shard_map/attend_back/pallas_call | solution.py:405
  418.2 16.7 %back_norm.3 = (bf16[1280,1024]{1,0:T(8,128)(2,1)}, f32[4,8,1024]{2,1,0:T(8,128)S(1)}) custom-call(s32[4]{0:T(128)S(1)} %and_select_fusion.2.at_ref, bf16[1024,768]{1,0:T(8,128)(2,1)S(1)} %copy-done.35, bf16[1024,768]{1,0:T(8,128)(2,1)S(1)} %bitcast.209, bf16[1024,768]{1,0:T(8,128)(2,1)} %pad_maximum_fusion.1.refs_1_.refs_2_, ...), custom_call_target="tpu_custom_call" | custom-call | flops 80000000000 | bytes 80000000 | tf_op jit(solution)/shard_map/back_norm/pallas_call | solution.py:560
  443.3 18.5 %reduce_rows.1 = (bf16[640,1024]{1,0:T(8,128)(2,1)}, bf16[640,1024]{1,0:T(8,128)(2,1)S(1)}) custom-call(s32[1]{0:T(128)} %bitcast.side_ref.flag_ref, bf16[1024,1024]{1,0:T(8,128)(2,1)} %bitcast.231, bf16[1024,1024]{1,0:T(8,128)(2,1)} %bitcast.229, bf16[1024,1024]{1,0:T(8,128)(2,1)} %get-tuple-element.340.refs_2_, ...), custom_call_target="tpu_custom_call" | custom-call | flops 400000000 | bytes 400000 | tf_op jit(solution)/shard_map/reduce_rows/pallas_call | solution.py:514
  476.3 6.0 %collective-permute-done.36 = bf16[256,384]{1,0:T(8,128)(2,1)} collective-permute-done((bf16[256,384]{1,0:T(8,128)(2,1)S(1)}, bf16[256,384]{1,0:T(8,128)(2,1)}, u32[]{:S(2)}, u32[]{:S(2)}) %collective-permute-start.36) | collective-permute-done | bytes 196640 | tf_op jit(solution)/shard_map/ppermute | solution.py:693
  489.4 5.8 %collective-permute-done.39 = bf16[256,384]{1,0:T(8,128)(2,1)S(1)} collective-permute-done((bf16[256,384]{1,0:T(8,128)(2,1)S(1)}, bf16[256,384]{1,0:T(8,128)(2,1)S(1)}, u32[]{:S(2)}, u32[]{:S(2)}) %collective-permute-start.39) | collective-permute-done | bytes 196640 | tf_op jit(solution)/shard_map/ppermute | solution.py:693
  (442 shorter events, 228.6 us)
Async XLA Ops:
  7.2 118.8 %all-gather.7.cloned.1.call-start = ((), (), s32[]{:S(2)}) async-start(), calls=%async_computation.1 | async-start | bytes 5570560 | tf_op jit(solution)/shard_map/all_gather | solution.py:791
  9.1 28.0 %collective-permute-start = (bf16[256,768]{1,0:T(8,128)(2,1)}, bf16[256,768]{1,0:T(8,128)(2,1)}, u32[]{:S(2)}, u32[]{:S(2)}) collective-permute-start(bf16[256,768]{1,0:T(8,128)(2,1)} %pad_maximum_fusion.3), channel_id=1, source_target_pairs={{0,1},{1,0},{2,3},{3,2},{4,5},{5,4},{6,7},{7,6},{8,9},{9,8},{10,11... | collective-permute-start | bytes 1179656 | tf_op jit(solution)/shard_map/ppermute | solution.py:696
  14.5 41.0 %collective-permute-start.2 = (bf16[640,1024]{1,0:T(8,128)(2,1)}, bf16[640,1024]{1,0:T(8,128)(2,1)}, u32[]{:S(2)}, u32[]{:S(2)}) collective-permute-start(bf16[640,1024]{1,0:T(8,128)(2,1)} %dynamic-slice_bitcast_fusion.1), channel_id=1, source_target_pairs={{0,1},{1,0},{2,3},{3,2},{4,5},{5,4},{6,7},{7,6},{8,9},{9,8},{10,11... | collective-permute-start | bytes 3932168 | tf_op jit(solution)/shard_map/ppermute | solution.py:696
  69.6 116.8 %all-gather.5.cloned.1.call-start = ((), (), s32[]{:S(2)}) async-start(), calls=%async_computation | async-start | bytes 4456448 | tf_op jit(solution)/shard_map/all_gather | solution.py:791
  69.6 55.1 %collective-permute-start.3 = (bf16[128,1024]{1,0:T(8,128)(2,1)}, bf16[128,1024]{1,0:T(8,128)(2,1)}, u32[]{:S(2)}, u32[]{:S(2)}) collective-permute-start(bf16[128,1024]{1,0:T(8,128)(2,1)} %constant_dynamic-slice_fusion.34), channel_id=1, source_target_pairs={{0,1},{1,0},{2,3},{3,2},{4,5},{5,4},{6,7},{7,6},{8,9},{9,8},{10,11... | collective-permute-start | bytes 786440 | tf_op jit(solution)/shard_map/ppermute | solution.py:696
  94.8 45.3 %collective-permute-start.8 = (bf16[640,1024]{1,0:T(8,128)(2,1)}, bf16[640,1024]{1,0:T(8,128)(2,1)}, u32[]{:S(2)}, u32[]{:S(2)}) collective-permute-start(bf16[640,1024]{1,0:T(8,128)(2,1)} %dynamic-slice_bitcast_fusion), channel_id=1, source_target_pairs={{0,1},{1,0},{2,3},{3,2},{4,5},{5,4},{6,7},{7,6},{8,9},{9,8},{10,11... | collective-permute-start | bytes 3932168 | tf_op jit(solution)/shard_map/ppermute | solution.py:696
  124.7 344.1 %all-gather.9.cloned.1.call-start = ((), (), s32[]{:S(2)}) async-start(), calls=%async_computation.2 | async-start | bytes 4456448 | tf_op jit(solution)/shard_map/all_gather | solution.py:915
  221.6 48.7 %collective-permute-start.15 = (bf16[1024,1024]{1,0:T(8,128)(2,1)}, bf16[1024,1024]{1,0:T(8,128)(2,1)S(1)}, u32[]{:S(2)}, u32[]{:S(2)}) collective-permute-start(bf16[1024,1024]{1,0:T(8,128)(2,1)} %add_convert_fusion.5), channel_id=1, source_target_pairs={{0,1},{1,0},{2,3},{3,2},{4,5},{5,4},{6,7},{7,6},{8,9},{9,8},{10,11... | collective-permute-start | bytes 6291464 | tf_op jit(solution)/shard_map/ppermute | solution.py:696
  225.7 89.6 %collective-permute-start.17 = (bf16[1024,1024]{1,0:T(8,128)(2,1)}, bf16[1024,1024]{1,0:T(8,128)(2,1)S(1)}, u32[]{:S(2)}, u32[]{:S(2)}) collective-permute-start(bf16[1024,1024]{1,0:T(8,128)(2,1)} %add_convert_fusion.3), channel_id=1, source_target_pairs={{0,1},{1,0},{2,3},{3,2},{4,5},{5,4},{6,7},{7,6},{8,9},{9,8},{10,11... | collective-permute-start | bytes 6291464 | tf_op jit(solution)/shard_map/ppermute | solution.py:696
  272.5 25.1 %collective-permute-start.16 = (bf16[512,1024]{1,0:T(8,128)(2,1)}, bf16[512,1024]{1,0:T(8,128)(2,1)}, u32[]{:S(2)}, u32[]{:S(2)}) collective-permute-start(bf16[512,1024]{1,0:T(8,128)(2,1)} %bitcast.41), channel_id=1, source_target_pairs={{0,4},{2,6},{4,0},{6,2},{8,12},{10,14},{12,8},{14,10},{16,20},{18,... | collective-permute-start | bytes 3145736 | tf_op jit(solution)/shard_map/ppermute | solution.py:693
  290.4 35.4 %collective-permute-start.18 = (bf16[256,1024]{1,0:T(8,128)(2,1)}, bf16[256,1024]{1,0:T(8,128)(2,1)}, u32[]{:S(2)}, u32[]{:S(2)}) collective-permute-start(bf16[256,1024]{1,0:T(8,128)(2,1)} %add_convert_fusion.14), channel_id=1, source_target_pairs={{0,1},{1,0},{2,3},{3,2},{4,5},{5,4},{6,7},{7,6},{8,9},{9,8},{10,11... | collective-permute-start | bytes 1572872 | tf_op jit(solution)/shard_map/ppermute | solution.py:696
  299.2 29.3 %collective-permute-start.19 = (bf16[256,1024]{1,0:T(8,128)(2,1)S(1)}, bf16[256,1024]{1,0:T(8,128)(2,1)S(1)}, u32[]{:S(2)}, u32[]{:S(2)}) collective-permute-start(bf16[256,1024]{1,0:T(8,128)(2,1)S(1)} %bitcast.282), channel_id=1, source_target_pairs={{0,8},{2,10},{4,12},{6,14},{8,0},{10,2},{12,4},{14,6},{16,24},{18,... | collective-permute-start | bytes 1572872 | tf_op jit(solution)/shard_map/ppermute | solution.py:693
  304.4 44.7 %collective-permute-start.20 = (bf16[1024,768]{1,0:T(8,128)(2,1)}, bf16[1024,768]{1,0:T(8,128)(2,1)}, u32[]{:S(2)}, u32[]{:S(2)}) collective-permute-start(bf16[1024,768]{1,0:T(8,128)(2,1)} %convolution_convert_fusion.9), channel_id=1, source_target_pairs={{0,2},{2,0},{4,6},{6,4},{8,10},{10,8},{12,14},{14,12},{16,18},{18,... | collective-permute-start | bytes 4718600 | tf_op jit(solution)/shard_map/ppermute | solution.py:693
  316.5 38.8 %collective-permute-start.21 = (bf16[512,1024]{1,0:T(8,128)(2,1)S(1)}, bf16[512,1024]{1,0:T(8,128)(2,1)S(1)}, u32[]{:S(2)}, u32[]{:S(2)}) collective-permute-start(bf16[512,1024]{1,0:T(8,128)(2,1)S(1)} %bitcast.270), channel_id=1, source_target_pairs={{0,4},{2,6},{4,0},{6,2},{8,12},{10,14},{12,8},{14,10},{16,20},{18,... | collective-permute-start | bytes 3145736 | tf_op jit(solution)/shard_map/ppermute | solution.py:693
  327.8 27.8 %collective-permute-start.22 = (bf16[128,1024]{1,0:T(8,128)(2,1)}, bf16[128,1024]{1,0:T(8,128)(2,1)}, u32[]{:S(2)}, u32[]{:S(2)}) collective-permute-start(bf16[128,1024]{1,0:T(8,128)(2,1)} %bitcast.52), channel_id=1, source_target_pairs={{0,4},{2,6},{4,0},{6,2},{8,12},{10,14},{12,8},{14,10},{16,20},{18,... | collective-permute-start | bytes 786440 | tf_op jit(solution)/shard_map/ppermute | solution.py:693
  349.0 148.6 %all-gather.11.cloned.1.call-start = ((), (), s32[]{:S(2)}) async-start(), calls=%async_computation.3 | async-start | bytes 5570560 | tf_op jit(solution)/shard_map/all_gather | solution.py:932
  356.8 22.8 %collective-permute-start.23 = (bf16[256,1024]{1,0:T(8,128)(2,1)S(1)}, bf16[256,1024]{1,0:T(8,128)(2,1)S(1)}, u32[]{:S(2)}, u32[]{:S(2)}) collective-permute-start(bf16[256,1024]{1,0:T(8,128)(2,1)S(1)} %bitcast.283), channel_id=1, source_target_pairs={{0,8},{2,10},{4,12},{6,14},{8,0},{10,2},{12,4},{14,6},{16,24},{18,... | collective-permute-start | bytes 1572872 | tf_op jit(solution)/shard_map/ppermute | solution.py:693
  359.0 54.6 %collective-permute-start.26 = (bf16[1024,768]{1,0:T(8,128)(2,1)}, bf16[1024,768]{1,0:T(8,128)(2,1)}, u32[]{:S(2)}, u32[]{:S(2)}) collective-permute-start(bf16[1024,768]{1,0:T(8,128)(2,1)} %add_convert_fusion.7), channel_id=1, source_target_pairs={{0,1},{1,0},{2,3},{3,2},{4,5},{5,4},{6,7},{7,6},{8,9},{9,8},{10,11... | collective-permute-start | bytes 4718600 | tf_op jit(solution)/shard_map/ppermute | solution.py:696
  380.8 32.0 %collective-permute-start.41 = (bf16[128,1024]{1,0:T(8,128)(2,1)S(1)}, bf16[128,1024]{1,0:T(8,128)(2,1)S(1)}, u32[]{:S(2)}, u32[]{:S(2)}) collective-permute-start(bf16[128,1024]{1,0:T(8,128)(2,1)S(1)} %dynamic-slice_bitcast_fusion.8), channel_id=1, source_target_pairs={{0,16},{2,18},{4,20},{6,22},{8,24},{10,26},{12,28},{14,30},{16,0},... | collective-permute-start | bytes 786440 | tf_op jit(solution)/shard_map/ppermute | solution.py:693
  381.8 30.9 %collective-permute-start.42 = (bf16[32,1024]{1,0:T(8,128)(2,1)S(1)}, bf16[32,1024]{1,0:T(8,128)(2,1)S(1)}, u32[]{:S(2)}, u32[]{:S(2)}) collective-permute-start(bf16[32,1024]{1,0:T(8,128)(2,1)S(1)} %dynamic-slice_bitcast_fusion.15), channel_id=1, source_target_pairs={{0,16},{2,18},{4,20},{6,22},{8,24},{10,26},{12,28},{14,30},{16,0},... | collective-permute-start | bytes 196616 | tf_op jit(solution)/shard_map/ppermute | solution.py:693
  388.8 24.8 %collective-permute-start.25 = (bf16[1024,768]{1,0:T(8,128)(2,1)}, bf16[1024,768]{1,0:T(8,128)(2,1)}, u32[]{:S(2)}, u32[]{:S(2)}) collective-permute-start(bf16[1024,768]{1,0:T(8,128)(2,1)} %convolution_convert_fusion.8), channel_id=1, source_target_pairs={{0,2},{2,0},{4,6},{6,4},{8,10},{10,8},{12,14},{14,12},{16,18},{18,... | collective-permute-start | bytes 4718600 | tf_op jit(solution)/shard_map/ppermute | solution.py:693
  416.6 23.8 %collective-permute-start.27 = (bf16[512,384]{1,0:T(8,128)(2,1)S(1)}, bf16[512,384]{1,0:T(8,128)(2,1)S(1)}, u32[]{:S(2)}, u32[]{:S(2)}) collective-permute-start(bf16[512,384]{1,0:T(8,128)(2,1)S(1)} %bitcast.284), channel_id=1, source_target_pairs={{0,4},{2,6},{4,0},{6,2},{8,12},{10,14},{12,8},{14,10},{16,20},{18,... | collective-permute-start | bytes 1179656 | tf_op jit(solution)/shard_map/ppermute | solution.py:693
  438.1 29.6 %collective-permute-start.29 = (bf16[640,1024]{1,0:T(8,128)(2,1)}, bf16[640,1024]{1,0:T(8,128)(2,1)S(1)}, u32[]{:S(2)}, u32[]{:S(2)}) collective-permute-start(bf16[640,1024]{1,0:T(8,128)(2,1)} %get-tuple-element.351), channel_id=1, source_target_pairs={{0,1},{1,0},{2,3},{3,2},{4,5},{5,4},{6,7},{7,6},{8,9},{9,8},{10,11... | collective-permute-start | bytes 3932168 | tf_op jit(solution)/shard_map/ppermute | solution.py:696
  467.7 39.6 %collective-permute-start.30 = (bf16[640,1024]{1,0:T(8,128)(2,1)}, bf16[640,1024]{1,0:T(8,128)(2,1)}, u32[]{:S(2)}, u32[]{:S(2)}) collective-permute-start(bf16[640,1024]{1,0:T(8,128)(2,1)} %get-tuple-element.262), channel_id=1, source_target_pairs={{0,1},{1,0},{2,3},{3,2},{4,5},{5,4},{6,7},{7,6},{8,9},{9,8},{10,11... | collective-permute-start | bytes 3932168 | tf_op jit(solution)/shard_map/ppermute | solution.py:696
  (116 other events, 1144.1 us)
Sparse Core Ops, SparseCore 0:
  69.7 56.2 all-gather.6
  128.2 49.1 all-gather.4
  349.1 66.7 all-gather.8
  418.6 68.2 all-gather.10

commit v8 on v7

--- a/solution.py
+++ b/solution.py
@@ -851,7 +851,7 @@
         return did(low(wide(after(keep)) + wide(arrived)))
 
     def rows_out(keep, arrived, dtype):
-        return place_rows(sides, keep, arrived, 1, dtype).reshape(2, 1, length // 2, -1)
+        return place_rows(sides, keep, arrived, 4, dtype).reshape(2, 1, length // 2, -1)
 
     widen(FAR)
     sent = swap(product(active[FAR, SEND], grad_two), 0)

time: 538 us -> 540 us (level)
  transfers between devices with their start and end apart: 53 -> 53, of which waited for: 17 -> 17; matrix products, arithmetic and copies ran while one was open for 29% -> 28% of each run, Pallas kernels for 44% -> 44%
where the time goes in v8:
time: 540 us; the launch traced here: 531 us
  Pallas kernels  238 us (44%)
  matrix products  84.3 us (16%)
  local copies, waits for them, and re-layouts  51 us (9%)
  waiting for transfers between devices  49.5 us (9%)
  other arithmetic  47.5 us (9%)
  starting transfers between devices  43.4 us (8%)
  between operations  16.9 us (3%)
    pallas_call x4, Pallas kernels, attend_back(): pl.pallas_call(attend_back_kernel, grid=(pairs,), in_specs=parts + [pl.Bl...  69.6 us
    dot_general x14, matrix products, dot_tn(): lax.dot_general(left, right, (((0,), (0,)), ((), ())), preferred_element_...  60.3 us
    pallas_call x2, Pallas kernels, back_norm(): pl.pallas_call(functools.partial(back_kernel, len(lefts)), grid_spec=pltp...  38 us
    pallas_call x2, Pallas kernels, attend(): pl.pallas_call(attend_kernel, grid=(pairs,), in_specs=parts + [whole(arra...  37.6 us
    pallas_call x2, Pallas kernels, expand(): pl.pallas_call(functools.partial(expand_kernel, chunk, count), grid=(widt...  28.6 us
    ppermute x36, waiting for transfers between devices, swap(): lax.ppermute(array, 'dp', [(i, i ^ 1 << level) for i in range(spread)])  27.4 us
    ppermute x36, starting transfers between devices, swap(): lax.ppermute(array, 'dp', [(i, i ^ 1 << level) for i in range(spread)])  26.7 us
    dot_general x8, matrix products, dot_nt(): lax.dot_general(left, right, (((1,), (1,)), ((), ())), preferred_element_...  21.1 us
  transfers between devices with their start and end apart: 53, of which 17 were waited for; matrix products, arithmetic and copies ran while one was open for 28% of the time, Pallas kernels for 44%

profile of v8, /device:TPU:0, one launch (start us, length us, event | category | flops | bytes accessed | tf_op | source)
XLA Modules:
  0.0 530.7 jit_solution(9421250302620407098)
XLA Ops:
  41.0 5.2 constant_dynamic-slice_fusion.27
  55.6 5.0 enter.1
  60.6 8.9 %project.2.q_ref.k_ref.v_ref = bf16[1280,1536]{1,0:T(8,128)(2,1)} custom-call(bf16[1280,1024]{1,0:T(8,128)(2,1)} %get-tuple-element.246.x_ref, bf16[1024,768]{1,0:T(8,128)(2,1)S(1)} %copy-done.5, bf16[1024,768]{1,0:T(8,128)(2,1)} %pad_maximum_fusion.1.refs_1_.refs_2_, f32[1,768]{1,0:T(1,128)S(1)} %bitcast.221, f32[1,768]{1,0:T(1,128)S(1)} %bitcast.222, ...), custom_call_target="tpu_custom_call" | custom-call | flops 35999997952 | bytes 36000000 | tf_op jit(solution)/shard_map/project/pallas_call | solution.py:213
  75.9 18.9 %attend.2 = (bf16[1280,512]{1,0:T(8,128)(2,1)S(1)}, f32[1280,512]{1,0:T(8,128)}, bf16[8,592,512]{2,1,0:T(8,128)(2,1)}, bf16[8,1280,768]{2,1,0:T(8,128)(2,1)}) custom-call(bf16[1280,1536]{1,0:T(8,128)(2,1)} %project.2.q_ref.k_ref.v_ref, bf16[1280,1536]{1,0:T(8,128)(2,1)} %project.2.q_ref.k_ref.v_ref, bf16[1280,1536]{1,0:T(8,128)(2,1)} %project.2.q_ref.k_ref.v_ref, ...), custom_call_target="tpu_custom_call" | custom-call | flops 80000000000 | bytes 80000000 | tf_op jit(solution)/shard_map/attend/pallas_call | solution.py:327
  96.5 8.4 %project.3.q_ref.k_ref.v_ref = bf16[1280,1536]{1,0:T(8,128)(2,1)} custom-call(bf16[1280,1024]{1,0:T(8,128)(2,1)} %get-tuple-element.246.x_ref, bf16[1024,768]{1,0:T(8,128)(2,1)S(1)} %bitcast.208, bf16[1024,768]{1,0:T(8,128)(2,1)} %copy-done.34, f32[1,768]{1,0:T(1,128)S(1)} %broadcast_in_dim.156.refs_2_, f32[1,768]{1,0:T(1,128)S(1)} %broadcast_in_dim.157.refs_3_, ...), custom_call_target="tpu_custom_call" | custom-call | flops 35999997952 | bytes 36000000 | tf_op jit(solution)/shard_map/project/pallas_call | solution.py:213
  104.9 18.8 %attend.3 = (bf16[1280,512]{1,0:T(8,128)(2,1)S(1)}, f32[1280,512]{1,0:T(8,128)}, bf16[8,592,512]{2,1,0:T(8,128)(2,1)}, bf16[8,1280,768]{2,1,0:T(8,128)(2,1)}) custom-call(bf16[1280,1536]{1,0:T(8,128)(2,1)} %project.3.q_ref.k_ref.v_ref, bf16[1280,1536]{1,0:T(8,128)(2,1)} %project.3.q_ref.k_ref.v_ref, bf16[1280,1536]{1,0:T(8,128)(2,1)} %project.3.q_ref.k_ref.v_ref, ...), custom_call_target="tpu_custom_call" | custom-call | flops 80000000000 | bytes 80000000 | tf_op jit(solution)/shard_map/attend/pallas_call | solution.py:327
  127.6 7.8 %merge.1 = (f32[1280,1024]{1,0:T(8,128)}, bf16[1280,1024]{1,0:T(8,128)(2,1)}) custom-call(bf16[256,1024]{1,0:T(8,128)(2,1)S(1)} %copy-done.18, bf16[256,1024]{1,0:T(8,128)(2,1)S(1)} %copy-done.20, bf16[256,1024]{1,0:T(8,128)(2,1)S(1)} %bitcast.210, bf16[256,1024]{1,0:T(8,128)(2,1)S(1)} %bitcast.212, bf16[1280,512]{1,0:T(8,128)(2,1)S(1)} %get-tuple-element.210.refs_4_.o_ref, ...), custom_call_target="tpu_custom_call" | custom-call | flops 32000000000 | bytes 32000000 | tf_op jit(solution)/shard_map/merge/pallas_call | solution.py:447
  142.8 14.6 %expand.2 = (bf16[1280,1024]{1,0:T(8,128)(2,1)}, bf16[1280,1024]{1,0:T(8,128)(2,1)}, bf16[1280,1024]{1,0:T(8,128)(2,1)}, bf16[1280,1024]{1,0:T(8,128)(2,1)}) custom-call(bf16[1280,1024]{1,0:T(8,128)(2,1)} %get-tuple-element.205.x_ref, bf16[1024,1024]{1,0:T(8,128)(2,1)S(1)} %bitcast.205, bf16[1024,1024]{1,0:T(8,128)(2,1)} %bitcast.203, ...), custom_call_target="tpu_custom_call" | custom-call | flops 56000000000 | bytes 56000000 | tf_op jit(solution)/shard_map/expand/pallas_call | solution.py:481
  157.4 5.9 %convolution_convert_fusion.7 = bf16[1024,1024]{1,0:T(8,128)(2,1)} fusion(bf16[1280,1024]{1,0:T(8,128)(2,1)} %get-tuple-element.189.refs_4_, bf16[1280,1024]{1,0:T(8,128)(2,1)S(1)} %collect.1.refs_9_), kind=kOutput, calls=%fused_computation.24 | convolution fusion | flops 2685403136 | bytes 7340032 | tf_op jit(solution)/shard_map/dot_general | solution.py:54
  163.6 14.0 %expand.3 = (bf16[1280,1024]{1,0:T(8,128)(2,1)}, bf16[1280,1024]{1,0:T(8,128)(2,1)}, bf16[1280,1024]{1,0:T(8,128)(2,1)}, bf16[1280,1024]{1,0:T(8,128)(2,1)}) custom-call(bf16[1280,1024]{1,0:T(8,128)(2,1)} %get-tuple-element.205.x_ref, bf16[1024,1024]{1,0:T(8,128)(2,1)S(1)} %get-tuple-element.421.refs_0_.refs_3_, ...), custom_call_target="tpu_custom_call" | custom-call | flops 56000000000 | bytes 56000000 | tf_op jit(solution)/shard_map/expand/pallas_call | solution.py:481
  226.9 6.3 %add_convert_fusion.2 = bf16[1024,1024]{1,0:T(8,128)(2,1)} fusion(bf16[1024,1024]{1,0:T(8,128)(2,1)} %collective-permute-done.12, bf16[1280,1024]{1,0:T(8,128)(2,1)} %get-tuple-element.205.x_ref, bf16[1280,1024]{1,0:T(8,128)(2,1)S(1)} %copy-done.43), kind=kOutput, calls=%fused_computation.8 | convolution fusion | flops 2687500288 | bytes 9437184 | tf_op jit(solution)/shard_map/dot_general | solution.py:54
  233.2 21.3 %back_norm.2 = (bf16[1280,1024]{1,0:T(8,128)(2,1)}, f32[4,8,1024]{2,1,0:T(8,128)S(1)}) custom-call(s32[4]{0:T(128)S(1)} %iota.92.at_ref, bf16[1024,1024]{1,0:T(8,128)(2,1)S(1)} %bitcast.204, bf16[1024,1024]{1,0:T(8,128)(2,1)} %bitcast.206, bf16[1024,1024]{1,0:T(8,128)(2,1)} %get-tuple-element.422.refs_1_.refs_2_, bf16[1024,1024]{1,0:T(8,128)(2,1)} %copy-done, ...), custom_call_target="tpu_custom_call" | custom-call | flops 400000000 | bytes 400000 | tf_op jit(solution)/shard_map/back_norm/pallas_call | solution.py:560
  273.2 17.3 %attend_back.4 = (bf16[1280,768]{1,0:T(8,128)(2,1)}, f32[8,768]{1,0:T(8,128)}) custom-call(bf16[1280,1536]{1,0:T(8,128)(2,1)} %project.3.q_ref.k_ref.v_ref, bf16[1280,1536]{1,0:T(8,128)(2,1)} %project.3.q_ref.k_ref.v_ref, bf16[1280,1536]{1,0:T(8,128)(2,1)} %project.3.q_ref.k_ref.v_ref, bf16[1280,256]{1,0:T(8,128)(2,1)} %convolution_convert_fusion.3.g_ref, ...), custom_call_target="tpu_custom_call" | custom-call | flops 64000000000 | bytes 64000000 | tf_op jit(solution)/shard_map/attend_back/pallas_call | solution.py:405
  304.4 10.9 %collective-permute-done.17 = bf16[1024,1024]{1,0:T(8,128)(2,1)S(1)} collective-permute-done((bf16[1024,1024]{1,0:T(8,128)(2,1)}, bf16[1024,1024]{1,0:T(8,128)(2,1)S(1)}, u32[]{:S(2)}, u32[]{:S(2)}) %collective-permute-start.17) | collective-permute-done | bytes 2097184 | tf_op jit(solution)/shard_map/ppermute | solution.py:696
  317.2 8.7 %collective-permute-done.18 = bf16[256,1024]{1,0:T(8,128)(2,1)} collective-permute-done((bf16[256,1024]{1,0:T(8,128)(2,1)}, bf16[256,1024]{1,0:T(8,128)(2,1)}, u32[]{:S(2)}, u32[]{:S(2)}) %collective-permute-start.18) | collective-permute-done | bytes 524320 | tf_op jit(solution)/shard_map/ppermute | solution.py:696
  330.8 17.4 %attend_back.5 = (bf16[1280,768]{1,0:T(8,128)(2,1)}, f32[8,768]{1,0:T(8,128)}) custom-call(bf16[1280,1536]{1,0:T(8,128)(2,1)} %project.3.q_ref.k_ref.v_ref, bf16[1280,1536]{1,0:T(8,128)(2,1)} %project.3.q_ref.k_ref.v_ref, bf16[1280,1536]{1,0:T(8,128)(2,1)} %project.3.q_ref.k_ref.v_ref, bf16[1280,256]{1,0:T(8,128)(2,1)} %convolution_convert_fusion.2.g_ref, ...), custom_call_target="tpu_custom_call" | custom-call | flops 64000000000 | bytes 64000000 | tf_op jit(solution)/shard_map/attend_back/pallas_call | solution.py:405
  349.0 6.2 %add_convert_fusion.7 = bf16[1024,768]{1,0:T(8,128)(2,1)} fusion(bf16[1024,768]{1,0:T(8,128)(2,1)} %collective-permute-done.20, bf16[1280,1024]{1,0:T(8,128)(2,1)} %get-tuple-element.246.x_ref, bf16[1280,768]{1,0:T(8,128)(2,1)} %get-tuple-element.228.refs_5_), kind=kOutput, calls=%fused_computation.13 | convolution fusion | flops 2015625216 | bytes 7733248 | tf_op jit(solution)/shard_map/dot_general | solution.py:54
  360.6 17.6 %attend_back.6 = (bf16[1280,768]{1,0:T(8,128)(2,1)}, f32[8,768]{1,0:T(8,128)}) custom-call(bf16[1280,1536]{1,0:T(8,128)(2,1)} %project.2.q_ref.k_ref.v_ref, bf16[1280,1536]{1,0:T(8,128)(2,1)} %project.2.q_ref.k_ref.v_ref, bf16[1280,1536]{1,0:T(8,128)(2,1)} %project.2.q_ref.k_ref.v_ref, bf16[1280,256]{1,0:T(8,128)(2,1)} %convolution_convert_fusion.1.g_ref, ...), custom_call_target="tpu_custom_call" | custom-call | flops 64000000000 | bytes 64000000 | tf_op jit(solution)/shard_map/attend_back/pallas_call | solution.py:405
  383.8 5.0 convolution_convert_fusion.8
  388.8 17.3 %attend_back.7 = (bf16[1280,768]{1,0:T(8,128)(2,1)}, f32[8,768]{1,0:T(8,128)}) custom-call(bf16[1280,1536]{1,0:T(8,128)(2,1)} %project.2.q_ref.k_ref.v_ref, bf16[1280,1536]{1,0:T(8,128)(2,1)} %project.2.q_ref.k_ref.v_ref, bf16[1280,1536]{1,0:T(8,128)(2,1)} %project.2.q_ref.k_ref.v_ref, bf16[1280,256]{1,0:T(8,128)(2,1)} %convolution_convert_fusion.g_ref, ...), custom_call_target="tpu_custom_call" | custom-call | flops 64000000000 | bytes 64000000 | tf_op jit(solution)/shard_map/attend_back/pallas_call | solution.py:405
  418.2 16.7 %back_norm.3 = (bf16[1280,1024]{1,0:T(8,128)(2,1)}, f32[4,8,1024]{2,1,0:T(8,128)S(1)}) custom-call(s32[4]{0:T(128)S(1)} %and_select_fusion.2.at_ref, bf16[1024,768]{1,0:T(8,128)(2,1)S(1)} %copy-done.35, bf16[1024,768]{1,0:T(8,128)(2,1)S(1)} %bitcast.209, bf16[1024,768]{1,0:T(8,128)(2,1)} %pad_maximum_fusion.1.refs_1_.refs_2_, ...), custom_call_target="tpu_custom_call" | custom-call | flops 80000000000 | bytes 80000000 | tf_op jit(solution)/shard_map/back_norm/pallas_call | solution.py:560
  443.3 18.5 %reduce_rows.1 = (bf16[640,1024]{1,0:T(8,128)(2,1)}, bf16[640,1024]{1,0:T(8,128)(2,1)S(1)}) custom-call(s32[1]{0:T(128)} %bitcast.side_ref.flag_ref, bf16[1024,1024]{1,0:T(8,128)(2,1)} %bitcast.231, bf16[1024,1024]{1,0:T(8,128)(2,1)} %bitcast.229, bf16[1024,1024]{1,0:T(8,128)(2,1)} %get-tuple-element.340.refs_2_, ...), custom_call_target="tpu_custom_call" | custom-call | flops 400000000 | bytes 400000 | tf_op jit(solution)/shard_map/reduce_rows/pallas_call | solution.py:514
  476.3 6.0 %collective-permute-done.36 = bf16[256,384]{1,0:T(8,128)(2,1)} collective-permute-done((bf16[256,384]{1,0:T(8,128)(2,1)S(1)}, bf16[256,384]{1,0:T(8,128)(2,1)}, u32[]{:S(2)}, u32[]{:S(2)}) %collective-permute-start.36) | collective-permute-done | bytes 196640 | tf_op jit(solution)/shard_map/ppermute | solution.py:693
  508.3 5.6 %place.3 = bf16[1280,1024]{1,0:T(8,128)(2,1)} custom-call(s32[1]{0:T(128)} %bitcast.side_ref.flag_ref, bf16[640,1024]{1,0:T(8,128)(2,1)S(1)} %copy-done.37, bf16[640,1024]{1,0:T(8,128)(2,1)} %collective-permute-done.30.theirs_ref), custom_call_target="tpu_custom_call" | custom-call | flops 16000000000 | bytes 16000000 | tf_op jit(solution)/shard_map/place/pallas_call | solution.py:597
  (442 shorter events, 231.6 us)
Async XLA Ops:
  7.2 118.8 %all-gather.7.cloned.1.call-start = ((), (), s32[]{:S(2)}) async-start(), calls=%async_computation.1 | async-start | bytes 5570560 | tf_op jit(solution)/shard_map/all_gather | solution.py:791
  9.1 28.0 %collective-permute-start = (bf16[256,768]{1,0:T(8,128)(2,1)}, bf16[256,768]{1,0:T(8,128)(2,1)}, u32[]{:S(2)}, u32[]{:S(2)}) collective-permute-start(bf16[256,768]{1,0:T(8,128)(2,1)} %pad_maximum_fusion.3), channel_id=1, source_target_pairs={{0,1},{1,0},{2,3},{3,2},{4,5},{5,4},{6,7},{7,6},{8,9},{9,8},{10,11... | collective-permute-start | bytes 1179656 | tf_op jit(solution)/shard_map/ppermute | solution.py:696
  14.5 41.0 %collective-permute-start.2 = (bf16[640,1024]{1,0:T(8,128)(2,1)}, bf16[640,1024]{1,0:T(8,128)(2,1)}, u32[]{:S(2)}, u32[]{:S(2)}) collective-permute-start(bf16[640,1024]{1,0:T(8,128)(2,1)} %dynamic-slice_bitcast_fusion.1), channel_id=1, source_target_pairs={{0,1},{1,0},{2,3},{3,2},{4,5},{5,4},{6,7},{7,6},{8,9},{9,8},{10,11... | collective-permute-start | bytes 3932168 | tf_op jit(solution)/shard_map/ppermute | solution.py:696
  69.6 116.8 %all-gather.5.cloned.1.call-start = ((), (), s32[]{:S(2)}) async-start(), calls=%async_computation | async-start | bytes 4456448 | tf_op jit(solution)/shard_map/all_gather | solution.py:791
  69.6 55.1 %collective-permute-start.3 = (bf16[128,1024]{1,0:T(8,128)(2,1)}, bf16[128,1024]{1,0:T(8,128)(2,1)}, u32[]{:S(2)}, u32[]{:S(2)}) collective-permute-start(bf16[128,1024]{1,0:T(8,128)(2,1)} %constant_dynamic-slice_fusion.34), channel_id=1, source_target_pairs={{0,1},{1,0},{2,3},{3,2},{4,5},{5,4},{6,7},{7,6},{8,9},{9,8},{10,11... | collective-permute-start | bytes 786440 | tf_op jit(solution)/shard_map/ppermute | solution.py:696
  94.8 45.3 %collective-permute-start.8 = (bf16[640,1024]{1,0:T(8,128)(2,1)}, bf16[640,1024]{1,0:T(8,128)(2,1)}, u32[]{:S(2)}, u32[]{:S(2)}) collective-permute-start(bf16[640,1024]{1,0:T(8,128)(2,1)} %dynamic-slice_bitcast_fusion), channel_id=1, source_target_pairs={{0,1},{1,0},{2,3},{3,2},{4,5},{5,4},{6,7},{7,6},{8,9},{9,8},{10,11... | collective-permute-start | bytes 3932168 | tf_op jit(solution)/shard_map/ppermute | solution.py:696
  124.7 344.1 %all-gather.9.cloned.1.call-start = ((), (), s32[]{:S(2)}) async-start(), calls=%async_computation.2 | async-start | bytes 4456448 | tf_op jit(solution)/shard_map/all_gather | solution.py:915
  221.6 48.7 %collective-permute-start.15 = (bf16[1024,1024]{1,0:T(8,128)(2,1)}, bf16[1024,1024]{1,0:T(8,128)(2,1)S(1)}, u32[]{:S(2)}, u32[]{:S(2)}) collective-permute-start(bf16[1024,1024]{1,0:T(8,128)(2,1)} %add_convert_fusion.5), channel_id=1, source_target_pairs={{0,1},{1,0},{2,3},{3,2},{4,5},{5,4},{6,7},{7,6},{8,9},{9,8},{10,11... | collective-permute-start | bytes 6291464 | tf_op jit(solution)/shard_map/ppermute | solution.py:696
  225.7 89.6 %collective-permute-start.17 = (bf16[1024,1024]{1,0:T(8,128)(2,1)}, bf16[1024,1024]{1,0:T(8,128)(2,1)S(1)}, u32[]{:S(2)}, u32[]{:S(2)}) collective-permute-start(bf16[1024,1024]{1,0:T(8,128)(2,1)} %add_convert_fusion.3), channel_id=1, source_target_pairs={{0,1},{1,0},{2,3},{3,2},{4,5},{5,4},{6,7},{7,6},{8,9},{9,8},{10,11... | collective-permute-start | bytes 6291464 | tf_op jit(solution)/shard_map/ppermute | solution.py:696
  272.5 25.1 %collective-permute-start.16 = (bf16[512,1024]{1,0:T(8,128)(2,1)}, bf16[512,1024]{1,0:T(8,128)(2,1)}, u32[]{:S(2)}, u32[]{:S(2)}) collective-permute-start(bf16[512,1024]{1,0:T(8,128)(2,1)} %bitcast.41), channel_id=1, source_target_pairs={{0,4},{2,6},{4,0},{6,2},{8,12},{10,14},{12,8},{14,10},{16,20},{18,... | collective-permute-start | bytes 3145736 | tf_op jit(solution)/shard_map/ppermute | solution.py:693
  290.4 35.4 %collective-permute-start.18 = (bf16[256,1024]{1,0:T(8,128)(2,1)}, bf16[256,1024]{1,0:T(8,128)(2,1)}, u32[]{:S(2)}, u32[]{:S(2)}) collective-permute-start(bf16[256,1024]{1,0:T(8,128)(2,1)} %add_convert_fusion.14), channel_id=1, source_target_pairs={{0,1},{1,0},{2,3},{3,2},{4,5},{5,4},{6,7},{7,6},{8,9},{9,8},{10,11... | collective-permute-start | bytes 1572872 | tf_op jit(solution)/shard_map/ppermute | solution.py:696
  299.2 29.3 %collective-permute-start.19 = (bf16[256,1024]{1,0:T(8,128)(2,1)S(1)}, bf16[256,1024]{1,0:T(8,128)(2,1)S(1)}, u32[]{:S(2)}, u32[]{:S(2)}) collective-permute-start(bf16[256,1024]{1,0:T(8,128)(2,1)S(1)} %bitcast.282), channel_id=1, source_target_pairs={{0,8},{2,10},{4,12},{6,14},{8,0},{10,2},{12,4},{14,6},{16,24},{18,... | collective-permute-start | bytes 1572872 | tf_op jit(solution)/shard_map/ppermute | solution.py:693
  304.4 44.7 %collective-permute-start.20 = (bf16[1024,768]{1,0:T(8,128)(2,1)}, bf16[1024,768]{1,0:T(8,128)(2,1)}, u32[]{:S(2)}, u32[]{:S(2)}) collective-permute-start(bf16[1024,768]{1,0:T(8,128)(2,1)} %convolution_convert_fusion.9), channel_id=1, source_target_pairs={{0,2},{2,0},{4,6},{6,4},{8,10},{10,8},{12,14},{14,12},{16,18},{18,... | collective-permute-start | bytes 4718600 | tf_op jit(solution)/shard_map/ppermute | solution.py:693
  316.5 38.8 %collective-permute-start.21 = (bf16[512,1024]{1,0:T(8,128)(2,1)S(1)}, bf16[512,1024]{1,0:T(8,128)(2,1)S(1)}, u32[]{:S(2)}, u32[]{:S(2)}) collective-permute-start(bf16[512,1024]{1,0:T(8,128)(2,1)S(1)} %bitcast.270), channel_id=1, source_target_pairs={{0,4},{2,6},{4,0},{6,2},{8,12},{10,14},{12,8},{14,10},{16,20},{18,... | collective-permute-start | bytes 3145736 | tf_op jit(solution)/shard_map/ppermute | solution.py:693
  327.8 27.8 %collective-permute-start.22 = (bf16[128,1024]{1,0:T(8,128)(2,1)}, bf16[128,1024]{1,0:T(8,128)(2,1)}, u32[]{:S(2)}, u32[]{:S(2)}) collective-permute-start(bf16[128,1024]{1,0:T(8,128)(2,1)} %bitcast.52), channel_id=1, source_target_pairs={{0,4},{2,6},{4,0},{6,2},{8,12},{10,14},{12,8},{14,10},{16,20},{18,... | collective-permute-start | bytes 786440 | tf_op jit(solution)/shard_map/ppermute | solution.py:693
  349.0 148.6 %all-gather.11.cloned.1.call-start = ((), (), s32[]{:S(2)}) async-start(), calls=%async_computation.3 | async-start | bytes 5570560 | tf_op jit(solution)/shard_map/all_gather | solution.py:932
  356.8 22.8 %collective-permute-start.23 = (bf16[256,1024]{1,0:T(8,128)(2,1)S(1)}, bf16[256,1024]{1,0:T(8,128)(2,1)S(1)}, u32[]{:S(2)}, u32[]{:S(2)}) collective-permute-start(bf16[256,1024]{1,0:T(8,128)(2,1)S(1)} %bitcast.283), channel_id=1, source_target_pairs={{0,8},{2,10},{4,12},{6,14},{8,0},{10,2},{12,4},{14,6},{16,24},{18,... | collective-permute-start | bytes 1572872 | tf_op jit(solution)/shard_map/ppermute | solution.py:693
  359.0 54.6 %collective-permute-start.26 = (bf16[1024,768]{1,0:T(8,128)(2,1)}, bf16[1024,768]{1,0:T(8,128)(2,1)}, u32[]{:S(2)}, u32[]{:S(2)}) collective-permute-start(bf16[1024,768]{1,0:T(8,128)(2,1)} %add_convert_fusion.7), channel_id=1, source_target_pairs={{0,1},{1,0},{2,3},{3,2},{4,5},{5,4},{6,7},{7,6},{8,9},{9,8},{10,11... | collective-permute-start | bytes 4718600 | tf_op jit(solution)/shard_map/ppermute | solution.py:696
  380.8 32.0 %collective-permute-start.41 = (bf16[128,1024]{1,0:T(8,128)(2,1)S(1)}, bf16[128,1024]{1,0:T(8,128)(2,1)S(1)}, u32[]{:S(2)}, u32[]{:S(2)}) collective-permute-start(bf16[128,1024]{1,0:T(8,128)(2,1)S(1)} %dynamic-slice_bitcast_fusion.8), channel_id=1, source_target_pairs={{0,16},{2,18},{4,20},{6,22},{8,24},{10,26},{12,28},{14,30},{16,0},... | collective-permute-start | bytes 786440 | tf_op jit(solution)/shard_map/ppermute | solution.py:693
  381.8 30.9 %collective-permute-start.42 = (bf16[32,1024]{1,0:T(8,128)(2,1)S(1)}, bf16[32,1024]{1,0:T(8,128)(2,1)S(1)}, u32[]{:S(2)}, u32[]{:S(2)}) collective-permute-start(bf16[32,1024]{1,0:T(8,128)(2,1)S(1)} %dynamic-slice_bitcast_fusion.15), channel_id=1, source_target_pairs={{0,16},{2,18},{4,20},{6,22},{8,24},{10,26},{12,28},{14,30},{16,0},... | collective-permute-start | bytes 196616 | tf_op jit(solution)/shard_map/ppermute | solution.py:693
  388.8 24.8 %collective-permute-start.25 = (bf16[1024,768]{1,0:T(8,128)(2,1)}, bf16[1024,768]{1,0:T(8,128)(2,1)}, u32[]{:S(2)}, u32[]{:S(2)}) collective-permute-start(bf16[1024,768]{1,0:T(8,128)(2,1)} %convolution_convert_fusion.8), channel_id=1, source_target_pairs={{0,2},{2,0},{4,6},{6,4},{8,10},{10,8},{12,14},{14,12},{16,18},{18,... | collective-permute-start | bytes 4718600 | tf_op jit(solution)/shard_map/ppermute | solution.py:693
  416.6 23.8 %collective-permute-start.27 = (bf16[512,384]{1,0:T(8,128)(2,1)S(1)}, bf16[512,384]{1,0:T(8,128)(2,1)S(1)}, u32[]{:S(2)}, u32[]{:S(2)}) collective-permute-start(bf16[512,384]{1,0:T(8,128)(2,1)S(1)} %bitcast.284), channel_id=1, source_target_pairs={{0,4},{2,6},{4,0},{6,2},{8,12},{10,14},{12,8},{14,10},{16,20},{18,... | collective-permute-start | bytes 1179656 | tf_op jit(solution)/shard_map/ppermute | solution.py:693
  438.1 29.6 %collective-permute-start.29 = (bf16[640,1024]{1,0:T(8,128)(2,1)}, bf16[640,1024]{1,0:T(8,128)(2,1)S(1)}, u32[]{:S(2)}, u32[]{:S(2)}) collective-permute-start(bf16[640,1024]{1,0:T(8,128)(2,1)} %get-tuple-element.351), channel_id=1, source_target_pairs={{0,1},{1,0},{2,3},{3,2},{4,5},{5,4},{6,7},{7,6},{8,9},{9,8},{10,11... | collective-permute-start | bytes 3932168 | tf_op jit(solution)/shard_map/ppermute | solution.py:696
  467.7 39.6 %collective-permute-start.30 = (bf16[640,1024]{1,0:T(8,128)(2,1)}, bf16[640,1024]{1,0:T(8,128)(2,1)}, u32[]{:S(2)}, u32[]{:S(2)}) collective-permute-start(bf16[640,1024]{1,0:T(8,128)(2,1)} %get-tuple-element.262), channel_id=1, source_target_pairs={{0,1},{1,0},{2,3},{3,2},{4,5},{5,4},{6,7},{7,6},{8,9},{9,8},{10,11... | collective-permute-start | bytes 3932168 | tf_op jit(solution)/shard_map/ppermute | solution.py:696
  (116 other events, 1149.4 us)
Sparse Core Ops, SparseCore 0:
  69.7 56.2 all-gather.6
  128.2 49.1 all-gather.4
  349.1 66.7 all-gather.8
  418.6 68.2 all-gather.10
